TPU v7x, 128 devices: a whole 4x4x4 slice. The times are simulated.
128 devices in a mesh: req: 4 (over x_lo, core), head: 32 (over z, y, x_hi).
Axes of the slice: x: 4 (x_hi: 2, x_lo: 2; x = x_hi * 2 + x_lo), y: 4, z: 4, core: 2. Of those that a mesh axis runs over, the one named last changes fastest.
Arguments:
- x_input: bfloat16 [8, 512, 16384], P('req', None, 'head'), may hold values from -6 to 6
- z_gate: bfloat16 [8, 512, 16384], P('req', None, 'head'), may hold values from -6 to 6
- bc_input: bfloat16 [8, 512, 4096], P('req'), may hold values from -6 to 6
- dt_raw: float32 [8, 256, 512], P('req', 'head'), may hold values from -7 to 1.25
- a_log: float32 [256], P('head'), may hold values from -3 to 1.26
- d_skip: float32 [256], P('head'), may hold values from 0.5 to 2
- conv_x: bfloat16 [4, 16384], P(None, 'head'), may hold values from -3 to 3
- conv_bc: bfloat16 [4, 4096], replicated, may hold values from -3 to 3
- out_weight: bfloat16 [16384, 8192], P('head'), may hold values from -0.046875 to 0.046875
- pool_state: float32 [16, 16384, 256], P('req', 'head'), may hold values from -1.75 to 1.75
- pool_xtail: bfloat16 [16, 3, 16384], P('req', None, 'head'), may hold values from -6 to 6
- pool_bctail: bfloat16 [16, 3, 4096], P('req'), may hold values from -6 to 6
- pool_dev: int32 [8, 1], replicated, may hold values from 0 to 3; in each aligned block of 2 rows (0 to 1, 2 to 3, ...) at most 2 rows name the same one
- pool_slot: int32 [8], replicated, may hold values from 0 to 3
- lengths: int32 [8], P('req'), may hold values from 128 to 512, as said below
Outputs:
- mixed: float32 [8, 512, 8192], P('req', 'head')
- final_state: float32 [8, 16384, 256], P('req', 'head')
Inputs may be any that keep to these rules, and one draw needn't show every extreme that they name: pool_dev[r, 0] is the pool shard, an index of req, that holds request r's cached prefix; among the 2 requests of one request group no shard is named by more than 2 requests, and in some group one shard is named by exactly 2. `lengths`: in every draw the longest suffix has exactly 512 positions and the shortest exactly 128.
All inputs are finite; a program needn't handle non-finite values.
Results may differ from a plain program's by a relative error of at most 0.0039.
Values sent between devices are 32-bit elements; how exact they have to be, the bound alone decides.
No kernel may reach another device: no remote copies, remote signals or barrier semaphores. Data moves between devices by JAX's collectives and lax.ppermute only.
A program may use at most 128 MiB of HBM per device.

v0:
```python
import jax
import jax.numpy as jnp
from jax import lax
from jax.sharding import PartitionSpec as P

HEADS = 256
STATE = 256
GROUPS = 8
BLOCK = 128


def from_root(value, axis, source):
    kept = jnp.where(lax.axis_index(axis) == source, value, 0).astype(value.dtype)
    return lax.psum(kept, axis)


def conv_silu(prefix_rows, sequence, kernel):
    window = jnp.concatenate([prefix_rows, sequence.astype(jnp.float32)], axis=-2)
    length = sequence.shape[-2]
    accumulated = jnp.zeros(sequence.shape, jnp.float32)
    for offset in range(kernel.shape[0]):
        accumulated = accumulated + window[..., offset : offset + length, :] * kernel[
            offset
        ].astype(jnp.float32)
    return jax.nn.silu(accumulated).astype(jnp.bfloat16)


def block_scan(values, b_rows, c_rows, time_step, decay_rate, d_skip, initial):
    length, head_count, head_width = values.shape
    state_size = b_rows.shape[1]
    blocks = length // BLOCK
    inputs = values.astype(jnp.float32).reshape(blocks, BLOCK, head_count, head_width)
    b_narrow = b_rows.reshape(blocks, BLOCK, state_size)
    c_narrow = c_rows.reshape(blocks, BLOCK, state_size)
    b_block = b_narrow.astype(jnp.float32)
    c_block = c_narrow.astype(jnp.float32)
    step_block = time_step.reshape(head_count, blocks, BLOCK)
    decay_log = jnp.cumsum(-decay_rate[:, None, None] * step_block, axis=2)
    scores = jnp.einsum("cin,cjn->cij", c_narrow, b_narrow, preferred_element_type=jnp.float32)
    causal = jnp.arange(BLOCK)[:, None] >= jnp.arange(BLOCK)[None, :]
    log_gap = jnp.where(causal, decay_log[:, :, :, None] - decay_log[:, :, None, :], 0.0)
    mixing = jnp.where(causal, jnp.exp(log_gap), 0.0) * scores[None] * step_block[:, :, None, :]
    within = jnp.einsum("hcij,cjhp->cihp", mixing, inputs, precision=lax.Precision.HIGHEST)
    weight_in = jnp.transpose(jnp.exp(decay_log[:, :, -1:] - decay_log) * step_block, (1, 2, 0))
    block_state = jnp.einsum(
        "cjhp,cjn->chpn",
        inputs * weight_in[:, :, :, None],
        b_block,
        precision=lax.Precision.HIGHEST,
    )
    factor = jnp.transpose(jnp.exp(decay_log[:, :, -1]))

    def advance(running, pieces):
        shrink, addend = pieces
        return (shrink[:, None, None] * running + addend, running)

    closing, entering = lax.scan(advance, initial, (factor, block_state))
    carried = jnp.einsum("cin,chpn->cihp", c_block, entering, precision=lax.Precision.HIGHEST)
    carried = carried * jnp.exp(jnp.transpose(decay_log, (1, 2, 0)))[:, :, :, None]
    output = within + carried + d_skip[None, None, :, None] * inputs
    return (output.reshape(length, head_count, head_width), closing)


def own_group(array, group_index):
    b_part = lax.dynamic_slice_in_dim(array, group_index * STATE, STATE, array.ndim - 1)
    c_part = lax.dynamic_slice_in_dim(array, (GROUPS + group_index) * STATE, STATE, array.ndim - 1)
    return jnp.concatenate([b_part, c_part], axis=-1)


def on_device(
    x_input,
    z_gate,
    bc_input,
    dt_raw,
    a_log,
    d_skip,
    conv_x,
    conv_bc,
    out_weight,
    pool_state,
    pool_xtail,
    pool_bctail,
    pool_dev,
    pool_slot,
    lengths,
):
    req_count = lax.axis_size("req")
    my_req = lax.axis_index("req")
    head_count = a_log.shape[0]
    requests = lengths.shape[0]
    length = x_input.shape[1]
    shard_width = x_input.shape[2]
    head_width = shard_width // head_count
    group_index = lax.axis_index("head") * head_count // (HEADS // GROUPS)
    tail_table = jnp.concatenate([pool_xtail, own_group(pool_bctail, group_index)], axis=-1).astype(
        jnp.float32
    )
    tail_shape = tail_table.shape[1:]
    hit_list = pool_dev[:, 0]
    state_cells = shard_width * STATE

    def fetch_one(request, carried):
        start_rows, tail_rows = carried
        slot_here = pool_slot[request]
        packed = jnp.concatenate(
            [
                lax.dynamic_index_in_dim(pool_state, slot_here, 0, keepdims=False).reshape(-1),
                lax.dynamic_index_in_dim(tail_table, slot_here, 0, keepdims=False).reshape(-1),
            ]
        )
        received = from_root(packed, "req", hit_list[request])
        local_row = request - my_req * requests
        owned_here = (local_row >= 0) & (local_row < requests)
        target = jnp.clip(local_row, 0, requests - 1)
        new_starts = lax.dynamic_update_index_in_dim(
            start_rows, received[:state_cells].reshape(shard_width, STATE), target, 0
        )
        new_tails = lax.dynamic_update_index_in_dim(
            tail_rows, received[state_cells:].reshape(tail_shape), target, 0
        )
        return (
            jnp.where(owned_here, new_starts, start_rows),
            jnp.where(owned_here, new_tails, tail_rows),
        )

    blank_rows = (
        jnp.zeros((requests, shard_width, STATE), jnp.float32),
        jnp.zeros((requests,) + tail_shape, jnp.float32),
    )
    start_rows, tail_rows = lax.fori_loop(0, req_count * requests, fetch_one, blank_rows)
    x_conv = conv_silu(tail_rows[:, :, :shard_width], x_input, conv_x)
    bc_conv = conv_silu(
        tail_rows[:, :, shard_width:],
        own_group(bc_input, group_index),
        own_group(conv_bc, group_index),
    )
    live_mask = (jnp.arange(length)[None, :] < lengths[:, None]).astype(jnp.float32)
    time_step = jax.nn.softplus(dt_raw) * live_mask[:, None, :]
    decay_rate = jnp.exp(a_log)
    head_x = x_conv.reshape(requests, length, head_count, head_width)
    initial = start_rows.reshape(requests, head_count, head_width, STATE)
    gate_rows = jax.nn.silu(z_gate.astype(jnp.float32)) * live_mask[:, :, None]
    rows_here = length // lax.axis_size("head")
    scan_batch = jax.vmap(block_scan, in_axes=(0, 0, 0, 0, None, None, 0))
    outputs, closing = scan_batch(
        head_x, bc_conv[..., :STATE], bc_conv[..., STATE:], time_step, decay_rate, d_skip, initial
    )
    gated_rows = (outputs.reshape(requests, length, shard_width) * gate_rows).astype(jnp.bfloat16)
    by_position = jnp.swapaxes(gated_rows, 0, 1)
    product = jnp.dot(
        by_position.reshape(rows_here * lax.axis_size("head") * requests, shard_width),
        out_weight,
        preferred_element_type=jnp.float32,
    )
    summed = lax.psum_scatter(
        product.reshape(rows_here * lax.axis_size("head"), requests, out_weight.shape[1]),
        "head",
        scatter_dimension=0,
        tiled=True,
    )
    mixed_out = jnp.swapaxes(summed, 0, 1)
    final_state = closing.reshape(requests, shard_width, STATE)
    return (mixed_out, final_state)


def solution(mesh):
    return jax.shard_map(
        on_device,
        mesh=mesh,
        in_specs=(
            P("req", None, "head"),
            P("req", None, "head"),
            P("req", None, None),
            P("req", "head", None),
            P("head"),
            P("head"),
            P(None, "head"),
            P(),
            P("head", None),
            P("req", "head", None),
            P("req", None, "head"),
            P("req", None, None),
            P(),
            P(),
            P("req"),
        ),
        out_specs=(P("req", "head", None), P("req", "head", None)),
        check_vma=False,
    )
```

profile of v0, /device:TPU:0, one launch (start us, length us, event | category | flops | bytes accessed | tf_op | source)
XLA Modules:
  0.0 1172.3 jit_solution(617825335062952739)
XLA Ops:
  8.7 0.7 compare_convert_fusion
  9.4 0.8 slice_convert_fusion.3
  11.7 0.7 copy.25
  12.5 0.8 broadcast_multiply_fusion
  13.3 2.3 reduce_window_sum.11
  15.8 1.4 constant_dynamic-slice_fusion.5
  17.2 1.0 copy.50
  18.2 1.0 copy.51
  19.8 1.6 convert_element_type.127
  21.4 1.3 copy.39
  22.9 371.3 %while.29 = (s32[]{:T(128)}, f32[2,512,256]{2,1,0:T(8,128)S(1)}, f32[2,3,1024]{2,1,0:T(4,128)S(1)}, s32[]{:T(128)}, s32[8]{0:T(128)S(1)}, /*index=5*/s32[8]{0:T(...) while((s32[]{:T(128)}, f32[2,512,256]{2,1,0:T(8,128)S(1)}, ...), condition=%wide.region_2.3_spmd, body=%wide.region_0.2_spmd.sunk | while | flops 536591 | bytes 10219892 | solution.py:130
  26.1 1.1 dynamic-slice_bitcast_fusion.2
  28.0 0.8 maximum_select_fusion.2
  28.9 40.3 %all-reduce.2.cloned.1.call-done = f32[134144]{0:T(1024)} async-done(((f32[134144]{0:T(1024)}), f32[134144]{0:T(1024)}) %all-reduce.2.cloned.1.call-update) | async-done | bytes 536592 | tf_op jit(solution)/shard_map/while/body/eval_jaxpr/psum | solution.py:14
  69.2 1.1 slice.221
  73.8 1.1 dynamic-slice_bitcast_fusion.2
  75.7 0.8 maximum_select_fusion.2
  76.6 38.8 %all-reduce.2.cloned.1.call-done = f32[134144]{0:T(1024)} async-done(((f32[134144]{0:T(1024)}), f32[134144]{0:T(1024)}) %all-reduce.2.cloned.1.call-update) | async-done | bytes 536592 | tf_op jit(solution)/shard_map/while/body/eval_jaxpr/psum | solution.py:14
  115.4 1.1 slice.221
  120.0 1.1 dynamic-slice_bitcast_fusion.2
  121.9 0.8 maximum_select_fusion.2
  122.8 38.8 %all-reduce.2.cloned.1.call-done = f32[134144]{0:T(1024)} async-done(((f32[134144]{0:T(1024)}), f32[134144]{0:T(1024)}) %all-reduce.2.cloned.1.call-update) | async-done | bytes 536592 | tf_op jit(solution)/shard_map/while/body/eval_jaxpr/psum | solution.py:14
  161.6 1.1 slice.221
  166.2 1.1 dynamic-slice_bitcast_fusion.2
  168.1 0.8 maximum_select_fusion.2
  169.0 38.8 %all-reduce.2.cloned.1.call-done = f32[134144]{0:T(1024)} async-done(((f32[134144]{0:T(1024)}), f32[134144]{0:T(1024)}) %all-reduce.2.cloned.1.call-update) | async-done | bytes 536592 | tf_op jit(solution)/shard_map/while/body/eval_jaxpr/psum | solution.py:14
  207.8 1.1 slice.221
  212.4 1.1 dynamic-slice_bitcast_fusion.2
  214.4 0.8 maximum_select_fusion.2
  215.2 38.8 %all-reduce.2.cloned.1.call-done = f32[134144]{0:T(1024)} async-done(((f32[134144]{0:T(1024)}), f32[134144]{0:T(1024)}) %all-reduce.2.cloned.1.call-update) | async-done | bytes 536592 | tf_op jit(solution)/shard_map/while/body/eval_jaxpr/psum | solution.py:14
  254.1 1.1 slice.221
  258.7 1.1 dynamic-slice_bitcast_fusion.2
  260.6 0.8 maximum_select_fusion.2
  261.5 38.8 %all-reduce.2.cloned.1.call-done = f32[134144]{0:T(1024)} async-done(((f32[134144]{0:T(1024)}), f32[134144]{0:T(1024)}) %all-reduce.2.cloned.1.call-update) | async-done | bytes 536592 | tf_op jit(solution)/shard_map/while/body/eval_jaxpr/psum | solution.py:14
  300.3 1.1 slice.221
  304.9 1.1 dynamic-slice_bitcast_fusion.2
  306.8 0.8 maximum_select_fusion.2
  307.7 38.8 %all-reduce.2.cloned.1.call-done = f32[134144]{0:T(1024)} async-done(((f32[134144]{0:T(1024)}), f32[134144]{0:T(1024)}) %all-reduce.2.cloned.1.call-update) | async-done | bytes 536592 | tf_op jit(solution)/shard_map/while/body/eval_jaxpr/psum | solution.py:14
  346.5 1.1 slice.221
  351.1 1.1 dynamic-slice_bitcast_fusion.2
  353.0 0.8 maximum_select_fusion.2
  353.9 38.8 %all-reduce.2.cloned.1.call-done = f32[134144]{0:T(1024)} async-done(((f32[134144]{0:T(1024)}), f32[134144]{0:T(1024)}) %all-reduce.2.cloned.1.call-update) | async-done | bytes 536592 | tf_op jit(solution)/shard_map/while/body/eval_jaxpr/psum | solution.py:14
  392.7 1.1 slice.221
  394.4 5.2 multiply_convert_fusion.1
  400.2 1.5 maximum_convert_fusion
  401.7 2.4 multiply_convert_fusion
  404.1 0.9 fusion.56
  405.2 1.2 copy.31
  406.5 3.8 convolution_bitcast_fusion
  410.2 10.5 while.30
  410.2 1.1 bitcast_dynamic-update-slice_fusion.2
  411.3 1.5 bitcast_add_fusion.3
  412.8 1.1 bitcast_dynamic-update-slice_fusion.2
  413.9 1.5 bitcast_add_fusion.3
  415.4 1.1 bitcast_dynamic-update-slice_fusion.2
  416.5 1.5 bitcast_add_fusion.3
  418.0 1.1 bitcast_dynamic-update-slice_fusion.2
  419.1 1.5 bitcast_add_fusion.3
  421.1 4.6 fusion.2
  425.8 2.1 fusion.9
  427.9 2.7 copy.38
  430.6 2.2 reshape.174
  432.8 19.0 %fusion = f32[512,2,8192]{2,0,1:T(8,128)} fusion(bf16[512,8192]{1,0:T(8,128)(2,1)} %param.27, f32[2,512,512]{1,2,0:T(8,128)S(1)} %reshape.174, bf16[2,512,512]{1,2,0:T(8,128)(2,1)S(1)} %copy-done.1, f32[2,512]{1,0:T(2,128)S(1)} %compare_convert_fusion), kind=kOutput, calls=%fused_computation.8 | convolution fusion | flops 8594128896 | bytes 45092864 | tf_op jit(solution)/shard_map/dot_general | solution.py:150
  451.9 713.0 %reduce-scatter.2.cloned.1.call-done = f32[16,2,8192]{2,0,1:T(8,128)} async-done(((f32[512,2,8192]{2,0,1:T(8,128)}), f32[16,2,8192]{2,0,1:T(8,128)}) %reduce-scatter.2.cloned.1.call-update) | async-done | bytes 1048592 | tf_op jit(solution)/shard_map/reduce_scatter | solution.py:155
  (147 shorter events, 18.8 us)
Async XLA Ops:
  15.8 3.4 copy-start.3
  19.8 1.6 copy-start.4
  21.4 1.4 copy-start.6
  21.4 1.4 copy-start.7
  22.9 46.3 %all-reduce.2.cloned.1.call-start = ((), (), s32[]{:S(2)}) async-start(), calls=%async_computation.2 | async-start | bytes 1073152 | tf_op jit(solution)/shard_map/while/body/eval_jaxpr/psum | solution.py:14
  69.1 1.3 slice-start
  70.6 44.8 %all-reduce.2.cloned.1.call-start = ((), (), s32[]{:S(2)}) async-start(), calls=%async_computation.2 | async-start | bytes 1073152 | tf_op jit(solution)/shard_map/while/body/eval_jaxpr/psum | solution.py:14
  115.4 1.3 slice-start
  116.8 44.8 %all-reduce.2.cloned.1.call-start = ((), (), s32[]{:S(2)}) async-start(), calls=%async_computation.2 | async-start | bytes 1073152 | tf_op jit(solution)/shard_map/while/body/eval_jaxpr/psum | solution.py:14
  161.6 1.3 slice-start
  163.0 44.8 %all-reduce.2.cloned.1.call-start = ((), (), s32[]{:S(2)}) async-start(), calls=%async_computation.2 | async-start | bytes 1073152 | tf_op jit(solution)/shard_map/while/body/eval_jaxpr/psum | solution.py:14
  207.8 1.3 slice-start
  209.2 44.8 %all-reduce.2.cloned.1.call-start = ((), (), s32[]{:S(2)}) async-start(), calls=%async_computation.2 | async-start | bytes 1073152 | tf_op jit(solution)/shard_map/while/body/eval_jaxpr/psum | solution.py:14
  254.0 1.3 slice-start
  255.5 44.8 %all-reduce.2.cloned.1.call-start = ((), (), s32[]{:S(2)}) async-start(), calls=%async_computation.2 | async-start | bytes 1073152 | tf_op jit(solution)/shard_map/while/body/eval_jaxpr/psum | solution.py:14
  300.3 1.3 slice-start
  301.7 44.8 %all-reduce.2.cloned.1.call-start = ((), (), s32[]{:S(2)}) async-start(), calls=%async_computation.2 | async-start | bytes 1073152 | tf_op jit(solution)/shard_map/while/body/eval_jaxpr/psum | solution.py:14
  346.5 1.3 slice-start
  347.9 44.8 %all-reduce.2.cloned.1.call-start = ((), (), s32[]{:S(2)}) async-start(), calls=%async_computation.2 | async-start | bytes 1073152 | tf_op jit(solution)/shard_map/while/body/eval_jaxpr/psum | solution.py:14
  392.7 1.3 slice-start
  394.1 770.7 %reduce-scatter.2.cloned.1.call-start = ((), (), s32[]{:S(2)}) async-start(), calls=%async_computation.1 | async-start | bytes 34603008 | tf_op jit(solution)/shard_map/reduce_scatter | solution.py:155
  420.8 5.0 copy-start
  421.1 4.7 copy-start.2
  421.1 4.7 copy-start.5
  430.6 2.2 copy-start.1
Sparse Core Ops, SparseCore 0:
  29.0 40.1 all-reduce.1
  76.7 38.6 all-reduce.1
  122.9 38.6 all-reduce.1
  169.1 38.6 all-reduce.1
  215.3 38.6 all-reduce.1
  261.6 38.6 all-reduce.1
  307.8 38.6 all-reduce.1
  354.0 38.6 all-reduce.1
Sparse Core Ops, SparseCore 1:
  451.9 712.9 reduce-scatter.1
where the time goes:
time: 1170 us
  waiting for transfers between devices  1030 us (88%)
  local copies, waits for them, and re-layouts  50.4 us (4%)
  matrix products  29.8 us (3%)
  other arithmetic  29.7 us (3%)
  loops' own time  21.2 us (2%)
  between operations  15.8 us (1%)
    reduce_scatter x1, waiting for transfers between devices, on_device(): lax.psum_scatter(product.reshape(rows_here * lax.axis_size('head'), reque...  713 us
    psum x8, waiting for transfers between devices, from_root(): return lax.psum(kept, axis)  312 us
  transfers between devices with their start and end apart: 9, of which 9 were waited for; matrix products, arithmetic and copies ran while one was open for 0% of the time, Pallas kernels for 0%

commit v1 on v0

--- a/solution.py
+++ b/solution.py
@@ -1,12 +1,31 @@
 import jax
 import jax.numpy as jnp
 from jax import lax
+from jax.experimental import pallas as pl
+from jax.experimental.pallas import tpu as pltpu
 from jax.sharding import PartitionSpec as P
 
 HEADS = 256
 STATE = 256
 GROUPS = 8
 BLOCK = 128
+AXES = ("req", "head")
+MIB = 1 << 20
+
+
+def partner(z=0, y=0, hi=0, lo=0, core=0):
+    pairs = []
+    for source in range(128):
+        pairs.append((source, source ^ (lo << 6 | core << 5 | z << 3 | y << 1 | hi)))
+    return pairs
+
+
+def swap(array, **bits):
+    return lax.ppermute(array, AXES, partner(**bits))
+
+
+def flip_if(bit, array, axis):
+    return jnp.where(bit == 1, jnp.flip(array, axis), array)
 
 
 def from_root(value, axis, source):
@@ -67,6 +86,135 @@
     return jnp.concatenate([b_part, c_part], axis=-1)
 
 
+ORDER = ((2, 1, 0, 3), (2, 3, 0, 1))
+TILE = 512
+ROWS = 16
+
+
+def product_kernel(own, near, far, cross_low, cross_high, w_own, w_far, *outs):
+    own_side = jnp.concatenate([own[...], near[...]], axis=0).astype(jnp.bfloat16)
+    far_side = jnp.concatenate([cross_low[...], cross_high[...], far[...]], axis=0).astype(
+        jnp.bfloat16
+    )
+    total = jnp.dot(own_side, w_own[...], preferred_element_type=jnp.float32)
+    total += jnp.dot(far_side, w_far[...].astype(jnp.bfloat16), preferred_element_type=jnp.float32)
+
+    def emit(major_is_y):
+        def piece(major, side):
+            rows = []
+            for minor in ORDER[side]:
+                z, y = (minor, major) if major_is_y else (major, minor)
+                start = side * 16 * ROWS + (z * 4 + y) * ROWS
+                rows.append(total[start : start + ROWS])
+            return rows
+
+        first, third, one_b, three_a, zero_a, zero_b = outs
+
+        def put(ref, rows):
+            for at, block in enumerate(rows):
+                ref[at * ROWS : (at + 1) * ROWS, :] = block
+
+        put(first, piece(2, 0) + piece(1, 0))
+        put(third, piece(2, 1) + piece(3, 1))
+        put(one_b, piece(1, 1))
+        put(three_a, piece(3, 0))
+        put(zero_a, piece(0, 0))
+        put(zero_b, piece(0, 1))
+
+    return emit
+
+
+def product(blocks, w_own, w_far, y_first):
+    width = w_own.shape[1]
+    depth = w_own.shape[0]
+
+    def kernel(*refs):
+        product_kernel(*refs)(y_first)
+
+    lines = 4 * ROWS
+    heights = (2 * lines, 2 * lines, lines, lines, lines, lines)
+    return pl.pallas_call(
+        kernel,
+        grid=(width // TILE,),
+        in_specs=[pl.BlockSpec(b.shape, lambda i: (0, 0)) for b in blocks]
+        + [pl.BlockSpec((depth, TILE), lambda i: (0, i))] * 2,
+        out_specs=[pl.BlockSpec((h, TILE), lambda i: (0, i)) for h in heights],
+        out_shape=[jax.ShapeDtypeStruct((h, width), jnp.float32) for h in heights],
+        compiler_params=pltpu.CompilerParams(vmem_limit_bytes=48 * MIB),
+        cost_estimate=pl.CostEstimate(
+            flops=2 * 512 * 2 * depth * width,
+            bytes_accessed=4 * (4 * 256 * depth + 2 * depth * width + 512 * width),
+            transcendentals=0,
+        ),
+    )(*blocks, w_own, w_far)
+
+
+def exchange(parts, axis):
+    first, third, one_b, three_a, zero_a, zero_b = parts
+    lines = one_b.shape[0]
+    got1 = swap(first, **{axis: 1})
+    got3 = swap(third, **{axis: 3})
+    back1 = swap(one_b + got3[:lines], **{axis: 1})
+    back3 = swap(three_a + got1[:lines], **{axis: 3})
+    return (zero_a + got1[lines:] + back3, zero_b + got3[lines:] + back1)
+
+
+def next_parts(sums):
+    a, b = sums
+    line = a.shape[0] // 4
+    return (
+        a[: 2 * line],
+        b[: 2 * line],
+        b[3 * line :],
+        a[3 * line :],
+        a[2 * line : 3 * line],
+        b[2 * line : 3 * line],
+    )
+
+
+def project(gated, out_weight, coords):
+    z, y, hi, lo, core = coords
+    place = 2 * hi + lo
+    width = out_weight.shape[1] // 4
+    half = width // 2
+    pieces = [
+        lax.dynamic_slice_in_dim(out_weight, place * width + c * half, half, 1)
+        for c in (core, 1 - core)
+    ]
+    outgoing = lax.dynamic_slice_in_dim(out_weight, (3 - place) * width + core * half, half, 1)
+    far_own = swap(outgoing.astype(jnp.float32), hi=1, lo=1)
+    far_other = swap(far_own, core=1)
+    w_far = (far_own, far_other)
+    requests = gated.shape[0]
+    mixed = []
+    for request in range(requests):
+        done = []
+        for part in range(2):
+            own = gated[request, :, :, part].reshape(16 * ROWS, -1)
+            near = swap(own, lo=1)
+            far = swap(own, hi=1, lo=1)
+            cross_low = swap(far[: 8 * ROWS], lo=1)
+            cross_high = swap(near[8 * ROWS :], hi=1, lo=1)
+            blocks = (own, near, far, cross_low, cross_high)
+            halves = []
+            for c, axes in enumerate((("y", "z"), ("z", "y"))):
+                sums = exchange(product(blocks, pieces[c], w_far[c], c == 0), axes[0])
+                halves.append(exchange(next_parts(sums), axes[1]))
+            done.append(halves)
+
+        def pick(part, side):
+            return jnp.stack([done[part][c][side] for c in range(2)])
+
+        kept = [jnp.where(hi == 0, pick(0, side), pick(1, side)) for side in range(2)]
+        away = [jnp.where(hi == 0, pick(1, side), pick(0, side)) for side in range(2)]
+        got = jnp.stack(
+            [kept[0], swap(kept[1], lo=1), swap(away[0], hi=1), swap(away[1], hi=1, lo=1)]
+        ).reshape(2, 2, 2, ROWS, half)
+        got = flip_if(core, flip_if(lo, flip_if(hi, got, 0), 1), 2)
+        mixed.append(jnp.transpose(got, (3, 0, 1, 2, 4)).reshape(ROWS, 4 * width))
+    return jnp.stack(mixed)
+
+
 def on_device(
     x_input,
     z_gate,
@@ -86,6 +234,8 @@
 ):
     req_count = lax.axis_size("req")
     my_req = lax.axis_index("req")
+    my_head = lax.axis_index("head")
+    coords = (my_head // 8, my_head // 2 % 4, my_head % 2, my_req // 2, my_req % 2)
     head_count = a_log.shape[0]
     requests = lengths.shape[0]
     length = x_input.shape[1]
@@ -140,25 +290,17 @@
     head_x = x_conv.reshape(requests, length, head_count, head_width)
     initial = start_rows.reshape(requests, head_count, head_width, STATE)
     gate_rows = jax.nn.silu(z_gate.astype(jnp.float32)) * live_mask[:, :, None]
-    rows_here = length // lax.axis_size("head")
     scan_batch = jax.vmap(block_scan, in_axes=(0, 0, 0, 0, None, None, 0))
     outputs, closing = scan_batch(
         head_x, bc_conv[..., :STATE], bc_conv[..., STATE:], time_step, decay_rate, d_skip, initial
     )
     gated_rows = (outputs.reshape(requests, length, shard_width) * gate_rows).astype(jnp.bfloat16)
-    by_position = jnp.swapaxes(gated_rows, 0, 1)
-    product = jnp.dot(
-        by_position.reshape(rows_here * lax.axis_size("head") * requests, shard_width),
-        out_weight,
-        preferred_element_type=jnp.float32,
-    )
-    summed = lax.psum_scatter(
-        product.reshape(rows_here * lax.axis_size("head"), requests, out_weight.shape[1]),
-        "head",
-        scatter_dimension=0,
-        tiled=True,
-    )
-    mixed_out = jnp.swapaxes(summed, 0, 1)
+    relative = gated_rows.reshape(requests, 2, 2, 2, 2, 2, ROWS, shard_width)
+    z, y = coords[:2]
+    for axis, bit in ((1, z // 2), (2, z % 2), (3, y // 2), (4, y % 2)):
+        relative = flip_if(bit, relative, axis)
+    relative = relative.reshape(requests, 4, 4, 2, ROWS, shard_width).astype(jnp.float32)
+    mixed_out = project(relative, out_weight, coords)
     final_state = closing.reshape(requests, shard_width, STATE)
     return (mixed_out, final_state)
 

time: 1170 us -> 799 us (0.68); the launches traced: 1170 us -> 788 us
  waiting for transfers between devices: 1030 us -> 433 us
  starting transfers between devices: 0.38 us -> 124 us
  local copies, waits for them, and re-layouts: 50.4 us -> 102 us
  Pallas kernels: 0 us -> 24.7 us
  other arithmetic: 29.7 us -> 51.3 us
  matrix products: 29.8 us -> 15 us
    reduce_scatter x1 -> x0, waiting for transfers between devices: 713 us -> none  [on_device(): lax.psum_scatter(product.reshape(rows_here * lax.axis_size('head'), reque...]
    ppermute x0 -> x88, starting transfers between devices: none -> 124 us  [swap(): return lax.ppermute(array, AXES, partner(**bits))]
    ppermute x0 -> x88, waiting for transfers between devices: none -> 120 us  [swap(): return lax.ppermute(array, AXES, partner(**bits))]
    pallas_call x0 -> x8, Pallas kernels: none -> 24.7 us  [product(): pl.pallas_call(kernel, grid=(width // TILE,), in_specs=[pl.BlockSpec(b.sh...]
    dot_general x1 -> x0, matrix products: 19 us -> none  [on_device(): jnp.dot(by_position.reshape(rows_here * lax.axis_size('head') * requests,...]
    broadcast_in_dim x8, local copies, waits for them, and re-layouts: 1.18 us -> 16.2 us  [fetch_one(): lax.dynamic_update_index_in_dim(start_rows, received[:state_cells].reshap...]
  transfers between devices with their start and end apart: 9 -> 96, of which waited for: 9 -> 41; matrix products, arithmetic and copies ran while one was open for 0% -> 19% of each run, Pallas kernels for 0% -> 3%
where the time goes in v1:
time: 799 us; the launch traced here: 788 us
  waiting for transfers between devices  433 us (54%)
  starting transfers between devices  124 us (16%)
  local copies, waits for them, and re-layouts  102 us (13%)
  other arithmetic  51.3 us (6%)
  Pallas kernels  24.7 us (3%)
  loops' own time  21.4 us (3%)
  between operations  16.1 us (2%)
  matrix products  15 us (2%)
    psum x8, waiting for transfers between devices, from_root(): return lax.psum(kept, axis)  313 us
    ppermute x88, starting transfers between devices, swap(): return lax.ppermute(array, AXES, partner(**bits))  124 us
    ppermute x88, waiting for transfers between devices, swap(): return lax.ppermute(array, AXES, partner(**bits))  120 us
    pallas_call x8, Pallas kernels, product(): pl.pallas_call(kernel, grid=(width // TILE,), in_specs=[pl.BlockSpec(b.sh...  24.7 us
    another operation x1, loops' own time, on_device(): lax.fori_loop(0, req_count * requests, fetch_one, blank_rows)  21.3 us
    while x16, local copies, waits for them, and re-layouts  17.2 us
    broadcast_in_dim x8, local copies, waits for them, and re-layouts, fetch_one(): lax.dynamic_update_index_in_dim(start_rows, received[:state_cells].reshap...  16.2 us
  transfers between devices with their start and end apart: 96, of which 41 were waited for; matrix products, arithmetic and copies ran while one was open for 19% of the time, Pallas kernels for 3%

profile of v1, /device:TPU:0, one launch (start us, length us, event | category | flops | bytes accessed | tf_op | source)
XLA Modules:
  0.0 788.0 jit_solution(14548268385637156488)
XLA Ops:
  7.2 3.7 constant_dynamic-slice_fusion.3
  10.9 2.8 collective-permute-start.4
  18.1 411.3 %while.29 = (s32[]{:T(128)}, f32[2,512,256]{2,1,0:T(8,128)S(1)}, f32[2,3,1024]{2,1,0:T(4,128)S(1)}, s32[]{:T(128)}, s32[8]{0:T(128)S(1)}, /*index=5*/s32[8]{0:T(...) while((s32[]{:T(128)}, f32[2,512,256]{2,1,0:T(8,128)S(1)}, ...), condition=%wide.region_2.3_spmd, body=%wide.region_0.2_spmd.sunk | while | flops 536591 | bytes 10219892 | solution.py:280
  26.0 38.5 %all-reduce.2.cloned.1.call-done = f32[134144]{0:T(1024)} async-done(((f32[134144]{0:T(1024)}), f32[134144]{0:T(1024)}) %all-reduce.2.cloned.1.call-update) | async-done | bytes 536592 | tf_op jit(solution)/shard_map/while/body/eval_jaxpr/psum | solution.py:33
  77.6 38.9 %all-reduce.2.cloned.1.call-done = f32[134144]{0:T(1024)} async-done(((f32[134144]{0:T(1024)}), f32[134144]{0:T(1024)}) %all-reduce.2.cloned.1.call-update) | async-done | bytes 536592 | tf_op jit(solution)/shard_map/while/body/eval_jaxpr/psum | solution.py:33
  129.5 38.8 %all-reduce.2.cloned.1.call-done = f32[134144]{0:T(1024)} async-done(((f32[134144]{0:T(1024)}), f32[134144]{0:T(1024)}) %all-reduce.2.cloned.1.call-update) | async-done | bytes 536592 | tf_op jit(solution)/shard_map/while/body/eval_jaxpr/psum | solution.py:33
  180.2 39.9 %all-reduce.2.cloned.1.call-done = f32[134144]{0:T(1024)} async-done(((f32[134144]{0:T(1024)}), f32[134144]{0:T(1024)}) %all-reduce.2.cloned.1.call-update) | async-done | bytes 536592 | tf_op jit(solution)/shard_map/while/body/eval_jaxpr/psum | solution.py:33
  232.1 39.9 %all-reduce.2.cloned.1.call-done = f32[134144]{0:T(1024)} async-done(((f32[134144]{0:T(1024)}), f32[134144]{0:T(1024)}) %all-reduce.2.cloned.1.call-update) | async-done | bytes 536592 | tf_op jit(solution)/shard_map/while/body/eval_jaxpr/psum | solution.py:33
  284.0 39.1 %all-reduce.2.cloned.1.call-done = f32[134144]{0:T(1024)} async-done(((f32[134144]{0:T(1024)}), f32[134144]{0:T(1024)}) %all-reduce.2.cloned.1.call-update) | async-done | bytes 536592 | tf_op jit(solution)/shard_map/while/body/eval_jaxpr/psum | solution.py:33
  335.1 39.1 %all-reduce.2.cloned.1.call-done = f32[134144]{0:T(1024)} async-done(((f32[134144]{0:T(1024)}), f32[134144]{0:T(1024)}) %all-reduce.2.cloned.1.call-update) | async-done | bytes 536592 | tf_op jit(solution)/shard_map/while/body/eval_jaxpr/psum | solution.py:33
  386.2 39.2 %all-reduce.2.cloned.1.call-done = f32[134144]{0:T(1024)} async-done(((f32[134144]{0:T(1024)}), f32[134144]{0:T(1024)}) %all-reduce.2.cloned.1.call-update) | async-done | bytes 536592 | tf_op jit(solution)/shard_map/while/body/eval_jaxpr/psum | solution.py:33
  432.8 2.4 multiply_convert_fusion
  439.4 2.3 copy.49
  443.3 3.2 multiply_convert_fusion.1
  446.5 2.1 reshape.295
  448.8 2.3 reduce_window_sum.11
  451.3 5.2 convolution_bitcast_fusion
  456.5 10.3 %while.30 = (s32[]{:T(128)}, f32[2,8,64,256]{3,2,1,0:T(8,128)S(1)}, f32[4,2,8,64,256]{4,3,2,0,1:T(8,128)}, f32[4,2,8]{2,0,1:T(4,128)S(1)}, f32[4,2,8,64,256]{4,3,2,0,1:T(8,128)}, /*index=5*/s32[]{:T(128)}) while((s32[]{:T(128)}, f32[2,8,64,256]{3,2,1,0:T(8,128)S(1)}, f32[4,2,8,64,256]{4,3,2,0,1:T(8,128)}, f32[4,2,8]{2,0,1:T(4,128)S(1)}, ...), condition=%wide.region_5.6_spmd, body=%wide.region_4.5_spmd.sunk | while | flops 524290 | bytes 5243661 | solution.py:76
  466.9 2.4 copy.54
  470.8 6.2 fusion
  479.2 2.8 copy.61
  482.0 3.1 reshape.300
  486.4 2.6 fusion.34
  498.4 11.3 %collective-permute-done.15.refs_2_ = f32[256,512]{1,0:T(8,128)S(1)} collective-permute-done((f32[256,512]{1,0:T(8,128)S(1)}, f32[256,512]{1,0:T(8,128)S(1)}, u32[]{:S(2)}, u32[]{:S(2)}) %collective-permute-start.15) | collective-permute-done | bytes 524320 | tf_op jit(solution)/shard_map/ppermute | solution.py:24
  511.2 9.7 %collective-permute-done.1.refs_2_ = f32[256,512]{1,0:T(8,128)S(1)} collective-permute-done((f32[256,512]{1,0:T(8,128)S(1)}, f32[256,512]{1,0:T(8,128)S(1)}, u32[]{:S(2)}, u32[]{:S(2)}) %collective-permute-start.1) | collective-permute-done | bytes 524320 | tf_op jit(solution)/shard_map/ppermute | solution.py:24
  522.5 9.6 %collective-permute-done.46.refs_2_ = f32[256,512]{1,0:T(8,128)S(1)} collective-permute-done((f32[256,512]{1,0:T(8,128)S(1)}, f32[256,512]{1,0:T(8,128)S(1)}, u32[]{:S(2)}, u32[]{:S(2)}) %collective-permute-start.46) | collective-permute-done | bytes 524320 | tf_op jit(solution)/shard_map/ppermute | solution.py:24
  534.2 15.3 %collective-permute-done.16.refs_3_ = f32[128,512]{1,0:T(8,128)S(1)} collective-permute-done((f32[128,512]{1,0:T(8,128)S(1)}, f32[128,512]{1,0:T(8,128)S(1)}, u32[]{:S(2)}, u32[]{:S(2)}) %collective-permute-start.16) | collective-permute-done | bytes 262176 | tf_op jit(solution)/shard_map/ppermute | solution.py:24
  551.9 3.4 shard_map.160
  559.4 2.3 collective-permute-start.48
  565.3 3.4 shard_map.158
  573.8 2.7 collective-permute-start.26
  578.6 3.0 shard_map.162
  582.5 3.0 shard_map.164
  588.4 2.8 collective-permute-start.69
  592.8 8.5 %collective-permute-done.34 = f32[128,1024]{1,0:T(8,128)S(1)} collective-permute-done((f32[128,1024]{1,0:T(8,128)S(1)}, f32[128,1024]{1,0:T(8,128)S(1)}, u32[]{:S(2)}, u32[]{:S(2)}) %collective-permute-start.34) | collective-permute-done | bytes 524320 | tf_op jit(solution)/shard_map/ppermute | solution.py:24
  601.3 2.8 collective-permute-start.19
  604.2 3.7 collective-permute-done.61
  607.9 2.1 collective-permute-start.6
  610.0 2.5 collective-permute-done.69
  612.8 10.9 %collective-permute-done.77 = f32[128,1024]{1,0:T(8,128)S(1)} collective-permute-done((f32[128,1024]{1,0:T(8,128)S(1)}, f32[128,1024]{1,0:T(8,128)S(1)}, u32[]{:S(2)}, u32[]{:S(2)}) %collective-permute-start.77) | collective-permute-done | bytes 524320 | tf_op jit(solution)/shard_map/ppermute | solution.py:24
  624.1 5.3 collective-permute-done.19
  629.4 2.7 collective-permute-start.50
  635.0 2.7 collective-permute-start.62
  645.2 3.0 collective-permute-start.28
  648.3 2.7 collective-permute-start.36
  653.4 2.2 collective-permute-start.71
  655.9 2.7 collective-permute-start.79
  659.3 2.8 collective-permute-start.8
  674.5 3.0 shard_map.161
  677.7 3.0 shard_map.159
  685.9 2.9 shard_map.163
  688.9 3.0 shard_map.165
  694.1 9.6 %collective-permute-done.10 = f32[128,1024]{1,0:T(8,128)S(1)} collective-permute-done((f32[128,1024]{1,0:T(8,128)S(1)}, f32[128,1024]{1,0:T(8,128)S(1)}, u32[]{:S(2)}, u32[]{:S(2)}) %collective-permute-start.10) | collective-permute-done | bytes 524320 | tf_op jit(solution)/shard_map/ppermute | solution.py:24
  714.1 8.3 %collective-permute-done.65 = f32[128,1024]{1,0:T(8,128)S(1)} collective-permute-done((f32[128,1024]{1,0:T(8,128)S(1)}, f32[128,1024]{1,0:T(8,128)S(1)}, u32[]{:S(2)}, u32[]{:S(2)}) %collective-permute-start.65) | collective-permute-done | bytes 524320 | tf_op jit(solution)/shard_map/ppermute | solution.py:24
  724.6 6.4 collective-permute-done.81
  733.0 2.2 collective-permute-done.23
  735.2 2.2 collective-permute-start.66
  738.1 2.1 collective-permute-start.82
  743.6 2.6 collective-permute-start.32
  749.4 2.7 collective-permute-start.75
  753.4 2.2 collective-permute-start.25
  759.0 2.5 collective-permute-start.56
  764.9 2.5 collective-permute-start.43
  769.4 2.5 collective-permute-start.86
  (555 shorter events, 216.8 us)
Async XLA Ops:
  10.9 540.1 %collective-permute-start.4 = (f32[512,1024]{1,0:T(8,128)}, f32[512,1024]{1,0:T(8,128)}, u32[]{:S(2)}, u32[]{:S(2)}) collective-permute-start(f32[512,1024]{1,0:T(8,128)} %get-tuple-element.376), channel_id=1, source_target_pairs={{0,65},{1,64},{2,67},{3,66},{4,69},{5,68},{6,71},{7,70},{8,73},{9,... | collective-permute-start | bytes 6291464 | tf_op jit(solution)/shard_map/ppermute | solution.py:24
  18.1 46.4 %all-reduce.2.cloned.1.call-start = ((), (), s32[]{:S(2)}) async-start(), calls=%async_computation | async-start | bytes 1073152 | tf_op jit(solution)/shard_map/while/body/eval_jaxpr/psum | solution.py:33
  69.6 46.8 %all-reduce.2.cloned.1.call-start = ((), (), s32[]{:S(2)}) async-start(), calls=%async_computation | async-start | bytes 1073152 | tf_op jit(solution)/shard_map/while/body/eval_jaxpr/psum | solution.py:33
  121.6 46.7 %all-reduce.2.cloned.1.call-start = ((), (), s32[]{:S(2)}) async-start(), calls=%async_computation | async-start | bytes 1073152 | tf_op jit(solution)/shard_map/while/body/eval_jaxpr/psum | solution.py:33
  172.3 47.8 %all-reduce.2.cloned.1.call-start = ((), (), s32[]{:S(2)}) async-start(), calls=%async_computation | async-start | bytes 1073152 | tf_op jit(solution)/shard_map/while/body/eval_jaxpr/psum | solution.py:33
  224.2 47.8 %all-reduce.2.cloned.1.call-start = ((), (), s32[]{:S(2)}) async-start(), calls=%async_computation | async-start | bytes 1073152 | tf_op jit(solution)/shard_map/while/body/eval_jaxpr/psum | solution.py:33
  276.1 47.0 %all-reduce.2.cloned.1.call-start = ((), (), s32[]{:S(2)}) async-start(), calls=%async_computation | async-start | bytes 1073152 | tf_op jit(solution)/shard_map/while/body/eval_jaxpr/psum | solution.py:33
  327.2 47.0 %all-reduce.2.cloned.1.call-start = ((), (), s32[]{:S(2)}) async-start(), calls=%async_computation | async-start | bytes 1073152 | tf_op jit(solution)/shard_map/while/body/eval_jaxpr/psum | solution.py:33
  378.3 47.1 %all-reduce.2.cloned.1.call-start = ((), (), s32[]{:S(2)}) async-start(), calls=%async_computation | async-start | bytes 1073152 | tf_op jit(solution)/shard_map/while/body/eval_jaxpr/psum | solution.py:33
  493.6 16.0 %collective-permute-start.15 = (f32[256,512]{1,0:T(8,128)S(1)}, f32[256,512]{1,0:T(8,128)S(1)}, u32[]{:S(2)}, u32[]{:S(2)}) collective-permute-start(f32[256,512]{1,0:T(8,128)S(1)} %bitcast.162), channel_id=1, source_target_pairs={{0,65},{1,64},{2,67},{3,66},{4,69},{5,68},{6,71},{7,70},{8,73},{9,... | collective-permute-start | bytes 1572872 | tf_op jit(solution)/shard_map/ppermute | solution.py:24
  495.6 15.5 %collective-permute-start.14 = (f32[256,512]{1,0:T(8,128)S(1)}, f32[256,512]{1,0:T(8,128)S(1)}, u32[]{:S(2)}, u32[]{:S(2)}) collective-permute-start(f32[256,512]{1,0:T(8,128)S(1)} %bitcast.163), channel_id=1, source_target_pairs={{0,64},{1,65},{2,66},{3,67},{4,68},{5,69},{6,70},{7,71},{8,72},{9,... | collective-permute-start | bytes 1572872 | tf_op jit(solution)/shard_map/ppermute | solution.py:24
  496.4 24.5 %collective-permute-start.1 = (f32[256,512]{1,0:T(8,128)S(1)}, f32[256,512]{1,0:T(8,128)S(1)}, u32[]{:S(2)}, u32[]{:S(2)}) collective-permute-start(f32[256,512]{1,0:T(8,128)S(1)} %bitcast.158), channel_id=1, source_target_pairs={{0,65},{1,64},{2,67},{3,66},{4,69},{5,68},{6,71},{7,70},{8,73},{9,... | collective-permute-start | bytes 1572872 | tf_op jit(solution)/shard_map/ppermute | solution.py:24
  497.1 25.4 %collective-permute-start = (f32[256,512]{1,0:T(8,128)S(1)}, f32[256,512]{1,0:T(8,128)S(1)}, u32[]{:S(2)}, u32[]{:S(2)}) collective-permute-start(f32[256,512]{1,0:T(8,128)S(1)} %bitcast.159), channel_id=1, source_target_pairs={{0,64},{1,65},{2,66},{3,67},{4,68},{5,69},{6,70},{7,71},{8,72},{9,... | collective-permute-start | bytes 1572872 | tf_op jit(solution)/shard_map/ppermute | solution.py:24
  509.6 22.5 %collective-permute-start.46 = (f32[256,512]{1,0:T(8,128)S(1)}, f32[256,512]{1,0:T(8,128)S(1)}, u32[]{:S(2)}, u32[]{:S(2)}) collective-permute-start(f32[256,512]{1,0:T(8,128)S(1)} %bitcast.154), channel_id=1, source_target_pairs={{0,65},{1,64},{2,67},{3,66},{4,69},{5,68},{6,71},{7,70},{8,73},{9,... | collective-permute-start | bytes 1572872 | tf_op jit(solution)/shard_map/ppermute | solution.py:24
  511.2 21.5 %collective-permute-start.45 = (f32[256,512]{1,0:T(8,128)S(1)}, f32[256,512]{1,0:T(8,128)S(1)}, u32[]{:S(2)}, u32[]{:S(2)}) collective-permute-start(f32[256,512]{1,0:T(8,128)S(1)} %bitcast.155), channel_id=1, source_target_pairs={{0,64},{1,65},{2,66},{3,67},{4,68},{5,69},{6,70},{7,71},{8,72},{9,... | collective-permute-start | bytes 1572872 | tf_op jit(solution)/shard_map/ppermute | solution.py:24
  520.9 36.2 %collective-permute-start.58 = (f32[256,512]{1,0:T(8,128)S(1)}, f32[256,512]{1,0:T(8,128)S(1)}, u32[]{:S(2)}, u32[]{:S(2)}) collective-permute-start(f32[256,512]{1,0:T(8,128)S(1)} %bitcast.150), channel_id=1, source_target_pairs={{0,65},{1,64},{2,67},{3,66},{4,69},{5,68},{6,71},{7,70},{8,73},{9,... | collective-permute-start | bytes 1572872 | tf_op jit(solution)/shard_map/ppermute | solution.py:24
  522.4 37.0 %collective-permute-start.57 = (f32[256,512]{1,0:T(8,128)S(1)}, f32[256,512]{1,0:T(8,128)S(1)}, u32[]{:S(2)}, u32[]{:S(2)}) collective-permute-start(f32[256,512]{1,0:T(8,128)S(1)} %bitcast.151), channel_id=1, source_target_pairs={{0,64},{1,65},{2,66},{3,67},{4,68},{5,69},{6,70},{7,71},{8,72},{9,... | collective-permute-start | bytes 1572872 | tf_op jit(solution)/shard_map/ppermute | solution.py:24
  532.1 17.4 %collective-permute-start.16 = (f32[128,512]{1,0:T(8,128)S(1)}, f32[128,512]{1,0:T(8,128)S(1)}, u32[]{:S(2)}, u32[]{:S(2)}) collective-permute-start(f32[128,512]{1,0:T(8,128)S(1)} %slice.630), channel_id=1, source_target_pairs={{0,64},{1,65},{2,66},{3,67},{4,68},{5,69},{6,70},{7,71},{8,72},{9,... | collective-permute-start | bytes 786440 | tf_op jit(solution)/shard_map/ppermute | solution.py:24
  532.6 17.7 %collective-permute-start.17 = (f32[128,512]{1,0:T(8,128)S(1)}, f32[128,512]{1,0:T(8,128)S(1)}, u32[]{:S(2)}, u32[]{:S(2)}) collective-permute-start(f32[128,512]{1,0:T(8,128)S(1)} %slice.631), channel_id=1, source_target_pairs={{0,65},{1,64},{2,67},{3,66},{4,69},{5,68},{6,71},{7,70},{8,73},{9,... | collective-permute-start | bytes 786440 | tf_op jit(solution)/shard_map/ppermute | solution.py:24
  549.5 13.6 %collective-permute-start.2 = (f32[128,512]{1,0:T(8,128)S(1)}, f32[128,512]{1,0:T(8,128)S(1)}, u32[]{:S(2)}, u32[]{:S(2)}) collective-permute-start(f32[128,512]{1,0:T(8,128)S(1)} %slice.613), channel_id=1, source_target_pairs={{0,64},{1,65},{2,66},{3,67},{4,68},{5,69},{6,70},{7,71},{8,72},{9,... | collective-permute-start | bytes 786440 | tf_op jit(solution)/shard_map/ppermute | solution.py:24
  550.3 14.0 %collective-permute-start.3 = (f32[128,512]{1,0:T(8,128)S(1)}, f32[128,512]{1,0:T(8,128)S(1)}, u32[]{:S(2)}, u32[]{:S(2)}) collective-permute-start(f32[128,512]{1,0:T(8,128)S(1)} %slice.614), channel_id=1, source_target_pairs={{0,65},{1,64},{2,67},{3,66},{4,69},{5,68},{6,71},{7,70},{8,73},{9,... | collective-permute-start | bytes 786440 | tf_op jit(solution)/shard_map/ppermute | solution.py:24
  551.0 22.2 %collective-permute-start.47 = (f32[128,512]{1,0:T(8,128)S(1)}, f32[128,512]{1,0:T(8,128)S(1)}, u32[]{:S(2)}, u32[]{:S(2)}) collective-permute-start(f32[128,512]{1,0:T(8,128)S(1)} %slice.675), channel_id=1, source_target_pairs={{0,64},{1,65},{2,66},{3,67},{4,68},{5,69},{6,70},{7,71},{8,72},{9,... | collective-permute-start | bytes 786440 | tf_op jit(solution)/shard_map/ppermute | solution.py:24
  557.1 28.5 %collective-permute-start.18 = (f32[128,1024]{1,0:T(8,128)}, f32[128,1024]{1,0:T(8,128)}, u32[]{:S(2)}, u32[]{:S(2)}) collective-permute-start(f32[128,1024]{1,0:T(8,128)} %get-tuple-element.289), channel_id=1, source_target_pairs={{0,2},{1,3},{2,0},{3,1},{4,6},{5,7},{6,4},{7,5},{8,10},{9,11},{10,... | collective-permute-start | bytes 1572872 | tf_op jit(solution)/shard_map/ppermute | solution.py:24
  559.4 14.4 %collective-permute-start.48 = (f32[128,512]{1,0:T(8,128)}, f32[128,512]{1,0:T(8,128)}, u32[]{:S(2)}, u32[]{:S(2)}) collective-permute-start(f32[128,512]{1,0:T(8,128)} %slice.676), channel_id=1, source_target_pairs={{0,65},{1,64},{2,67},{3,66},{4,69},{5,68},{6,71},{7,70},{8,73},{9,... | collective-permute-start | bytes 786440 | tf_op jit(solution)/shard_map/ppermute | solution.py:24
  563.1 18.4 %collective-permute-start.59 = (f32[128,512]{1,0:T(8,128)}, f32[128,512]{1,0:T(8,128)}, u32[]{:S(2)}, u32[]{:S(2)}) collective-permute-start(f32[128,512]{1,0:T(8,128)} %slice.692), channel_id=1, source_target_pairs={{0,64},{1,65},{2,66},{3,67},{4,68},{5,69},{6,70},{7,71},{8,72},{9,... | collective-permute-start | bytes 786440 | tf_op jit(solution)/shard_map/ppermute | solution.py:24
  564.4 17.8 %collective-permute-start.60 = (f32[128,512]{1,0:T(8,128)}, f32[128,512]{1,0:T(8,128)}, u32[]{:S(2)}, u32[]{:S(2)}) collective-permute-start(f32[128,512]{1,0:T(8,128)} %slice.693), channel_id=1, source_target_pairs={{0,65},{1,64},{2,67},{3,66},{4,69},{5,68},{6,71},{7,70},{8,73},{9,... | collective-permute-start | bytes 786440 | tf_op jit(solution)/shard_map/ppermute | solution.py:24
  573.2 15.2 %collective-permute-start.5 = (f32[128,1024]{1,0:T(8,128)}, f32[128,1024]{1,0:T(8,128)}, u32[]{:S(2)}, u32[]{:S(2)}) collective-permute-start(f32[128,1024]{1,0:T(8,128)} %get-tuple-element.283), channel_id=1, source_target_pairs={{0,2},{1,3},{2,0},{3,1},{4,6},{5,7},{6,4},{7,5},{8,10},{9,11},{10,... | collective-permute-start | bytes 1572872 | tf_op jit(solution)/shard_map/ppermute | solution.py:24
  573.8 18.4 %collective-permute-start.26 = (f32[128,1024]{1,0:T(8,128)}, f32[128,1024]{1,0:T(8,128)S(1)}, u32[]{:S(2)}, u32[]{:S(2)}) collective-permute-start(f32[128,1024]{1,0:T(8,128)} %copy-done.48), channel_id=1, source_target_pairs={{0,6},{1,7},{2,4},{3,5},{4,2},{5,3},{6,0},{7,1},{8,14},{9,15},{10,... | collective-permute-start | bytes 1572872 | tf_op jit(solution)/shard_map/ppermute | solution.py:24
  581.6 19.7 %collective-permute-start.34 = (f32[128,1024]{1,0:T(8,128)S(1)}, f32[128,1024]{1,0:T(8,128)S(1)}, u32[]{:S(2)}, u32[]{:S(2)}) collective-permute-start(f32[128,1024]{1,0:T(8,128)S(1)} %copy-done.47), channel_id=1, source_target_pairs={{0,6},{1,7},{2,4},{3,5},{4,2},{5,3},{6,0},{7,1},{8,14},{9,15},{10,... | collective-permute-start | bytes 1572872 | tf_op jit(solution)/shard_map/ppermute | solution.py:24
  582.2 19.1 %collective-permute-start.49 = (f32[128,1024]{1,0:T(8,128)S(1)}, f32[128,1024]{1,0:T(8,128)S(1)}, u32[]{:S(2)}, u32[]{:S(2)}) collective-permute-start(f32[128,1024]{1,0:T(8,128)S(1)} %get-tuple-element.307), channel_id=1, source_target_pairs={{0,2},{1,3},{2,0},{3,1},{4,6},{5,7},{6,4},{7,5},{8,10},{9,11},{10,... | collective-permute-start | bytes 1572872 | tf_op jit(solution)/shard_map/ppermute | solution.py:24
  585.6 22.4 %collective-permute-start.61 = (f32[128,1024]{1,0:T(8,128)S(1)}, f32[128,1024]{1,0:T(8,128)S(1)}, u32[]{:S(2)}, u32[]{:S(2)}) collective-permute-start(f32[128,1024]{1,0:T(8,128)S(1)} %get-tuple-element.313), channel_id=1, source_target_pairs={{0,2},{1,3},{2,0},{3,1},{4,6},{5,7},{6,4},{7,5},{8,10},{9,11},{10,... | collective-permute-start | bytes 1572872 | tf_op jit(solution)/shard_map/ppermute | solution.py:24
  588.4 24.1 %collective-permute-start.69 = (f32[128,1024]{1,0:T(8,128)S(1)}, f32[128,1024]{1,0:T(8,128)S(1)}, u32[]{:S(2)}, u32[]{:S(2)}) collective-permute-start(f32[128,1024]{1,0:T(8,128)S(1)} %get-tuple-element.319), channel_id=1, source_target_pairs={{0,6},{1,7},{2,4},{3,5},{4,2},{5,3},{6,0},{7,1},{8,14},{9,15},{10,... | collective-permute-start | bytes 1572872 | tf_op jit(solution)/shard_map/ppermute | solution.py:24
  592.2 31.6 %collective-permute-start.77 = (f32[128,1024]{1,0:T(8,128)S(1)}, f32[128,1024]{1,0:T(8,128)S(1)}, u32[]{:S(2)}, u32[]{:S(2)}) collective-permute-start(f32[128,1024]{1,0:T(8,128)S(1)} %get-tuple-element.325), channel_id=1, source_target_pairs={{0,6},{1,7},{2,4},{3,5},{4,2},{5,3},{6,0},{7,1},{8,14},{9,15},{10,... | collective-permute-start | bytes 1572872 | tf_op jit(solution)/shard_map/ppermute | solution.py:24
  601.3 71.8 %collective-permute-start.9 = (f32[512,1024]{1,0:T(8,128)}, f32[512,1024]{1,0:T(8,128)S(1)}, u32[]{:S(2)}, u32[]{:S(2)}) collective-permute-start(f32[512,1024]{1,0:T(8,128)} %collective-permute-done.4.refs_6_), channel_id=1, source_target_pairs={{0,32},{1,33},{2,34},{3,35},{4,36},{5,37},{6,38},{7,39},{8,40},{9,... | collective-permute-start | bytes 6291464 | tf_op jit(solution)/shard_map/ppermute | solution.py:24
  601.3 28.0 %collective-permute-start.19 = (f32[64,1024]{1,0:T(8,128)S(1)}, f32[64,1024]{1,0:T(8,128)S(1)}, u32[]{:S(2)}, u32[]{:S(2)}) collective-permute-start(f32[64,1024]{1,0:T(8,128)S(1)} %slice_add_fusion.26), channel_id=1, source_target_pairs={{0,6},{1,7},{2,4},{3,5},{4,2},{5,3},{6,0},{7,1},{8,14},{9,15},{10,... | collective-permute-start | bytes 786440 | tf_op jit(solution)/shard_map/ppermute | solution.py:24
  607.9 27.1 %collective-permute-start.6 = (f32[64,1024]{1,0:T(8,128)S(1)}, f32[64,1024]{1,0:T(8,128)S(1)}, u32[]{:S(2)}, u32[]{:S(2)}) collective-permute-start(f32[64,1024]{1,0:T(8,128)S(1)} %slice_add_fusion.30), channel_id=1, source_target_pairs={{0,6},{1,7},{2,4},{3,5},{4,2},{5,3},{6,0},{7,1},{8,14},{9,15},{10,... | collective-permute-start | bytes 786440 | tf_op jit(solution)/shard_map/ppermute | solution.py:24
  612.5 26.2 %collective-permute-start.27 = (f32[64,1024]{1,0:T(8,128)S(1)}, f32[64,1024]{1,0:T(8,128)S(1)}, u32[]{:S(2)}, u32[]{:S(2)}) collective-permute-start(f32[64,1024]{1,0:T(8,128)S(1)} %slice_add_fusion.22), channel_id=1, source_target_pairs={{0,2},{1,3},{2,0},{3,1},{4,6},{5,7},{6,4},{7,5},{8,10},{9,11},{10,... | collective-permute-start | bytes 786440 | tf_op jit(solution)/shard_map/ppermute | solution.py:24
  623.8 15.1 %collective-permute-start.35 = (f32[64,1024]{1,0:T(8,128)S(1)}, f32[64,1024]{1,0:T(8,128)S(1)}, u32[]{:S(2)}, u32[]{:S(2)}) collective-permute-start(f32[64,1024]{1,0:T(8,128)S(1)} %slice_add_fusion.18), channel_id=1, source_target_pairs={{0,2},{1,3},{2,0},{3,1},{4,6},{5,7},{6,4},{7,5},{8,10},{9,11},{10,... | collective-permute-start | bytes 786440 | tf_op jit(solution)/shard_map/ppermute | solution.py:24
  629.4 11.7 %collective-permute-start.50 = (f32[64,1024]{1,0:T(8,128)S(1)}, f32[64,1024]{1,0:T(8,128)S(1)}, u32[]{:S(2)}, u32[]{:S(2)}) collective-permute-start(f32[64,1024]{1,0:T(8,128)S(1)} %slice_add_fusion.14), channel_id=1, source_target_pairs={{0,6},{1,7},{2,4},{3,5},{4,2},{5,3},{6,0},{7,1},{8,14},{9,15},{10,... | collective-permute-start | bytes 786440 | tf_op jit(solution)/shard_map/ppermute | solution.py:24
  638.9 9.4 %collective-permute-start.78 = (f32[64,1024]{1,0:T(8,128)S(1)}, f32[64,1024]{1,0:T(8,128)S(1)}, u32[]{:S(2)}, u32[]{:S(2)}) collective-permute-start(f32[64,1024]{1,0:T(8,128)S(1)} %slice_add_fusion.2), channel_id=1, source_target_pairs={{0,2},{1,3},{2,0},{3,1},{4,6},{5,7},{6,4},{7,5},{8,10},{9,11},{10,... | collective-permute-start | bytes 786440 | tf_op jit(solution)/shard_map/ppermute | solution.py:24
  641.1 10.1 %collective-permute-start.20 = (f32[32,1024]{1,0:T(8,128)S(1)}, f32[32,1024]{1,0:T(8,128)S(1)}, u32[]{:S(2)}, u32[]{:S(2)}) collective-permute-start(f32[32,1024]{1,0:T(8,128)S(1)} %slice.635), channel_id=1, source_target_pairs={{0,8},{1,9},{2,10},{3,11},{4,12},{5,13},{6,14},{7,15},{8,0},{9,1},... | collective-permute-start | bytes 393224 | tf_op jit(solution)/shard_map/ppermute | solution.py:24
  653.4 8.8 %collective-permute-start.71 = (f32[32,1024]{1,0:T(8,128)S(1)}, f32[32,1024]{1,0:T(8,128)S(1)}, u32[]{:S(2)}, u32[]{:S(2)}) collective-permute-start(f32[32,1024]{1,0:T(8,128)S(1)} %slice.711), channel_id=1, source_target_pairs={{0,24},{1,25},{2,26},{3,27},{4,28},{5,29},{6,30},{7,31},{8,16},{9,... | collective-permute-start | bytes 393224 | tf_op jit(solution)/shard_map/ppermute | solution.py:24
  668.1 14.5 %collective-permute-start.80 = (f32[16,1024]{1,0:T(8,128)S(1)}, f32[16,1024]{1,0:T(8,128)S(1)}, u32[]{:S(2)}, u32[]{:S(2)}) collective-permute-start(f32[16,1024]{1,0:T(8,128)S(1)} %slice_add_fusion.34), channel_id=1, source_target_pairs={{0,8},{1,9},{2,10},{3,11},{4,12},{5,13},{6,14},{7,15},{8,0},{9,1},... | collective-permute-start | bytes 196616 | tf_op jit(solution)/shard_map/ppermute | solution.py:24
  677.5 14.9 %collective-permute-start.22 = (f32[128,1024]{1,0:T(8,128)S(1)}, f32[128,1024]{1,0:T(8,128)S(1)}, u32[]{:S(2)}, u32[]{:S(2)}) collective-permute-start(f32[128,1024]{1,0:T(8,128)S(1)} %get-tuple-element.292), channel_id=1, source_target_pairs={{0,8},{1,9},{2,10},{3,11},{4,12},{5,13},{6,14},{7,15},{8,0},{9,1},... | collective-permute-start | bytes 1572872 | tf_op jit(solution)/shard_map/ppermute | solution.py:24
  680.6 23.1 %collective-permute-start.10 = (f32[128,1024]{1,0:T(8,128)S(1)}, f32[128,1024]{1,0:T(8,128)S(1)}, u32[]{:S(2)}, u32[]{:S(2)}) collective-permute-start(f32[128,1024]{1,0:T(8,128)S(1)} %get-tuple-element.286), channel_id=1, source_target_pairs={{0,8},{1,9},{2,10},{3,11},{4,12},{5,13},{6,14},{7,15},{8,0},{9,1},... | collective-permute-start | bytes 1572872 | tf_op jit(solution)/shard_map/ppermute | solution.py:24
  682.6 23.1 %collective-permute-start.30 = (f32[128,1024]{1,0:T(8,128)S(1)}, f32[128,1024]{1,0:T(8,128)S(1)}, u32[]{:S(2)}, u32[]{:S(2)}) collective-permute-start(f32[128,1024]{1,0:T(8,128)S(1)} %get-tuple-element.298), channel_id=1, source_target_pairs={{0,24},{1,25},{2,26},{3,27},{4,28},{5,29},{6,30},{7,31},{8,16},{9,... | collective-permute-start | bytes 1572872 | tf_op jit(solution)/shard_map/ppermute | solution.py:24
  684.7 23.8 %collective-permute-start.38 = (f32[128,1024]{1,0:T(8,128)S(1)}, f32[128,1024]{1,0:T(8,128)S(1)}, u32[]{:S(2)}, u32[]{:S(2)}) collective-permute-start(f32[128,1024]{1,0:T(8,128)S(1)} %get-tuple-element.304), channel_id=1, source_target_pairs={{0,24},{1,25},{2,26},{3,27},{4,28},{5,29},{6,30},{7,31},{8,16},{9,... | collective-permute-start | bytes 1572872 | tf_op jit(solution)/shard_map/ppermute | solution.py:24
  688.8 23.3 %collective-permute-start.53 = (f32[128,1024]{1,0:T(8,128)S(1)}, f32[128,1024]{1,0:T(8,128)S(1)}, u32[]{:S(2)}, u32[]{:S(2)}) collective-permute-start(f32[128,1024]{1,0:T(8,128)S(1)} %get-tuple-element.310), channel_id=1, source_target_pairs={{0,8},{1,9},{2,10},{3,11},{4,12},{5,13},{6,14},{7,15},{8,0},{9,1},... | collective-permute-start | bytes 1572872 | tf_op jit(solution)/shard_map/ppermute | solution.py:24
  692.5 30.0 %collective-permute-start.65 = (f32[128,1024]{1,0:T(8,128)S(1)}, f32[128,1024]{1,0:T(8,128)S(1)}, u32[]{:S(2)}, u32[]{:S(2)}) collective-permute-start(f32[128,1024]{1,0:T(8,128)S(1)} %get-tuple-element.316), channel_id=1, source_target_pairs={{0,8},{1,9},{2,10},{3,11},{4,12},{5,13},{6,14},{7,15},{8,0},{9,1},... | collective-permute-start | bytes 1572872 | tf_op jit(solution)/shard_map/ppermute | solution.py:24
  703.7 19.0 %collective-permute-start.73 = (f32[128,1024]{1,0:T(8,128)S(1)}, f32[128,1024]{1,0:T(8,128)S(1)}, u32[]{:S(2)}, u32[]{:S(2)}) collective-permute-start(f32[128,1024]{1,0:T(8,128)S(1)} %get-tuple-element.322), channel_id=1, source_target_pairs={{0,24},{1,25},{2,26},{3,27},{4,28},{5,29},{6,30},{7,31},{8,16},{9,... | collective-permute-start | bytes 1572872 | tf_op jit(solution)/shard_map/ppermute | solution.py:24
  705.7 25.3 %collective-permute-start.81 = (f32[128,1024]{1,0:T(8,128)S(1)}, f32[128,1024]{1,0:T(8,128)S(1)}, u32[]{:S(2)}, u32[]{:S(2)}) collective-permute-start(f32[128,1024]{1,0:T(8,128)S(1)} %get-tuple-element.328), channel_id=1, source_target_pairs={{0,24},{1,25},{2,26},{3,27},{4,28},{5,29},{6,30},{7,31},{8,16},{9,... | collective-permute-start | bytes 1572872 | tf_op jit(solution)/shard_map/ppermute | solution.py:24
  708.5 26.7 %collective-permute-start.23 = (f32[64,1024]{1,0:T(8,128)S(1)}, f32[64,1024]{1,0:T(8,128)S(1)}, u32[]{:S(2)}, u32[]{:S(2)}) collective-permute-start(f32[64,1024]{1,0:T(8,128)S(1)} %slice_add_fusion.24), channel_id=1, source_target_pairs={{0,24},{1,25},{2,26},{3,27},{4,28},{5,29},{6,30},{7,31},{8,16},{9,... | collective-permute-start | bytes 786440 | tf_op jit(solution)/shard_map/ppermute | solution.py:24
  712.2 25.9 %collective-permute-start.11 = (f32[64,1024]{1,0:T(8,128)S(1)}, f32[64,1024]{1,0:T(8,128)S(1)}, u32[]{:S(2)}, u32[]{:S(2)}) collective-permute-start(f32[64,1024]{1,0:T(8,128)S(1)} %slice_add_fusion.28), channel_id=1, source_target_pairs={{0,24},{1,25},{2,26},{3,27},{4,28},{5,29},{6,30},{7,31},{8,16},{9,... | collective-permute-start | bytes 786440 | tf_op jit(solution)/shard_map/ppermute | solution.py:24
  722.4 15.7 %collective-permute-start.31 = (f32[64,1024]{1,0:T(8,128)S(1)}, f32[64,1024]{1,0:T(8,128)S(1)}, u32[]{:S(2)}, u32[]{:S(2)}) collective-permute-start(f32[64,1024]{1,0:T(8,128)S(1)} %slice_add_fusion.20), channel_id=1, source_target_pairs={{0,8},{1,9},{2,10},{3,11},{4,12},{5,13},{6,14},{7,15},{8,0},{9,1},... | collective-permute-start | bytes 786440 | tf_op jit(solution)/shard_map/ppermute | solution.py:24
  722.7 17.5 %collective-permute-start.39 = (f32[64,1024]{1,0:T(8,128)S(1)}, f32[64,1024]{1,0:T(8,128)S(1)}, u32[]{:S(2)}, u32[]{:S(2)}) collective-permute-start(f32[64,1024]{1,0:T(8,128)S(1)} %slice_add_fusion.16), channel_id=1, source_target_pairs={{0,8},{1,9},{2,10},{3,11},{4,12},{5,13},{6,14},{7,15},{8,0},{9,1},... | collective-permute-start | bytes 786440 | tf_op jit(solution)/shard_map/ppermute | solution.py:24
  730.9 9.9 %collective-permute-start.54 = (f32[64,1024]{1,0:T(8,128)S(1)}, f32[64,1024]{1,0:T(8,128)S(1)}, u32[]{:S(2)}, u32[]{:S(2)}) collective-permute-start(f32[64,1024]{1,0:T(8,128)S(1)} %slice_add_fusion.12), channel_id=1, source_target_pairs={{0,24},{1,25},{2,26},{3,27},{4,28},{5,29},{6,30},{7,31},{8,16},{9,... | collective-permute-start | bytes 786440 | tf_op jit(solution)/shard_map/ppermute | solution.py:24
  735.2 8.4 %collective-permute-start.66 = (f32[64,1024]{1,0:T(8,128)S(1)}, f32[64,1024]{1,0:T(8,128)S(1)}, u32[]{:S(2)}, u32[]{:S(2)}) collective-permute-start(f32[64,1024]{1,0:T(8,128)S(1)} %slice_add_fusion.8), channel_id=1, source_target_pairs={{0,24},{1,25},{2,26},{3,27},{4,28},{5,29},{6,30},{7,31},{8,16},{9,... | collective-permute-start | bytes 786440 | tf_op jit(solution)/shard_map/ppermute | solution.py:24
  738.1 9.1 %collective-permute-start.82 = (f32[64,1024]{1,0:T(8,128)S(1)}, f32[64,1024]{1,0:T(8,128)S(1)}, u32[]{:S(2)}, u32[]{:S(2)}) collective-permute-start(f32[64,1024]{1,0:T(8,128)S(1)} %slice_add_fusion), channel_id=1, source_target_pairs={{0,8},{1,9},{2,10},{3,11},{4,12},{5,13},{6,14},{7,15},{8,0},{9,1},... | collective-permute-start | bytes 786440 | tf_op jit(solution)/shard_map/ppermute | solution.py:24
  740.8 8.6 %collective-permute-start.12 = (f32[32,1024]{1,0:T(8,128)S(1)}, f32[32,1024]{1,0:T(8,128)S(1)}, u32[]{:S(2)}, u32[]{:S(2)}) collective-permute-start(f32[32,1024]{1,0:T(8,128)S(1)} %slice.625), channel_id=1, source_target_pairs={{0,2},{1,3},{2,0},{3,1},{4,6},{5,7},{6,4},{7,5},{8,10},{9,11},{10,... | collective-permute-start | bytes 393224 | tf_op jit(solution)/shard_map/ppermute | solution.py:24
  743.6 8.5 %collective-permute-start.32 = (f32[32,1024]{1,0:T(8,128)S(1)}, f32[32,1024]{1,0:T(8,128)S(1)}, u32[]{:S(2)}, u32[]{:S(2)}) collective-permute-start(f32[32,1024]{1,0:T(8,128)S(1)} %slice.656), channel_id=1, source_target_pairs={{0,6},{1,7},{2,4},{3,5},{4,2},{5,3},{6,0},{7,1},{8,14},{9,15},{10,... | collective-permute-start | bytes 393224 | tf_op jit(solution)/shard_map/ppermute | solution.py:24
  747.2 8.4 %collective-permute-start.55 = (f32[32,1024]{1,0:T(8,128)S(1)}, f32[32,1024]{1,0:T(8,128)S(1)}, u32[]{:S(2)}, u32[]{:S(2)}) collective-permute-start(f32[32,1024]{1,0:T(8,128)S(1)} %slice.687), channel_id=1, source_target_pairs={{0,2},{1,3},{2,0},{3,1},{4,6},{5,7},{6,4},{7,5},{8,10},{9,11},{10,... | collective-permute-start | bytes 393224 | tf_op jit(solution)/shard_map/ppermute | solution.py:24
  747.3 9.4 %collective-permute-start.67 = (f32[32,1024]{1,0:T(8,128)S(1)}, f32[32,1024]{1,0:T(8,128)S(1)}, u32[]{:S(2)}, u32[]{:S(2)}) collective-permute-start(f32[32,1024]{1,0:T(8,128)S(1)} %slice.704), channel_id=1, source_target_pairs={{0,2},{1,3},{2,0},{3,1},{4,6},{5,7},{6,4},{7,5},{8,10},{9,11},{10,... | collective-permute-start | bytes 393224 | tf_op jit(solution)/shard_map/ppermute | solution.py:24
  759.0 8.5 %collective-permute-start.56 = (f32[16,1024]{1,0:T(8,128)S(1)}, f32[16,1024]{1,0:T(8,128)S(1)}, u32[]{:S(2)}, u32[]{:S(2)}) collective-permute-start(f32[16,1024]{1,0:T(8,128)S(1)} %slice_add_fusion.44), channel_id=1, source_target_pairs={{0,6},{1,7},{2,4},{3,5},{4,2},{5,3},{6,0},{7,1},{8,14},{9,15},{10,... | collective-permute-start | bytes 196616 | tf_op jit(solution)/shard_map/ppermute | solution.py:24
  762.7 9.1 %collective-permute-start.84 = (f32[16,1024]{1,0:T(8,128)S(1)}, f32[16,1024]{1,0:T(8,128)S(1)}, u32[]{:S(2)}, u32[]{:S(2)}) collective-permute-start(f32[16,1024]{1,0:T(8,128)S(1)} %slice_add_fusion.32), channel_id=1, source_target_pairs={{0,2},{1,3},{2,0},{3,1},{4,6},{5,7},{6,4},{7,5},{8,10},{9,11},{10,... | collective-permute-start | bytes 196616 | tf_op jit(solution)/shard_map/ppermute | solution.py:24
  (105 other events, 982.0 us)
Sparse Core Ops, SparseCore 0:
  26.1 38.3 all-reduce.1
  77.7 38.7 all-reduce.1
  129.6 38.6 all-reduce.1
  180.3 39.7 all-reduce.1
  232.2 39.7 all-reduce.1
  284.1 38.9 all-reduce.1
  335.2 38.9 all-reduce.1
  386.3 39.0 all-reduce.1

commit v2 on v0

v2 whole, which is shorter than its diff:
```python
import jax
import jax.numpy as jnp
from jax import lax
from jax.experimental import pallas as pl
from jax.experimental.pallas import tpu as pltpu
from jax.sharding import PartitionSpec as P

HEADS = 256
HEADDIM = 64
STATE = 256
GROUPS = 8
BLOCK = 128
AXES = ("req", "head")
MIB = 1 << 20


def partner(z=0, y=0, hi=0, lo=0, core=0):
    pairs = []
    for source in range(128):
        pairs.append((source, source ^ (lo << 6 | core << 5 | z << 3 | y << 1 | hi)))
    return pairs


def swap(array, **bits):
    return lax.ppermute(array, AXES, partner(**bits))


def flip_if(bit, array, axis):
    return jnp.where(bit == 1, jnp.flip(array, axis), array)


def conv_rows(window, previous, rows, taps):
    window[0:8, :] = previous
    window[8 : 8 + BLOCK, :] = rows
    total = window[5 : 5 + BLOCK, :] * taps[0:1, :]
    for offset in range(1, 4):
        total = total + window[5 + offset : 5 + offset + BLOCK, :] * taps[offset : offset + 1, :]
    return total * (1.0 / (1.0 + jnp.exp(-total)))


def spread(columns, lane):
    pairs = []
    for pair in range(4):
        even = columns[:, 2 * pair : 2 * pair + 1]
        odd = columns[:, 2 * pair + 1 : 2 * pair + 2]
        pairs.append(jnp.where(lane < HEADDIM, even, odd))
    return jnp.concatenate(pairs, axis=1)


def scan_kernel(
    scalars,
    x_ref,
    b_ref,
    c_ref,
    x_tail,
    b_tail,
    c_tail,
    x_taps,
    b_taps,
    c_taps,
    dt_ref,
    rate_ref,
    skip_ref,
    y_ref,
    c_out,
    decay_out,
    state_out,
    x_window,
    b_window,
    c_window,
    x_last,
    b_last,
    c_last,
    state,
    passed,
):
    request, block = pl.program_id(0), pl.program_id(1)

    @pl.when(block == 0)
    def _():
        x_last[...] = x_tail[0]
        b_last[...] = b_tail[0]
        c_last[...] = c_tail[0]
        state[...] = jnp.zeros_like(state)
        passed[...] = jnp.zeros_like(passed)

    def convolve(window, last, ref, taps):
        rows = ref[0].astype(jnp.float32)
        made = conv_rows(window, last[...], rows, taps[...].astype(jnp.float32))
        last[...] = rows[BLOCK - 8 :]
        return made.astype(jnp.bfloat16)

    x = convolve(x_window, x_last, x_ref, x_taps)
    b = convolve(b_window, b_last, b_ref, b_taps)
    c = convolve(c_window, c_last, c_ref, c_taps)
    c_out[0] = c

    place = lax.broadcasted_iota(jnp.int32, (8, BLOCK), 1)
    raw = dt_ref[0]
    step = jnp.maximum(raw, 0.0) + jnp.log1p(jnp.exp(-jnp.abs(raw)))
    step = jnp.where(place + block * BLOCK < scalars[2 + request], step, 0.0)
    decay = -rate_ref[...] * step
    reach = 1
    while reach < BLOCK:
        decay = decay + jnp.where(place >= reach, pltpu.roll(decay, reach, 1), 0.0)
        reach *= 2
    closing = decay[:, BLOCK - 1 : BLOCK]
    weight = jnp.exp(closing - decay) * step
    turned = jnp.transpose(
        jnp.concatenate(
            [decay, weight, passed[...] + decay, jnp.zeros((BLOCK - 24, BLOCK), jnp.float32)],
            axis=0,
        )
    )
    passed[...] = passed[...] + closing
    decay_out[0] = jnp.exp(turned[:, 16:24])

    lane = lax.broadcasted_iota(jnp.int32, (BLOCK, BLOCK), 1)
    causal = lax.broadcasted_iota(jnp.int32, (BLOCK, BLOCK), 0) >= lane
    scores = lax.dot_general(c, b, (((1,), (1,)), ((), ())), preferred_element_type=jnp.float32)
    scores = jnp.where(causal, scores, 0.0)
    within = []
    for pair in range(4):
        inputs = x[:, pair * 128 : (pair + 1) * 128]
        halves = []
        for head in (2 * pair, 2 * pair + 1):
            gap = jnp.where(causal, turned[:, head : head + 1] - decay[head : head + 1, :], 0.0)
            mixing = jnp.exp(gap) * scores * step[head : head + 1, :]
            halves.append(
                jnp.dot(mixing.astype(jnp.bfloat16), inputs, preferred_element_type=jnp.float32)
            )
        within.append(jnp.where(lane < HEADDIM, halves[0], halves[1]))
    carried = lax.dot_general(
        c,
        state[...].astype(jnp.bfloat16),
        (((1,), (1,)), ((), ())),
        preferred_element_type=jnp.float32,
    )
    wide = x.astype(jnp.float32)
    y_ref[0] = (
        jnp.concatenate(within, axis=1)
        + carried * spread(jnp.exp(turned[:, 0:8]), lane)
        + skip_ref[...] * wide
    )
    weighted = (wide * spread(turned[:, 8:16], lane)).astype(jnp.bfloat16)
    added = lax.dot_general(
        weighted, b, (((0,), (0,)), ((), ())), preferred_element_type=jnp.float32
    )
    factor = jnp.exp(closing)
    for head in range(8):
        rows = slice(head * HEADDIM, (head + 1) * HEADDIM)
        state[rows, :] = state[rows, :] * factor[head : head + 1, :] + added[rows, :]

    @pl.when(block == pl.num_programs(1) - 1)
    def _():
        state_out[0] = state[...]


def scan(scalars, x_input, bc_input, x_tail, bc_tail, conv_x, conv_bc, dt_raw, rate, skip):
    requests, length, width = x_input.shape
    heads = dt_raw.shape[1]

    def grouped(shape, shift):
        def at(r, i, s):
            return (r, i, s[0] + shift)

        return pl.BlockSpec(shape, at)

    def table(shift):
        return pl.BlockSpec((4, STATE), lambda r, i, s: (0, s[0] + shift))

    return pl.pallas_call(
        scan_kernel,
        grid_spec=pltpu.PrefetchScalarGridSpec(
            num_scalar_prefetch=1,
            grid=(requests, length // BLOCK),
            in_specs=[
                pl.BlockSpec((1, BLOCK, width), lambda r, i, s: (r, i, 0)),
                grouped((1, BLOCK, STATE), 0),
                grouped((1, BLOCK, STATE), GROUPS),
                pl.BlockSpec((1, 8, width), lambda r, i, s: (r, 0, 0)),
                pl.BlockSpec((1, 8, STATE), lambda r, i, s: (r, 0, 0)),
                pl.BlockSpec((1, 8, STATE), lambda r, i, s: (r, 0, 1)),
                pl.BlockSpec((4, width), lambda r, i, s: (0, 0)),
                table(0),
                table(GROUPS),
                pl.BlockSpec((1, heads, BLOCK), lambda r, i, s: (r, 0, i)),
                pl.BlockSpec((heads, 1), lambda r, i, s: (0, 0)),
                pl.BlockSpec((1, width), lambda r, i, s: (0, 0)),
            ],
            out_specs=[
                pl.BlockSpec((1, BLOCK, width), lambda r, i, s: (r, i, 0)),
                pl.BlockSpec((1, BLOCK, STATE), lambda r, i, s: (r, i, 0)),
                pl.BlockSpec((1, BLOCK, heads), lambda r, i, s: (r, i, 0)),
                pl.BlockSpec((1, width, STATE), lambda r, i, s: (r, 0, 0)),
            ],
            scratch_shapes=[
                pltpu.VMEM((8 + BLOCK, width), jnp.float32),
                pltpu.VMEM((8 + BLOCK, STATE), jnp.float32),
                pltpu.VMEM((8 + BLOCK, STATE), jnp.float32),
                pltpu.VMEM((8, width), jnp.float32),
                pltpu.VMEM((8, STATE), jnp.float32),
                pltpu.VMEM((8, STATE), jnp.float32),
                pltpu.VMEM((width, STATE), jnp.float32),
                pltpu.VMEM((heads, 1), jnp.float32),
            ],
        ),
        out_shape=[
            jax.ShapeDtypeStruct((requests, length, width), jnp.float32),
            jax.ShapeDtypeStruct((requests, length, STATE), jnp.bfloat16),
            jax.ShapeDtypeStruct((requests, length, heads), jnp.float32),
            jax.ShapeDtypeStruct((requests, width, STATE), jnp.float32),
        ],
        compiler_params=pltpu.CompilerParams(vmem_limit_bytes=32 * MIB),
        cost_estimate=pl.CostEstimate(
            flops=2 * requests * length * (8 * 128 * 128 + 2 * width * STATE + 128 * STATE),
            bytes_accessed=12 * MIB,
            transcendentals=4 * requests * length * width,
        ),
    )(
        scalars,
        x_input,
        bc_input,
        bc_input,
        x_tail,
        bc_tail,
        bc_tail,
        conv_x,
        conv_bc,
        conv_bc,
        dt_raw,
        rate,
        skip,
    )


def gate_kernel(
    scalars, y_ref, c_ref, decay_ref, part_ref, z_ref, mine, near, far, gated_ref, state_ref
):
    request = scalars[4]
    source = scalars[5]
    initial = jnp.where(source == 0, mine[...], jnp.where(source == 1, near[...], far[...]))
    lane = lax.broadcasted_iota(jnp.int32, (BLOCK, BLOCK), 1)
    narrow = initial.astype(jnp.bfloat16)
    for block in range(y_ref.shape[1] // BLOCK):
        rows = slice(block * BLOCK, (block + 1) * BLOCK)
        carried = lax.dot_general(
            c_ref[0, rows], narrow, (((1,), (1,)), ((), ())), preferred_element_type=jnp.float32
        )
        y = y_ref[0, rows] + carried * spread(decay_ref[0, rows], lane)
        z = z_ref[0, rows].astype(jnp.float32)
        position = lax.broadcasted_iota(jnp.int32, y.shape, 0) + block * BLOCK
        gated = y * (z * (1.0 / (1.0 + jnp.exp(-z))))
        gated = jnp.where(position < scalars[2 + request], gated, 0.0)
        gated = gated.astype(jnp.bfloat16).astype(jnp.float32)
        for at in range(4):
            target = (block * 4 + at) ^ scalars[1]
            gated_ref[pl.ds(pl.multiple_of(target * 32, 32), 32), :] = gated[at * 32 : at * 32 + 32]
    last = decay_ref.shape[1] - 8
    final = decay_ref[0, last:, :]
    for head in range(8):
        rows = slice(head * HEADDIM, (head + 1) * HEADDIM)
        state_ref[0, rows] = part_ref[0, rows] + initial[rows] * final[7:8, head : head + 1]


def gate(scalars, request, source, parts, z_gate, candidates):
    y, c, decay, part = parts
    _, length, width = y.shape
    scalars = jnp.concatenate([scalars, jnp.stack([jnp.int32(request), source])])

    def whole(shape):
        return pl.BlockSpec((1,) + shape, lambda i, s: (request, 0, 0))

    flat = pl.BlockSpec((width, STATE), lambda i, s: (0, 0))
    return pl.pallas_call(
        gate_kernel,
        grid_spec=pltpu.PrefetchScalarGridSpec(
            num_scalar_prefetch=1,
            grid=(1,),
            in_specs=[
                whole((length, width)),
                whole((length, STATE)),
                whole((length, decay.shape[2])),
                whole((width, STATE)),
                whole((length, width)),
                flat,
                flat,
                flat,
            ],
            out_specs=[
                pl.BlockSpec((length, width), lambda i, s: (0, 0)),
                pl.BlockSpec((1, width, STATE), lambda i, s: (0, 0, 0)),
            ],
        ),
        out_shape=[
            jax.ShapeDtypeStruct((length, width), jnp.float32),
            jax.ShapeDtypeStruct((1, width, STATE), jnp.float32),
        ],
        compiler_params=pltpu.CompilerParams(vmem_limit_bytes=32 * MIB),
        cost_estimate=pl.CostEstimate(
            flops=2 * length * width * STATE, bytes_accessed=6 * MIB, transcendentals=length * width
        ),
    )(scalars, y, c, decay, part, z_gate, *candidates)


def fetch(table, owner, slot, coords):
    _, _, _, lo, core = coords
    me = 2 * lo + core

    def entry(device, j):
        at = 2 * device + j
        return lax.dynamic_index_in_dim(table, slot[at], 0, keepdims=False), owner[at]

    away_core = 2 * lo + 1 - core
    away_chip = 2 * (1 - lo) + core
    away_both = 2 * (1 - lo) + 1 - core
    found = []
    for j in range(2):
        sent = jnp.stack([entry(away_core, j)[0], entry(away_both, j)[0]])
        got = swap(sent, core=1)
        here, holder = entry(away_chip, j)
        far = swap(jnp.where(holder == me, here, got[1]), lo=1)
        here, holder = entry(me, j)
        source = jnp.where(holder == me, 0, jnp.where(holder == away_core, 1, 2))
        found.append(((here, got[0], far), source.astype(jnp.int32)))
    return found


ORDER = ((2, 1, 0, 3), (2, 3, 0, 1))
TILE = 512
ROWS = 32


def product(blocks, w_own, w_far, y_first):
    depth, width = w_own.shape
    lines = 4 * ROWS
    side_rows = 16 * ROWS

    def kernel(own, near, cross, far, w_own_ref, w_far_ref, *rest):
        outs, own_side, far_side = rest[:6], rest[6], rest[7]

        @pl.when(pl.program_id(0) == 0)
        def _():
            own_side[:side_rows] = own[...].astype(jnp.bfloat16)
            own_side[side_rows:] = near[...].astype(jnp.bfloat16)
            far_side[:side_rows] = cross[...].astype(jnp.bfloat16)
            far_side[side_rows:] = far[...].astype(jnp.bfloat16)

        total = jnp.dot(own_side[...], w_own_ref[...], preferred_element_type=jnp.float32)
        total += jnp.dot(
            far_side[...], w_far_ref[...].astype(jnp.bfloat16), preferred_element_type=jnp.float32
        )

        def put(ref, at, major, side):
            for minor in ORDER[side]:
                z, y = (minor, major) if y_first else (major, minor)
                start = side * side_rows + (z * 4 + y) * ROWS
                ref[at * ROWS : (at + 1) * ROWS, :] = total[start : start + ROWS]
                at += 1

        put(outs[0], 0, 2, 0)
        put(outs[0], 4, 1, 0)
        put(outs[1], 0, 2, 1)
        put(outs[1], 4, 3, 1)
        put(outs[2], 0, 1, 1)
        put(outs[3], 0, 3, 0)
        put(outs[4], 0, 0, 0)
        put(outs[5], 0, 0, 1)

    heights = (2 * lines, 2 * lines, lines, lines, lines, lines)
    return pl.pallas_call(
        kernel,
        grid=(width // TILE,),
        in_specs=[pl.BlockSpec(b.shape, lambda i: (0, 0)) for b in blocks]
        + [pl.BlockSpec((depth, TILE), lambda i: (0, i))] * 2,
        out_specs=[pl.BlockSpec((h, TILE), lambda i: (0, i)) for h in heights],
        out_shape=[jax.ShapeDtypeStruct((h, width), jnp.float32) for h in heights],
        scratch_shapes=[pltpu.VMEM((2 * side_rows, depth), jnp.bfloat16)] * 2,
        compiler_params=pltpu.CompilerParams(vmem_limit_bytes=40 * MIB),
        cost_estimate=pl.CostEstimate(
            flops=2 * 4 * side_rows * depth * width,
            bytes_accessed=16 * side_rows * depth + 6 * depth * width + 8 * side_rows * width,
            transcendentals=0,
        ),
    )(*blocks, w_own, w_far)


def exchange(parts, axis):
    first, third, one_b, three_a, zero_a, zero_b = parts
    lines = one_b.shape[0]
    got1 = swap(first, **{axis: 1})
    got3 = swap(third, **{axis: 3})
    back1 = swap(one_b + got3[:lines], **{axis: 1})
    back3 = swap(three_a + got1[:lines], **{axis: 3})
    return (zero_a + got1[lines:] + back3, zero_b + got3[lines:] + back1)


def next_parts(sums):
    def rows(side, start, stop):
        chosen = [s[side][start * ROWS : stop * ROWS] for s in sums]
        if stop - start == 2:
            chosen = [c[:ROWS] for c in chosen] + [c[ROWS:] for c in chosen]
        return jnp.concatenate(chosen, axis=0)

    return (
        rows(0, 0, 2),
        rows(1, 0, 2),
        rows(1, 3, 4),
        rows(0, 3, 4),
        rows(0, 2, 3),
        rows(1, 2, 3),
    )


def far_weights(out_weight, coords):
    _, _, hi, lo, core = coords
    place = 2 * hi + lo
    width = out_weight.shape[1] // 4
    half = width // 2
    outgoing = lax.dynamic_slice_in_dim(out_weight, (3 - place) * width + core * half, half, 1)
    far_own = swap(outgoing.astype(jnp.float32), hi=1, lo=1)
    return (far_own, swap(far_own, core=1))


def project(gated, out_weight, w_far, coords):
    z, y, hi, lo, core = coords
    place = 2 * hi + lo
    width = out_weight.shape[1] // 4
    half = width // 2
    pieces = [
        lax.dynamic_slice_in_dim(out_weight, place * width + c * half, half, 1)
        for c in (core, 1 - core)
    ]
    requests = len(gated)
    first_axis = ("y", "z")
    reduced = ([], [])
    for own in gated:
        near = swap(own, lo=1)
        far = swap(own, hi=1, lo=1)
        middle = own.shape[0] // 2
        cross = jnp.concatenate(
            [swap(far[:middle], lo=1), swap(near[middle:], hi=1, lo=1)], axis=0
        )
        for c in range(2):
            parts = product((own, near, cross, far), pieces[c], w_far[c], c == 0)
            reduced[c].append(exchange(parts, first_axis[c]))
    halves = [exchange(next_parts(reduced[c]), first_axis[1 - c]) for c in range(2)]
    done = jnp.stack([jnp.stack(pair) for pair in halves]).reshape(2, 2, requests, 2, 16, half)
    kept = jnp.where(hi == 0, done[:, :, :, 0], done[:, :, :, 1])
    away = jnp.where(hi == 0, done[:, :, :, 1], done[:, :, :, 0])
    got = jnp.stack(
        [
            kept[:, 0],
            swap(kept[:, 1], lo=1),
            swap(away[:, 0], hi=1),
            swap(away[:, 1], hi=1, lo=1),
        ]
    ).reshape(2, 2, 2, requests, 16, half)
    got = flip_if(core, flip_if(lo, flip_if(hi, got, 0), 1), 2)
    return jnp.transpose(got, (3, 4, 0, 1, 2, 5)).reshape(requests, 16, 4 * width)


def on_device(
    x_input,
    z_gate,
    bc_input,
    dt_raw,
    a_log,
    d_skip,
    conv_x,
    conv_bc,
    out_weight,
    pool_state,
    pool_xtail,
    pool_bctail,
    pool_dev,
    pool_slot,
    lengths,
):
    my_req = lax.axis_index("req")
    my_head = lax.axis_index("head")
    coords = (my_head // 8, my_head // 2 % 4, my_head % 2, my_req // 2, my_req % 2)
    head_count = a_log.shape[0]
    group = my_head * head_count // (HEADS // GROUPS)
    owner = pool_dev[:, 0]

    def own_group(start):
        return lax.dynamic_slice_in_dim(pool_bctail, start * STATE, STATE, 2)

    tails = jnp.concatenate(
        [pool_xtail, own_group(group), own_group(GROUPS + group)], axis=-1
    ).astype(jnp.float32)
    tails = jnp.pad(tails, ((0, 0), (5, 0), (0, 0)))
    tail_rows = jnp.stack(
        [
            jnp.where(source == 0, mine, jnp.where(source == 1, near, far))
            for (mine, near, far), source in fetch(tails, owner, pool_slot, coords)
        ]
    )
    width = x_input.shape[2]
    w_far = far_weights(out_weight, coords)
    states = fetch(pool_state, owner, pool_slot, coords)
    scalars = jnp.concatenate([jnp.stack([group, my_head // 2]), lengths]).astype(jnp.int32)
    parts = scan(
        scalars,
        x_input,
        bc_input,
        tail_rows[:, :, :width],
        tail_rows[:, :, width:],
        conv_x,
        conv_bc,
        dt_raw,
        jnp.exp(a_log)[:, None],
        jnp.repeat(d_skip, HEADDIM)[None, :],
    )
    made = [
        gate(scalars, j, source, parts, z_gate, candidates)
        for j, (candidates, source) in enumerate(states)
    ]
    mixed_out = project([g for g, _ in made], out_weight, w_far, coords)
    return (mixed_out, jnp.concatenate([s for _, s in made], axis=0))


def solution(mesh):
    return jax.shard_map(
        on_device,
        mesh=mesh,
        in_specs=(
            P("req", None, "head"),
            P("req", None, "head"),
            P("req", None, None),
            P("req", "head", None),
            P("head"),
            P("head"),
            P(None, "head"),
            P(),
            P("head", None),
            P("req", "head", None),
            P("req", None, "head"),
            P("req", None, None),
            P(),
            P(),
            P("req"),
        ),
        out_specs=(P("req", "head", None), P("req", "head", None)),
        check_vma=False,
    )
```

time: 1170 us -> 306 us (0.26)
  waiting for transfers between devices: 1030 us -> 129 us
  starting transfers between devices: 0.38 us -> 67.2 us
  Pallas kernels: 0 us -> 37 us
  matrix products: 29.8 us -> 0 us
  loops' own time: 21.2 us -> 0 us
  local copies, waits for them, and re-layouts: 50.4 us -> 30.6 us
    reduce_scatter x1 -> x0, waiting for transfers between devices: 713 us -> none  [on_device(): lax.psum_scatter(product.reshape(rows_here * lax.axis_size('head'), reque...]
    psum x8 -> x0, waiting for transfers between devices: 312 us -> none  [from_root(): return lax.psum(kept, axis)]
    ppermute x0 -> x45, waiting for transfers between devices: none -> 129 us  [swap(): return lax.ppermute(array, AXES, partner(**bits))]
    ppermute x0 -> x45, starting transfers between devices: none -> 67.2 us  [swap(): return lax.ppermute(array, AXES, partner(**bits))]
    pallas_call x0 -> x7, Pallas kernels: none -> 37 us  [the longest x4 18.7 us: product(): pl.pallas_call(kernel, grid=(width // TILE,), in_specs=[pl.BlockSpec(b.sh...]
    dot_general x5 -> x0, matrix products: 29.8 us -> none  [the longest x1 19 us: on_device(): jnp.dot(by_position.reshape(rows_here * lax.axis_size('head') * requests,...]
    another operation x2 -> x0, loops' own time: 21.2 us -> none  [the longest x1 20.9 us: on_device(): lax.fori_loop(0, req_count * requests, fetch_one, blank_rows)]
    convert_element_type x8 -> x0, other arithmetic: 12.4 us -> none  [the longest x2 7.66 us: conv_silu(): return jax.nn.silu(accumulated).astype(jnp.bfloat16)]
  transfers between devices with their start and end apart: 9 -> 45, of which waited for: 9 -> 21; matrix products, arithmetic and copies ran while one was open for 0% -> 9% of each run, Pallas kernels for 0% -> 12%
where the time goes in v2:
time: 306 us; the launch traced here: 304 us
  waiting for transfers between devices  129 us (42%)
  starting transfers between devices  67.2 us (22%)
  Pallas kernels  37 us (12%)
  local copies, waits for them, and re-layouts  30.6 us (10%)
  other arithmetic  20.4 us (7%)
  between operations  19.9 us (7%)
    ppermute x45, waiting for transfers between devices, swap(): return lax.ppermute(array, AXES, partner(**bits))  129 us
    ppermute x45, starting transfers between devices, swap(): return lax.ppermute(array, AXES, partner(**bits))  67.2 us
    pallas_call x4, Pallas kernels, product(): pl.pallas_call(kernel, grid=(width // TILE,), in_specs=[pl.BlockSpec(b.sh...  18.7 us
    pallas_call x1, Pallas kernels, scan(): pl.pallas_call(scan_kernel, grid_spec=pltpu.PrefetchScalarGridSpec(num_sc...  14.2 us
    unnamed x89, local copies, waits for them, and re-layouts  13.7 us
  transfers between devices with their start and end apart: 45, of which 21 were waited for; matrix products, arithmetic and copies ran while one was open for 9% of the time, Pallas kernels for 12%

profile of v2, /device:TPU:0, one launch (start us, length us, event | category | flops | bytes accessed | tf_op | source)
XLA Modules:
  0.0 304.5 jit_solution(7898894946458618023)
XLA Ops:
  0.7 1.6 fusion.39
  5.9 1.3 constant_dynamic-slice_fusion.5
  12.9 4.1 %constant_dynamic-slice_fusion.3 = (bf16[512,1024]{1,0:T(8,128)(2,1)}, bf16[512,1024]{1,0:T(8,128)(2,1)}, f32[512,1024]{1,0:T(8,128)}) fusion(bf16[512,8192]{1,0:T(8,128)(2,1)} %param.23, s32[]{:T(128)S(6)} %select_n.278, s32[]{:T(128)S(6)} %select_n.283, s32[]{:T(128)S(6)} %select_n.279), kind=kLoop, calls=%fused_computation.96 | loop fusion | flops 524288 | bytes 7340044 | tf_op jit(solution)/shard_map/dynamic_slice | solution.py:431
  17.1 2.8 collective-permute-start.10
  32.7 1.8 collective-permute-start.3
  34.5 2.2 fusion.9
  38.0 3.4 %copy-done = bf16[2,512,4096]{2,1,0:T(8,128)(2,1)S(1)} copy-done((bf16[2,512,4096]{2,1,0:T(8,128)(2,1)S(1)}, bf16[2,512,4096]{2,1,0:T(8,128)(2,1)}, u32[]{:S(2)}) %copy-start) | copy-done | bytes 8388632
  41.3 14.2 %shard_map.158 = (f32[2,512,512]{2,1,0:T(8,128)S(1)}, bf16[2,512,256]{2,1,0:T(8,128)(2,1)S(1)}, f32[2,512,8]{2,1,0:T(8,128)S(1)}, f32[2,512,256]{2,1,0:T(8,128)S(1)}) custom-call(s32[4]{0:T(128)S(1)} %pad_add_fusion.scalars, bf16[2,512,512]{2,1,0:T(8,128)(2,1)S(1)} %copy-done.10, bf16[2,512,4096]{2,1,0:T(8,128)(2,1)S(1)} %copy-done, ...), custom_call_target="tpu_custom_call" | custom-call | flops 872415232 | bytes 12582912 | tf_op jit(solution)/shard_map/pallas_call | solution.py:172
  55.6 1.5 shard_map.159
  58.5 2.1 fusion.7
  60.6 1.3 collective-permute-start.14
  61.9 27.1 %collective-permute-done.7.far = f32[512,512]{1,0:T(8,128)S(1)} collective-permute-done((f32[512,512]{1,0:T(8,128)S(1)}, f32[512,512]{1,0:T(8,128)S(1)}, u32[]{:S(2)}, u32[]{:S(2)}) %collective-permute-start.7) | collective-permute-done | bytes 1048608 | tf_op jit(solution)/shard_map/ppermute | solution.py:25
  91.1 2.5 collective-permute-start.9
  93.7 1.4 collective-permute-done.14.far
  95.1 1.2 copy-done.3
  100.5 2.6 shard_map.161
  103.1 2.6 collective-permute-start.16
  107.0 1.1 constant_dynamic-update-slice_fusion.cross
  108.1 5.2 %shard_map.160 = (f32[256,1024]{1,0:T(8,128)}, f32[256,1024]{1,0:T(8,128)}, f32[128,1024]{1,0:T(8,128)S(1)}, f32[128,1024]{1,0:T(8,128)S(1)}, f32[128,1024]{1,0:T(8,128)S(1)}, /*index=5*/f32[128,1024]{1,0:T(8,128)S(1)}) custom-call(f32[512,512]{1,0:T(8,128)S(1)} %copy-done.33, f32[512,512]{1,0:T(8,128)S(1)} %copy-done.21, ...), custom_call_target="tpu_custom_call" | custom-call | flops 2147483648 | bytes 11534336 | tf_op jit(solution)/shard_map/pallas_call | solution.py:371
  113.4 1.7 collective-permute-start.11
  115.0 2.2 collective-permute-start.23
  117.2 11.4 %collective-permute-done.16.far = f32[512,512]{1,0:T(8,128)S(1)} collective-permute-done((f32[512,512]{1,0:T(8,128)S(1)}, f32[512,512]{1,0:T(8,128)S(1)}, u32[]{:S(2)}, u32[]{:S(2)}) %collective-permute-start.16) | collective-permute-done | bytes 1048608 | tf_op jit(solution)/shard_map/ppermute | solution.py:25
  132.8 2.3 collective-permute-start.18
  135.1 2.8 collective-permute-done.11
  137.9 1.1 slice_add_fusion.14
  139.0 3.1 %collective-permute-start.12 = (f32[128,1024]{1,0:T(8,128)S(1)}, f32[128,1024]{1,0:T(8,128)}, u32[]{:S(2)}, u32[]{:S(2)}) collective-permute-start(f32[128,1024]{1,0:T(8,128)S(1)} %slice_add_fusion.14), channel_id=1, source_target_pairs={{0,6},{1,7},{2,4},{3,5},{4,2},{5,3},{6,0},{7,1},{8,14},{9,15},{10,... | collective-permute-start | bytes 1572872 | tf_op jit(solution)/shard_map/ppermute | solution.py:25
  144.0 3.3 %collective-permute-done.18 = f32[256,512]{1,0:T(8,128)} collective-permute-done((f32[256,512]{1,0:T(8,128)}, f32[256,512]{1,0:T(8,128)}, u32[]{:S(2)}, u32[]{:S(2)}) %collective-permute-start.18) | collective-permute-done | bytes 524320 | tf_op jit(solution)/shard_map/ppermute | solution.py:25
  148.4 4.9 %shard_map.162 = (f32[256,1024]{1,0:T(8,128)}, f32[256,1024]{1,0:T(8,128)S(1)}, f32[128,1024]{1,0:T(8,128)S(1)}, f32[128,1024]{1,0:T(8,128)S(1)}, f32[128,1024]{1,0:T(8,128)S(1)}, /*index=5*/f32[128,1024]{1,0:T(8,128)S(1)}) custom-call(f32[512,512]{1,0:T(8,128)S(1)} %copy-done.36, f32[512,512]{1,0:T(8,128)S(1)} %copy-done.26, ...), custom_call_target="tpu_custom_call" | custom-call | flops 2147483648 | bytes 11534336 | tf_op jit(solution)/shard_map/pallas_call | solution.py:371
  153.3 1.6 collective-permute-start.19
  154.9 1.1 slice_add_fusion.10
  156.5 3.0 collective-permute-start.25
  159.6 4.3 %shard_map.163 = (f32[256,1024]{1,0:T(8,128)S(1)}, f32[256,1024]{1,0:T(8,128)S(1)}, f32[128,1024]{1,0:T(8,128)S(1)}, f32[128,1024]{1,0:T(8,128)S(1)}, f32[128,1024]{1,0:T(8,128)S(1)}, /*index=5*/f32[128,1024]{1,0:T(8,128)S(1)}) custom-call(f32[512,512]{1,0:T(8,128)S(1)} %copy-done.34, f32[512,512]{1,0:T(8,128)S(1)} %copy-done.22, f32[512,512]{1,0:T(8,128)S(1)} %copy-done.28, ...), custom_call_target="tpu_custom_call" | custom-call | flops 2147483648 | bytes 11534336 | tf_op jit(solution)/shard_map/pallas_call | solution.py:371
  163.9 2.0 collective-permute-start.30
  165.8 4.3 %shard_map.164 = (f32[256,1024]{1,0:T(8,128)S(1)}, f32[256,1024]{1,0:T(8,128)S(1)}, f32[128,1024]{1,0:T(8,128)S(1)}, f32[128,1024]{1,0:T(8,128)S(1)}, f32[128,1024]{1,0:T(8,128)S(1)}, /*index=5*/f32[128,1024]{1,0:T(8,128)S(1)}) custom-call(f32[512,512]{1,0:T(8,128)S(1)} %copy-done.36, f32[512,512]{1,0:T(8,128)S(1)} %copy-done.26, ...), custom_call_target="tpu_custom_call" | custom-call | flops 2147483648 | bytes 11534336 | tf_op jit(solution)/shard_map/pallas_call | solution.py:371
  170.3 1.3 fusion.8
  171.6 16.4 %collective-permute-done.24 = f32[128,1024]{1,0:T(8,128)S(1)} collective-permute-done((f32[128,1024]{1,0:T(8,128)S(1)}, f32[128,1024]{1,0:T(8,128)S(1)}, u32[]{:S(2)}, u32[]{:S(2)}) %collective-permute-start.24) | collective-permute-done | bytes 524320 | tf_op jit(solution)/shard_map/ppermute | solution.py:25
  188.0 4.0 %collective-permute-start.36 = (f32[256,1024]{1,0:T(8,128)S(1)}, f32[256,1024]{1,0:T(8,128)S(1)}, u32[]{:S(2)}, u32[]{:S(2)}) collective-permute-start(f32[256,1024]{1,0:T(8,128)S(1)} %get-tuple-element.59), channel_id=1, source_target_pairs={{0,24},{1,25},{2,26},{3,27},{4,28},{5,29},{6,30},{7,31},{8,16},{9,... | collective-permute-start | bytes 3145736 | tf_op jit(solution)/shard_map/ppermute | solution.py:25
  192.0 1.1 fusion.5
  193.3 1.1 slice_add_fusion.12
  194.5 3.1 %collective-permute-start.20 = (f32[128,1024]{1,0:T(8,128)S(1)}, f32[128,1024]{1,0:T(8,128)S(1)}, u32[]{:S(2)}, u32[]{:S(2)}) collective-permute-start(f32[128,1024]{1,0:T(8,128)S(1)} %slice_add_fusion.12), channel_id=1, source_target_pairs={{0,6},{1,7},{2,4},{3,5},{4,2},{5,3},{6,0},{7,1},{8,14},{9,15},{10,... | collective-permute-start | bytes 1572872 | tf_op jit(solution)/shard_map/ppermute | solution.py:25
  197.9 11.1 %collective-permute-done.32 = f32[256,1024]{1,0:T(8,128)S(1)} collective-permute-done((f32[256,1024]{1,0:T(8,128)S(1)}, f32[256,1024]{1,0:T(8,128)S(1)}, u32[]{:S(2)}, u32[]{:S(2)}) %collective-permute-start.32) | collective-permute-done | bytes 1048608 | tf_op jit(solution)/shard_map/ppermute | solution.py:25
  209.0 3.9 %collective-permute-start.31 = (f32[128,1024]{1,0:T(8,128)S(1)}, f32[128,1024]{1,0:T(8,128)S(1)}, u32[]{:S(2)}, u32[]{:S(2)}) collective-permute-start(f32[128,1024]{1,0:T(8,128)S(1)} %slice_add_fusion.6), channel_id=1, source_target_pairs={{0,24},{1,25},{2,26},{3,27},{4,28},{5,29},{6,30},{7,31},{8,16},{9,... | collective-permute-start | bytes 1572872 | tf_op jit(solution)/shard_map/ppermute | solution.py:25
  212.9 3.2 %collective-permute-done.36 = f32[256,1024]{1,0:T(8,128)S(1)} collective-permute-done((f32[256,1024]{1,0:T(8,128)S(1)}, f32[256,1024]{1,0:T(8,128)S(1)}, u32[]{:S(2)}, u32[]{:S(2)}) %collective-permute-start.36) | collective-permute-done | bytes 1048608 | tf_op jit(solution)/shard_map/ppermute | solution.py:25
  216.1 3.2 %collective-permute-start.33 = (f32[128,1024]{1,0:T(8,128)S(1)}, f32[128,1024]{1,0:T(8,128)S(1)}, u32[]{:S(2)}, u32[]{:S(2)}) collective-permute-start(f32[128,1024]{1,0:T(8,128)S(1)} %slice_add_fusion.4), channel_id=1, source_target_pairs={{0,24},{1,25},{2,26},{3,27},{4,28},{5,29},{6,30},{7,31},{8,16},{9,... | collective-permute-start | bytes 1572872 | tf_op jit(solution)/shard_map/ppermute | solution.py:25
  219.4 19.2 %collective-permute-done.38 = f32[256,1024]{1,0:T(8,128)S(1)} collective-permute-done((f32[256,1024]{1,0:T(8,128)S(1)}, f32[256,1024]{1,0:T(8,128)S(1)}, u32[]{:S(2)}, u32[]{:S(2)}) %collective-permute-start.38) | collective-permute-done | bytes 1048608 | tf_op jit(solution)/shard_map/ppermute | solution.py:25
  238.6 2.1 collective-permute-start.39
  240.7 1.1 fusion.6
  242.3 7.5 %collective-permute-done.31 = f32[128,1024]{1,0:T(8,128)S(1)} collective-permute-done((f32[128,1024]{1,0:T(8,128)S(1)}, f32[128,1024]{1,0:T(8,128)S(1)}, u32[]{:S(2)}, u32[]{:S(2)}) %collective-permute-start.31) | collective-permute-done | bytes 524320 | tf_op jit(solution)/shard_map/ppermute | solution.py:25
  249.8 3.2 %collective-permute-start.27 = (f32[128,1024]{1,0:T(8,128)S(1)}, f32[128,1024]{1,0:T(8,128)S(1)}, u32[]{:S(2)}, u32[]{:S(2)}) collective-permute-start(f32[128,1024]{1,0:T(8,128)S(1)} %pad_maximum_fusion.5), channel_id=1, source_target_pairs={{0,24},{1,25},{2,26},{3,27},{4,28},{5,29},{6,30},{7,31},{8,16},{9,... | collective-permute-start | bytes 1572872 | tf_op jit(solution)/shard_map/ppermute | solution.py:25
  253.1 7.9 %collective-permute-done.33 = f32[128,1024]{1,0:T(8,128)S(1)} collective-permute-done((f32[128,1024]{1,0:T(8,128)S(1)}, f32[128,1024]{1,0:T(8,128)S(1)}, u32[]{:S(2)}, u32[]{:S(2)}) %collective-permute-start.33) | collective-permute-done | bytes 524320 | tf_op jit(solution)/shard_map/ppermute | solution.py:25
  261.3 1.7 collective-permute-start.34
  263.3 2.4 collective-permute-start.40
  265.7 2.3 collective-permute-done.21
  268.0 2.8 collective-permute-start.22
  271.7 3.8 %collective-permute-start.35 = (f32[64,1024]{1,0:T(8,128)S(1)}, f32[64,1024]{1,0:T(8,128)S(1)}, u32[]{:S(2)}, u32[]{:S(2)}) collective-permute-start(f32[64,1024]{1,0:T(8,128)S(1)} %slice_add_fusion.18), channel_id=1, source_target_pairs={{0,6},{1,7},{2,4},{3,5},{4,2},{5,3},{6,0},{7,1},{8,14},{9,15},{10,... | collective-permute-start | bytes 786440 | tf_op jit(solution)/shard_map/ppermute | solution.py:25
  278.1 1.8 collective-permute-done.35
  280.0 3.4 %collective-permute-done.41 = f32[64,1024]{1,0:T(8,128)S(1)} collective-permute-done((f32[64,1024]{1,0:T(8,128)S(1)}, f32[64,1024]{1,0:T(8,128)S(1)}, u32[]{:S(2)}, u32[]{:S(2)}) %collective-permute-start.41) | collective-permute-done | bytes 262176 | tf_op jit(solution)/shard_map/ppermute | solution.py:25
  283.9 3.1 %collective-permute-start.43 = (f32[2,2,16,1024]{3,2,1,0:T(8,128)S(1)}, f32[2,2,16,1024]{3,2,1,0:T(8,128)S(1)}, u32[]{:S(2)}, u32[]{:S(2)}) collective-permute-start(f32[2,2,16,1024]{3,2,1,0:T(8,128)S(1)} %get-tuple-element.84), channel_id=1, source_target_pairs={{0,1},{1,0},{2,3},{3,2},{4,5},{5,4},{6,7},{7,6},{8,9},{9,8},{10,11... | collective-permute-start | bytes 786440 | tf_op jit(solution)/shard_map/ppermute | solution.py:25
  287.0 1.7 collective-permute-start.44
  290.2 3.9 %collective-permute-done.43 = f32[2,2,16,1024]{3,2,1,0:T(8,128)S(1)} collective-permute-done((f32[2,2,16,1024]{3,2,1,0:T(8,128)S(1)}, f32[2,2,16,1024]{3,2,1,0:T(8,128)S(1)}, u32[]{:S(2)}, u32[]{:S(2)}) %collective-permute-start.43) | collective-permute-done | bytes 262176 | tf_op jit(solution)/shard_map/ppermute | solution.py:25
  294.1 2.7 collective-permute-done.44
  298.7 2.8 rev.14
  301.4 1.1 select_bitcast_fusion
  302.6 1.9 reshape.44
  (200 shorter events, 31.0 us)
Async XLA Ops:
  7.3 27.2 %collective-permute-start.4 = (f32[2,512,256]{2,1,0:T(8,128)S(1)}, f32[2,512,256]{2,1,0:T(8,128)}, u32[]{:S(2)}, u32[]{:S(2)}) collective-permute-start(f32[2,512,256]{2,1,0:T(8,128)S(1)} %pad_maximum_fusion), channel_id=1, source_target_pairs={{0,32},{1,33},{2,34},{3,35},{4,36},{5,37},{6,38},{7,39},{8,40},{9,... | collective-permute-start | bytes 3145736 | tf_op jit(solution)/shard_map/ppermute | solution.py:25
  12.2 20.1 %collective-permute-start = (f32[2,8,1024]{2,1,0:T(8,128)S(1)}, f32[2,8,1024]{2,1,0:T(8,128)S(1)}, u32[]{:S(2)}, u32[]{:S(2)}) collective-permute-start(f32[2,8,1024]{2,1,0:T(8,128)S(1)} %pad_maximum_fusion.8), channel_id=1, source_target_pairs={{0,32},{1,33},{2,34},{3,35},{4,36},{5,37},{6,38},{7,39},{8,40},{9,... | collective-permute-start | bytes 196616 | tf_op jit(solution)/shard_map/ppermute | solution.py:25
  12.8 19.5 %collective-permute-start.2 = (f32[2,8,1024]{2,1,0:T(8,128)S(1)}, f32[2,8,1024]{2,1,0:T(8,128)S(1)}, u32[]{:S(2)}, u32[]{:S(2)}) collective-permute-start(f32[2,8,1024]{2,1,0:T(8,128)S(1)} %pad_maximum_fusion.9), channel_id=1, source_target_pairs={{0,32},{1,33},{2,34},{3,35},{4,36},{5,37},{6,38},{7,39},{8,40},{9,... | collective-permute-start | bytes 196616 | tf_op jit(solution)/shard_map/ppermute | solution.py:25
  12.9 11.6 %copy-start.39 = (s32[8,1]{0,1:T(1,128)S(1)}, s32[8,1]{0,1:T(1,128)}, u32[]{:S(2)}) copy-start(s32[8,1]{0,1:T(1,128)} %param.27) | copy-start | bytes 100
  12.9 16.0 %copy-start.41 = (f32[8]{0:T(128)S(1)}, f32[8]{0:T(128)}, u32[]{:S(2)}) copy-start(f32[8]{0:T(128)} %param.20) | copy-start | bytes 100
  12.9 19.2 %copy-start.40 = (s32[2]{0:T(128)S(1)}, s32[2]{0:T(128)}, u32[]{:S(2)}) copy-start(s32[2]{0:T(128)} %param.29) | copy-start | bytes 28
  12.9 21.5 %copy-start.37 = (f32[4,512,256]{2,1,0:T(8,128)S(1)}, f32[4,512,256]{2,1,0:T(8,128)}, u32[]{:S(2)}) copy-start(f32[4,512,256]{2,1,0:T(8,128)} %param.24) | copy-start | bytes 6291460
  17.1 76.6 %collective-permute-start.10 = (f32[512,1024]{1,0:T(8,128)}, f32[512,1024]{1,0:T(8,128)}, u32[]{:S(2)}, u32[]{:S(2)}) collective-permute-start(f32[512,1024]{1,0:T(8,128)} %get-tuple-element.68), channel_id=1, source_target_pairs={{0,65},{1,64},{2,67},{3,66},{4,69},{5,68},{6,71},{7,70},{8,73},{9,... | collective-permute-start | bytes 6291464 | tf_op jit(solution)/shard_map/ppermute | solution.py:25
  32.4 4.8 %collective-permute-start.1 = (f32[8,1024]{1,0:T(8,128)S(1)}, f32[8,1024]{1,0:T(8,128)S(1)}, u32[]{:S(2)}, u32[]{:S(2)}) collective-permute-start(f32[8,1024]{1,0:T(8,128)S(1)} %get-tuple-element.121), channel_id=1, source_target_pairs={{0,64},{1,65},{2,66},{3,67},{4,68},{5,69},{6,70},{7,71},{8,72},{9,... | collective-permute-start | bytes 98312 | tf_op jit(solution)/shard_map/ppermute | solution.py:25
  32.7 4.6 %collective-permute-start.3 = (f32[8,1024]{1,0:T(8,128)S(1)}, f32[8,1024]{1,0:T(8,128)S(1)}, u32[]{:S(2)}, u32[]{:S(2)}) collective-permute-start(f32[8,1024]{1,0:T(8,128)S(1)} %get-tuple-element.120), channel_id=1, source_target_pairs={{0,64},{1,65},{2,66},{3,67},{4,68},{5,69},{6,70},{7,71},{8,72},{9,... | collective-permute-start | bytes 98312 | tf_op jit(solution)/shard_map/ppermute | solution.py:25
  36.7 18.9 %collective-permute-start.5 = (f32[512,256]{1,0:T(8,128)S(1)}, f32[512,256]{1,0:T(8,128)S(1)}, u32[]{:S(2)}, u32[]{:S(2)}) collective-permute-start(f32[512,256]{1,0:T(8,128)S(1)} %get-tuple-element.69), channel_id=1, source_target_pairs={{0,64},{1,65},{2,66},{3,67},{4,68},{5,69},{6,70},{7,71},{8,72},{9,... | collective-permute-start | bytes 1572872 | tf_op jit(solution)/shard_map/ppermute | solution.py:25
  37.1 21.4 %collective-permute-start.13 = (f32[2,512,256]{2,1,0:T(8,128)S(1)}, f32[2,512,256]{2,1,0:T(8,128)S(1)}, u32[]{:S(2)}, u32[]{:S(2)}) collective-permute-start(f32[2,512,256]{2,1,0:T(8,128)S(1)} %pad_maximum_fusion.1), channel_id=1, source_target_pairs={{0,32},{1,33},{2,34},{3,35},{4,36},{5,37},{6,38},{7,39},{8,40},{9,... | collective-permute-start | bytes 3145736 | tf_op jit(solution)/shard_map/ppermute | solution.py:25
  41.3 14.3 %copy-start.1 = (bf16[2,512,512]{2,1,0:T(8,128)(2,1)S(1)}, bf16[2,512,512]{2,1,0:T(8,128)(2,1)}, u32[]{:S(2)}) copy-start(bf16[2,512,512]{2,1,0:T(8,128)(2,1)} %z_ref.3) | copy-start | bytes 3145732
  57.1 34.0 %copy-start.13 = (f32[1,512,256]{2,1,0:T(8,128)}, f32[1,512,256]{2,1,0:T(8,128)S(1)}, u32[]{:S(2)}) copy-start(f32[1,512,256]{2,1,0:T(8,128)S(1)} %get-tuple-element.64) | copy-start | bytes 1572868
  57.2 34.0 %copy-start.32 = (f32[512,512]{1,0:T(8,128)}, f32[512,512]{1,0:T(8,128)S(1)}, u32[]{:S(2)}) copy-start(f32[512,512]{1,0:T(8,128)S(1)} %get-tuple-element.38.own) | copy-start | bytes 3145732
  57.2 31.8 %collective-permute-start.7 = (f32[512,512]{1,0:T(8,128)S(1)}, f32[512,512]{1,0:T(8,128)S(1)}, u32[]{:S(2)}, u32[]{:S(2)}) collective-permute-start(f32[512,512]{1,0:T(8,128)S(1)} %get-tuple-element.38.own), channel_id=1, source_target_pairs={{0,65},{1,64},{2,67},{3,66},{4,69},{5,68},{6,71},{7,70},{8,73},{9,... | collective-permute-start | bytes 3145736 | tf_op jit(solution)/shard_map/ppermute | solution.py:25
  57.7 32.5 %collective-permute-start.6 = (f32[512,512]{1,0:T(8,128)S(1)}, f32[512,512]{1,0:T(8,128)S(1)}, u32[]{:S(2)}, u32[]{:S(2)}) collective-permute-start(f32[512,512]{1,0:T(8,128)S(1)} %get-tuple-element.38.own), channel_id=1, source_target_pairs={{0,64},{1,65},{2,66},{3,67},{4,68},{5,69},{6,70},{7,71},{8,72},{9,... | collective-permute-start | bytes 3145736 | tf_op jit(solution)/shard_map/ppermute | solution.py:25
  60.6 34.5 %collective-permute-start.14 = (f32[512,256]{1,0:T(8,128)}, f32[512,256]{1,0:T(8,128)}, u32[]{:S(2)}, u32[]{:S(2)}) collective-permute-start(f32[512,256]{1,0:T(8,128)} %get-tuple-element.80), channel_id=1, source_target_pairs={{0,64},{1,65},{2,66},{3,67},{4,68},{5,69},{6,70},{7,71},{8,72},{9,... | collective-permute-start | bytes 1572872 | tf_op jit(solution)/shard_map/ppermute | solution.py:25
  89.9 16.0 %collective-permute-start.8 = (f32[256,512]{1,0:T(8,128)}, f32[256,512]{1,0:T(8,128)}, u32[]{:S(2)}, u32[]{:S(2)}) collective-permute-start(f32[256,512]{1,0:T(8,128)} %slice.338), channel_id=1, source_target_pairs={{0,64},{1,65},{2,66},{3,67},{4,68},{5,69},{6,70},{7,71},{8,72},{9,... | collective-permute-start | bytes 1572872 | tf_op jit(solution)/shard_map/ppermute | solution.py:25
  91.1 15.9 %collective-permute-start.9 = (f32[256,512]{1,0:T(8,128)}, f32[256,512]{1,0:T(8,128)}, u32[]{:S(2)}, u32[]{:S(2)}) collective-permute-start(f32[256,512]{1,0:T(8,128)} %slice.339), channel_id=1, source_target_pairs={{0,65},{1,64},{2,67},{3,66},{4,69},{5,68},{6,71},{7,70},{8,73},{9,... | collective-permute-start | bytes 1572872 | tf_op jit(solution)/shard_map/ppermute | solution.py:25
  93.7 65.8 %collective-permute-start.29 = (f32[512,1024]{1,0:T(8,128)}, f32[512,1024]{1,0:T(8,128)}, u32[]{:S(2)}, u32[]{:S(2)}) collective-permute-start(f32[512,1024]{1,0:T(8,128)} %collective-permute-done.10.w_far_ref), channel_id=1, source_target_pairs={{0,32},{1,33},{2,34},{3,35},{4,36},{5,37},{6,38},{7,39},{8,40},{9,... | collective-permute-start | bytes 6291464 | tf_op jit(solution)/shard_map/ppermute | solution.py:25
  100.5 7.6 %copy-start.21 = (f32[512,512]{1,0:T(8,128)S(1)}, f32[512,512]{1,0:T(8,128)}, u32[]{:S(2)}) copy-start(f32[512,512]{1,0:T(8,128)} %copy-done.20) | copy-start | bytes 3145732
  100.5 7.6 %copy-start.33 = (f32[512,512]{1,0:T(8,128)S(1)}, f32[512,512]{1,0:T(8,128)}, u32[]{:S(2)}) copy-start(f32[512,512]{1,0:T(8,128)} %copy-done.32) | copy-start | bytes 3145732
  103.1 10.3 %copy-start.35 = (f32[512,512]{1,0:T(8,128)}, f32[512,512]{1,0:T(8,128)S(1)}, u32[]{:S(2)}) copy-start(f32[512,512]{1,0:T(8,128)S(1)} %get-tuple-element.42.own) | copy-start | bytes 3145732
  103.1 25.5 %collective-permute-start.16 = (f32[512,512]{1,0:T(8,128)S(1)}, f32[512,512]{1,0:T(8,128)S(1)}, u32[]{:S(2)}, u32[]{:S(2)}) collective-permute-start(f32[512,512]{1,0:T(8,128)S(1)} %get-tuple-element.42.own), channel_id=1, source_target_pairs={{0,65},{1,64},{2,67},{3,66},{4,69},{5,68},{6,71},{7,70},{8,73},{9,... | collective-permute-start | bytes 3145736 | tf_op jit(solution)/shard_map/ppermute | solution.py:25
  105.7 25.3 %collective-permute-start.15 = (f32[512,512]{1,0:T(8,128)S(1)}, f32[512,512]{1,0:T(8,128)S(1)}, u32[]{:S(2)}, u32[]{:S(2)}) collective-permute-start(f32[512,512]{1,0:T(8,128)S(1)} %get-tuple-element.42.own), channel_id=1, source_target_pairs={{0,64},{1,65},{2,66},{3,67},{4,68},{5,69},{6,70},{7,71},{8,72},{9,... | collective-permute-start | bytes 3145736 | tf_op jit(solution)/shard_map/ppermute | solution.py:25
  108.1 5.3 %copy-start.27 = (f32[512,512]{1,0:T(8,128)}, f32[512,512]{1,0:T(8,128)S(1)}, u32[]{:S(2)}) copy-start(f32[512,512]{1,0:T(8,128)S(1)} %constant_dynamic-update-slice_fusion.cross) | copy-start | bytes 3145732
  113.4 24.5 %collective-permute-start.11 = (f32[256,1024]{1,0:T(8,128)}, f32[256,1024]{1,0:T(8,128)}, u32[]{:S(2)}, u32[]{:S(2)}) collective-permute-start(f32[256,1024]{1,0:T(8,128)} %get-tuple-element.40), channel_id=1, source_target_pairs={{0,2},{1,3},{2,0},{3,1},{4,6},{5,7},{6,4},{7,5},{8,10},{9,11},{10,... | collective-permute-start | bytes 3145736 | tf_op jit(solution)/shard_map/ppermute | solution.py:25
  115.0 39.8 %collective-permute-start.23 = (f32[256,1024]{1,0:T(8,128)}, f32[256,1024]{1,0:T(8,128)}, u32[]{:S(2)}, u32[]{:S(2)}) collective-permute-start(f32[256,1024]{1,0:T(8,128)} %get-tuple-element.47), channel_id=1, source_target_pairs={{0,6},{1,7},{2,4},{3,5},{4,2},{5,3},{6,0},{7,1},{8,14},{9,15},{10,... | collective-permute-start | bytes 3145736 | tf_op jit(solution)/shard_map/ppermute | solution.py:25
  130.4 12.5 %collective-permute-start.17 = (f32[256,512]{1,0:T(8,128)}, f32[256,512]{1,0:T(8,128)}, u32[]{:S(2)}, u32[]{:S(2)}) collective-permute-start(f32[256,512]{1,0:T(8,128)} %slice.345), channel_id=1, source_target_pairs={{0,64},{1,65},{2,66},{3,67},{4,68},{5,69},{6,70},{7,71},{8,72},{9,... | collective-permute-start | bytes 1572872 | tf_op jit(solution)/shard_map/ppermute | solution.py:25
  132.8 14.5 %collective-permute-start.18 = (f32[256,512]{1,0:T(8,128)}, f32[256,512]{1,0:T(8,128)}, u32[]{:S(2)}, u32[]{:S(2)}) collective-permute-start(f32[256,512]{1,0:T(8,128)} %slice.346), channel_id=1, source_target_pairs={{0,65},{1,64},{2,67},{3,66},{4,69},{5,68},{6,71},{7,70},{8,73},{9,... | collective-permute-start | bytes 1572872 | tf_op jit(solution)/shard_map/ppermute | solution.py:25
  135.1 13.2 %copy-start.24 = (f32[512,512]{1,0:T(8,128)S(1)}, f32[512,512]{1,0:T(8,128)}, u32[]{:S(2)}) copy-start(f32[512,512]{1,0:T(8,128)} %copy-done.23) | copy-start | bytes 3145732
  135.1 13.2 %copy-start.26 = (f32[512,512]{1,0:T(8,128)S(1)}, f32[512,512]{1,0:T(8,128)}, u32[]{:S(2)}) copy-start(f32[512,512]{1,0:T(8,128)} %copy-done.25) | copy-start | bytes 3145732
  135.1 13.2 %copy-start.36 = (f32[512,512]{1,0:T(8,128)S(1)}, f32[512,512]{1,0:T(8,128)}, u32[]{:S(2)}) copy-start(f32[512,512]{1,0:T(8,128)} %copy-done.35) | copy-start | bytes 3145732
  139.0 31.1 %collective-permute-start.12 = (f32[128,1024]{1,0:T(8,128)S(1)}, f32[128,1024]{1,0:T(8,128)}, u32[]{:S(2)}, u32[]{:S(2)}) collective-permute-start(f32[128,1024]{1,0:T(8,128)S(1)} %slice_add_fusion.14), channel_id=1, source_target_pairs={{0,6},{1,7},{2,4},{3,5},{4,2},{5,3},{6,0},{7,1},{8,14},{9,15},{10,... | collective-permute-start | bytes 1572872 | tf_op jit(solution)/shard_map/ppermute | solution.py:25
  148.3 11.2 %copy-start.11 = (bf16[512,1024]{1,0:T(8,128)(2,1)S(1)}, bf16[512,1024]{1,0:T(8,128)(2,1)}, u32[]{:S(2)}) copy-start(bf16[512,1024]{1,0:T(8,128)(2,1)} %get-tuple-element.67.w_own_ref) | copy-start | bytes 3145732
  148.3 11.2 %copy-start.19 = (f32[512,512]{1,0:T(8,128)S(1)}, f32[512,512]{1,0:T(8,128)}, u32[]{:S(2)}) copy-start(f32[512,512]{1,0:T(8,128)} %copy-done.17) | copy-start | bytes 3145732
  148.3 11.2 %copy-start.22 = (f32[512,512]{1,0:T(8,128)S(1)}, f32[512,512]{1,0:T(8,128)}, u32[]{:S(2)}) copy-start(f32[512,512]{1,0:T(8,128)} %copy-done.20) | copy-start | bytes 3145732
  148.4 11.2 %copy-start.28 = (f32[512,512]{1,0:T(8,128)S(1)}, f32[512,512]{1,0:T(8,128)}, u32[]{:S(2)}) copy-start(f32[512,512]{1,0:T(8,128)} %copy-done.27) | copy-start | bytes 3145732
  148.4 11.2 %copy-start.34 = (f32[512,512]{1,0:T(8,128)S(1)}, f32[512,512]{1,0:T(8,128)}, u32[]{:S(2)}) copy-start(f32[512,512]{1,0:T(8,128)} %copy-done.32) | copy-start | bytes 3145732
  153.3 40.0 %collective-permute-start.19 = (f32[256,1024]{1,0:T(8,128)}, f32[256,1024]{1,0:T(8,128)}, u32[]{:S(2)}, u32[]{:S(2)}) collective-permute-start(f32[256,1024]{1,0:T(8,128)} %get-tuple-element.44), channel_id=1, source_target_pairs={{0,2},{1,3},{2,0},{3,1},{4,6},{5,7},{6,4},{7,5},{8,10},{9,11},{10,... | collective-permute-start | bytes 3145736 | tf_op jit(solution)/shard_map/ppermute | solution.py:25
  156.0 32.0 %collective-permute-start.24 = (f32[128,1024]{1,0:T(8,128)S(1)}, f32[128,1024]{1,0:T(8,128)S(1)}, u32[]{:S(2)}, u32[]{:S(2)}) collective-permute-start(f32[128,1024]{1,0:T(8,128)S(1)} %slice_add_fusion.10), channel_id=1, source_target_pairs={{0,2},{1,3},{2,0},{3,1},{4,6},{5,7},{6,4},{7,5},{8,10},{9,11},{10,... | collective-permute-start | bytes 1572872 | tf_op jit(solution)/shard_map/ppermute | solution.py:25
  156.5 38.0 %collective-permute-start.25 = (f32[256,1024]{1,0:T(8,128)S(1)}, f32[256,1024]{1,0:T(8,128)S(1)}, u32[]{:S(2)}, u32[]{:S(2)}) collective-permute-start(f32[256,1024]{1,0:T(8,128)S(1)} %get-tuple-element.50), channel_id=1, source_target_pairs={{0,6},{1,7},{2,4},{3,5},{4,2},{5,3},{6,0},{7,1},{8,14},{9,15},{10,... | collective-permute-start | bytes 3145736 | tf_op jit(solution)/shard_map/ppermute | solution.py:25
  163.9 33.8 %collective-permute-start.30 = (f32[256,1024]{1,0:T(8,128)S(1)}, f32[256,1024]{1,0:T(8,128)S(1)}, u32[]{:S(2)}, u32[]{:S(2)}) collective-permute-start(f32[256,1024]{1,0:T(8,128)S(1)} %get-tuple-element.53), channel_id=1, source_target_pairs={{0,8},{1,9},{2,10},{3,11},{4,12},{5,13},{6,14},{7,15},{8,0},{9,1},... | collective-permute-start | bytes 3145736 | tf_op jit(solution)/shard_map/ppermute | solution.py:25
  170.1 38.9 %collective-permute-start.32 = (f32[256,1024]{1,0:T(8,128)S(1)}, f32[256,1024]{1,0:T(8,128)S(1)}, u32[]{:S(2)}, u32[]{:S(2)}) collective-permute-start(f32[256,1024]{1,0:T(8,128)S(1)} %get-tuple-element.56), channel_id=1, source_target_pairs={{0,8},{1,9},{2,10},{3,11},{4,12},{5,13},{6,14},{7,15},{8,0},{9,1},... | collective-permute-start | bytes 3145736 | tf_op jit(solution)/shard_map/ppermute | solution.py:25
  188.0 28.1 %collective-permute-start.36 = (f32[256,1024]{1,0:T(8,128)S(1)}, f32[256,1024]{1,0:T(8,128)S(1)}, u32[]{:S(2)}, u32[]{:S(2)}) collective-permute-start(f32[256,1024]{1,0:T(8,128)S(1)} %get-tuple-element.59), channel_id=1, source_target_pairs={{0,24},{1,25},{2,26},{3,27},{4,28},{5,29},{6,30},{7,31},{8,16},{9,... | collective-permute-start | bytes 3145736 | tf_op jit(solution)/shard_map/ppermute | solution.py:25
  193.3 45.3 %collective-permute-start.38 = (f32[256,1024]{1,0:T(8,128)S(1)}, f32[256,1024]{1,0:T(8,128)S(1)}, u32[]{:S(2)}, u32[]{:S(2)}) collective-permute-start(f32[256,1024]{1,0:T(8,128)S(1)} %get-tuple-element.62), channel_id=1, source_target_pairs={{0,24},{1,25},{2,26},{3,27},{4,28},{5,29},{6,30},{7,31},{8,16},{9,... | collective-permute-start | bytes 3145736 | tf_op jit(solution)/shard_map/ppermute | solution.py:25
  194.5 44.2 %collective-permute-start.20 = (f32[128,1024]{1,0:T(8,128)S(1)}, f32[128,1024]{1,0:T(8,128)S(1)}, u32[]{:S(2)}, u32[]{:S(2)}) collective-permute-start(f32[128,1024]{1,0:T(8,128)S(1)} %slice_add_fusion.12), channel_id=1, source_target_pairs={{0,6},{1,7},{2,4},{3,5},{4,2},{5,3},{6,0},{7,1},{8,14},{9,15},{10,... | collective-permute-start | bytes 1572872 | tf_op jit(solution)/shard_map/ppermute | solution.py:25
  197.6 44.4 %collective-permute-start.26 = (f32[128,1024]{1,0:T(8,128)S(1)}, f32[128,1024]{1,0:T(8,128)S(1)}, u32[]{:S(2)}, u32[]{:S(2)}) collective-permute-start(f32[128,1024]{1,0:T(8,128)S(1)} %slice_add_fusion.8), channel_id=1, source_target_pairs={{0,2},{1,3},{2,0},{3,1},{4,6},{5,7},{6,4},{7,5},{8,10},{9,11},{10,... | collective-permute-start | bytes 1572872 | tf_op jit(solution)/shard_map/ppermute | solution.py:25
  209.0 40.8 %collective-permute-start.31 = (f32[128,1024]{1,0:T(8,128)S(1)}, f32[128,1024]{1,0:T(8,128)S(1)}, u32[]{:S(2)}, u32[]{:S(2)}) collective-permute-start(f32[128,1024]{1,0:T(8,128)S(1)} %slice_add_fusion.6), channel_id=1, source_target_pairs={{0,24},{1,25},{2,26},{3,27},{4,28},{5,29},{6,30},{7,31},{8,16},{9,... | collective-permute-start | bytes 1572872 | tf_op jit(solution)/shard_map/ppermute | solution.py:25
  216.1 44.9 %collective-permute-start.33 = (f32[128,1024]{1,0:T(8,128)S(1)}, f32[128,1024]{1,0:T(8,128)S(1)}, u32[]{:S(2)}, u32[]{:S(2)}) collective-permute-start(f32[128,1024]{1,0:T(8,128)S(1)} %slice_add_fusion.4), channel_id=1, source_target_pairs={{0,24},{1,25},{2,26},{3,27},{4,28},{5,29},{6,30},{7,31},{8,16},{9,... | collective-permute-start | bytes 1572872 | tf_op jit(solution)/shard_map/ppermute | solution.py:25
  238.6 24.4 %collective-permute-start.37 = (f32[128,1024]{1,0:T(8,128)S(1)}, f32[128,1024]{1,0:T(8,128)S(1)}, u32[]{:S(2)}, u32[]{:S(2)}) collective-permute-start(f32[128,1024]{1,0:T(8,128)S(1)} %slice_add_fusion.2), channel_id=1, source_target_pairs={{0,8},{1,9},{2,10},{3,11},{4,12},{5,13},{6,14},{7,15},{8,0},{9,1},... | collective-permute-start | bytes 1572872 | tf_op jit(solution)/shard_map/ppermute | solution.py:25
  238.6 24.4 %collective-permute-start.39 = (f32[128,1024]{1,0:T(8,128)S(1)}, f32[128,1024]{1,0:T(8,128)S(1)}, u32[]{:S(2)}, u32[]{:S(2)}) collective-permute-start(f32[128,1024]{1,0:T(8,128)S(1)} %slice_add_fusion), channel_id=1, source_target_pairs={{0,8},{1,9},{2,10},{3,11},{4,12},{5,13},{6,14},{7,15},{8,0},{9,1},... | collective-permute-start | bytes 1572872 | tf_op jit(solution)/shard_map/ppermute | solution.py:25
  242.0 26.0 %collective-permute-start.21 = (f32[128,1024]{1,0:T(8,128)S(1)}, f32[128,1024]{1,0:T(8,128)S(1)}, u32[]{:S(2)}, u32[]{:S(2)}) collective-permute-start(f32[128,1024]{1,0:T(8,128)S(1)} %pad_maximum_fusion.4), channel_id=1, source_target_pairs={{0,8},{1,9},{2,10},{3,11},{4,12},{5,13},{6,14},{7,15},{8,0},{9,1},... | collective-permute-start | bytes 1572872 | tf_op jit(solution)/shard_map/ppermute | solution.py:25
  249.8 21.8 %collective-permute-start.27 = (f32[128,1024]{1,0:T(8,128)S(1)}, f32[128,1024]{1,0:T(8,128)S(1)}, u32[]{:S(2)}, u32[]{:S(2)}) collective-permute-start(f32[128,1024]{1,0:T(8,128)S(1)} %pad_maximum_fusion.5), channel_id=1, source_target_pairs={{0,24},{1,25},{2,26},{3,27},{4,28},{5,29},{6,30},{7,31},{8,16},{9,... | collective-permute-start | bytes 1572872 | tf_op jit(solution)/shard_map/ppermute | solution.py:25
  261.3 10.4 %collective-permute-start.34 = (f32[128,1024]{1,0:T(8,128)S(1)}, f32[128,1024]{1,0:T(8,128)S(1)}, u32[]{:S(2)}, u32[]{:S(2)}) collective-permute-start(f32[128,1024]{1,0:T(8,128)S(1)} %pad_maximum_fusion.6), channel_id=1, source_target_pairs={{0,2},{1,3},{2,0},{3,1},{4,6},{5,7},{6,4},{7,5},{8,10},{9,11},{10,... | collective-permute-start | bytes 1572872 | tf_op jit(solution)/shard_map/ppermute | solution.py:25
  263.3 13.3 %collective-permute-start.40 = (f32[128,1024]{1,0:T(8,128)S(1)}, f32[128,1024]{1,0:T(8,128)S(1)}, u32[]{:S(2)}, u32[]{:S(2)}) collective-permute-start(f32[128,1024]{1,0:T(8,128)S(1)} %pad_maximum_fusion.7), channel_id=1, source_target_pairs={{0,6},{1,7},{2,4},{3,5},{4,2},{5,3},{6,0},{7,1},{8,14},{9,15},{10,... | collective-permute-start | bytes 1572872 | tf_op jit(solution)/shard_map/ppermute | solution.py:25
  268.0 9.0 %collective-permute-start.22 = (f32[64,1024]{1,0:T(8,128)S(1)}, f32[64,1024]{1,0:T(8,128)S(1)}, u32[]{:S(2)}, u32[]{:S(2)}) collective-permute-start(f32[64,1024]{1,0:T(8,128)S(1)} %slice_add_fusion.22), channel_id=1, source_target_pairs={{0,24},{1,25},{2,26},{3,27},{4,28},{5,29},{6,30},{7,31},{8,16},{9,... | collective-permute-start | bytes 786440 | tf_op jit(solution)/shard_map/ppermute | solution.py:25
  271.6 6.5 %collective-permute-start.28 = (f32[64,1024]{1,0:T(8,128)S(1)}, f32[64,1024]{1,0:T(8,128)S(1)}, u32[]{:S(2)}, u32[]{:S(2)}) collective-permute-start(f32[64,1024]{1,0:T(8,128)S(1)} %slice_add_fusion.20), channel_id=1, source_target_pairs={{0,8},{1,9},{2,10},{3,11},{4,12},{5,13},{6,14},{7,15},{8,0},{9,1},... | collective-permute-start | bytes 786440 | tf_op jit(solution)/shard_map/ppermute | solution.py:25
  271.7 8.2 %collective-permute-start.35 = (f32[64,1024]{1,0:T(8,128)S(1)}, f32[64,1024]{1,0:T(8,128)S(1)}, u32[]{:S(2)}, u32[]{:S(2)}) collective-permute-start(f32[64,1024]{1,0:T(8,128)S(1)} %slice_add_fusion.18), channel_id=1, source_target_pairs={{0,6},{1,7},{2,4},{3,5},{4,2},{5,3},{6,0},{7,1},{8,14},{9,15},{10,... | collective-permute-start | bytes 786440 | tf_op jit(solution)/shard_map/ppermute | solution.py:25
  276.6 6.7 %collective-permute-start.41 = (f32[64,1024]{1,0:T(8,128)S(1)}, f32[64,1024]{1,0:T(8,128)S(1)}, u32[]{:S(2)}, u32[]{:S(2)}) collective-permute-start(f32[64,1024]{1,0:T(8,128)S(1)} %slice_add_fusion.16), channel_id=1, source_target_pairs={{0,2},{1,3},{2,0},{3,1},{4,6},{5,7},{6,4},{7,5},{8,10},{9,11},{10,... | collective-permute-start | bytes 786440 | tf_op jit(solution)/shard_map/ppermute | solution.py:25
  283.8 6.5 %collective-permute-start.42 = (f32[2,2,16,1024]{3,2,1,0:T(8,128)S(1)}, f32[2,2,16,1024]{3,2,1,0:T(8,128)S(1)}, u32[]{:S(2)}, u32[]{:S(2)}) collective-permute-start(f32[2,2,16,1024]{3,2,1,0:T(8,128)S(1)} %get-tuple-element.83), channel_id=1, source_target_pairs={{0,64},{1,65},{2,66},{3,67},{4,68},{5,69},{6,70},{7,71},{8,72},{9,... | collective-permute-start | bytes 786440 | tf_op jit(solution)/shard_map/ppermute | solution.py:25
  283.9 10.2 %collective-permute-start.43 = (f32[2,2,16,1024]{3,2,1,0:T(8,128)S(1)}, f32[2,2,16,1024]{3,2,1,0:T(8,128)S(1)}, u32[]{:S(2)}, u32[]{:S(2)}) collective-permute-start(f32[2,2,16,1024]{3,2,1,0:T(8,128)S(1)} %get-tuple-element.84), channel_id=1, source_target_pairs={{0,1},{1,0},{2,3},{3,2},{4,5},{5,4},{6,7},{7,6},{8,9},{9,8},{10,11... | collective-permute-start | bytes 786440 | tf_op jit(solution)/shard_map/ppermute | solution.py:25
  287.0 9.8 %collective-permute-start.44 = (f32[2,2,16,1024]{3,2,1,0:T(8,128)S(1)}, f32[2,2,16,1024]{3,2,1,0:T(8,128)S(1)}, u32[]{:S(2)}, u32[]{:S(2)}) collective-permute-start(f32[2,2,16,1024]{3,2,1,0:T(8,128)S(1)} %get-tuple-element.85), channel_id=1, source_target_pairs={{0,65},{1,64},{2,67},{3,66},{4,69},{5,68},{6,71},{7,70},{8,73},{9,... | collective-permute-start | bytes 786440 | tf_op jit(solution)/shard_map/ppermute | solution.py:25
  (23 other events, 58.3 us)

commit v3 on v2

v3 whole, which is shorter than its diff:
```python
import functools

import jax
import jax.numpy as jnp
from jax import lax
from jax.experimental import pallas as pl
from jax.experimental.pallas import tpu as pltpu
from jax.sharding import PartitionSpec as P

HEADS = 256
HEADDIM = 64
STATE = 256
GROUPS = 8
BLOCK = 128
PARTS = 1
ROWS = 32 // PARTS
AXES = ("req", "head")
MIB = 1 << 20


def swap(array, first=0, second=0, hi=0, lo=0, core=0):
    pairs = []
    for source in range(128):
        y, z = (second, first) if source >> 5 & 1 else (first, second)
        pairs.append((source, source ^ (lo << 6 | core << 5 | z << 3 | y << 1 | hi)))
    return lax.ppermute(array, AXES, pairs)


def place_in_mesh():
    req, head = lax.axis_index("req"), lax.axis_index("head")
    return head >> 3, head >> 1 & 3, head & 1, req >> 1, req & 1


def conv_rows(window, previous, rows, taps):
    window[0:8, :] = previous
    window[8 : 8 + BLOCK, :] = rows
    total = window[5 : 5 + BLOCK, :] * taps[0:1, :]
    for offset in range(1, 4):
        total = total + window[5 + offset : 5 + offset + BLOCK, :] * taps[offset : offset + 1, :]
    return total * (1.0 / (1.0 + jnp.exp(-total)))


def spread(columns, lane):
    pairs = []
    for pair in range(4):
        even = columns[:, 2 * pair : 2 * pair + 1]
        odd = columns[:, 2 * pair + 1 : 2 * pair + 2]
        pairs.append(jnp.where(lane < HEADDIM, even, odd))
    return jnp.concatenate(pairs, axis=1)


def scan_kernel(
    lengths,
    x_ref,
    b_ref,
    c_ref,
    x_tail,
    b_tail,
    c_tail,
    x_taps,
    b_taps,
    c_taps,
    dt_ref,
    rate_ref,
    skip_ref,
    y_ref,
    c_out,
    decay_out,
    state_out,
    x_window,
    b_window,
    c_window,
    x_last,
    b_last,
    c_last,
    state,
    passed,
):
    request, block = pl.program_id(0), pl.program_id(1)

    @pl.when(block == 0)
    def _():
        x_last[...] = x_tail[0]
        b_last[...] = b_tail[0]
        c_last[...] = c_tail[0]
        state[...] = jnp.zeros_like(state)
        passed[...] = jnp.zeros_like(passed)

    def convolve(window, last, ref, taps):
        rows = ref[0].astype(jnp.float32)
        made = conv_rows(window, last[...], rows, taps[...].astype(jnp.float32))
        last[...] = rows[BLOCK - 8 :]
        return made.astype(jnp.bfloat16)

    x = convolve(x_window, x_last, x_ref, x_taps)
    b = convolve(b_window, b_last, b_ref, b_taps)
    c = convolve(c_window, c_last, c_ref, c_taps)
    c_out[0] = c

    place = lax.broadcasted_iota(jnp.int32, (8, BLOCK), 1)
    raw = dt_ref[0]
    step = jnp.maximum(raw, 0.0) + jnp.log1p(jnp.exp(-jnp.abs(raw)))
    step = jnp.where(place + block * BLOCK < lengths[request], step, 0.0)
    decay = -jnp.exp(rate_ref[...]) * step
    reach = 1
    while reach < BLOCK:
        decay = decay + jnp.where(place >= reach, pltpu.roll(decay, reach, 1), 0.0)
        reach *= 2
    closing = decay[:, BLOCK - 1 : BLOCK]
    weight = jnp.exp(closing - decay) * step
    turned = jnp.transpose(
        jnp.concatenate(
            [decay, weight, passed[...] + decay, jnp.zeros((BLOCK - 24, BLOCK), jnp.float32)],
            axis=0,
        )
    )
    passed[...] = passed[...] + closing
    decay_out[0] = jnp.exp(turned[:, 16:24])

    lane = lax.broadcasted_iota(jnp.int32, (BLOCK, BLOCK), 1)
    causal = lax.broadcasted_iota(jnp.int32, (BLOCK, BLOCK), 0) >= lane
    scores = lax.dot_general(c, b, (((1,), (1,)), ((), ())), preferred_element_type=jnp.float32)
    scores = jnp.where(causal, scores, 0.0)
    within = []
    for pair in range(4):
        inputs = x[:, pair * 128 : (pair + 1) * 128]
        halves = []
        for head in (2 * pair, 2 * pair + 1):
            gap = jnp.where(causal, turned[:, head : head + 1] - decay[head : head + 1, :], 0.0)
            mixing = jnp.exp(gap) * scores * step[head : head + 1, :]
            halves.append(
                jnp.dot(mixing.astype(jnp.bfloat16), inputs, preferred_element_type=jnp.float32)
            )
        within.append(jnp.where(lane < HEADDIM, halves[0], halves[1]))
    carried = lax.dot_general(
        c,
        state[...].astype(jnp.bfloat16),
        (((1,), (1,)), ((), ())),
        preferred_element_type=jnp.float32,
    )
    wide = x.astype(jnp.float32)
    y_ref[0] = (
        jnp.concatenate(within, axis=1)
        + carried * spread(jnp.exp(turned[:, 0:8]), lane)
        + spread(skip_ref[...], lane) * wide
    )
    weighted = (wide * spread(turned[:, 8:16], lane)).astype(jnp.bfloat16)
    added = lax.dot_general(
        weighted, b, (((0,), (0,)), ((), ())), preferred_element_type=jnp.float32
    )
    factor = jnp.exp(closing)
    for head in range(8):
        rows = slice(head * HEADDIM, (head + 1) * HEADDIM)
        state[rows, :] = state[rows, :] * factor[head : head + 1, :] + added[rows, :]

    @pl.when(block == pl.num_programs(1) - 1)
    def _():
        state_out[0] = state[...]


def scan(lengths, x_input, bc_input, tails, conv_x, conv_bc, dt_raw, a_log, d_skip):
    requests, length, width = x_input.shape
    heads = dt_raw.shape[1]

    def group():
        return lax.axis_index("head") * heads >> 5

    def grouped(shift):
        return pl.BlockSpec((1, BLOCK, STATE), lambda r, i: (r, i, group() + shift))

    def table(shift):
        return pl.BlockSpec((4, STATE), lambda r, i: (0, group() + shift))

    def tail(columns, at):
        return pl.BlockSpec((1, 8, columns), lambda r, i: (r, 0, at))

    return pl.pallas_call(
        scan_kernel,
        grid=(requests, length // BLOCK),
        in_specs=[
            pl.BlockSpec(memory_space=pltpu.SMEM),
            pl.BlockSpec((1, BLOCK, width), lambda r, i: (r, i, 0)),
            grouped(0),
            grouped(GROUPS),
            tail(width, 0),
            tail(STATE, width // STATE),
            tail(STATE, width // STATE + 1),
            pl.BlockSpec((4, width), lambda r, i: (0, 0)),
            table(0),
            table(GROUPS),
            pl.BlockSpec((1, heads, BLOCK), lambda r, i: (r, 0, i)),
            pl.BlockSpec((heads, 1), lambda r, i: (0, 0)),
            pl.BlockSpec((1, heads), lambda r, i: (0, 0)),
        ],
        out_specs=[
            pl.BlockSpec((1, BLOCK, width), lambda r, i: (r, i, 0)),
            pl.BlockSpec((1, BLOCK, STATE), lambda r, i: (r, i, 0)),
            pl.BlockSpec((1, BLOCK, heads), lambda r, i: (r, i, 0)),
            pl.BlockSpec((1, width, STATE), lambda r, i: (r, 0, 0)),
        ],
        scratch_shapes=[
            pltpu.VMEM((8 + BLOCK, width), jnp.float32),
            pltpu.VMEM((8 + BLOCK, STATE), jnp.float32),
            pltpu.VMEM((8 + BLOCK, STATE), jnp.float32),
            pltpu.VMEM((8, width), jnp.float32),
            pltpu.VMEM((8, STATE), jnp.float32),
            pltpu.VMEM((8, STATE), jnp.float32),
            pltpu.VMEM((width, STATE), jnp.float32),
            pltpu.VMEM((heads, 1), jnp.float32),
        ],
        out_shape=[
            jax.ShapeDtypeStruct((requests, length, width), jnp.float32),
            jax.ShapeDtypeStruct((requests, length, STATE), jnp.bfloat16),
            jax.ShapeDtypeStruct((requests, length, heads), jnp.float32),
            jax.ShapeDtypeStruct((requests, width, STATE), jnp.float32),
        ],
        compiler_params=pltpu.CompilerParams(vmem_limit_bytes=56 * MIB),
        cost_estimate=pl.CostEstimate(
            flops=2 * requests * length * (8 * 128 * 128 + 2 * width * STATE + 128 * STATE),
            bytes_accessed=12 * MIB,
            transcendentals=4 * requests * length * width,
        ),
    )(
        lengths,
        x_input,
        bc_input,
        bc_input,
        tails,
        tails,
        tails,
        conv_x,
        conv_bc,
        conv_bc,
        dt_raw,
        a_log[:, None],
        d_skip[None, :],
    )


def prepare_kernel(
    owner, slot, pool, tails, weight, away_0, away_1, mine, chip, tail_away, tail_mine, tail_chip,
    outgoing, columns, semaphore
):
    _, _, hi, lo, core = place_in_mesh()
    half = columns.shape[1]
    start = ((3 - 2 * hi - lo) * 2 + core) * half
    copy = pltpu.make_async_copy(
        weight.at[:, pl.ds(pl.multiple_of(start, half), half)], columns, semaphore
    )
    copy.start()
    me = 2 * lo + core
    for j in range(2):
        away = (away_0, away_1)[j]
        for device, state, tail in (
            (me ^ 1, away.at[0], tail_away.at[j, 0]),
            (me ^ 3, away.at[1], tail_away.at[j, 1]),
            (me ^ 2, chip.at[j], tail_chip.at[j]),
            (me, mine.at[j], tail_mine.at[j]),
        ):
            request = 2 * device + j
            here = owner[request, 0] == me
            at = slot[request]
            state[...] = jnp.where(here, pool[at], 0.0)
            tail[...] = jnp.where(here, tails[at], 0.0)
    copy.wait()
    outgoing[...] = columns[...].astype(jnp.float32)


def prepare(owner, slot, pool, tails, weight):
    _, width, state = pool.shape
    columns = tails.shape[2]
    half = weight.shape[1] // 8
    vmem = pl.BlockSpec(memory_space=pltpu.VMEM)
    smem = pl.BlockSpec(memory_space=pltpu.SMEM)
    shapes = (
        (2, width, state),
        (2, width, state),
        (2, width, state),
        (2, width, state),
        (2, 2, 8, columns),
        (2, 8, columns),
        (2, 8, columns),
        (weight.shape[0], half),
    )
    return pl.pallas_call(
        prepare_kernel,
        in_specs=[smem, smem, vmem, vmem, pl.BlockSpec(memory_space=pl.ANY)],
        out_specs=[vmem] * len(shapes),
        out_shape=[jax.ShapeDtypeStruct(s, jnp.float32) for s in shapes],
        scratch_shapes=[
            pltpu.VMEM((weight.shape[0], half), weight.dtype),
            pltpu.SemaphoreType.DMA,
        ],
        compiler_params=pltpu.CompilerParams(vmem_limit_bytes=48 * MIB),
        cost_estimate=pl.CostEstimate(flops=0, bytes_accessed=10 * MIB, transcendentals=0),
    )(owner, slot, pool, tails, weight)


def gate_kernel(
    lengths, y_ref, c_ref, decay_ref, part_ref, z_ref, mine, near, far, *outs, request
):
    z_at, y_at, _, _, core = place_in_mesh()
    gated_refs, state_ref = outs[:PARTS], outs[PARTS]
    initial = mine[0] + near[0] + far[...]
    lane = lax.broadcasted_iota(jnp.int32, (BLOCK, BLOCK), 1)
    narrow = initial.astype(jnp.bfloat16)
    for block in range(y_ref.shape[1] // BLOCK):
        rows = slice(block * BLOCK, (block + 1) * BLOCK)
        carried = lax.dot_general(
            c_ref[0, rows], narrow, (((1,), (1,)), ((), ())), preferred_element_type=jnp.float32
        )
        y = y_ref[0, rows] + carried * spread(decay_ref[0, rows], lane)
        z = z_ref[0, rows].astype(jnp.float32)
        position = lax.broadcasted_iota(jnp.int32, y.shape, 0) + block * BLOCK
        gated = y * (z * (1.0 / (1.0 + jnp.exp(-z))))
        gated = jnp.where(position < lengths[request], gated, 0.0)
        gated = gated.astype(jnp.bfloat16).astype(jnp.float32)
        for at in range(4):
            z_far, y_far = block ^ z_at, at ^ y_at
            target = jnp.where(core == 0, y_far * 4 + z_far, z_far * 4 + y_far) * ROWS
            for part in range(PARTS):
                start = at * 32 + part * ROWS
                gated_refs[part][pl.ds(pl.multiple_of(target, ROWS), ROWS), :] = gated[
                    start : start + ROWS
                ]
    last = decay_ref.shape[1] - 8
    final = decay_ref[0, last:, :]
    for head in range(8):
        rows = slice(head * HEADDIM, (head + 1) * HEADDIM)
        state_ref[0, rows] = part_ref[0, rows] + initial[rows] * final[7:8, head : head + 1]


def gate(lengths, request, parts, z_gate, mine, near, far):
    y, c, decay, part = parts
    _, length, width = y.shape

    def whole(shape, at):
        return pl.BlockSpec((1,) + shape, lambda i: (at, 0, 0))

    return pl.pallas_call(
        functools.partial(gate_kernel, request=request),
        grid=(1,),
        in_specs=[
            pl.BlockSpec(memory_space=pltpu.SMEM),
            whole((length, width), request),
            whole((length, STATE), request),
            whole((length, decay.shape[2]), request),
            whole((width, STATE), request),
            whole((length, width), request),
            whole((width, STATE), request),
            whole((width, STATE), 0),
            pl.BlockSpec((width, STATE), lambda i: (0, 0)),
        ],
        out_specs=[pl.BlockSpec((length // PARTS, width), lambda i: (0, 0))] * PARTS
        + [whole((width, STATE), 0)],
        out_shape=[jax.ShapeDtypeStruct((length // PARTS, width), jnp.float32)] * PARTS
        + [jax.ShapeDtypeStruct((1, width, STATE), jnp.float32)],
        compiler_params=pltpu.CompilerParams(vmem_limit_bytes=48 * MIB),
        cost_estimate=pl.CostEstimate(
            flops=2 * length * width * STATE, bytes_accessed=6 * MIB, transcendentals=length * width
        ),
    )(lengths, y, c, decay, part, z_gate, mine, near, far)


ORDER = ((2, 1, 0, 3), (2, 3, 0, 1))
TILE = 512


def product(blocks, weight, w_far):
    depth, half = w_far[0].shape
    lines = 4 * ROWS
    side_rows = 16 * ROWS
    tiles = half // TILE

    def kernel(own, near, cross_near, cross_far, far, w_own_ref, w_near_ref, w_far_ref, *rest):
        outs, own_side, far_side, far_weight = rest[:6], rest[6], rest[7], rest[8]
        step = pl.program_id(0)

        @pl.when(step == 0)
        def _():
            middle = side_rows // 2
            own_side[:side_rows] = own[...].astype(jnp.bfloat16)
            own_side[side_rows:] = near[...].astype(jnp.bfloat16)
            far_side[:middle] = cross_near[...].astype(jnp.bfloat16)
            far_side[middle:side_rows] = cross_far[...].astype(jnp.bfloat16)
            far_side[side_rows:] = far[...].astype(jnp.bfloat16)

        @pl.when(step < tiles)
        def _():
            far_weight[...] = w_near_ref[...].astype(jnp.bfloat16)

        @pl.when(step >= tiles)
        def _():
            far_weight[...] = w_far_ref[...].astype(jnp.bfloat16)

        total = jnp.dot(own_side[...], w_own_ref[...], preferred_element_type=jnp.float32)
        total += jnp.dot(far_side[...], far_weight[...], preferred_element_type=jnp.float32)

        def put(ref, at, major, side):
            for minor in ORDER[side]:
                start = side * side_rows + (major * 4 + minor) * ROWS
                ref[at * ROWS : (at + 1) * ROWS, :] = total[start : start + ROWS]
                at += 1

        put(outs[0], 0, 2, 0)
        put(outs[0], 4, 1, 0)
        put(outs[1], 0, 2, 1)
        put(outs[1], 4, 3, 1)
        put(outs[2], 0, 1, 1)
        put(outs[3], 0, 3, 0)
        put(outs[4], 0, 0, 0)
        put(outs[5], 0, 0, 1)

    def own_columns(i):
        _, _, hi, lo, core = place_in_mesh()
        side = jnp.where(i < tiles, core, 1 - core)
        return (0, ((2 * hi + lo) * 2 + side) * tiles + jnp.where(i < tiles, i, i - tiles))

    heights = (2 * lines, 2 * lines, lines, lines, lines, lines)
    return pl.pallas_call(
        kernel,
        grid=(2 * tiles,),
        in_specs=[pl.BlockSpec(b.shape, lambda i: (0, 0)) for b in blocks]
        + [
            pl.BlockSpec((depth, TILE), own_columns),
            pl.BlockSpec((depth, TILE), lambda i: (0, jnp.minimum(i, tiles - 1))),
            pl.BlockSpec((depth, TILE), lambda i: (0, jnp.maximum(i - tiles, 0))),
        ],
        out_specs=[pl.BlockSpec((h, TILE), lambda i: (0, i)) for h in heights],
        out_shape=[jax.ShapeDtypeStruct((h, 2 * half), jnp.float32) for h in heights],
        scratch_shapes=[pltpu.VMEM((2 * side_rows, depth), jnp.bfloat16)] * 2
        + [pltpu.VMEM((depth, TILE), jnp.bfloat16)],
        compiler_params=pltpu.CompilerParams(vmem_limit_bytes=48 * MIB),
        cost_estimate=pl.CostEstimate(
            flops=8 * side_rows * depth * 2 * half,
            bytes_accessed=16 * side_rows * depth + 12 * depth * half + 16 * side_rows * half,
            transcendentals=0,
        ),
    )(*blocks, weight, *w_far)


def exchange(parts, axis):
    first, third, one_b, three_a, zero_a, zero_b = parts
    lines = one_b.shape[0]
    got1 = swap(first, **{axis: 1})
    got3 = swap(third, **{axis: 3})
    back1 = swap(one_b + got3[:lines], **{axis: 1})
    back3 = swap(three_a + got1[:lines], **{axis: 3})
    return ((zero_a, got1, back3), (zero_b, got3, back1))


def next_parts(chunks):
    def rows(side, start, stop):
        chosen = []
        for chunk in chunks:
            kept, got, back = chunk[side]
            lines = kept.shape[0]
            span = slice(start * ROWS, stop * ROWS)
            after = slice(lines + start * ROWS, lines + stop * ROWS)
            chosen.append(kept[span] + got[after] + back[span])
        if stop - start == 2:
            chosen = [c[:ROWS] for c in chosen] + [c[ROWS:] for c in chosen]
        return jnp.concatenate(chosen, axis=0)

    return (
        rows(0, 0, 2),
        rows(1, 0, 2),
        rows(1, 3, 4),
        rows(0, 3, 4),
        rows(0, 2, 3),
        rows(1, 2, 3),
    )


def finish_kernel(kept_0, got_0, back_0, kept_1, got_1, back_1, *outs):
    hi = lax.axis_index("head") & 1
    for side, (kept, got, back) in enumerate(((kept_0, got_0, back_0), (kept_1, got_1, back_1))):
        lines = kept.shape[0]
        for request in range(2):
            for way in range(2):
                part = hi ^ way
                row = pl.multiple_of(request * 32 + part * 16, 16)
                later = pl.multiple_of(lines + request * 32 + part * 16, 16)
                outs[2 * way + side][request] = (
                    kept[pl.ds(row, 16), :] + got[pl.ds(later, 16), :] + back[pl.ds(row, 16), :]
                )


def finish(sides):
    columns = sides[0][0].shape[1]
    vmem = pl.BlockSpec(memory_space=pltpu.VMEM)
    return pl.pallas_call(
        finish_kernel,
        in_specs=[vmem] * 6,
        out_specs=[vmem] * 4,
        out_shape=[jax.ShapeDtypeStruct((2, 16, columns), jnp.float32)] * 4,
        compiler_params=pltpu.CompilerParams(vmem_limit_bytes=32 * MIB),
        cost_estimate=pl.CostEstimate(flops=0, bytes_accessed=4 * MIB, transcendentals=0),
    )(*sides[0], *sides[1])


def assemble_kernel(own, near, across, far, mixed):
    _, _, hi, lo, core = place_in_mesh()
    half = own.shape[2] // 2
    for flip, source in enumerate((own, near, across, far)):
        place = (2 * hi + lo) ^ flip
        for side in range(2):
            start = pl.multiple_of((place * 2 + (side ^ core)) * half, half)
            mixed[:, :, pl.ds(start, half)] = source[:, :, side * half : (side + 1) * half]


def assemble(pieces):
    requests, rows, columns = pieces[0].shape
    vmem = pl.BlockSpec(memory_space=pltpu.VMEM)
    return pl.pallas_call(
        assemble_kernel,
        in_specs=[vmem] * 4,
        out_specs=vmem,
        out_shape=jax.ShapeDtypeStruct((requests, rows, 4 * columns), jnp.float32),
        compiler_params=pltpu.CompilerParams(vmem_limit_bytes=32 * MIB),
        cost_estimate=pl.CostEstimate(flops=0, bytes_accessed=2 * MIB, transcendentals=0),
    )(*pieces)


def project(gated, out_weight, w_far):
    chunks = []
    for own in gated:
        near = swap(own, lo=1)
        far = swap(own, hi=1, lo=1)
        middle = own.shape[0] // 2
        cross_near = swap(far[:middle], lo=1)
        cross_far = swap(near[middle:], hi=1, lo=1)
        parts = product((own, near, cross_near, cross_far, far), out_weight, w_far)
        chunks.append(exchange(parts, "first"))
    kept_0, kept_1, away_0, away_1 = finish(exchange(next_parts(chunks), "second"))
    return assemble(
        (kept_0, swap(kept_1, lo=1), swap(away_0, hi=1), swap(away_1, hi=1, lo=1))
    )


def on_device(
    x_input,
    z_gate,
    bc_input,
    dt_raw,
    a_log,
    d_skip,
    conv_x,
    conv_bc,
    out_weight,
    pool_state,
    pool_xtail,
    pool_bctail,
    pool_dev,
    pool_slot,
    lengths,
):
    group = lax.axis_index("head").astype(jnp.uint32) * a_log.shape[0] >> 5
    bc_tail = pool_bctail.reshape(pool_bctail.shape[:2] + (2, GROUPS, STATE))
    bc_tail = lax.dynamic_index_in_dim(bc_tail, group, 3, keepdims=False)
    tails = jnp.concatenate([pool_xtail, bc_tail.reshape(bc_tail.shape[:2] + (2 * STATE,))], axis=-1)
    tails = jnp.pad(tails.astype(jnp.float32), ((0, 0), (5, 0), (0, 0)))
    away_0, away_1, mine, chip, tail_away, tail_mine, tail_chip, outgoing = prepare(
        pool_dev, pool_slot, pool_state, tails, out_weight
    )
    tail_near = swap(tail_away, core=1)
    tail_far = swap(tail_chip + tail_near[:, 1], lo=1)
    tail_rows = tail_mine + tail_near[:, 0] + tail_far
    w_near = swap(outgoing, hi=1, lo=1)
    w_far = (w_near, swap(w_near, core=1))
    parts = scan(
        lengths, x_input, bc_input, tail_rows, conv_x, conv_bc, dt_raw, a_log, d_skip
    )
    gated, closing = [], []
    for j, away in enumerate((away_0, away_1)):
        near = swap(away, core=1)
        far = swap(chip[j] + near[1], lo=1)
        *rows, state = gate(lengths, j, parts, z_gate, mine, near, far)
        gated += rows
        closing.append(state)
    mixed_out = project(gated, out_weight, w_far)
    return (mixed_out, jnp.concatenate(closing, axis=0))


def solution(mesh):
    return jax.shard_map(
        on_device,
        mesh=mesh,
        in_specs=(
            P("req", None, "head"),
            P("req", None, "head"),
            P("req", None, None),
            P("req", "head", None),
            P("head"),
            P("head"),
            P(None, "head"),
            P(),
            P("head", None),
            P("req", "head", None),
            P("req", None, "head"),
            P("req", None, None),
            P(),
            P(),
            P("req"),
        ),
        out_specs=(P("req", "head", None), P("req", "head", None)),
        check_vma=False,
    )
```

time: 306 us -> 290 us (0.948)
  waiting for transfers between devices: 129 us -> 183 us
  local copies, waits for them, and re-layouts: 30.6 us -> 8.42 us
  starting transfers between devices: 67.2 us -> 46.1 us
  between operations: 19.9 us -> 0.99 us
  other arithmetic: 20.4 us -> 4.6 us
  Pallas kernels: 37 us -> 46.5 us
    ppermute x45 -> x31, waiting for transfers between devices: 129 us -> 183 us  [swap(): return lax.ppermute(array, AXES, pairs)]
    ppermute x45 -> x31, starting transfers between devices: 67.2 us -> 46.1 us  [swap(): return lax.ppermute(array, AXES, pairs)]
    pallas_call x7 -> x8, Pallas kernels: 37 us -> 46.5 us  [the longest x2 19.6 us: product(): pl.pallas_call(kernel, grid=(2 * tiles,), in_specs=[pl.BlockSpec(b.shape,...]
    unnamed x89 -> x38, local copies, waits for them, and re-layouts: 13.7 us -> 6.41 us
    select_n x6 -> x0, other arithmetic: 5.3 us -> none  [the longest x3 4.36 us: fetch(): far = swap(jnp.where(holder == me, here, got[1]), lo=1)]
    dynamic_slice x5 -> x1, local copies, waits for them, and re-layouts: 4.34 us -> 0.09 us  [on_device(): bc_tail = lax.dynamic_index_in_dim(bc_tail, group, 3, keepdims=False)]
    dynamic_slice x1 -> x0, other arithmetic: 4.14 us -> none  [project(): lax.dynamic_slice_in_dim(out_weight, place * width + c * half, half, 1)]
    slice x12 -> x8, local copies, waits for them, and re-layouts: 3.82 us -> 0.28 us  [the longest x4 0.15 us: rows(): chosen = [c[:ROWS] for c in chosen] + [c[ROWS:] for c in chosen]]
  transfers between devices with their start and end apart: 45 -> 31, of which waited for: 21 -> 21; matrix products, arithmetic and copies ran while one was open for 9% -> 2% of each run, Pallas kernels for 12% -> 14%
where the time goes in v3:
time: 290 us; the launch traced here: 289 us
  waiting for transfers between devices  183 us (63%)
  Pallas kernels  46.5 us (16%)
  starting transfers between devices  46.1 us (16%)
  local copies, waits for them, and re-layouts  8.42 us (3%)
  other arithmetic  4.6 us (2%)
    ppermute x31, waiting for transfers between devices, swap(): return lax.ppermute(array, AXES, pairs)  183 us
    ppermute x31, starting transfers between devices, swap(): return lax.ppermute(array, AXES, pairs)  46.1 us
    pallas_call x2, Pallas kernels, product(): pl.pallas_call(kernel, grid=(2 * tiles,), in_specs=[pl.BlockSpec(b.shape,...  19.6 us
    pallas_call x1, Pallas kernels, scan(): pl.pallas_call(scan_kernel, grid=(requests, length // BLOCK), in_specs=[p...  16.5 us
    unnamed x38, local copies, waits for them, and re-layouts  6.41 us
  transfers between devices with their start and end apart: 31, of which 21 were waited for; matrix products, arithmetic and copies ran while one was open for 2% of the time, Pallas kernels for 14%

profile of v3, /device:TPU:0, one launch (start us, length us, event | category | flops | bytes accessed | tf_op | source)
XLA Modules:
  0.0 289.2 jit_solution(7030834651701703240)
XLA Ops:
  0.6 0.7 copy.25.owner
  1.4 0.7 copy.23
  2.1 0.9 reshape.13
  3.2 0.6 copy-done.8
  3.8 4.3 %shard_map.158 = (f32[2,512,256]{2,1,0:T(8,128)S(1)}, f32[2,512,256]{2,1,0:T(8,128)S(1)}, f32[2,512,256]{2,1,0:T(8,128)S(1)}, f32[2,512,256]{2,1,0:T(8,128)S(1)}...) custom-call(s32[8,1]{1,0:T(8,128)S(1)} %copy.25.owner, ...), custom_call_target="tpu_custom_call" | custom-call | bytes 10485760 | tf_op jit(solution)/shard_map/pallas_call | solution.py:285
  8.2 1.0 copy-done.1
  9.2 2.8 collective-permute-start.8
  12.0 0.5 collective-permute-start.12
  12.6 2.0 collective-permute-done.2.near
  14.7 1.5 collective-permute-done.12.near
  16.2 1.1 fusion.1
  17.2 0.2 collective-permute-start.13
  17.5 40.4 %collective-permute-done.8.w_near_ref = f32[512,1024]{1,0:T(8,128)S(1)} collective-permute-done((f32[512,1024]{1,0:T(8,128)}, f32[512,1024]{1,0:T(8,128)S(1)}, u32[]{:S(2)}, u32[]{:S(2)}) %collective-permute-start.8) | collective-permute-done | bytes 2097184 | tf_op jit(solution)/shard_map/ppermute | solution.py:26
  57.9 0.6 collective-permute-start.1
  58.4 0.7 copy.27.rate_ref
  59.1 3.4 %collective-permute-done.1 = f32[2,8,1024]{2,1,0:T(8,128)S(1)} collective-permute-done((f32[2,8,1024]{2,1,0:T(8,128)S(1)}, f32[2,8,1024]{2,1,0:T(8,128)S(1)}, u32[]{:S(2)}, u32[]{:S(2)}) %collective-permute-start.1) | collective-permute-done | bytes 65568 | tf_op jit(solution)/shard_map/ppermute | solution.py:26
  62.5 0.6 fusion.8.x_tail.b_tail.c_tail
  63.1 16.5 %shard_map.159 = (f32[2,512,512]{2,1,0:T(8,128)}, bf16[2,512,256]{2,1,0:T(8,128)(2,1)}, f32[2,512,8]{2,1,0:T(8,128)}, f32[2,512,256]{2,1,0:T(8,128)}) custom-call(s32[2]{0:T(128)} %lengths.5, bf16[2,512,512]{2,1,0:T(8,128)(2,1)} %x_ref.1, bf16[2,512,4096]{2,1,0:T(8,128)(2,1)} %c_ref.1, bf16[2,512,4096]{2,1,0:T(8,128)(2,1)} %c_ref.1, ...), custom_call_target="tpu_custom_call" | custom-call | flops 872415232 | bytes 12582912 | tf_op jit(solution)/shard_map/pallas_call | solution.py:177
  79.6 0.6 collective-permute-start.3
  80.2 1.2 copy-done.2
  81.4 1.0 copy-done.3
  82.4 1.0 copy-done.4
  83.5 2.4 shard_map.162
  85.9 2.8 collective-permute-start.15
  88.8 1.1 collective-permute-start.14
  89.9 4.6 %collective-permute-done.3.far = f32[512,256]{1,0:T(8,128)S(1)} collective-permute-done((f32[512,256]{1,0:T(8,128)S(1)}, f32[512,256]{1,0:T(8,128)S(1)}, u32[]{:S(2)}, u32[]{:S(2)}) %collective-permute-start.3) | collective-permute-done | bytes 524320 | tf_op jit(solution)/shard_map/ppermute | solution.py:26
  94.5 2.4 shard_map.160
  96.9 3.0 %collective-permute-start.5 = (f32[512,512]{1,0:T(8,128)S(1)}, f32[512,512]{1,0:T(8,128)S(1)}, u32[]{:S(2)}, u32[]{:S(2)}) collective-permute-start(f32[512,512]{1,0:T(8,128)S(1)} %get-tuple-element.44.own), channel_id=1, source_target_pairs={{0,65},{1,64},{2,67},{3,66},{4,69},{5,68},{6,71},{7,70},{8,73},{9,... | collective-permute-start | bytes 3145736 | tf_op jit(solution)/shard_map/ppermute | solution.py:26
  100.0 13.3 %collective-permute-done.15.far = f32[512,512]{1,0:T(8,128)S(1)} collective-permute-done((f32[512,512]{1,0:T(8,128)S(1)}, f32[512,512]{1,0:T(8,128)S(1)}, u32[]{:S(2)}, u32[]{:S(2)}) %collective-permute-start.15) | collective-permute-done | bytes 1048608 | tf_op jit(solution)/shard_map/ppermute | solution.py:26
  113.3 0.7 collective-permute-start.16
  114.1 2.9 %collective-permute-done.14.near = f32[512,512]{1,0:T(8,128)S(1)} collective-permute-done((f32[512,512]{1,0:T(8,128)S(1)}, f32[512,512]{1,0:T(8,128)S(1)}, u32[]{:S(2)}, u32[]{:S(2)}) %collective-permute-start.14) | collective-permute-done | bytes 1048608 | tf_op jit(solution)/shard_map/ppermute | solution.py:26
  117.0 3.0 %collective-permute-start.17 = (f32[256,512]{1,0:T(8,128)S(1)}, f32[256,512]{1,0:T(8,128)S(1)}, u32[]{:S(2)}, u32[]{:S(2)}) collective-permute-start(f32[256,512]{1,0:T(8,128)S(1)} %slice.250), channel_id=1, source_target_pairs={{0,65},{1,64},{2,67},{3,66},{4,69},{5,68},{6,71},{7,70},{8,73},{9,... | collective-permute-start | bytes 1572872 | tf_op jit(solution)/shard_map/ppermute | solution.py:26
  120.0 15.7 %collective-permute-done.5.far = f32[512,512]{1,0:T(8,128)S(1)} collective-permute-done((f32[512,512]{1,0:T(8,128)S(1)}, f32[512,512]{1,0:T(8,128)S(1)}, u32[]{:S(2)}, u32[]{:S(2)}) %collective-permute-start.5) | collective-permute-done | bytes 1048608 | tf_op jit(solution)/shard_map/ppermute | solution.py:26
  135.8 0.7 collective-permute-start.6
  136.5 2.9 %collective-permute-done.4.near = f32[512,512]{1,0:T(8,128)S(1)} collective-permute-done((f32[512,512]{1,0:T(8,128)S(1)}, f32[512,512]{1,0:T(8,128)S(1)}, u32[]{:S(2)}, u32[]{:S(2)}) %collective-permute-start.4) | collective-permute-done | bytes 1048608 | tf_op jit(solution)/shard_map/ppermute | solution.py:26
  139.5 3.0 %collective-permute-start.7 = (f32[256,512]{1,0:T(8,128)S(1)}, f32[256,512]{1,0:T(8,128)S(1)}, u32[]{:S(2)}, u32[]{:S(2)}) collective-permute-start(f32[256,512]{1,0:T(8,128)S(1)} %slice.244), channel_id=1, source_target_pairs={{0,65},{1,64},{2,67},{3,66},{4,69},{5,68},{6,71},{7,70},{8,73},{9,... | collective-permute-start | bytes 1572872 | tf_op jit(solution)/shard_map/ppermute | solution.py:26
  142.5 8.1 %collective-permute-done.16.cross_near = f32[256,512]{1,0:T(8,128)S(1)} collective-permute-done((f32[256,512]{1,0:T(8,128)S(1)}, f32[256,512]{1,0:T(8,128)S(1)}, u32[]{:S(2)}, u32[]{:S(2)}) %collective-permute-start.16) | collective-permute-done | bytes 524320 | tf_op jit(solution)/shard_map/ppermute | solution.py:26
  150.7 9.9 %shard_map.163 = (f32[256,2048]{1,0:T(8,128)}, f32[256,2048]{1,0:T(8,128)}, f32[128,2048]{1,0:T(8,128)S(1)}, f32[128,2048]{1,0:T(8,128)S(1)}, f32[128,2048]{1,0:T(8,128)S(1)}, /*index=5*/f32[128,2048]{1,0:T(8,128)S(1)}) custom-call(f32[512,512]{1,0:T(8,128)} %copy-done.6, f32[512,512]{1,0:T(8,128)} %copy-done.13, ...), custom_call_target="tpu_custom_call" | custom-call | flops 4294967296 | bytes 18874368 | tf_op jit(solution)/shard_map/pallas_call | solution.py:420
  160.6 2.0 collective-permute-start.18
  162.6 9.8 %shard_map.161 = (f32[256,2048]{1,0:T(8,128)}, f32[256,2048]{1,0:T(8,128)}, f32[128,2048]{1,0:T(8,128)S(1)}, f32[128,2048]{1,0:T(8,128)S(1)}, f32[128,2048]{1,0:T(8,128)S(1)}, /*index=5*/f32[128,2048]{1,0:T(8,128)S(1)}) custom-call(f32[512,512]{1,0:T(8,128)} %copy-done.5, f32[512,512]{1,0:T(8,128)} %copy-done.11, ...), custom_call_target="tpu_custom_call" | custom-call | flops 4294967296 | bytes 18874368 | tf_op jit(solution)/shard_map/pallas_call | solution.py:420
  172.4 0.3 collective-permute-start.10
  172.7 3.2 %collective-permute-start.24 = (f32[256,2048]{1,0:T(8,128)S(1)}, f32[256,2048]{1,0:T(8,128)S(1)}, u32[]{:S(2)}, u32[]{:S(2)}) collective-permute-start(f32[256,2048]{1,0:T(8,128)S(1)} %copy-done.17), channel_id=1, source_target_pairs={{0,6},{1,7},{2,4},{3,5},{4,2},{5,3},{6,0},{7,1},{8,14},{9,15},{10,... | collective-permute-start | bytes 6291464 | tf_op jit(solution)/shard_map/ppermute | solution.py:26
  175.9 11.2 %collective-permute-done.18 = f32[256,2048]{1,0:T(8,128)S(1)} collective-permute-done((f32[256,2048]{1,0:T(8,128)}, f32[256,2048]{1,0:T(8,128)S(1)}, u32[]{:S(2)}, u32[]{:S(2)}) %collective-permute-start.18) | collective-permute-done | bytes 2097184 | tf_op jit(solution)/shard_map/ppermute | solution.py:26
  187.2 3.3 %collective-permute-start.19 = (f32[128,2048]{1,0:T(8,128)S(1)}, f32[128,2048]{1,0:T(8,128)S(1)}, u32[]{:S(2)}, u32[]{:S(2)}) collective-permute-start(f32[128,2048]{1,0:T(8,128)S(1)} %slice_add_fusion.2), channel_id=1, source_target_pairs={{0,6},{1,7},{2,4},{3,5},{4,2},{5,3},{6,0},{7,1},{8,14},{9,15},{10,... | collective-permute-start | bytes 3145736 | tf_op jit(solution)/shard_map/ppermute | solution.py:26
  190.5 19.1 %collective-permute-done.10 = f32[256,2048]{1,0:T(8,128)S(1)} collective-permute-done((f32[256,2048]{1,0:T(8,128)}, f32[256,2048]{1,0:T(8,128)S(1)}, u32[]{:S(2)}, u32[]{:S(2)}) %collective-permute-start.10) | collective-permute-done | bytes 2097184 | tf_op jit(solution)/shard_map/ppermute | solution.py:26
  209.7 3.3 %collective-permute-start.11 = (f32[128,2048]{1,0:T(8,128)S(1)}, f32[128,2048]{1,0:T(8,128)S(1)}, u32[]{:S(2)}, u32[]{:S(2)}) collective-permute-start(f32[128,2048]{1,0:T(8,128)S(1)} %slice_add_fusion.3), channel_id=1, source_target_pairs={{0,6},{1,7},{2,4},{3,5},{4,2},{5,3},{6,0},{7,1},{8,14},{9,15},{10,... | collective-permute-start | bytes 3145736 | tf_op jit(solution)/shard_map/ppermute | solution.py:26
  213.4 9.0 %collective-permute-done.22 = f32[256,2048]{1,0:T(8,128)S(1)} collective-permute-done((f32[256,2048]{1,0:T(8,128)}, f32[256,2048]{1,0:T(8,128)S(1)}, u32[]{:S(2)}, u32[]{:S(2)}) %collective-permute-start.22) | collective-permute-done | bytes 2097184 | tf_op jit(solution)/shard_map/ppermute | solution.py:26
  222.6 0.6 collective-permute-start.23
  223.1 10.5 %collective-permute-done.19 = f32[128,2048]{1,0:T(8,128)S(1)} collective-permute-done((f32[128,2048]{1,0:T(8,128)S(1)}, f32[128,2048]{1,0:T(8,128)S(1)}, u32[]{:S(2)}, u32[]{:S(2)}) %collective-permute-start.19) | collective-permute-done | bytes 1048608 | tf_op jit(solution)/shard_map/ppermute | solution.py:26
  233.7 11.1 %collective-permute-done.11 = f32[128,2048]{1,0:T(8,128)S(1)} collective-permute-done((f32[128,2048]{1,0:T(8,128)S(1)}, f32[128,2048]{1,0:T(8,128)S(1)}, u32[]{:S(2)}, u32[]{:S(2)}) %collective-permute-start.11) | collective-permute-done | bytes 1048608 | tf_op jit(solution)/shard_map/ppermute | solution.py:26
  245.2 2.1 collective-permute-start.20
  247.7 2.6 collective-permute-start.26
  250.7 9.3 %collective-permute-done.20.got_0 = f32[128,2048]{1,0:T(8,128)S(1)} collective-permute-done((f32[128,2048]{1,0:T(8,128)S(1)}, f32[128,2048]{1,0:T(8,128)S(1)}, u32[]{:S(2)}, u32[]{:S(2)}) %collective-permute-start.20) | collective-permute-done | bytes 1048608 | tf_op jit(solution)/shard_map/ppermute | solution.py:26
  260.2 4.2 %collective-permute-start.21 = (f32[64,2048]{1,0:T(8,128)S(1)}, f32[64,2048]{1,0:T(8,128)S(1)}, u32[]{:S(2)}, u32[]{:S(2)}) collective-permute-start(f32[64,2048]{1,0:T(8,128)S(1)} %slice_add_fusion.9), channel_id=1, source_target_pairs={{0,24},{1,25},{2,26},{3,27},{4,28},{5,29},{6,30},{7,31},{8,16},{9,... | collective-permute-start | bytes 1572872 | tf_op jit(solution)/shard_map/ppermute | solution.py:26
  264.7 6.9 %collective-permute-done.21.back_0 = f32[64,2048]{1,0:T(8,128)S(1)} collective-permute-done((f32[64,2048]{1,0:T(8,128)S(1)}, f32[64,2048]{1,0:T(8,128)S(1)}, u32[]{:S(2)}, u32[]{:S(2)}) %collective-permute-start.21) | collective-permute-done | bytes 524320 | tf_op jit(solution)/shard_map/ppermute | solution.py:26
  271.5 2.2 collective-permute-done.27.back_1
  273.9 0.4 collective-permute-start.28
  274.2 3.9 %collective-permute-start.29 = (f32[2,16,2048]{2,1,0:T(8,128)S(1)}, f32[2,16,2048]{2,1,0:T(8,128)S(1)}, u32[]{:S(2)}, u32[]{:S(2)}) collective-permute-start(f32[2,16,2048]{2,1,0:T(8,128)S(1)} %get-tuple-element.62), channel_id=1, source_target_pairs={{0,1},{1,0},{2,3},{3,2},{4,5},{5,4},{6,7},{7,6},{8,9},{9,8},{10,11... | collective-permute-start | bytes 786440 | tf_op jit(solution)/shard_map/ppermute | solution.py:26
  278.2 0.5 collective-permute-start.30
  278.7 1.0 pad_maximum_fusion.2
  279.7 0.6 collective-permute-done.28.near
  280.3 5.1 %collective-permute-done.29.across = f32[2,16,2048]{2,1,0:T(8,128)S(1)} collective-permute-done((f32[2,16,2048]{2,1,0:T(8,128)S(1)}, f32[2,16,2048]{2,1,0:T(8,128)S(1)}, u32[]{:S(2)}, u32[]{:S(2)}) %collective-permute-start.29) | collective-permute-done | bytes 262176 | tf_op jit(solution)/shard_map/ppermute | solution.py:26
  285.4 2.7 collective-permute-done.30.far
  288.1 1.0 shard_map.165
  (80 shorter events, 3.0 us)
Async XLA Ops:
  3.2 0.7 copy-start.8
  8.2 1.0 copy-start.1
  9.2 49.3 %copy-start.16 = (f32[8]{0:T(128)S(1)}, f32[8]{0:T(128)}, u32[]{:S(2)}) copy-start(f32[8]{0:T(128)} %param.19) | copy-start | bytes 100
  9.2 48.7 %collective-permute-start.8 = (f32[512,1024]{1,0:T(8,128)}, f32[512,1024]{1,0:T(8,128)S(1)}, u32[]{:S(2)}, u32[]{:S(2)}) collective-permute-start(f32[512,1024]{1,0:T(8,128)} %get-tuple-element.45), channel_id=1, source_target_pairs={{0,65},{1,64},{2,67},{3,66},{4,69},{5,68},{6,71},{7,70},{8,73},{9,... | collective-permute-start | bytes 6291464 | tf_op jit(solution)/shard_map/ppermute | solution.py:26
  12.0 2.7 collective-permute-start.2
  12.0 4.2 %collective-permute-start.12 = (f32[2,512,256]{2,1,0:T(8,128)S(1)}, f32[2,512,256]{2,1,0:T(8,128)S(1)}, u32[]{:S(2)}, u32[]{:S(2)}) collective-permute-start(f32[2,512,256]{2,1,0:T(8,128)S(1)} %get-tuple-element.49), channel_id=1, source_target_pairs={{0,32},{1,33},{2,34},{3,35},{4,36},{5,37},{6,38},{7,39},{8,40},{9,... | collective-permute-start | bytes 3145736 | tf_op jit(solution)/shard_map/ppermute | solution.py:26
  12.5 45.3 %collective-permute-start = (f32[2,2,8,1024]{3,2,0,1:T(8,128)S(1)}, f32[2,2,8,1024]{3,2,0,1:T(8,128)S(1)}, u32[]{:S(2)}, u32[]{:S(2)}) collective-permute-start(f32[2,2,8,1024]{3,2,0,1:T(8,128)S(1)} %copy.26), channel_id=1, source_target_pairs={{0,32},{1,33},{2,34},{3,35},{4,36},{5,37},{6,38},{7,39},{8,40},{9,... | collective-permute-start | bytes 393224 | tf_op jit(solution)/shard_map/ppermute | solution.py:26
  14.7 43.2 %copy-start.14 = (f32[2,512,256]{2,1,0:T(8,128)}, f32[2,512,256]{2,1,0:T(8,128)S(1)}, u32[]{:S(2)}) copy-start(f32[2,512,256]{2,1,0:T(8,128)S(1)} %collective-permute-done.2.near) | copy-start | bytes 3145732
  16.2 42.3 %copy-start.15 = (f32[2,512,256]{2,1,0:T(8,128)}, f32[2,512,256]{2,1,0:T(8,128)S(1)}, u32[]{:S(2)}) copy-start(f32[2,512,256]{2,1,0:T(8,128)S(1)} %collective-permute-done.12.near) | copy-start | bytes 3145732
  17.2 62.9 %collective-permute-start.13 = (f32[512,256]{1,0:T(8,128)}, f32[512,256]{1,0:T(8,128)S(1)}, u32[]{:S(2)}, u32[]{:S(2)}) collective-permute-start(f32[512,256]{1,0:T(8,128)} %get-tuple-element.75), channel_id=1, source_target_pairs={{0,64},{1,65},{2,66},{3,67},{4,68},{5,69},{6,70},{7,71},{8,72},{9,... | collective-permute-start | bytes 1572872 | tf_op jit(solution)/shard_map/ppermute | solution.py:26
  57.8 21.7 %copy-start.9 = (f32[512,1024]{1,0:T(8,128)}, f32[512,1024]{1,0:T(8,128)S(1)}, u32[]{:S(2)}) copy-start(f32[512,1024]{1,0:T(8,128)S(1)} %collective-permute-done.8.w_near_ref) | copy-start | bytes 6291460
  57.8 92.8 %collective-permute-start.9 = (f32[512,1024]{1,0:T(8,128)S(1)}, f32[512,1024]{1,0:T(8,128)}, u32[]{:S(2)}, u32[]{:S(2)}) collective-permute-start(f32[512,1024]{1,0:T(8,128)S(1)} %collective-permute-done.8.w_near_ref), channel_id=1, source_target_pairs={{0,32},{1,33},{2,34},{3,35},{4,36},{5,37},{6,38},{7,39},{8,40},{9,... | collective-permute-start | bytes 6291464 | tf_op jit(solution)/shard_map/ppermute | solution.py:26
  57.9 4.6 %collective-permute-start.1 = (f32[2,8,1024]{2,1,0:T(8,128)S(1)}, f32[2,8,1024]{2,1,0:T(8,128)S(1)}, u32[]{:S(2)}, u32[]{:S(2)}) collective-permute-start(f32[2,8,1024]{2,1,0:T(8,128)S(1)} %fusion.6), channel_id=1, source_target_pairs={{0,64},{1,65},{2,66},{3,67},{4,68},{5,69},{6,70},{7,71},{8,72},{9,... | collective-permute-start | bytes 196616 | tf_op jit(solution)/shard_map/ppermute | solution.py:26
  63.1 17.0 %copy-start = (bf16[2,512,512]{2,1,0:T(8,128)(2,1)S(1)}, bf16[2,512,512]{2,1,0:T(8,128)(2,1)}, u32[]{:S(2)}) copy-start(bf16[2,512,512]{2,1,0:T(8,128)(2,1)} %z_ref.3) | copy-start | bytes 3145732
  63.1 17.0 %copy-start.7 = (s32[2]{0:T(128)S(1)}, s32[2]{0:T(128)}, u32[]{:S(2)}) copy-start(s32[2]{0:T(128)} %lengths.5) | copy-start | bytes 28
  79.6 14.9 %collective-permute-start.3 = (f32[512,256]{1,0:T(8,128)S(1)}, f32[512,256]{1,0:T(8,128)S(1)}, u32[]{:S(2)}, u32[]{:S(2)}) collective-permute-start(f32[512,256]{1,0:T(8,128)S(1)} %get-tuple-element.74), channel_id=1, source_target_pairs={{0,64},{1,65},{2,66},{3,67},{4,68},{5,69},{6,70},{7,71},{8,72},{9,... | collective-permute-start | bytes 1572872 | tf_op jit(solution)/shard_map/ppermute | solution.py:26
  80.1 1.2 copy-start.2
  81.4 1.0 copy-start.3
  82.4 1.0 copy-start.4
  85.9 11.0 %copy-start.6 = (f32[512,512]{1,0:T(8,128)}, f32[512,512]{1,0:T(8,128)S(1)}, u32[]{:S(2)}) copy-start(f32[512,512]{1,0:T(8,128)S(1)} %get-tuple-element.50.own) | copy-start | bytes 3145732
  85.9 27.4 %collective-permute-start.15 = (f32[512,512]{1,0:T(8,128)S(1)}, f32[512,512]{1,0:T(8,128)S(1)}, u32[]{:S(2)}, u32[]{:S(2)}) collective-permute-start(f32[512,512]{1,0:T(8,128)S(1)} %get-tuple-element.50.own), channel_id=1, source_target_pairs={{0,65},{1,64},{2,67},{3,66},{4,69},{5,68},{6,71},{7,70},{8,73},{9,... | collective-permute-start | bytes 3145736 | tf_op jit(solution)/shard_map/ppermute | solution.py:26
  88.8 28.2 %collective-permute-start.14 = (f32[512,512]{1,0:T(8,128)S(1)}, f32[512,512]{1,0:T(8,128)S(1)}, u32[]{:S(2)}, u32[]{:S(2)}) collective-permute-start(f32[512,512]{1,0:T(8,128)S(1)} %get-tuple-element.50.own), channel_id=1, source_target_pairs={{0,64},{1,65},{2,66},{3,67},{4,68},{5,69},{6,70},{7,71},{8,72},{9,... | collective-permute-start | bytes 3145736 | tf_op jit(solution)/shard_map/ppermute | solution.py:26
  96.9 42.5 %copy-start.5 = (f32[512,512]{1,0:T(8,128)}, f32[512,512]{1,0:T(8,128)S(1)}, u32[]{:S(2)}) copy-start(f32[512,512]{1,0:T(8,128)S(1)} %get-tuple-element.44.own) | copy-start | bytes 3145732
  96.9 38.8 %collective-permute-start.5 = (f32[512,512]{1,0:T(8,128)S(1)}, f32[512,512]{1,0:T(8,128)S(1)}, u32[]{:S(2)}, u32[]{:S(2)}) collective-permute-start(f32[512,512]{1,0:T(8,128)S(1)} %get-tuple-element.44.own), channel_id=1, source_target_pairs={{0,65},{1,64},{2,67},{3,66},{4,69},{5,68},{6,71},{7,70},{8,73},{9,... | collective-permute-start | bytes 3145736 | tf_op jit(solution)/shard_map/ppermute | solution.py:26
  100.0 39.4 %collective-permute-start.4 = (f32[512,512]{1,0:T(8,128)S(1)}, f32[512,512]{1,0:T(8,128)S(1)}, u32[]{:S(2)}, u32[]{:S(2)}) collective-permute-start(f32[512,512]{1,0:T(8,128)S(1)} %get-tuple-element.44.own), channel_id=1, source_target_pairs={{0,64},{1,65},{2,66},{3,67},{4,68},{5,69},{6,70},{7,71},{8,72},{9,... | collective-permute-start | bytes 3145736 | tf_op jit(solution)/shard_map/ppermute | solution.py:26
  113.3 26.2 %copy-start.12 = (f32[512,512]{1,0:T(8,128)}, f32[512,512]{1,0:T(8,128)S(1)}, u32[]{:S(2)}) copy-start(f32[512,512]{1,0:T(8,128)S(1)} %collective-permute-done.15.far) | copy-start | bytes 3145732
  113.3 37.3 %collective-permute-start.16 = (f32[256,512]{1,0:T(8,128)S(1)}, f32[256,512]{1,0:T(8,128)S(1)}, u32[]{:S(2)}, u32[]{:S(2)}) collective-permute-start(f32[256,512]{1,0:T(8,128)S(1)} %slice.249), channel_id=1, source_target_pairs={{0,64},{1,65},{2,66},{3,67},{4,68},{5,69},{6,70},{7,71},{8,72},{9,... | collective-permute-start | bytes 1572872 | tf_op jit(solution)/shard_map/ppermute | solution.py:26
  117.0 33.7 %copy-start.13 = (f32[512,512]{1,0:T(8,128)}, f32[512,512]{1,0:T(8,128)S(1)}, u32[]{:S(2)}) copy-start(f32[512,512]{1,0:T(8,128)S(1)} %collective-permute-done.14.near) | copy-start | bytes 3145732
  117.0 33.7 %collective-permute-start.17 = (f32[256,512]{1,0:T(8,128)S(1)}, f32[256,512]{1,0:T(8,128)S(1)}, u32[]{:S(2)}, u32[]{:S(2)}) collective-permute-start(f32[256,512]{1,0:T(8,128)S(1)} %slice.250), channel_id=1, source_target_pairs={{0,65},{1,64},{2,67},{3,66},{4,69},{5,68},{6,71},{7,70},{8,73},{9,... | collective-permute-start | bytes 1572872 | tf_op jit(solution)/shard_map/ppermute | solution.py:26
  135.8 24.8 %copy-start.10 = (f32[512,512]{1,0:T(8,128)}, f32[512,512]{1,0:T(8,128)S(1)}, u32[]{:S(2)}) copy-start(f32[512,512]{1,0:T(8,128)S(1)} %collective-permute-done.5.far) | copy-start | bytes 3145732
  135.8 26.8 %collective-permute-start.6 = (f32[256,512]{1,0:T(8,128)S(1)}, f32[256,512]{1,0:T(8,128)S(1)}, u32[]{:S(2)}, u32[]{:S(2)}) collective-permute-start(f32[256,512]{1,0:T(8,128)S(1)} %slice.243), channel_id=1, source_target_pairs={{0,64},{1,65},{2,66},{3,67},{4,68},{5,69},{6,70},{7,71},{8,72},{9,... | collective-permute-start | bytes 1572872 | tf_op jit(solution)/shard_map/ppermute | solution.py:26
  139.4 21.1 %copy-start.11 = (f32[512,512]{1,0:T(8,128)}, f32[512,512]{1,0:T(8,128)S(1)}, u32[]{:S(2)}) copy-start(f32[512,512]{1,0:T(8,128)S(1)} %collective-permute-done.4.near) | copy-start | bytes 3145732
  139.5 23.1 %collective-permute-start.7 = (f32[256,512]{1,0:T(8,128)S(1)}, f32[256,512]{1,0:T(8,128)S(1)}, u32[]{:S(2)}, u32[]{:S(2)}) collective-permute-start(f32[256,512]{1,0:T(8,128)S(1)} %slice.244), channel_id=1, source_target_pairs={{0,65},{1,64},{2,67},{3,66},{4,69},{5,68},{6,71},{7,70},{8,73},{9,... | collective-permute-start | bytes 1572872 | tf_op jit(solution)/shard_map/ppermute | solution.py:26
  160.6 12.1 %copy-start.17 = (f32[256,2048]{1,0:T(8,128)S(1)}, f32[256,2048]{1,0:T(8,128)}, u32[]{:S(2)}) copy-start(f32[256,2048]{1,0:T(8,128)} %get-tuple-element.58) | copy-start | bytes 6291460
  160.6 26.5 %collective-permute-start.18 = (f32[256,2048]{1,0:T(8,128)}, f32[256,2048]{1,0:T(8,128)S(1)}, u32[]{:S(2)}, u32[]{:S(2)}) collective-permute-start(f32[256,2048]{1,0:T(8,128)} %get-tuple-element.52), channel_id=1, source_target_pairs={{0,2},{1,3},{2,0},{3,1},{4,6},{5,7},{6,4},{7,5},{8,10},{9,11},{10,... | collective-permute-start | bytes 6291464 | tf_op jit(solution)/shard_map/ppermute | solution.py:26
  172.4 37.2 %collective-permute-start.10 = (f32[256,2048]{1,0:T(8,128)}, f32[256,2048]{1,0:T(8,128)S(1)}, u32[]{:S(2)}, u32[]{:S(2)}) collective-permute-start(f32[256,2048]{1,0:T(8,128)} %get-tuple-element.47), channel_id=1, source_target_pairs={{0,2},{1,3},{2,0},{3,1},{4,6},{5,7},{6,4},{7,5},{8,10},{9,11},{10,... | collective-permute-start | bytes 6291464 | tf_op jit(solution)/shard_map/ppermute | solution.py:26
  172.7 40.3 %collective-permute-start.24 = (f32[256,2048]{1,0:T(8,128)S(1)}, f32[256,2048]{1,0:T(8,128)S(1)}, u32[]{:S(2)}, u32[]{:S(2)}) collective-permute-start(f32[256,2048]{1,0:T(8,128)S(1)} %copy-done.17), channel_id=1, source_target_pairs={{0,6},{1,7},{2,4},{3,5},{4,2},{5,3},{6,0},{7,1},{8,14},{9,15},{10,... | collective-permute-start | bytes 6291464 | tf_op jit(solution)/shard_map/ppermute | solution.py:26
  175.8 46.6 %collective-permute-start.22 = (f32[256,2048]{1,0:T(8,128)}, f32[256,2048]{1,0:T(8,128)S(1)}, u32[]{:S(2)}, u32[]{:S(2)}) collective-permute-start(f32[256,2048]{1,0:T(8,128)} %get-tuple-element.55), channel_id=1, source_target_pairs={{0,6},{1,7},{2,4},{3,5},{4,2},{5,3},{6,0},{7,1},{8,14},{9,15},{10,... | collective-permute-start | bytes 6291464 | tf_op jit(solution)/shard_map/ppermute | solution.py:26
  187.2 46.4 %collective-permute-start.19 = (f32[128,2048]{1,0:T(8,128)S(1)}, f32[128,2048]{1,0:T(8,128)S(1)}, u32[]{:S(2)}, u32[]{:S(2)}) collective-permute-start(f32[128,2048]{1,0:T(8,128)S(1)} %slice_add_fusion.2), channel_id=1, source_target_pairs={{0,6},{1,7},{2,4},{3,5},{4,2},{5,3},{6,0},{7,1},{8,14},{9,15},{10,... | collective-permute-start | bytes 3145736 | tf_op jit(solution)/shard_map/ppermute | solution.py:26
  209.7 35.2 %collective-permute-start.11 = (f32[128,2048]{1,0:T(8,128)S(1)}, f32[128,2048]{1,0:T(8,128)S(1)}, u32[]{:S(2)}, u32[]{:S(2)}) collective-permute-start(f32[128,2048]{1,0:T(8,128)S(1)} %slice_add_fusion.3), channel_id=1, source_target_pairs={{0,6},{1,7},{2,4},{3,5},{4,2},{5,3},{6,0},{7,1},{8,14},{9,15},{10,... | collective-permute-start | bytes 3145736 | tf_op jit(solution)/shard_map/ppermute | solution.py:26
  213.1 34.1 %collective-permute-start.25 = (f32[128,2048]{1,0:T(8,128)S(1)}, f32[128,2048]{1,0:T(8,128)S(1)}, u32[]{:S(2)}, u32[]{:S(2)}) collective-permute-start(f32[128,2048]{1,0:T(8,128)S(1)} %slice_add_fusion), channel_id=1, source_target_pairs={{0,2},{1,3},{2,0},{3,1},{4,6},{5,7},{6,4},{7,5},{8,10},{9,11},{10,... | collective-permute-start | bytes 3145736 | tf_op jit(solution)/shard_map/ppermute | solution.py:26
  222.6 24.9 %collective-permute-start.23 = (f32[128,2048]{1,0:T(8,128)S(1)}, f32[128,2048]{1,0:T(8,128)S(1)}, u32[]{:S(2)}, u32[]{:S(2)}) collective-permute-start(f32[128,2048]{1,0:T(8,128)S(1)} %slice_add_fusion.1), channel_id=1, source_target_pairs={{0,2},{1,3},{2,0},{3,1},{4,6},{5,7},{6,4},{7,5},{8,10},{9,11},{10,... | collective-permute-start | bytes 3145736 | tf_op jit(solution)/shard_map/ppermute | solution.py:26
  245.2 14.9 %collective-permute-start.20 = (f32[128,2048]{1,0:T(8,128)S(1)}, f32[128,2048]{1,0:T(8,128)S(1)}, u32[]{:S(2)}, u32[]{:S(2)}) collective-permute-start(f32[128,2048]{1,0:T(8,128)S(1)} %pad_maximum_fusion), channel_id=1, source_target_pairs={{0,8},{1,9},{2,10},{3,11},{4,12},{5,13},{6,14},{7,15},{8,0},{9,1},... | collective-permute-start | bytes 3145736 | tf_op jit(solution)/shard_map/ppermute | solution.py:26
  247.7 16.7 %collective-permute-start.26 = (f32[128,2048]{1,0:T(8,128)S(1)}, f32[128,2048]{1,0:T(8,128)S(1)}, u32[]{:S(2)}, u32[]{:S(2)}) collective-permute-start(f32[128,2048]{1,0:T(8,128)S(1)} %pad_maximum_fusion.1), channel_id=1, source_target_pairs={{0,24},{1,25},{2,26},{3,27},{4,28},{5,29},{6,30},{7,31},{8,16},{9,... | collective-permute-start | bytes 3145736 | tf_op jit(solution)/shard_map/ppermute | solution.py:26
  260.2 11.4 %collective-permute-start.21 = (f32[64,2048]{1,0:T(8,128)S(1)}, f32[64,2048]{1,0:T(8,128)S(1)}, u32[]{:S(2)}, u32[]{:S(2)}) collective-permute-start(f32[64,2048]{1,0:T(8,128)S(1)} %slice_add_fusion.9), channel_id=1, source_target_pairs={{0,24},{1,25},{2,26},{3,27},{4,28},{5,29},{6,30},{7,31},{8,16},{9,... | collective-permute-start | bytes 1572872 | tf_op jit(solution)/shard_map/ppermute | solution.py:26
  264.5 9.3 %collective-permute-start.27 = (f32[64,2048]{1,0:T(8,128)S(1)}, f32[64,2048]{1,0:T(8,128)S(1)}, u32[]{:S(2)}, u32[]{:S(2)}) collective-permute-start(f32[64,2048]{1,0:T(8,128)S(1)} %slice_add_fusion.4), channel_id=1, source_target_pairs={{0,8},{1,9},{2,10},{3,11},{4,12},{5,13},{6,14},{7,15},{8,0},{9,1},... | collective-permute-start | bytes 1572872 | tf_op jit(solution)/shard_map/ppermute | solution.py:26
  273.9 6.5 %collective-permute-start.28 = (f32[2,16,2048]{2,1,0:T(8,128)S(1)}, f32[2,16,2048]{2,1,0:T(8,128)S(1)}, u32[]{:S(2)}, u32[]{:S(2)}) collective-permute-start(f32[2,16,2048]{2,1,0:T(8,128)S(1)} %get-tuple-element.61), channel_id=1, source_target_pairs={{0,64},{1,65},{2,66},{3,67},{4,68},{5,69},{6,70},{7,71},{8,72},{9,... | collective-permute-start | bytes 786440 | tf_op jit(solution)/shard_map/ppermute | solution.py:26
  274.2 11.2 %collective-permute-start.29 = (f32[2,16,2048]{2,1,0:T(8,128)S(1)}, f32[2,16,2048]{2,1,0:T(8,128)S(1)}, u32[]{:S(2)}, u32[]{:S(2)}) collective-permute-start(f32[2,16,2048]{2,1,0:T(8,128)S(1)} %get-tuple-element.62), channel_id=1, source_target_pairs={{0,1},{1,0},{2,3},{3,2},{4,5},{5,4},{6,7},{7,6},{8,9},{9,8},{10,11... | collective-permute-start | bytes 786440 | tf_op jit(solution)/shard_map/ppermute | solution.py:26
  278.2 10.0 %collective-permute-start.30 = (f32[2,16,2048]{2,1,0:T(8,128)S(1)}, f32[2,16,2048]{2,1,0:T(8,128)S(1)}, u32[]{:S(2)}, u32[]{:S(2)}) collective-permute-start(f32[2,16,2048]{2,1,0:T(8,128)S(1)} %get-tuple-element.63), channel_id=1, source_target_pairs={{0,65},{1,64},{2,67},{3,66},{4,69},{5,68},{6,71},{7,70},{8,73},{9,... | collective-permute-start | bytes 786440 | tf_op jit(solution)/shard_map/ppermute | solution.py:26

commit v4 on v3

--- a/solution.py
+++ b/solution.py
@@ -12,7 +12,7 @@
 STATE = 256
 GROUPS = 8
 BLOCK = 128
-PARTS = 1
+PARTS = 2
 ROWS = 32 // PARTS
 AXES = ("req", "head")
 MIB = 1 << 20
@@ -24,6 +24,18 @@
         y, z = (second, first) if source >> 5 & 1 else (first, second)
         pairs.append((source, source ^ (lo << 6 | core << 5 | z << 3 | y << 1 | hi)))
     return lax.ppermute(array, AXES, pairs)
+
+
+def after(array, *others):
+    return lax.optimization_barrier((array,) + others)[0]
+
+
+def cross(near, far):
+    pairs = []
+    for source in range(128):
+        pairs.append((source, source ^ (64 | (source >> 5 & 1))))
+    core = lax.axis_index("req") & 1
+    return lax.ppermute(jnp.where(core == 0, far, near), AXES, pairs)
 
 
 def place_in_mesh():
@@ -237,17 +249,36 @@
     )
 
 
-def prepare_kernel(
-    owner, slot, pool, tails, weight, away_0, away_1, mine, chip, tail_away, tail_mine, tail_chip,
-    outgoing, columns, semaphore
-):
+def outgoing_kernel(weight, outgoing, columns, semaphore):
     _, _, hi, lo, core = place_in_mesh()
     half = columns.shape[1]
-    start = ((3 - 2 * hi - lo) * 2 + core) * half
-    copy = pltpu.make_async_copy(
-        weight.at[:, pl.ds(pl.multiple_of(start, half), half)], columns, semaphore
-    )
+    start = pl.multiple_of(((3 - 2 * hi - lo) * 2 + core) * half, half)
+    copy = pltpu.make_async_copy(weight.at[:, pl.ds(start, half)], columns, semaphore)
     copy.start()
+    copy.wait()
+    outgoing[...] = columns[...].astype(jnp.float32)
+
+
+def outgoing_weights(weight):
+    half = weight.shape[1] // 8
+    return pl.pallas_call(
+        outgoing_kernel,
+        in_specs=[pl.BlockSpec(memory_space=pl.ANY)],
+        out_specs=pl.BlockSpec(memory_space=pltpu.VMEM),
+        out_shape=jax.ShapeDtypeStruct((weight.shape[0], half), jnp.float32),
+        scratch_shapes=[
+            pltpu.VMEM((weight.shape[0], half), weight.dtype),
+            pltpu.SemaphoreType.DMA,
+        ],
+        compiler_params=pltpu.CompilerParams(vmem_limit_bytes=48 * MIB),
+        cost_estimate=pl.CostEstimate(flops=0, bytes_accessed=3 * MIB, transcendentals=0),
+    )(weight)
+
+
+def prepare_kernel(
+    owner, slot, pool, tails, away_0, away_1, mine, chip, tail_away, tail_mine, tail_chip
+):
+    _, _, _, lo, core = place_in_mesh()
     me = 2 * lo + core
     for j in range(2):
         away = (away_0, away_1)[j]
@@ -258,18 +289,15 @@
             (me, mine.at[j], tail_mine.at[j]),
         ):
             request = 2 * device + j
-            here = owner[request, 0] == me
+            here = owner[request] == me
             at = slot[request]
             state[...] = jnp.where(here, pool[at], 0.0)
             tail[...] = jnp.where(here, tails[at], 0.0)
-    copy.wait()
-    outgoing[...] = columns[...].astype(jnp.float32)
-
-
-def prepare(owner, slot, pool, tails, weight):
+
+
+def prepare(owner, slot, pool, tails):
     _, width, state = pool.shape
     columns = tails.shape[2]
-    half = weight.shape[1] // 8
     vmem = pl.BlockSpec(memory_space=pltpu.VMEM)
     smem = pl.BlockSpec(memory_space=pltpu.SMEM)
     shapes = (
@@ -280,20 +308,15 @@
         (2, 2, 8, columns),
         (2, 8, columns),
         (2, 8, columns),
-        (weight.shape[0], half),
     )
     return pl.pallas_call(
         prepare_kernel,
-        in_specs=[smem, smem, vmem, vmem, pl.BlockSpec(memory_space=pl.ANY)],
+        in_specs=[smem, smem, vmem, vmem],
         out_specs=[vmem] * len(shapes),
         out_shape=[jax.ShapeDtypeStruct(s, jnp.float32) for s in shapes],
-        scratch_shapes=[
-            pltpu.VMEM((weight.shape[0], half), weight.dtype),
-            pltpu.SemaphoreType.DMA,
-        ],
         compiler_params=pltpu.CompilerParams(vmem_limit_bytes=48 * MIB),
-        cost_estimate=pl.CostEstimate(flops=0, bytes_accessed=10 * MIB, transcendentals=0),
-    )(owner, slot, pool, tails, weight)
+        cost_estimate=pl.CostEstimate(flops=0, bytes_accessed=7 * MIB, transcendentals=0),
+    )(owner, slot, pool, tails)
 
 
 def gate_kernel(
@@ -366,32 +389,41 @@
 TILE = 512
 
 
-def product(blocks, weight, w_far):
-    depth, half = w_far[0].shape
+def product(blocks, weight, w_far, before):
+    depth = weight.shape[0]
+    width = weight.shape[1] // 4
     lines = 4 * ROWS
     side_rows = 16 * ROWS
-    tiles = half // TILE
-
-    def kernel(own, near, cross_near, cross_far, far, w_own_ref, w_near_ref, w_far_ref, *rest):
-        outs, own_side, far_side, far_weight = rest[:6], rest[6], rest[7], rest[8]
+    tiles = width // (2 * TILE)
+    opening = not before
+
+    def kernel(*refs):
+        own, near, opposite, far, w_own_ref = refs[:5]
+        inputs, outs = refs[5 : -2 - 6 - opening], refs[-2 - 6 - opening : -2]
+        own_side, far_side = refs[-2:]
         step = pl.program_id(0)
 
         @pl.when(step == 0)
         def _():
-            middle = side_rows // 2
             own_side[:side_rows] = own[...].astype(jnp.bfloat16)
             own_side[side_rows:] = near[...].astype(jnp.bfloat16)
-            far_side[:middle] = cross_near[...].astype(jnp.bfloat16)
-            far_side[middle:side_rows] = cross_far[...].astype(jnp.bfloat16)
+            far_side[:side_rows] = opposite[...].astype(jnp.bfloat16)
             far_side[side_rows:] = far[...].astype(jnp.bfloat16)
 
-        @pl.when(step < tiles)
-        def _():
-            far_weight[...] = w_near_ref[...].astype(jnp.bfloat16)
-
-        @pl.when(step >= tiles)
-        def _():
-            far_weight[...] = w_far_ref[...].astype(jnp.bfloat16)
+        if opening:
+            far_weight = outs[6]
+
+            @pl.when(step < tiles)
+            def _():
+                far_weight[...] = inputs[0][...].astype(jnp.bfloat16)
+
+            @pl.when(step >= tiles)
+            def _():
+                far_weight[...] = inputs[1][...].astype(jnp.bfloat16)
+        else:
+            far_weight, got1, got3, one_b, three_a = inputs
+            outs[0][2 * lines :, :] = one_b[...] + got3[...]
+            outs[1][2 * lines :, :] = three_a[...] + got1[...]
 
         total = jnp.dot(own_side[...], w_own_ref[...], preferred_element_type=jnp.float32)
         total += jnp.dot(far_side[...], far_weight[...], preferred_element_type=jnp.float32)
@@ -416,27 +448,41 @@
         side = jnp.where(i < tiles, core, 1 - core)
         return (0, ((2 * hi + lo) * 2 + side) * tiles + jnp.where(i < tiles, i, i - tiles))
 
-    heights = (2 * lines, 2 * lines, lines, lines, lines, lines)
+    def tile(rows):
+        return pl.BlockSpec((rows, TILE), lambda i: (0, i))
+
+    if opening:
+        extra_specs = [
+            pl.BlockSpec((depth, TILE), lambda i: (0, jnp.minimum(i, tiles - 1))),
+            pl.BlockSpec((depth, TILE), lambda i: (0, jnp.maximum(i - tiles, 0))),
+        ]
+        extra = w_far
+    else:
+        extra_specs = [tile(depth)] + [tile(lines)] * 4
+        extra = (w_far,) + before
+    sent = 2 * lines if opening else 3 * lines
+    heights = (sent, sent, lines, lines, lines, lines)
+    out_specs = [tile(h) for h in heights]
+    out_shape = [jax.ShapeDtypeStruct((h, width), jnp.float32) for h in heights]
+    if opening:
+        out_specs.append(tile(depth))
+        out_shape.append(jax.ShapeDtypeStruct((depth, width), jnp.bfloat16))
     return pl.pallas_call(
         kernel,
         grid=(2 * tiles,),
         in_specs=[pl.BlockSpec(b.shape, lambda i: (0, 0)) for b in blocks]
-        + [
-            pl.BlockSpec((depth, TILE), own_columns),
-            pl.BlockSpec((depth, TILE), lambda i: (0, jnp.minimum(i, tiles - 1))),
-            pl.BlockSpec((depth, TILE), lambda i: (0, jnp.maximum(i - tiles, 0))),
-        ],
-        out_specs=[pl.BlockSpec((h, TILE), lambda i: (0, i)) for h in heights],
-        out_shape=[jax.ShapeDtypeStruct((h, 2 * half), jnp.float32) for h in heights],
-        scratch_shapes=[pltpu.VMEM((2 * side_rows, depth), jnp.bfloat16)] * 2
-        + [pltpu.VMEM((depth, TILE), jnp.bfloat16)],
+        + [pl.BlockSpec((depth, TILE), own_columns)]
+        + extra_specs,
+        out_specs=out_specs,
+        out_shape=out_shape,
+        scratch_shapes=[pltpu.VMEM((2 * side_rows, depth), jnp.bfloat16)] * 2,
         compiler_params=pltpu.CompilerParams(vmem_limit_bytes=48 * MIB),
         cost_estimate=pl.CostEstimate(
-            flops=8 * side_rows * depth * 2 * half,
-            bytes_accessed=16 * side_rows * depth + 12 * depth * half + 16 * side_rows * half,
+            flops=8 * side_rows * depth * width,
+            bytes_accessed=16 * side_rows * depth + 4 * depth * width + 12 * side_rows * width,
             transcendentals=0,
         ),
-    )(*blocks, weight, *w_far)
+    )(*blocks, weight, *extra)
 
 
 def exchange(parts, axis):
@@ -449,27 +495,41 @@
     return ((zero_a, got1, back3), (zero_b, got3, back1))
 
 
-def next_parts(chunks):
-    def rows(side, start, stop):
-        chosen = []
-        for chunk in chunks:
-            kept, got, back = chunk[side]
-            lines = kept.shape[0]
-            span = slice(start * ROWS, stop * ROWS)
-            after = slice(lines + start * ROWS, lines + stop * ROWS)
-            chosen.append(kept[span] + got[after] + back[span])
-        if stop - start == 2:
-            chosen = [c[:ROWS] for c in chosen] + [c[ROWS:] for c in chosen]
-        return jnp.concatenate(chosen, axis=0)
-
-    return (
-        rows(0, 0, 2),
-        rows(1, 0, 2),
-        rows(1, 3, 4),
-        rows(0, 3, 4),
-        rows(0, 2, 3),
-        rows(1, 2, 3),
-    )
+def combine_kernel(*refs):
+    count = (len(refs) - 6) // 6
+    first, third, one_b, three_a, zero_a, zero_b = refs[6 * count :]
+    lines = 4 * ROWS
+    for chunk in range(count):
+        kept_a, got_a, back_a, kept_b, got_b, back_b = refs[6 * chunk : 6 * chunk + 6]
+        behind = slice(2 * lines, 3 * lines) if chunk < count - 1 else slice(0, lines)
+        here = slice(chunk * ROWS, (chunk + 1) * ROWS)
+        later = slice((count + chunk) * ROWS, (count + chunk + 1) * ROWS)
+        sum_a = kept_a[...] + got_a[lines : 2 * lines] + back_a[behind]
+        sum_b = kept_b[...] + got_b[lines : 2 * lines] + back_b[behind]
+        first[here] = sum_a[:ROWS]
+        first[later] = sum_a[ROWS : 2 * ROWS]
+        zero_a[here] = sum_a[2 * ROWS : 3 * ROWS]
+        three_a[here] = sum_a[3 * ROWS :]
+        third[here] = sum_b[:ROWS]
+        third[later] = sum_b[ROWS : 2 * ROWS]
+        zero_b[here] = sum_b[2 * ROWS : 3 * ROWS]
+        one_b[here] = sum_b[3 * ROWS :]
+
+
+def combine(chunks):
+    operands = [array for chunk in chunks for side in chunk for array in side]
+    count = len(chunks)
+    columns = operands[0].shape[1]
+    heights = (2 * count, 2 * count, count, count, count, count)
+    return pl.pallas_call(
+        combine_kernel,
+        grid=(columns // TILE,),
+        in_specs=[pl.BlockSpec((a.shape[0], TILE), lambda i: (0, i)) for a in operands],
+        out_specs=[pl.BlockSpec((h * ROWS, TILE), lambda i: (0, i)) for h in heights],
+        out_shape=[jax.ShapeDtypeStruct((h * ROWS, columns), jnp.float32) for h in heights],
+        compiler_params=pltpu.CompilerParams(vmem_limit_bytes=56 * MIB),
+        cost_estimate=pl.CostEstimate(flops=0, bytes_accessed=12 * MIB, transcendentals=0),
+    )(*operands)
 
 
 def finish_kernel(kept_0, got_0, back_0, kept_1, got_1, back_1, *outs):
@@ -522,17 +582,42 @@
     )(*pieces)
 
 
-def project(gated, out_weight, w_far):
-    chunks = []
-    for own in gated:
-        near = swap(own, lo=1)
-        far = swap(own, hi=1, lo=1)
-        middle = own.shape[0] // 2
-        cross_near = swap(far[:middle], lo=1)
-        cross_far = swap(near[middle:], hi=1, lo=1)
-        parts = product((own, near, cross_near, cross_far, far), out_weight, w_far)
-        chunks.append(exchange(parts, "first"))
-    kept_0, kept_1, away_0, away_1 = finish(exchange(next_parts(chunks), "second"))
+def project(gated, out_weight, w_near):
+    lines = 4 * ROWS
+    chunks, sent, before = [], [], ()
+
+    def ring(own, *others):
+        own = after(own, *others)
+        return (own, swap(own, lo=1), swap(own, hi=1, lo=1))
+
+    around = ring(gated[0])
+    for at in range(len(gated)):
+        own, near, far = around
+        opposite = cross(near, far)
+        if at == 0:
+            w_far = (w_near, swap(after(w_near, near), core=1))
+        if at + 1 < len(gated):
+            around = ring(gated[at + 1], *((opposite,) if at == 0 else (near, far)))
+            if at > 0:
+                own = after(own, *around[1:])
+        parts = product((own, near, opposite, far), out_weight, w_far, before)
+        first, third, one_b, three_a, zero_a, zero_b = parts[:6]
+        if at == 0:
+            w_far = parts[6]
+        got1 = swap(first, first=1)
+        got3 = swap(third, first=3)
+        before = (got1, got3, one_b, three_a)
+        sent.append((zero_a, got1, zero_b, got3))
+    got1, got3, one_b, three_a = before
+    back1 = swap(one_b + got3[:lines], first=1)
+    back3 = swap(three_a + got1[:lines], first=3)
+    for at, (zero_a, got1, zero_b, got3) in enumerate(sent):
+        if at + 1 < len(sent):
+            back_a, back_b = sent[at + 1][3], sent[at + 1][1]
+        else:
+            back_a, back_b = back3, back1
+        chunks.append(((zero_a, got1, back_a), (zero_b, got3, back_b)))
+    kept_0, kept_1, away_0, away_1 = finish(exchange(combine(chunks), "second"))
     return assemble(
         (kept_0, swap(kept_1, lo=1), swap(away_0, hi=1), swap(away_1, hi=1, lo=1))
     )
@@ -555,30 +640,33 @@
     pool_slot,
     lengths,
 ):
+    outgoing = outgoing_weights(out_weight)
+    w_near = swap(outgoing, hi=1, lo=1)
     group = lax.axis_index("head").astype(jnp.uint32) * a_log.shape[0] >> 5
     bc_tail = pool_bctail.reshape(pool_bctail.shape[:2] + (2, GROUPS, STATE))
     bc_tail = lax.dynamic_index_in_dim(bc_tail, group, 3, keepdims=False)
     tails = jnp.concatenate([pool_xtail, bc_tail.reshape(bc_tail.shape[:2] + (2 * STATE,))], axis=-1)
     tails = jnp.pad(tails.astype(jnp.float32), ((0, 0), (5, 0), (0, 0)))
-    away_0, away_1, mine, chip, tail_away, tail_mine, tail_chip, outgoing = prepare(
-        pool_dev, pool_slot, pool_state, tails, out_weight
+    away_0, away_1, mine, chip, tail_away, tail_mine, tail_chip = prepare(
+        pool_dev.reshape(-1), pool_slot, pool_state, after(tails, outgoing)
     )
     tail_near = swap(tail_away, core=1)
+    near_0 = swap(after(away_0, tail_away), core=1)
+    near_1 = swap(after(away_1, away_0), core=1)
     tail_far = swap(tail_chip + tail_near[:, 1], lo=1)
     tail_rows = tail_mine + tail_near[:, 0] + tail_far
-    w_near = swap(outgoing, hi=1, lo=1)
-    w_far = (w_near, swap(w_near, core=1))
+    far_0 = swap(chip[0] + near_0[1], lo=1)
+    far_1 = swap(chip[1] + near_1[1], lo=1)
+    far_0 = after(far_0, far_1)
     parts = scan(
         lengths, x_input, bc_input, tail_rows, conv_x, conv_bc, dt_raw, a_log, d_skip
     )
     gated, closing = [], []
-    for j, away in enumerate((away_0, away_1)):
-        near = swap(away, core=1)
-        far = swap(chip[j] + near[1], lo=1)
+    for j, (near, far) in enumerate(((near_0, far_0), (near_1, far_1))):
         *rows, state = gate(lengths, j, parts, z_gate, mine, near, far)
         gated += rows
         closing.append(state)
-    mixed_out = project(gated, out_weight, w_far)
+    mixed_out = project(gated, out_weight, w_near)
     return (mixed_out, jnp.concatenate(closing, axis=0))
 
 

time: 290 us -> 301 us (1.038)
  Pallas kernels: 46.5 us -> 64.4 us
  waiting for transfers between devices: 183 us -> 169 us
  local copies, waits for them, and re-layouts: 8.42 us -> 15.5 us
    ppermute x31 -> x33, waiting for transfers between devices: 183 us -> 142 us  [swap(): return lax.ppermute(array, AXES, pairs)]
    ppermute x0 -> x4, waiting for transfers between devices: none -> 26.8 us  [cross(): return lax.ppermute(jnp.where(core == 0, far, near), AXES, pairs)]
    pallas_call x1 -> x3, Pallas kernels: 4.34 us -> 14.6 us  [the longest x1 11 us: combine(): pl.pallas_call(combine_kernel, grid=(columns // TILE,), in_specs=[pl.Bloc...]
    unnamed x38 -> x79, local copies, waits for them, and re-layouts: 6.41 us -> 13.8 us
    pallas_call x2 -> x4, Pallas kernels: 19.6 us -> 26 us  [product(): pl.pallas_call(kernel, grid=(2 * tiles,), in_specs=[pl.BlockSpec(b.shape,...]
    ppermute x31 -> x33, starting transfers between devices: 46.1 us -> 41.8 us  [swap(): return lax.ppermute(array, AXES, pairs)]
    ppermute x0 -> x4, starting transfers between devices: none -> 3.81 us  [cross(): return lax.ppermute(jnp.where(core == 0, far, near), AXES, pairs)]
  transfers between devices with their start and end apart: 31 -> 37, of which waited for: 21 -> 22; matrix products, arithmetic and copies ran while one was open for 2% -> 2% of each run, Pallas kernels for 14% -> 10%
where the time goes in v4:
time: 301 us; the launch traced here: 300 us
  waiting for transfers between devices  169 us (56%)
  Pallas kernels  64.4 us (21%)
  starting transfers between devices  45.6 us (15%)
  local copies, waits for them, and re-layouts  15.5 us (5%)
  other arithmetic  4.62 us (2%)
    ppermute x33, waiting for transfers between devices, swap(): return lax.ppermute(array, AXES, pairs)  142 us
    ppermute x33, starting transfers between devices, swap(): return lax.ppermute(array, AXES, pairs)  41.8 us
    ppermute x4, waiting for transfers between devices, cross(): return lax.ppermute(jnp.where(core == 0, far, near), AXES, pairs)  26.8 us
    pallas_call x4, Pallas kernels, product(): pl.pallas_call(kernel, grid=(2 * tiles,), in_specs=[pl.BlockSpec(b.shape,...  26 us
    pallas_call x1, Pallas kernels, scan(): pl.pallas_call(scan_kernel, grid=(requests, length // BLOCK), in_specs=[p...  16.5 us
    unnamed x79, local copies, waits for them, and re-layouts  13.8 us
    pallas_call x1, Pallas kernels, combine(): pl.pallas_call(combine_kernel, grid=(columns // TILE,), in_specs=[pl.Bloc...  11 us
    pallas_call x2, Pallas kernels, gate(): pl.pallas_call(functools.partial(gate_kernel, request=request), grid=(1,)...  6.11 us
  transfers between devices with their start and end apart: 37, of which 22 were waited for; matrix products, arithmetic and copies ran while one was open for 2% of the time, Pallas kernels for 10%

profile of v4, /device:TPU:0, one launch (start us, length us, event | category | flops | bytes accessed | tf_op | source)
XLA Modules:
  0.0 299.8 jit_solution(9597249206154440709)
XLA Ops:
  1.3 0.9 reshape.17
  2.4 1.4 shard_map.158
  3.9 2.2 shard_map.159
  6.7 2.8 collective-permute-start.9
  10.4 1.2 fusion
  11.7 1.6 collective-permute-start.5
  13.7 1.7 collective-permute-start.1
  16.0 22.5 %collective-permute-done.1 = f32[2,8,1024]{2,1,0:T(8,128)S(1)} collective-permute-done((f32[2,8,1024]{2,1,0:T(8,128)S(1)}, f32[2,8,1024]{2,1,0:T(8,128)S(1)}, u32[]{:S(2)}, u32[]{:S(2)}) %collective-permute-start.1) | collective-permute-done | bytes 65568 | tf_op jit(solution)/shard_map/ppermute | solution.py:26
  39.1 16.5 %shard_map.160 = (f32[2,512,512]{2,1,0:T(8,128)}, bf16[2,512,256]{2,1,0:T(8,128)(2,1)}, f32[2,512,8]{2,1,0:T(8,128)}, f32[2,512,256]{2,1,0:T(8,128)}) custom-call(s32[2]{0:T(128)} %lengths.5, bf16[2,512,512]{2,1,0:T(8,128)(2,1)} %x_ref.1, bf16[2,512,4096]{2,1,0:T(8,128)(2,1)} %c_ref.1, bf16[2,512,4096]{2,1,0:T(8,128)(2,1)} %c_ref.1, ...), custom_call_target="tpu_custom_call" | custom-call | flops 872415232 | bytes 12582912 | tf_op jit(solution)/shard_map/pallas_call | solution.py:189
  55.7 1.2 copy-done.2
  56.9 1.0 copy-done.4
  57.9 1.0 copy-done.6
  59.0 3.5 %shard_map.161 = (f32[256,512]{1,0:T(8,128)}, f32[256,512]{1,0:T(8,128)S(1)}, f32[1,512,256]{2,1,0:T(8,128)S(1)}) custom-call(s32[2]{0:T(128)S(1)} %copy-done.22, f32[2,512,512]{2,1,0:T(8,128)} %get-tuple-element.68.y_ref, bf16[2,512,256]{2,1,0:T(8,128)(2,1)S(1)} %copy-done.4, f32[2,512,8]{2,1,0:T(8,128)S(1)} %copy-done.6, f32[2,512,256]{2,1,0:T(8,128)S(1)} %copy-done.2, ...), custom_call_target="tpu_custom_call" | custom-call | flops 134217728 | bytes 6291456 | tf_op jit(solution)/shard_map/pallas_call | solution.py:363
  62.4 0.8 copy-done.12
  63.2 0.8 copy-done.18
  64.0 1.6 collective-permute-start.6
  65.6 12.0 %collective-permute-done.6.refs_1_ = f32[256,512]{1,0:T(8,128)} collective-permute-done((f32[256,512]{1,0:T(8,128)}, f32[256,512]{1,0:T(8,128)}, u32[]{:S(2)}, u32[]{:S(2)}) %collective-permute-start.6) | collective-permute-done | bytes 524320 | tf_op jit(solution)/shard_map/ppermute | solution.py:26
  77.6 2.8 collective-permute-start.7
  80.4 12.9 %collective-permute-done.7.refs_3_ = f32[256,512]{1,0:T(8,128)S(1)} collective-permute-done((f32[256,512]{1,0:T(8,128)}, f32[256,512]{1,0:T(8,128)S(1)}, u32[]{:S(2)}, u32[]{:S(2)}) %collective-permute-start.7) | collective-permute-done | bytes 524320 | tf_op jit(solution)/shard_map/ppermute | solution.py:26
  93.9 8.8 %collective-permute-done.8.refs_2_ = f32[256,512]{1,0:T(8,128)S(1)} collective-permute-done((f32[256,512]{1,0:T(8,128)S(1)}, f32[256,512]{1,0:T(8,128)S(1)}, u32[]{:S(2)}, u32[]{:S(2)}) %collective-permute-start.8) | collective-permute-done | bytes 524320 | tf_op jit(solution)/shard_map/ppermute | solution.py:38
  102.7 2.9 collective-permute-start.13
  105.6 7.6 %shard_map.162 = (f32[128,2048]{1,0:T(8,128)S(1)}, f32[128,2048]{1,0:T(8,128)}, f32[64,2048]{1,0:T(8,128)S(1)}, f32[64,2048]{1,0:T(8,128)S(1)}, f32[64,2048]{1,0...) custom-call(f32[256,512]{1,0:T(8,128)} %get-tuple-element.79.refs_0_, ...), custom_call_target="tpu_custom_call" | custom-call | flops 2147483648 | bytes 12582912 | tf_op jit(solution)/shard_map/pallas_call | solution.py:470
  113.2 0.8 copy-done.9
  114.0 1.6 collective-permute-start.11
  115.6 2.2 collective-permute-start.17
  117.8 2.7 shard_map.163
  120.5 1.0 collective-permute-start.15
  121.5 1.2 collective-permute-start.14
  122.8 0.9 collective-permute-start.16
  123.7 12.9 %collective-permute-done.15.refs_3_ = f32[256,512]{1,0:T(8,128)S(1)} collective-permute-done((f32[256,512]{1,0:T(8,128)S(1)}, f32[256,512]{1,0:T(8,128)S(1)}, u32[]{:S(2)}, u32[]{:S(2)}) %collective-permute-start.15) | collective-permute-done | bytes 524320 | tf_op jit(solution)/shard_map/ppermute | solution.py:26
  136.6 4.4 %collective-permute-done.16.refs_2_ = f32[256,512]{1,0:T(8,128)S(1)} collective-permute-done((f32[256,512]{1,0:T(8,128)S(1)}, f32[256,512]{1,0:T(8,128)S(1)}, u32[]{:S(2)}, u32[]{:S(2)}) %collective-permute-start.16) | collective-permute-done | bytes 524320 | tf_op jit(solution)/shard_map/ppermute | solution.py:38
  141.0 1.0 copy-done.31
  142.3 6.1 %shard_map.164 = (f32[192,2048]{1,0:T(8,128)}, f32[192,2048]{1,0:T(8,128)}, f32[64,2048]{1,0:T(8,128)S(1)}, f32[64,2048]{1,0:T(8,128)S(1)}, f32[64,2048]{1,0:T(8,128)S(1)}, /*index=5*/f32[64,2048]{1,0:T(8,128)S(1)}) custom-call(f32[256,512]{1,0:T(8,128)S(1)} %copy-done.13, f32[256,512]{1,0:T(8,128)S(1)} %collective-permute-done.12.refs_1_, ...), custom_call_target="tpu_custom_call" | custom-call | flops 2147483648 | bytes 12582912 | tf_op jit(solution)/shard_map/pallas_call | solution.py:470
  148.5 3.1 %collective-permute-start.18 = (f32[192,2048]{1,0:T(8,128)}, f32[192,2048]{1,0:T(8,128)S(1)}, u32[]{:S(2)}, u32[]{:S(2)}) collective-permute-start(f32[192,2048]{1,0:T(8,128)} %get-tuple-element.92), channel_id=1, source_target_pairs={{0,6},{1,7},{2,4},{3,5},{4,2},{5,3},{6,0},{7,1},{8,14},{9,15},{10,... | collective-permute-start | bytes 4718600 | tf_op jit(solution)/shard_map/ppermute | solution.py:26
  151.7 2.6 collective-permute-start.21
  154.4 2.1 collective-permute-start.22
  156.5 11.2 %collective-permute-done.21.refs_3_ = f32[256,512]{1,0:T(8,128)S(1)} collective-permute-done((f32[256,512]{1,0:T(8,128)S(1)}, f32[256,512]{1,0:T(8,128)S(1)}, u32[]{:S(2)}, u32[]{:S(2)}) %collective-permute-start.21) | collective-permute-done | bytes 524320 | tf_op jit(solution)/shard_map/ppermute | solution.py:26
  167.7 4.7 %collective-permute-done.22.refs_2_ = f32[256,512]{1,0:T(8,128)S(1)} collective-permute-done((f32[256,512]{1,0:T(8,128)S(1)}, f32[256,512]{1,0:T(8,128)S(1)}, u32[]{:S(2)}, u32[]{:S(2)}) %collective-permute-start.22) | collective-permute-done | bytes 524320 | tf_op jit(solution)/shard_map/ppermute | solution.py:38
  172.4 1.1 copy-done.25
  174.1 6.1 %shard_map.165 = (f32[192,2048]{1,0:T(8,128)}, f32[192,2048]{1,0:T(8,128)}, f32[64,2048]{1,0:T(8,128)S(1)}, f32[64,2048]{1,0:T(8,128)S(1)}, f32[64,2048]{1,0:T(8,128)S(1)}, /*index=5*/f32[64,2048]{1,0:T(8,128)S(1)}) custom-call(f32[256,512]{1,0:T(8,128)S(1)} %get-tuple-element.98.refs_0_, f32[256,512]{1,0:T(8,128)S(1)} %collective-permute-done.14.refs_1_, ...), custom_call_target="tpu_custom_call" | custom-call | flops 2147483648 | bytes 12582912 | tf_op jit(solution)/shard_map/pallas_call | solution.py:470
  181.0 0.8 copy-done.15
  181.8 3.0 %collective-permute-start.23 = (f32[192,2048]{1,0:T(8,128)}, f32[192,2048]{1,0:T(8,128)S(1)}, u32[]{:S(2)}, u32[]{:S(2)}) collective-permute-start(f32[192,2048]{1,0:T(8,128)} %get-tuple-element.101), channel_id=1, source_target_pairs={{0,6},{1,7},{2,4},{3,5},{4,2},{5,3},{6,0},{7,1},{8,14},{9,15},{10,... | collective-permute-start | bytes 4718600 | tf_op jit(solution)/shard_map/ppermute | solution.py:26
  185.4 8.9 %collective-permute-done.25.refs_2_ = f32[256,512]{1,0:T(8,128)S(1)} collective-permute-done((f32[256,512]{1,0:T(8,128)S(1)}, f32[256,512]{1,0:T(8,128)S(1)}, u32[]{:S(2)}, u32[]{:S(2)}) %collective-permute-start.25) | collective-permute-done | bytes 524320 | tf_op jit(solution)/shard_map/ppermute | solution.py:38
  194.3 9.3 %collective-permute-done.23.refs_7_.refs_8_.refs_16_ = f32[192,2048]{1,0:T(8,128)S(1)} collective-permute-done((f32[192,2048]{1,0:T(8,128)}, f32[192,2048]{1,0:T(8,128)S(1)}, u32[]{:S(2)}, u32[]{:S(2)}) %collective-permute-start.23) | collective-permute-done | bytes 1572896 | tf_op jit(solution)/shard_map/ppermute | solution.py:26
  203.7 1.8 collective-permute-done.24.refs_6_.refs_11_.refs_13_
  205.5 1.2 copy-done.28
  206.7 6.2 %shard_map.166 = (f32[192,2048]{1,0:T(8,128)}, f32[192,2048]{1,0:T(8,128)}, f32[64,2048]{1,0:T(8,128)S(1)}, f32[64,2048]{1,0:T(8,128)S(1)}, f32[64,2048]{1,0:T(8,128)S(1)}, /*index=5*/f32[64,2048]{1,0:T(8,128)S(1)}) custom-call(f32[256,512]{1,0:T(8,128)S(1)} %get-tuple-element.97.refs_0_, f32[256,512]{1,0:T(8,128)S(1)} %collective-permute-done.20.refs_1_, ...), custom_call_target="tpu_custom_call" | custom-call | flops 2147483648 | bytes 12582912 | tf_op jit(solution)/shard_map/pallas_call | solution.py:470
  212.9 1.8 collective-permute-start.26
  214.7 20.2 %collective-permute-done.26.refs_14_.refs_22_ = f32[192,2048]{1,0:T(8,128)S(1)} collective-permute-done((f32[192,2048]{1,0:T(8,128)}, f32[192,2048]{1,0:T(8,128)S(1)}, u32[]{:S(2)}, u32[]{:S(2)}) %collective-permute-start.26) | collective-permute-done | bytes 1572896 | tf_op jit(solution)/shard_map/ppermute | solution.py:26
  236.0 1.7 collective-permute-start.28
  237.7 6.5 %collective-permute-done.29.refs_23_ = f32[64,2048]{1,0:T(8,128)S(1)} collective-permute-done((f32[64,2048]{1,0:T(8,128)S(1)}, f32[64,2048]{1,0:T(8,128)S(1)}, u32[]{:S(2)}, u32[]{:S(2)}) %collective-permute-start.29) | collective-permute-done | bytes 524320 | tf_op jit(solution)/shard_map/ppermute | solution.py:26
  244.2 2.2 collective-permute-done.28.refs_20_
  247.2 11.0 %shard_map.167 = (f32[128,2048]{1,0:T(8,128)}, f32[128,2048]{1,0:T(8,128)}, f32[64,2048]{1,0:T(8,128)}, f32[64,2048]{1,0:T(8,128)}, f32[64,2048]{1,0:T(8,128)}, /*index=5*/f32[64,2048]{1,0:T(8,128)}) custom-call(f32[64,2048]{1,0:T(8,128)} %copy-done.8, f32[128,2048]{1,0:T(8,128)} %copy-done.31, f32[192,2048]{1,0:T(8,128)} %copy-done.25, ...), custom_call_target="tpu_custom_call" | custom-call | bytes 12582912 | tf_op jit(solution)/shard_map/pallas_call | solution.py:524
  258.2 1.5 collective-permute-start.30
  260.4 12.9 %collective-permute-done.30.got_0 = f32[128,2048]{1,0:T(8,128)S(1)} collective-permute-done((f32[128,2048]{1,0:T(8,128)}, f32[128,2048]{1,0:T(8,128)S(1)}, u32[]{:S(2)}, u32[]{:S(2)}) %collective-permute-start.30) | collective-permute-done | bytes 1048608 | tf_op jit(solution)/shard_map/ppermute | solution.py:26
  273.3 1.2 slice_add_fusion.1
  274.5 1.7 collective-permute-start.31
  276.4 8.6 %collective-permute-done.31.back_0 = f32[64,2048]{1,0:T(8,128)S(1)} collective-permute-done((f32[64,2048]{1,0:T(8,128)S(1)}, f32[64,2048]{1,0:T(8,128)S(1)}, u32[]{:S(2)}, u32[]{:S(2)}) %collective-permute-start.31) | collective-permute-done | bytes 524320 | tf_op jit(solution)/shard_map/ppermute | solution.py:26
  286.1 2.7 collective-permute-start.35
  288.8 1.7 collective-permute-start.36
  290.5 1.0 pad_maximum_fusion
  292.2 3.9 %collective-permute-done.35.across = f32[2,16,2048]{2,1,0:T(8,128)S(1)} collective-permute-done((f32[2,16,2048]{2,1,0:T(8,128)S(1)}, f32[2,16,2048]{2,1,0:T(8,128)S(1)}, u32[]{:S(2)}, u32[]{:S(2)}) %collective-permute-start.35) | collective-permute-done | bytes 262176 | tf_op jit(solution)/shard_map/ppermute | solution.py:26
  296.1 2.7 collective-permute-done.36.far
  298.8 1.0 shard_map.169
  (120 shorter events, 11.8 us)
Async XLA Ops:
  2.4 1.5 copy-start.23
  2.4 1.5 copy-start.24
  6.1 5.5 %copy-start.1 = (f32[2,512,256]{2,1,0:T(8,128)}, f32[2,512,256]{2,1,0:T(8,128)S(1)}, u32[]{:S(2)}) copy-start(f32[2,512,256]{2,1,0:T(8,128)S(1)} %get-tuple-element.72.mine) | copy-start | bytes 3145732
  6.1 3.5 %collective-permute-start.2 = (f32[2,512,256]{2,1,0:T(8,128)S(1)}, f32[2,512,256]{2,1,0:T(8,128)S(1)}, u32[]{:S(2)}, u32[]{:S(2)}) collective-permute-start(f32[2,512,256]{2,1,0:T(8,128)S(1)} %get-tuple-element.74), channel_id=1, source_target_pairs={{0,32},{1,33},{2,34},{3,35},{4,36},{5,37},{6,38},{7,39},{8,40},{9,... | collective-permute-start | bytes 3145736 | tf_op jit(solution)/shard_map/ppermute | solution.py:26
  6.2 4.1 %collective-permute-start.4 = (f32[2,512,256]{2,1,0:T(8,128)S(1)}, f32[2,512,256]{2,1,0:T(8,128)S(1)}, u32[]{:S(2)}, u32[]{:S(2)}) collective-permute-start(f32[2,512,256]{2,1,0:T(8,128)S(1)} %get-tuple-element.77), channel_id=1, source_target_pairs={{0,32},{1,33},{2,34},{3,35},{4,36},{5,37},{6,38},{7,39},{8,40},{9,... | collective-permute-start | bytes 3145736 | tf_op jit(solution)/shard_map/ppermute | solution.py:26
  6.7 58.9 %collective-permute-start.9 = (f32[512,1024]{1,0:T(8,128)S(1)}, f32[512,1024]{1,0:T(8,128)}, u32[]{:S(2)}, u32[]{:S(2)}) collective-permute-start(f32[512,1024]{1,0:T(8,128)S(1)} %shard_map.158), channel_id=1, source_target_pairs={{0,65},{1,64},{2,67},{3,66},{4,69},{5,68},{6,71},{7,70},{8,73},{9,... | collective-permute-start | bytes 6291464 | tf_op jit(solution)/shard_map/ppermute | solution.py:26
  9.6 4.2 %collective-permute-start = (f32[2,2,8,1024]{3,2,0,1:T(8,128)S(1)}, f32[2,2,8,1024]{3,2,0,1:T(8,128)S(1)}, u32[]{:S(2)}, u32[]{:S(2)}) collective-permute-start(f32[2,2,8,1024]{3,2,0,1:T(8,128)S(1)} %copy.24), channel_id=1, source_target_pairs={{0,32},{1,33},{2,34},{3,35},{4,36},{5,37},{6,38},{7,39},{8,40},{9,... | collective-permute-start | bytes 393224 | tf_op jit(solution)/shard_map/ppermute | solution.py:26
  9.7 1.9 copy-start.34
  10.4 1.3 copy-start.33
  10.4 5.0 %copy-start.38 = (f32[8]{0:T(128)S(1)}, f32[8]{0:T(128)}, u32[]{:S(2)}) copy-start(f32[8]{0:T(128)} %param.19) | copy-start | bytes 100
  11.7 43.9 %collective-permute-start.5 = (f32[512,256]{1,0:T(8,128)}, f32[512,256]{1,0:T(8,128)}, u32[]{:S(2)}, u32[]{:S(2)}) collective-permute-start(f32[512,256]{1,0:T(8,128)} %get-tuple-element.126), channel_id=1, source_target_pairs={{0,64},{1,65},{2,66},{3,67},{4,68},{5,69},{6,70},{7,71},{8,72},{9,... | collective-permute-start | bytes 1572872 | tf_op jit(solution)/shard_map/ppermute | solution.py:26
  13.3 42.4 %collective-permute-start.3 = (f32[512,256]{1,0:T(8,128)}, f32[512,256]{1,0:T(8,128)}, u32[]{:S(2)}, u32[]{:S(2)}) collective-permute-start(f32[512,256]{1,0:T(8,128)} %get-tuple-element.127), channel_id=1, source_target_pairs={{0,64},{1,65},{2,66},{3,67},{4,68},{5,69},{6,70},{7,71},{8,72},{9,... | collective-permute-start | bytes 1572872 | tf_op jit(solution)/shard_map/ppermute | solution.py:26
  13.7 24.8 %collective-permute-start.1 = (f32[2,8,1024]{2,1,0:T(8,128)S(1)}, f32[2,8,1024]{2,1,0:T(8,128)S(1)}, u32[]{:S(2)}, u32[]{:S(2)}) collective-permute-start(f32[2,8,1024]{2,1,0:T(8,128)S(1)} %fusion.6), channel_id=1, source_target_pairs={{0,64},{1,65},{2,66},{3,67},{4,68},{5,69},{6,70},{7,71},{8,72},{9,... | collective-permute-start | bytes 196616 | tf_op jit(solution)/shard_map/ppermute | solution.py:26
  39.1 16.5 %copy-start = (bf16[2,512,512]{2,1,0:T(8,128)(2,1)S(1)}, bf16[2,512,512]{2,1,0:T(8,128)(2,1)}, u32[]{:S(2)}) copy-start(bf16[2,512,512]{2,1,0:T(8,128)(2,1)} %z_ref.3) | copy-start | bytes 3145732
  39.1 16.5 %copy-start.22 = (s32[2]{0:T(128)S(1)}, s32[2]{0:T(128)}, u32[]{:S(2)}) copy-start(s32[2]{0:T(128)} %lengths.5) | copy-start | bytes 28
  64.0 13.6 %collective-permute-start.6 = (f32[256,512]{1,0:T(8,128)}, f32[256,512]{1,0:T(8,128)}, u32[]{:S(2)}, u32[]{:S(2)}) collective-permute-start(f32[256,512]{1,0:T(8,128)} %get-tuple-element.79.refs_0_), channel_id=1, source_target_pairs={{0,64},{1,65},{2,66},{3,67},{4,68},{5,69},{6,70},{7,71},{8,72},{9,... | collective-permute-start | bytes 1572872 | tf_op jit(solution)/shard_map/ppermute | solution.py:26
  65.6 37.1 %copy-start.13 = (f32[256,512]{1,0:T(8,128)S(1)}, f32[256,512]{1,0:T(8,128)}, u32[]{:S(2)}) copy-start(f32[256,512]{1,0:T(8,128)} %copy-done.12) | copy-start | bytes 1572868
  77.6 28.0 %collective-permute-start.10 = (f32[512,1024]{1,0:T(8,128)}, f32[512,1024]{1,0:T(8,128)}, u32[]{:S(2)}, u32[]{:S(2)}) collective-permute-start(f32[512,1024]{1,0:T(8,128)} %collective-permute-done.9.refs_5_), channel_id=1, source_target_pairs={{0,32},{1,33},{2,34},{3,35},{4,36},{5,37},{6,38},{7,39},{8,40},{9,... | collective-permute-start | bytes 6291464 | tf_op jit(solution)/shard_map/ppermute | solution.py:26
  77.6 15.8 %collective-permute-start.7 = (f32[256,512]{1,0:T(8,128)}, f32[256,512]{1,0:T(8,128)S(1)}, u32[]{:S(2)}, u32[]{:S(2)}) collective-permute-start(f32[256,512]{1,0:T(8,128)} %get-tuple-element.79.refs_0_), channel_id=1, source_target_pairs={{0,65},{1,64},{2,67},{3,66},{4,69},{5,68},{6,71},{7,70},{8,73},{9,... | collective-permute-start | bytes 1572872 | tf_op jit(solution)/shard_map/ppermute | solution.py:26
  93.4 9.3 %collective-permute-start.8 = (f32[256,512]{1,0:T(8,128)S(1)}, f32[256,512]{1,0:T(8,128)S(1)}, u32[]{:S(2)}, u32[]{:S(2)}) collective-permute-start(f32[256,512]{1,0:T(8,128)S(1)} %broadcast_select_fusion.3), channel_id=1, source_target_pairs={{0,64},{1,65},{2,66},{3,67},{4,68},{5,69},{6,70},{7,71},{8,72},{9,... | collective-permute-start | bytes 1572872 | tf_op jit(solution)/shard_map/ppermute | solution.py:38
  102.7 15.1 %copy-start.3 = (f32[2,512,256]{2,1,0:T(8,128)S(1)}, f32[2,512,256]{2,1,0:T(8,128)}, u32[]{:S(2)}) copy-start(f32[2,512,256]{2,1,0:T(8,128)} %get-tuple-element.71.part_ref) | copy-start | bytes 3145732
  102.7 15.1 %copy-start.5 = (bf16[2,512,256]{2,1,0:T(8,128)(2,1)S(1)}, bf16[2,512,256]{2,1,0:T(8,128)(2,1)}, u32[]{:S(2)}) copy-start(bf16[2,512,256]{2,1,0:T(8,128)(2,1)} %get-tuple-element.69.c_ref) | copy-start | bytes 1572868
  102.7 15.1 %copy-start.7 = (f32[2,512,8]{2,1,0:T(8,128)S(1)}, f32[2,512,8]{2,1,0:T(8,128)}, u32[]{:S(2)}) copy-start(f32[2,512,8]{2,1,0:T(8,128)} %get-tuple-element.70.decay_ref) | copy-start | bytes 98308
  102.7 17.7 %collective-permute-start.13 = (f32[256,512]{1,0:T(8,128)S(1)}, f32[256,512]{1,0:T(8,128)S(1)}, u32[]{:S(2)}, u32[]{:S(2)}) collective-permute-start(f32[256,512]{1,0:T(8,128)S(1)} %copy-done.13), channel_id=1, source_target_pairs={{0,65},{1,64},{2,67},{3,66},{4,69},{5,68},{6,71},{7,70},{8,73},{9,... | collective-permute-start | bytes 1572872 | tf_op jit(solution)/shard_map/ppermute | solution.py:26
  105.6 14.8 %collective-permute-start.12 = (f32[256,512]{1,0:T(8,128)S(1)}, f32[256,512]{1,0:T(8,128)S(1)}, u32[]{:S(2)}, u32[]{:S(2)}) collective-permute-start(f32[256,512]{1,0:T(8,128)S(1)} %copy-done.13), channel_id=1, source_target_pairs={{0,64},{1,65},{2,66},{3,67},{4,68},{5,69},{6,70},{7,71},{8,72},{9,... | collective-permute-start | bytes 1572872 | tf_op jit(solution)/shard_map/ppermute | solution.py:26
  114.0 6.4 %copy-start.8 = (f32[64,2048]{1,0:T(8,128)}, f32[64,2048]{1,0:T(8,128)S(1)}, u32[]{:S(2)}) copy-start(f32[64,2048]{1,0:T(8,128)S(1)} %get-tuple-element.81.refs_0_) | copy-start | bytes 1572868
  114.0 27.0 %collective-permute-start.11 = (f32[128,2048]{1,0:T(8,128)S(1)}, f32[128,2048]{1,0:T(8,128)S(1)}, u32[]{:S(2)}, u32[]{:S(2)}) collective-permute-start(f32[128,2048]{1,0:T(8,128)S(1)} %get-tuple-element.82), channel_id=1, source_target_pairs={{0,2},{1,3},{2,0},{3,1},{4,6},{5,7},{6,4},{7,5},{8,10},{9,11},{10,... | collective-permute-start | bytes 3145736 | tf_op jit(solution)/shard_map/ppermute | solution.py:26
  115.6 25.4 %collective-permute-start.17 = (f32[128,2048]{1,0:T(8,128)}, f32[128,2048]{1,0:T(8,128)S(1)}, u32[]{:S(2)}, u32[]{:S(2)}) collective-permute-start(f32[128,2048]{1,0:T(8,128)} %get-tuple-element.89), channel_id=1, source_target_pairs={{0,6},{1,7},{2,4},{3,5},{4,2},{5,3},{6,0},{7,1},{8,14},{9,15},{10,... | collective-permute-start | bytes 3145736 | tf_op jit(solution)/shard_map/ppermute | solution.py:26
  120.5 16.1 %collective-permute-start.15 = (f32[256,512]{1,0:T(8,128)S(1)}, f32[256,512]{1,0:T(8,128)S(1)}, u32[]{:S(2)}, u32[]{:S(2)}) collective-permute-start(f32[256,512]{1,0:T(8,128)S(1)} %get-tuple-element.98.refs_0_), channel_id=1, source_target_pairs={{0,65},{1,64},{2,67},{3,66},{4,69},{5,68},{6,71},{7,70},{8,73},{9,... | collective-permute-start | bytes 1572872 | tf_op jit(solution)/shard_map/ppermute | solution.py:26
  121.5 15.1 %collective-permute-start.14 = (f32[256,512]{1,0:T(8,128)S(1)}, f32[256,512]{1,0:T(8,128)S(1)}, u32[]{:S(2)}, u32[]{:S(2)}) collective-permute-start(f32[256,512]{1,0:T(8,128)S(1)} %get-tuple-element.98.refs_0_), channel_id=1, source_target_pairs={{0,64},{1,65},{2,66},{3,67},{4,68},{5,69},{6,70},{7,71},{8,72},{9,... | collective-permute-start | bytes 1572872 | tf_op jit(solution)/shard_map/ppermute | solution.py:26
  122.8 18.2 %collective-permute-start.16 = (f32[256,512]{1,0:T(8,128)S(1)}, f32[256,512]{1,0:T(8,128)S(1)}, u32[]{:S(2)}, u32[]{:S(2)}) collective-permute-start(f32[256,512]{1,0:T(8,128)S(1)} %broadcast_select_fusion.2), channel_id=1, source_target_pairs={{0,64},{1,65},{2,66},{3,67},{4,68},{5,69},{6,70},{7,71},{8,72},{9,... | collective-permute-start | bytes 1572872 | tf_op jit(solution)/shard_map/ppermute | solution.py:38
  141.0 1.3 copy-start.32
  148.4 19.3 %copy-start.11 = (f32[64,2048]{1,0:T(8,128)}, f32[64,2048]{1,0:T(8,128)S(1)}, u32[]{:S(2)}) copy-start(f32[64,2048]{1,0:T(8,128)S(1)} %get-tuple-element.102.refs_9_) | copy-start | bytes 1572868
  148.4 31.8 %copy-start.10 = (f32[64,2048]{1,0:T(8,128)}, f32[64,2048]{1,0:T(8,128)S(1)}, u32[]{:S(2)}) copy-start(f32[64,2048]{1,0:T(8,128)S(1)} %get-tuple-element.95.refs_6_) | copy-start | bytes 1572868
  148.5 24.0 %collective-permute-start.18 = (f32[192,2048]{1,0:T(8,128)}, f32[192,2048]{1,0:T(8,128)S(1)}, u32[]{:S(2)}, u32[]{:S(2)}) collective-permute-start(f32[192,2048]{1,0:T(8,128)} %get-tuple-element.92), channel_id=1, source_target_pairs={{0,6},{1,7},{2,4},{3,5},{4,2},{5,3},{6,0},{7,1},{8,14},{9,15},{10,... | collective-permute-start | bytes 4718600 | tf_op jit(solution)/shard_map/ppermute | solution.py:26
  151.6 20.9 %collective-permute-start.19 = (f32[192,2048]{1,0:T(8,128)}, f32[192,2048]{1,0:T(8,128)S(1)}, u32[]{:S(2)}, u32[]{:S(2)}) collective-permute-start(f32[192,2048]{1,0:T(8,128)} %get-tuple-element.94), channel_id=1, source_target_pairs={{0,2},{1,3},{2,0},{3,1},{4,6},{5,7},{6,4},{7,5},{8,10},{9,11},{10,... | collective-permute-start | bytes 4718600 | tf_op jit(solution)/shard_map/ppermute | solution.py:26
  151.7 16.0 %collective-permute-start.21 = (f32[256,512]{1,0:T(8,128)S(1)}, f32[256,512]{1,0:T(8,128)S(1)}, u32[]{:S(2)}, u32[]{:S(2)}) collective-permute-start(f32[256,512]{1,0:T(8,128)S(1)} %get-tuple-element.97.refs_0_), channel_id=1, source_target_pairs={{0,65},{1,64},{2,67},{3,66},{4,69},{5,68},{6,71},{7,70},{8,73},{9,... | collective-permute-start | bytes 1572872 | tf_op jit(solution)/shard_map/ppermute | solution.py:26
  154.3 13.4 %collective-permute-start.20 = (f32[256,512]{1,0:T(8,128)S(1)}, f32[256,512]{1,0:T(8,128)S(1)}, u32[]{:S(2)}, u32[]{:S(2)}) collective-permute-start(f32[256,512]{1,0:T(8,128)S(1)} %get-tuple-element.97.refs_0_), channel_id=1, source_target_pairs={{0,64},{1,65},{2,66},{3,67},{4,68},{5,69},{6,70},{7,71},{8,72},{9,... | collective-permute-start | bytes 1572872 | tf_op jit(solution)/shard_map/ppermute | solution.py:26
  154.4 18.0 %collective-permute-start.22 = (f32[256,512]{1,0:T(8,128)S(1)}, f32[256,512]{1,0:T(8,128)S(1)}, u32[]{:S(2)}, u32[]{:S(2)}) collective-permute-start(f32[256,512]{1,0:T(8,128)S(1)} %broadcast_select_fusion.1), channel_id=1, source_target_pairs={{0,64},{1,65},{2,66},{3,67},{4,68},{5,69},{6,70},{7,71},{8,72},{9,... | collective-permute-start | bytes 1572872 | tf_op jit(solution)/shard_map/ppermute | solution.py:38
  172.4 1.7 copy-start.26
  181.8 21.8 %collective-permute-start.23 = (f32[192,2048]{1,0:T(8,128)}, f32[192,2048]{1,0:T(8,128)S(1)}, u32[]{:S(2)}, u32[]{:S(2)}) collective-permute-start(f32[192,2048]{1,0:T(8,128)} %get-tuple-element.101), channel_id=1, source_target_pairs={{0,6},{1,7},{2,4},{3,5},{4,2},{5,3},{6,0},{7,1},{8,14},{9,15},{10,... | collective-permute-start | bytes 4718600 | tf_op jit(solution)/shard_map/ppermute | solution.py:26
  184.9 20.6 %collective-permute-start.24 = (f32[192,2048]{1,0:T(8,128)}, f32[192,2048]{1,0:T(8,128)S(1)}, u32[]{:S(2)}, u32[]{:S(2)}) collective-permute-start(f32[192,2048]{1,0:T(8,128)} %get-tuple-element.103), channel_id=1, source_target_pairs={{0,2},{1,3},{2,0},{3,1},{4,6},{5,7},{6,4},{7,5},{8,10},{9,11},{10,... | collective-permute-start | bytes 4718600 | tf_op jit(solution)/shard_map/ppermute | solution.py:26
  185.1 9.3 %collective-permute-start.25 = (f32[256,512]{1,0:T(8,128)S(1)}, f32[256,512]{1,0:T(8,128)S(1)}, u32[]{:S(2)}, u32[]{:S(2)}) collective-permute-start(f32[256,512]{1,0:T(8,128)S(1)} %broadcast_select_fusion), channel_id=1, source_target_pairs={{0,64},{1,65},{2,66},{3,67},{4,68},{5,69},{6,70},{7,71},{8,72},{9,... | collective-permute-start | bytes 1572872 | tf_op jit(solution)/shard_map/ppermute | solution.py:38
  203.7 1.8 copy-start.27
  205.5 1.3 copy-start.28
  212.9 22.5 %copy-start.16 = (f32[64,2048]{1,0:T(8,128)}, f32[64,2048]{1,0:T(8,128)S(1)}, u32[]{:S(2)}) copy-start(f32[64,2048]{1,0:T(8,128)S(1)} %get-tuple-element.110.refs_18_) | copy-start | bytes 1572868
  212.9 22.5 %copy-start.17 = (f32[64,2048]{1,0:T(8,128)}, f32[64,2048]{1,0:T(8,128)S(1)}, u32[]{:S(2)}) copy-start(f32[64,2048]{1,0:T(8,128)S(1)} %get-tuple-element.112.refs_21_) | copy-start | bytes 1572868
  212.9 21.9 %collective-permute-start.26 = (f32[192,2048]{1,0:T(8,128)}, f32[192,2048]{1,0:T(8,128)S(1)}, u32[]{:S(2)}, u32[]{:S(2)}) collective-permute-start(f32[192,2048]{1,0:T(8,128)} %get-tuple-element.107), channel_id=1, source_target_pairs={{0,6},{1,7},{2,4},{3,5},{4,2},{5,3},{6,0},{7,1},{8,14},{9,15},{10,... | collective-permute-start | bytes 4718600 | tf_op jit(solution)/shard_map/ppermute | solution.py:26
  214.7 20.6 %collective-permute-start.27 = (f32[192,2048]{1,0:T(8,128)}, f32[192,2048]{1,0:T(8,128)S(1)}, u32[]{:S(2)}, u32[]{:S(2)}) collective-permute-start(f32[192,2048]{1,0:T(8,128)} %get-tuple-element.109), channel_id=1, source_target_pairs={{0,2},{1,3},{2,0},{3,1},{4,6},{5,7},{6,4},{7,5},{8,10},{9,11},{10,... | collective-permute-start | bytes 4718600 | tf_op jit(solution)/shard_map/ppermute | solution.py:26
  234.9 9.3 %collective-permute-start.29 = (f32[64,2048]{1,0:T(8,128)S(1)}, f32[64,2048]{1,0:T(8,128)S(1)}, u32[]{:S(2)}, u32[]{:S(2)}) collective-permute-start(f32[64,2048]{1,0:T(8,128)S(1)} %slice_add_fusion.2), channel_id=1, source_target_pairs={{0,2},{1,3},{2,0},{3,1},{4,6},{5,7},{6,4},{7,5},{8,10},{9,11},{10,... | collective-permute-start | bytes 1572872 | tf_op jit(solution)/shard_map/ppermute | solution.py:26
  235.3 11.1 %copy-start.30 = (f32[192,2048]{1,0:T(8,128)}, f32[192,2048]{1,0:T(8,128)S(1)}, u32[]{:S(2)}) copy-start(f32[192,2048]{1,0:T(8,128)S(1)} %collective-permute-done.27.refs_17_.refs_19_) | copy-start | bytes 4718596
  236.0 10.4 %collective-permute-start.28 = (f32[64,2048]{1,0:T(8,128)S(1)}, f32[64,2048]{1,0:T(8,128)S(1)}, u32[]{:S(2)}, u32[]{:S(2)}) collective-permute-start(f32[64,2048]{1,0:T(8,128)S(1)} %slice_add_fusion.3), channel_id=1, source_target_pairs={{0,6},{1,7},{2,4},{3,5},{4,2},{5,3},{6,0},{7,1},{8,14},{9,15},{10,... | collective-permute-start | bytes 1572872 | tf_op jit(solution)/shard_map/ppermute | solution.py:26
  244.2 2.2 copy-start.35
  258.2 18.0 %copy-start.36 = (f32[64,2048]{1,0:T(8,128)S(1)}, f32[64,2048]{1,0:T(8,128)}, u32[]{:S(2)}) copy-start(f32[64,2048]{1,0:T(8,128)} %get-tuple-element.119) | copy-start | bytes 1572868
  258.2 15.1 %collective-permute-start.30 = (f32[128,2048]{1,0:T(8,128)}, f32[128,2048]{1,0:T(8,128)S(1)}, u32[]{:S(2)}, u32[]{:S(2)}) collective-permute-start(f32[128,2048]{1,0:T(8,128)} %get-tuple-element.115), channel_id=1, source_target_pairs={{0,8},{1,9},{2,10},{3,11},{4,12},{5,13},{6,14},{7,15},{8,0},{9,1},... | collective-permute-start | bytes 3145736 | tf_op jit(solution)/shard_map/ppermute | solution.py:26
  259.7 16.5 %collective-permute-start.32 = (f32[128,2048]{1,0:T(8,128)}, f32[128,2048]{1,0:T(8,128)S(1)}, u32[]{:S(2)}, u32[]{:S(2)}) collective-permute-start(f32[128,2048]{1,0:T(8,128)} %get-tuple-element.118), channel_id=1, source_target_pairs={{0,24},{1,25},{2,26},{3,27},{4,28},{5,29},{6,30},{7,31},{8,16},{9,... | collective-permute-start | bytes 3145736 | tf_op jit(solution)/shard_map/ppermute | solution.py:26
  273.3 12.2 %copy-start.20 = (f32[64,2048]{1,0:T(8,128)S(1)}, f32[64,2048]{1,0:T(8,128)}, u32[]{:S(2)}) copy-start(f32[64,2048]{1,0:T(8,128)} %get-tuple-element.114.kept_0) | copy-start | bytes 1572868
  273.3 12.2 %copy-start.21 = (f32[64,2048]{1,0:T(8,128)S(1)}, f32[64,2048]{1,0:T(8,128)}, u32[]{:S(2)}) copy-start(f32[64,2048]{1,0:T(8,128)} %get-tuple-element.117.kept_1) | copy-start | bytes 1572868
  274.5 10.5 %collective-permute-start.31 = (f32[64,2048]{1,0:T(8,128)S(1)}, f32[64,2048]{1,0:T(8,128)S(1)}, u32[]{:S(2)}, u32[]{:S(2)}) collective-permute-start(f32[64,2048]{1,0:T(8,128)S(1)} %slice_add_fusion.1), channel_id=1, source_target_pairs={{0,24},{1,25},{2,26},{3,27},{4,28},{5,29},{6,30},{7,31},{8,16},{9,... | collective-permute-start | bytes 1572872 | tf_op jit(solution)/shard_map/ppermute | solution.py:26
  276.3 9.3 %collective-permute-start.33 = (f32[64,2048]{1,0:T(8,128)S(1)}, f32[64,2048]{1,0:T(8,128)S(1)}, u32[]{:S(2)}, u32[]{:S(2)}) collective-permute-start(f32[64,2048]{1,0:T(8,128)S(1)} %slice_add_fusion), channel_id=1, source_target_pairs={{0,8},{1,9},{2,10},{3,11},{4,12},{5,13},{6,14},{7,15},{8,0},{9,1},... | collective-permute-start | bytes 1572872 | tf_op jit(solution)/shard_map/ppermute | solution.py:26
  285.5 5.0 %copy-start.19 = (f32[1,512,256]{2,1,0:T(8,128)S(1)}, f32[1,512,256]{2,1,0:T(8,128)}, u32[]{:S(2)}) copy-start(f32[1,512,256]{2,1,0:T(8,128)} %copy-done.18) | copy-start | bytes 1572868
  285.7 6.5 %collective-permute-start.34 = (f32[2,16,2048]{2,1,0:T(8,128)S(1)}, f32[2,16,2048]{2,1,0:T(8,128)S(1)}, u32[]{:S(2)}, u32[]{:S(2)}) collective-permute-start(f32[2,16,2048]{2,1,0:T(8,128)S(1)} %get-tuple-element.121), channel_id=1, source_target_pairs={{0,64},{1,65},{2,66},{3,67},{4,68},{5,69},{6,70},{7,71},{8,72},{9,... | collective-permute-start | bytes 786440 | tf_op jit(solution)/shard_map/ppermute | solution.py:26
  286.1 10.0 %collective-permute-start.35 = (f32[2,16,2048]{2,1,0:T(8,128)S(1)}, f32[2,16,2048]{2,1,0:T(8,128)S(1)}, u32[]{:S(2)}, u32[]{:S(2)}) collective-permute-start(f32[2,16,2048]{2,1,0:T(8,128)S(1)} %get-tuple-element.122), channel_id=1, source_target_pairs={{0,1},{1,0},{2,3},{3,2},{4,5},{5,4},{6,7},{7,6},{8,9},{9,8},{10,11... | collective-permute-start | bytes 786440 | tf_op jit(solution)/shard_map/ppermute | solution.py:26
  288.8 10.0 %collective-permute-start.36 = (f32[2,16,2048]{2,1,0:T(8,128)S(1)}, f32[2,16,2048]{2,1,0:T(8,128)S(1)}, u32[]{:S(2)}, u32[]{:S(2)}) collective-permute-start(f32[2,16,2048]{2,1,0:T(8,128)S(1)} %get-tuple-element.123), channel_id=1, source_target_pairs={{0,65},{1,64},{2,67},{3,66},{4,69},{5,68},{6,71},{7,70},{8,73},{9,... | collective-permute-start | bytes 786440 | tf_op jit(solution)/shard_map/ppermute | solution.py:26
  (12 other events, 11.4 us)

commit v5 on v4

v5 whole, which is shorter than its diff:
```python
import jax
import jax.numpy as jnp
from jax import lax
from jax.experimental import pallas as pl
from jax.experimental.pallas import tpu as pltpu
from jax.sharding import PartitionSpec as P

HEADS = 256
HEADDIM = 64
STATE = 256
GROUPS = 8
BLOCK = 128
ROWS = (16, 32, 16)
AXES = ("req", "head")
MIB = 1 << 20
VMEM = 60 * MIB


def swap(array, first=0, second=0, hi=0, lo=0, core=0):
    pairs = []
    for source in range(128):
        y, z = (second, first) if source >> 5 & 1 else (first, second)
        pairs.append((source, source ^ (lo << 6 | core << 5 | z << 3 | y << 1 | hi)))
    return lax.ppermute(array, AXES, pairs)


def cross(array):
    pairs = []
    for source in range(128):
        pairs.append((source, source ^ (64 | (source >> 5 & 1))))
    return lax.ppermute(array, AXES, pairs)


def place_in_mesh():
    req, head = lax.axis_index("req"), lax.axis_index("head")
    return head >> 3, head >> 1 & 3, head & 1, req >> 1, req & 1


def conv_rows(window, previous, rows, taps):
    window[0:8, :] = previous
    window[8 : 8 + BLOCK, :] = rows
    total = window[5 : 5 + BLOCK, :] * taps[0:1, :]
    for offset in range(1, 4):
        total = total + window[5 + offset : 5 + offset + BLOCK, :] * taps[offset : offset + 1, :]
    return total * (1.0 / (1.0 + jnp.exp(-total)))


def spread(columns, lane):
    pairs = []
    for pair in range(4):
        even = columns[:, 2 * pair : 2 * pair + 1]
        odd = columns[:, 2 * pair + 1 : 2 * pair + 2]
        pairs.append(jnp.where(lane < HEADDIM, even, odd))
    return jnp.concatenate(pairs, axis=1)


def scan_kernel(
    lengths,
    x_ref,
    b_ref,
    c_ref,
    x_tail,
    b_tail,
    c_tail,
    x_taps,
    b_taps,
    c_taps,
    dt_ref,
    rate_ref,
    skip_ref,
    y_ref,
    c_out,
    decay_out,
    state_out,
    x_window,
    b_window,
    c_window,
    x_last,
    b_last,
    c_last,
    state,
    passed,
):
    request, block = pl.program_id(0), pl.program_id(1)

    @pl.when(block == 0)
    def _():
        x_last[...] = x_tail[0]
        b_last[...] = b_tail[0]
        c_last[...] = c_tail[0]
        state[...] = jnp.zeros_like(state)
        passed[...] = jnp.zeros_like(passed)

    def convolve(window, last, ref, taps):
        rows = ref[0].astype(jnp.float32)
        made = conv_rows(window, last[...], rows, taps[...].astype(jnp.float32))
        last[...] = rows[BLOCK - 8 :]
        return made.astype(jnp.bfloat16)

    x = convolve(x_window, x_last, x_ref, x_taps)
    b = convolve(b_window, b_last, b_ref, b_taps)
    c = convolve(c_window, c_last, c_ref, c_taps)
    c_out[0] = c

    place = lax.broadcasted_iota(jnp.int32, (8, BLOCK), 1)
    raw = dt_ref[0]
    step = jnp.maximum(raw, 0.0) + jnp.log1p(jnp.exp(-jnp.abs(raw)))
    step = jnp.where(place + block * BLOCK < lengths[request], step, 0.0)
    decay = -jnp.exp(rate_ref[...]) * step
    reach = 1
    while reach < BLOCK:
        decay = decay + jnp.where(place >= reach, pltpu.roll(decay, reach, 1), 0.0)
        reach *= 2
    closing = decay[:, BLOCK - 1 : BLOCK]
    weight = jnp.exp(closing - decay) * step
    turned = jnp.transpose(
        jnp.concatenate(
            [decay, weight, passed[...] + decay, jnp.zeros((BLOCK - 24, BLOCK), jnp.float32)],
            axis=0,
        )
    )
    passed[...] = passed[...] + closing
    decay_out[0] = jnp.exp(turned[:, 16:24])

    lane = lax.broadcasted_iota(jnp.int32, (BLOCK, BLOCK), 1)
    causal = lax.broadcasted_iota(jnp.int32, (BLOCK, BLOCK), 0) >= lane
    scores = lax.dot_general(c, b, (((1,), (1,)), ((), ())), preferred_element_type=jnp.float32)
    scores = jnp.where(causal, scores, 0.0)
    within = []
    for pair in range(4):
        inputs = x[:, pair * 128 : (pair + 1) * 128]
        halves = []
        for head in (2 * pair, 2 * pair + 1):
            gap = jnp.where(causal, turned[:, head : head + 1] - decay[head : head + 1, :], 0.0)
            mixing = jnp.exp(gap) * scores * step[head : head + 1, :]
            halves.append(
                jnp.dot(mixing.astype(jnp.bfloat16), inputs, preferred_element_type=jnp.float32)
            )
        within.append(jnp.where(lane < HEADDIM, halves[0], halves[1]))
    carried = lax.dot_general(
        c,
        state[...].astype(jnp.bfloat16),
        (((1,), (1,)), ((), ())),
        preferred_element_type=jnp.float32,
    )
    wide = x.astype(jnp.float32)
    y_ref[0] = (
        jnp.concatenate(within, axis=1)
        + carried * spread(jnp.exp(turned[:, 0:8]), lane)
        + spread(skip_ref[...], lane) * wide
    )
    weighted = (wide * spread(turned[:, 8:16], lane)).astype(jnp.bfloat16)
    added = lax.dot_general(
        weighted, b, (((0,), (0,)), ((), ())), preferred_element_type=jnp.float32
    )
    factor = jnp.exp(closing)
    for head in range(8):
        rows = slice(head * HEADDIM, (head + 1) * HEADDIM)
        state[rows, :] = state[rows, :] * factor[head : head + 1, :] + added[rows, :]

    @pl.when(block == pl.num_programs(1) - 1)
    def _():
        state_out[0] = state[...]


def scan(lengths, x_input, bc_input, tails, conv_x, conv_bc, dt_raw, a_log, d_skip):
    requests, length, width = x_input.shape
    heads = dt_raw.shape[1]

    def group():
        return lax.axis_index("head") * heads >> 5

    def grouped(shift):
        return pl.BlockSpec((1, BLOCK, STATE), lambda r, i: (r, i, group() + shift))

    def table(shift):
        return pl.BlockSpec((4, STATE), lambda r, i: (0, group() + shift))

    def tail(columns, at):
        return pl.BlockSpec((1, 8, columns), lambda r, i: (r, 0, at))

    return pl.pallas_call(
        scan_kernel,
        grid=(requests, length // BLOCK),
        in_specs=[
            pl.BlockSpec(memory_space=pltpu.SMEM),
            pl.BlockSpec((1, BLOCK, width), lambda r, i: (r, i, 0)),
            grouped(0),
            grouped(GROUPS),
            tail(width, 0),
            tail(STATE, width // STATE),
            tail(STATE, width // STATE + 1),
            pl.BlockSpec((4, width), lambda r, i: (0, 0)),
            table(0),
            table(GROUPS),
            pl.BlockSpec((1, heads, BLOCK), lambda r, i: (r, 0, i)),
            pl.BlockSpec((heads, 1), lambda r, i: (0, 0)),
            pl.BlockSpec((1, heads), lambda r, i: (0, 0)),
        ],
        out_specs=[
            pl.BlockSpec((1, BLOCK, width), lambda r, i: (r, i, 0)),
            pl.BlockSpec((1, BLOCK, STATE), lambda r, i: (r, i, 0)),
            pl.BlockSpec((1, BLOCK, heads), lambda r, i: (r, i, 0)),
            pl.BlockSpec((1, width, STATE), lambda r, i: (r, 0, 0)),
        ],
        scratch_shapes=[
            pltpu.VMEM((8 + BLOCK, width), jnp.float32),
            pltpu.VMEM((8 + BLOCK, STATE), jnp.float32),
            pltpu.VMEM((8 + BLOCK, STATE), jnp.float32),
            pltpu.VMEM((8, width), jnp.float32),
            pltpu.VMEM((8, STATE), jnp.float32),
            pltpu.VMEM((8, STATE), jnp.float32),
            pltpu.VMEM((width, STATE), jnp.float32),
            pltpu.VMEM((heads, 1), jnp.float32),
        ],
        out_shape=[
            jax.ShapeDtypeStruct((requests, length, width), jnp.float32),
            jax.ShapeDtypeStruct((requests, length, STATE), jnp.bfloat16),
            jax.ShapeDtypeStruct((requests, length, heads), jnp.float32),
            jax.ShapeDtypeStruct((requests, width, STATE), jnp.float32),
        ],
        compiler_params=pltpu.CompilerParams(vmem_limit_bytes=VMEM),
        cost_estimate=pl.CostEstimate(
            flops=2 * requests * length * (8 * 128 * 128 + 2 * width * STATE + 128 * STATE),
            bytes_accessed=12 * MIB,
            transcendentals=4 * requests * length * width,
        ),
    )(
        lengths,
        x_input,
        bc_input,
        bc_input,
        tails,
        tails,
        tails,
        conv_x,
        conv_bc,
        conv_bc,
        dt_raw,
        a_log[:, None],
        d_skip[None, :],
    )


def outgoing_kernel(weight, outgoing, columns, semaphore):
    _, _, hi, lo, core = place_in_mesh()
    half = columns.shape[1]
    start = pl.multiple_of(((3 - 2 * hi - lo) * 2 + core) * half, half)
    copy = pltpu.make_async_copy(weight.at[:, pl.ds(start, half)], columns, semaphore)
    copy.start()
    copy.wait()
    outgoing[...] = columns[...].astype(jnp.float32)


def outgoing_weights(weight):
    half = weight.shape[1] // 8
    return pl.pallas_call(
        outgoing_kernel,
        in_specs=[pl.BlockSpec(memory_space=pl.ANY)],
        out_specs=pl.BlockSpec(memory_space=pltpu.VMEM),
        out_shape=jax.ShapeDtypeStruct((weight.shape[0], half), jnp.float32),
        scratch_shapes=[
            pltpu.VMEM((weight.shape[0], half), weight.dtype),
            pltpu.SemaphoreType.DMA,
        ],
        compiler_params=pltpu.CompilerParams(vmem_limit_bytes=VMEM),
        cost_estimate=pl.CostEstimate(flops=0, bytes_accessed=3 * MIB, transcendentals=0),
    )(weight)


def prepare_kernel(
    owner, slot, pool, tails, _, away_0, away_1, mine, chip, tail_away, tail_mine, tail_chip
):
    _, _, _, lo, core = place_in_mesh()
    me = 2 * lo + core
    for j in range(2):
        away = (away_0, away_1)[j]
        for device, state, tail in (
            (me ^ 1, away.at[0], tail_away.at[j, 0]),
            (me ^ 3, away.at[1], tail_away.at[j, 1]),
            (me ^ 2, chip.at[j], tail_chip.at[j]),
            (me, mine.at[j], tail_mine.at[j]),
        ):
            request = 2 * device + j
            here = owner[request] == me
            at = slot[request]
            state[...] = jnp.where(here, pool[at], 0.0)
            tail[...] = jnp.where(here, tails[at], 0.0)


def prepare(owner, slot, pool, tails, outgoing):
    _, width, state = pool.shape
    columns = tails.shape[2]
    vmem = pl.BlockSpec(memory_space=pltpu.VMEM)
    smem = pl.BlockSpec(memory_space=pltpu.SMEM)
    shapes = (
        (2, width, state),
        (2, width, state),
        (2, width, state),
        (2, width, state),
        (2, 2, 8, columns),
        (2, 8, columns),
        (2, 8, columns),
    )
    return pl.pallas_call(
        prepare_kernel,
        in_specs=[smem, smem, vmem, vmem, pl.BlockSpec(memory_space=pl.ANY)],
        out_specs=[vmem] * len(shapes),
        out_shape=[jax.ShapeDtypeStruct(s, jnp.float32) for s in shapes],
        compiler_params=pltpu.CompilerParams(vmem_limit_bytes=VMEM),
        cost_estimate=pl.CostEstimate(flops=0, bytes_accessed=7 * MIB, transcendentals=0),
    )(owner, slot, pool, tails, outgoing)


def gate_kernel(
    lengths, y_ref, c_ref, decay_ref, part_ref, z_ref, mine, near_0, near_1, far_0, far_1, *outs
):
    z_at, y_at, _, _, core = place_in_mesh()
    chunks, state_ref = outs[:3], outs[3]
    lane = lax.broadcasted_iota(jnp.int32, (BLOCK, BLOCK), 1)
    length = y_ref.shape[1]
    homes = (((0, 0), (1, 0)), ((1, 16), (2, 0)))
    for request, (near, far) in enumerate(((near_0, far_0), (near_1, far_1))):
        initial = mine[request] + near[0] + far[...]
        narrow = initial.astype(jnp.bfloat16)
        for block in range(length // BLOCK):
            rows = slice(block * BLOCK, (block + 1) * BLOCK)
            carried = lax.dot_general(
                c_ref[request, rows],
                narrow,
                (((1,), (1,)), ((), ())),
                preferred_element_type=jnp.float32,
            )
            y = y_ref[request, rows] + carried * spread(decay_ref[request, rows], lane)
            z = z_ref[request, rows].astype(jnp.float32)
            position = lax.broadcasted_iota(jnp.int32, y.shape, 0) + block * BLOCK
            gated = y * (z * (1.0 / (1.0 + jnp.exp(-z))))
            gated = jnp.where(position < lengths[request], gated, 0.0)
            gated = gated.astype(jnp.bfloat16).astype(jnp.float32)
            for at in range(4):
                z_far, y_far = block ^ z_at, at ^ y_at
                cell = jnp.where(core == 0, y_far * 4 + z_far, z_far * 4 + y_far)
                for part, (chunk, offset) in enumerate(homes[request]):
                    for hi in range(2):
                        start = at * 32 + hi * 16 + part * 8
                        target = pl.multiple_of(cell * ROWS[chunk] + offset + hi * 8, 8)
                        chunks[chunk][pl.ds(target, 8), :] = gated[start : start + 8]
        final = decay_ref[request, length - 8 :, :]
        for head in range(8):
            rows = slice(head * HEADDIM, (head + 1) * HEADDIM)
            state_ref[request, rows] = (
                part_ref[request, rows] + initial[rows] * final[7:8, head : head + 1]
            )


def gate(lengths, parts, z_gate, *states):
    y, c, decay, part = parts
    requests, length, width = y.shape
    vmem = pl.BlockSpec(memory_space=pltpu.VMEM)
    return pl.pallas_call(
        gate_kernel,
        in_specs=[pl.BlockSpec(memory_space=pltpu.SMEM)] + [vmem] * 10,
        out_specs=[vmem] * 4,
        out_shape=[jax.ShapeDtypeStruct((16 * rows, width), jnp.float32) for rows in ROWS]
        + [jax.ShapeDtypeStruct(part.shape, jnp.float32)],
        compiler_params=pltpu.CompilerParams(vmem_limit_bytes=VMEM),
        cost_estimate=pl.CostEstimate(
            flops=4 * length * width * STATE, bytes_accessed=12 * MIB, transcendentals=0
        ),
    )(lengths, y, c, decay, part, z_gate, *states)


def hold(array, *others):
    anywhere = pl.BlockSpec(memory_space=pl.ANY)

    def kernel(*refs):
        pass

    return pl.pallas_call(
        kernel,
        in_specs=[anywhere] * (1 + len(others)),
        out_specs=anywhere,
        out_shape=jax.ShapeDtypeStruct(array.shape, array.dtype),
        input_output_aliases={0: 0},
        compiler_params=pltpu.CompilerParams(vmem_limit_bytes=VMEM),
        cost_estimate=pl.CostEstimate(flops=0, bytes_accessed=0, transcendentals=0),
    )(array, *others)


def choose(near, far, *others):
    rows, columns = near.shape
    tile = pl.BlockSpec((rows, 128), lambda i: (0, i))

    def kernel(near_ref, far_ref, *refs):
        core = lax.axis_index("req") & 1
        refs[-1][...] = jnp.where(core == 0, far_ref[...], near_ref[...])

    return pl.pallas_call(
        kernel,
        grid=(columns // 128,),
        in_specs=[tile] * 2 + [pl.BlockSpec(memory_space=pl.ANY)] * len(others),
        out_specs=tile,
        out_shape=jax.ShapeDtypeStruct(near.shape, near.dtype),
        compiler_params=pltpu.CompilerParams(vmem_limit_bytes=VMEM),
        cost_estimate=pl.CostEstimate(flops=0, bytes_accessed=3 * MIB, transcendentals=0),
    )(near, far, *others)


ORDER = ((2, 1, 0, 3), (2, 3, 0, 1))
TILE = 512


SENT = ((2, 1), (2, 3))
KEPT = ((3, 0), (1, 0))


def product(blocks, majors, weight, w_far, others):
    depth = weight.shape[0]
    width = weight.shape[1] // 4
    rows = blocks[0].shape[0] // 16
    lines = 4 * rows
    tiles = width // (2 * TILE)
    opening = isinstance(w_far, tuple)
    join = majors is SENT
    heights = (2 * lines, 2 * lines) if join else (lines,) * 4

    def kernel(*refs):
        own, near, opposite, far, w_own_ref = refs[:5]
        outs, own_side, far_side = refs[-2 - opening - len(heights) : -2], refs[-2], refs[-1]
        step = pl.program_id(0)

        @pl.when(step == 0)
        def _():
            at = 0
            for side, (own_ref, far_ref) in enumerate(((own, opposite), (near, far))):
                for major in majors[side]:
                    span = slice(major * lines, (major + 1) * lines)
                    own_side[at : at + lines] = own_ref[span].astype(jnp.bfloat16)
                    far_side[at : at + lines] = far_ref[span].astype(jnp.bfloat16)
                    at += lines

        if opening:
            far_weight = outs[len(heights)]

            @pl.when(step < tiles)
            def _():
                far_weight[...] = refs[5][...].astype(jnp.bfloat16)

            @pl.when(step >= tiles)
            def _():
                far_weight[...] = refs[6][...].astype(jnp.bfloat16)
        else:
            far_weight = refs[5]

        total = jnp.dot(own_side[...], w_own_ref[...], preferred_element_type=jnp.float32)
        total += jnp.dot(far_side[...], far_weight[...], preferred_element_type=jnp.float32)
        for side in range(2):
            for which in range(2):
                ref = outs[side] if join else outs[2 * side + which]
                for at, minor in enumerate(ORDER[side]):
                    to = (join * which * 4 + at) * rows
                    start = (side * 2 + which) * lines + minor * rows
                    ref[to : to + rows, :] = total[start : start + rows]

    def own_columns(i):
        _, _, hi, lo, core = place_in_mesh()
        side = jnp.where(i < tiles, core, 1 - core)
        return (0, ((2 * hi + lo) * 2 + side) * tiles + jnp.where(i < tiles, i, i - tiles))

    def tile(rows):
        return pl.BlockSpec((rows, TILE), lambda i: (0, i))

    if opening:
        extra_specs = [
            pl.BlockSpec((depth, TILE), lambda i: (0, jnp.minimum(i, tiles - 1))),
            pl.BlockSpec((depth, TILE), lambda i: (0, jnp.maximum(i - tiles, 0))),
        ]
        extra = w_far
    else:
        extra_specs = [tile(depth)]
        extra = (w_far,)
    out_specs = [tile(h) for h in heights]
    out_shape = [jax.ShapeDtypeStruct((h, width), jnp.float32) for h in heights]
    if opening:
        out_specs.append(tile(depth))
        out_shape.append(jax.ShapeDtypeStruct((depth, width), jnp.bfloat16))
    return pl.pallas_call(
        kernel,
        grid=(2 * tiles,),
        in_specs=[pl.BlockSpec(b.shape, lambda i: (0, 0)) for b in blocks]
        + [pl.BlockSpec((depth, TILE), own_columns)]
        + extra_specs
        + [pl.BlockSpec(memory_space=pl.ANY)] * len(others),
        out_specs=out_specs,
        out_shape=out_shape,
        scratch_shapes=[pltpu.VMEM((4 * lines, depth), jnp.bfloat16)] * 2,
        compiler_params=pltpu.CompilerParams(vmem_limit_bytes=VMEM),
        cost_estimate=pl.CostEstimate(
            flops=16 * lines * depth * width,
            bytes_accessed=16 * lines * depth + 4 * depth * width + 16 * lines * width,
            transcendentals=0,
        ),
    )(*blocks, weight, *extra, *others)


def relay(one_b, three_a, got1, got3, *others):
    lines, columns = one_b.shape
    tile = pl.BlockSpec((lines, columns // 2), lambda i: (0, i))

    def kernel(*refs):
        one_ref, three_ref, got1_ref, got3_ref = refs[:4]
        refs[-2][...] = one_ref[...] + got3_ref[...]
        refs[-1][...] = three_ref[...] + got1_ref[...]

    return pl.pallas_call(
        kernel,
        grid=(2,),
        in_specs=[tile] * 4 + [pl.BlockSpec(memory_space=pl.ANY)] * len(others),
        out_specs=[tile] * 2,
        out_shape=[jax.ShapeDtypeStruct((lines, columns), jnp.float32)] * 2,
        compiler_params=pltpu.CompilerParams(vmem_limit_bytes=VMEM),
        cost_estimate=pl.CostEstimate(
            flops=0, bytes_accessed=24 * lines * columns, transcendentals=0
        ),
    )(one_b, three_a, got1, got3, *others)


def combine(chunks, *others):
    operands, specs, heights = [], [], []
    for chunk in chunks:
        lines, columns = chunk[0].shape
        heights.append(lines // 4)
        for place, array in enumerate(chunk):
            operands.append(array)
            specs.append(pl.BlockSpec((lines, TILE), lambda i, at=place % 3 == 1: (int(at), i)))
    total = sum(heights)

    def kernel(*refs):
        first, third, one_b, three_a, zero_a, zero_b = refs[-6:]
        here = 0
        for chunk, rows in enumerate(heights):
            kept_a, got_a, back_a, kept_b, got_b, back_b = refs[6 * chunk : 6 * chunk + 6]
            sum_a = kept_a[...] + got_a[...] + back_a[...]
            sum_b = kept_b[...] + got_b[...] + back_b[...]
            for ref, summed, minor, start in (
                (first, sum_a, 0, here),
                (first, sum_a, 1, total + here),
                (zero_a, sum_a, 2, here),
                (three_a, sum_a, 3, here),
                (third, sum_b, 0, here),
                (third, sum_b, 1, total + here),
                (zero_b, sum_b, 2, here),
                (one_b, sum_b, 3, here),
            ):
                ref[start : start + rows] = summed[minor * rows : (minor + 1) * rows]
            here += rows

    made = (2 * total, 2 * total, total, total, total, total)
    return pl.pallas_call(
        kernel,
        grid=(columns // TILE,),
        in_specs=specs + [pl.BlockSpec(memory_space=pl.ANY)] * len(others),
        out_specs=[pl.BlockSpec((h, TILE), lambda i: (0, i)) for h in made],
        out_shape=[jax.ShapeDtypeStruct((h, columns), jnp.float32) for h in made],
        compiler_params=pltpu.CompilerParams(vmem_limit_bytes=VMEM),
        cost_estimate=pl.CostEstimate(
            flops=0, bytes_accessed=128 * total * columns, transcendentals=0
        ),
    )(*operands, *others)


def finish_kernel(*refs):
    hi = lax.axis_index("head") & 1
    outs = refs[12:]
    for side in range(2):
        for way in range(2):
            to = 0
            for part in range(2):
                kept, got, back = refs[6 * part + 3 * side : 6 * part + 3 * side + 3]
                lines = kept.shape[0]
                for block in range(lines // 16):
                    row = pl.multiple_of(block * 16 + (hi ^ way) * 8, 8)
                    later = pl.multiple_of(lines + row, 8)
                    outs[2 * way + side][to : to + 8, :] = (
                        kept[pl.ds(row, 8), :] + got[pl.ds(later, 8), :] + back[pl.ds(row, 8), :]
                    )
                    to += 8


def finish(*terms):
    columns = terms[0].shape[1]
    vmem = pl.BlockSpec(memory_space=pltpu.VMEM)
    return pl.pallas_call(
        finish_kernel,
        in_specs=[vmem] * 12,
        out_specs=[vmem] * 4,
        out_shape=[jax.ShapeDtypeStruct((32, columns), jnp.float32)] * 4,
        compiler_params=pltpu.CompilerParams(vmem_limit_bytes=VMEM),
        cost_estimate=pl.CostEstimate(flops=0, bytes_accessed=4 * MIB, transcendentals=0),
    )(*terms)


def assemble_kernel(own, near, across, far, mixed):
    _, _, hi, lo, core = place_in_mesh()
    half = own.shape[1] // 2
    for flip, source in enumerate((own, near, across, far)):
        place = (2 * hi + lo) ^ flip
        for side in range(2):
            start = pl.multiple_of((place * 2 + (side ^ core)) * half, half)
            for request in range(2):
                mixed[request, :, pl.ds(start, half)] = source[
                    request * 16 : request * 16 + 16, side * half : (side + 1) * half
                ]


def assemble(pieces):
    rows, columns = pieces[0].shape
    vmem = pl.BlockSpec(memory_space=pltpu.VMEM)
    return pl.pallas_call(
        assemble_kernel,
        in_specs=[vmem] * 4,
        out_specs=vmem,
        out_shape=jax.ShapeDtypeStruct((2, rows // 2, 4 * columns), jnp.float32),
        compiler_params=pltpu.CompilerParams(vmem_limit_bytes=VMEM),
        cost_estimate=pl.CostEstimate(flops=0, bytes_accessed=2 * MIB, transcendentals=0),
    )(*pieces)


def project(gated, out_weight, w_near):
    def ring(own):
        return (own, swap(own, lo=1), swap(own, hi=1, lo=1))

    def first_round(parts, axis):
        return (swap(parts[0], **{axis: 1}), swap(parts[1], **{axis: 3}))

    def second_round(parts, got, axis, *others):
        sent = relay(parts[2], parts[3], *got, *others)
        return (swap(sent[0], **{axis: 1}), swap(sent[1], **{axis: 3})), sent[0]

    def multiply(blocks, w_far, *others):
        sent = product(blocks, SENT, out_weight, w_far, others)
        w_far = sent[2] if isinstance(w_far, tuple) else w_far
        three_a, zero_a, one_b, zero_b = product(blocks, KEPT, out_weight, w_far, (sent[0],))
        return (sent[0], sent[1], one_b, three_a, zero_a, zero_b), w_far

    def terms(parts, got, back):
        return (parts[4], got[0], back[1], parts[5], got[1], back[0])

    own, near, far = ring(gated[0])
    chosen = choose(near, far)
    w_near = hold(w_near, chosen)
    w_far = (w_near, swap(w_near, core=1))
    opposite = cross(chosen)
    blocks = (own, near, opposite, far)
    own, near, far = ring(hold(gated[1], opposite))
    parts_0, w_far = multiply(blocks, w_far)
    got_0 = first_round(parts_0, "first")

    chosen = choose(near, far, parts_0[4])
    opposite = cross(chosen)
    blocks = (own, near, opposite, far)
    back_0, token = second_round(parts_0, got_0, "first", chosen)
    own, near, far = ring(hold(gated[2], opposite, token))
    parts_1, _ = multiply(blocks, w_far, back_0[0], back_0[1])
    got_1 = first_round(parts_1, "first")

    chosen = choose(near, far, parts_1[4])
    blocks = (own, near, cross(chosen), far)
    back_1, token = second_round(parts_1, got_1, "first", chosen)
    parts_2, _ = multiply(blocks, w_far, token)
    got_2 = first_round(parts_2, "first")

    later_a = combine([terms(parts_0, got_0, back_0), terms(parts_1, got_1, back_1)], parts_2[4])
    over_a = first_round(later_a, "second")
    back_2, token = second_round(parts_2, got_2, "first", later_a[4])
    last_a, token = second_round(later_a, over_a, "second", token)
    later_b = combine([terms(parts_2, got_2, back_2)], token)
    over_b = first_round(later_b, "second")
    last_b, _ = second_round(later_b, over_b, "second")
    kept_0, kept_1, away_0, away_1 = finish(
        *terms(later_a, over_a, last_a), *terms(later_b, over_b, last_b)
    )
    return assemble(
        (kept_0, swap(kept_1, lo=1), swap(away_0, hi=1), swap(away_1, hi=1, lo=1))
    )


def on_device(
    x_input,
    z_gate,
    bc_input,
    dt_raw,
    a_log,
    d_skip,
    conv_x,
    conv_bc,
    out_weight,
    pool_state,
    pool_xtail,
    pool_bctail,
    pool_dev,
    pool_slot,
    lengths,
):
    outgoing = outgoing_weights(out_weight)
    w_near = swap(outgoing, hi=1, lo=1)
    group = lax.axis_index("head").astype(jnp.uint32) * a_log.shape[0] >> 5
    bc_tail = pool_bctail.reshape(pool_bctail.shape[:2] + (2, GROUPS, STATE))
    bc_tail = lax.dynamic_index_in_dim(bc_tail, group, 3, keepdims=False)
    tails = jnp.concatenate([pool_xtail, bc_tail.reshape(bc_tail.shape[:2] + (2 * STATE,))], axis=-1)
    tails = jnp.pad(tails.astype(jnp.float32), ((0, 0), (5, 0), (0, 0)))
    away_0, away_1, mine, chip, tail_away, tail_mine, tail_chip = prepare(
        pool_dev.reshape(-1), pool_slot, pool_state, tails, outgoing
    )
    tail_near = swap(tail_away, core=1)
    near_0 = swap(away_0, core=1)
    near_1 = swap(away_1, core=1)
    tail_far = swap(tail_chip + tail_near[:, 1], lo=1)
    chip = hold(chip, tail_far)
    tail_rows = tail_mine + tail_near[:, 0] + tail_far
    far_0 = swap(chip[0] + near_0[1], lo=1)
    far_1 = swap(chip[1] + near_1[1], lo=1)
    parts = scan(
        lengths, x_input, bc_input, tail_rows, conv_x, conv_bc, dt_raw, a_log, d_skip
    )
    *gated, final_state = gate(lengths, parts, z_gate, mine, near_0, near_1, far_0, far_1)
    mixed_out = project(gated, out_weight, w_near)
    return (mixed_out, final_state)


def solution(mesh):
    return jax.shard_map(
        on_device,
        mesh=mesh,
        in_specs=(
            P("req", None, "head"),
            P("req", None, "head"),
            P("req", None, None),
            P("req", "head", None),
            P("head"),
            P("head"),
            P(None, "head"),
            P(),
            P("head", None),
            P("req", "head", None),
            P("req", None, "head"),
            P("req", None, None),
            P(),
            P(),
            P("req"),
        ),
        out_specs=(P("req", "head", None), P("req", "head", None)),
        check_vma=False,
    )
```

time: 301 us -> 271 us (0.900)
  waiting for transfers between devices: 169 us -> 93.9 us
  Pallas kernels: 64.4 us -> 106 us
    ppermute x33 -> x37, waiting for transfers between devices: 142 us -> 76.9 us  [swap(): return lax.ppermute(array, AXES, pairs)]
    pallas_call x5 -> x17, Pallas kernels: 19.5 us -> 46.3 us  [the longest x5 11.9 us: relay(): pl.pallas_call(kernel, grid=(2,), in_specs=[tile] * 4 + [pl.BlockSpec(mem...]
    pallas_call x4 -> x6, Pallas kernels: 26 us -> 38.8 us  [product(): pl.pallas_call(kernel, grid=(2 * tiles,), in_specs=[pl.BlockSpec(b.shape,...]
    ppermute x4 -> x3, waiting for transfers between devices: 26.8 us -> 17 us  [cross(): return lax.ppermute(array, AXES, pairs)]
    ppermute x33 -> x37, starting transfers between devices: 41.8 us -> 45.3 us  [swap(): return lax.ppermute(array, AXES, pairs)]
    unnamed x79 -> x77, local copies, waits for them, and re-layouts: 13.8 us -> 14.2 us
  transfers between devices with their start and end apart: 37 -> 40, of which waited for: 22 -> 25; matrix products, arithmetic and copies ran while one was open for 2% -> 2% of each run, Pallas kernels for 10% -> 31%
where the time goes in v5:
time: 271 us; the launch traced here: 269 us
  Pallas kernels  106 us (39%)
  waiting for transfers between devices  93.9 us (35%)
  starting transfers between devices  46.3 us (17%)
  local copies, waits for them, and re-layouts  16.8 us (6%)
  other arithmetic  5.04 us (2%)
    ppermute x37, waiting for transfers between devices, swap(): return lax.ppermute(array, AXES, pairs)  76.9 us
    ppermute x37, starting transfers between devices, swap(): return lax.ppermute(array, AXES, pairs)  45.3 us
    pallas_call x6, Pallas kernels, product(): pl.pallas_call(kernel, grid=(2 * tiles,), in_specs=[pl.BlockSpec(b.shape,...  38.8 us
    ppermute x3, waiting for transfers between devices, cross(): return lax.ppermute(array, AXES, pairs)  17 us
    pallas_call x1, Pallas kernels, scan(): pl.pallas_call(scan_kernel, grid=(requests, length // BLOCK), in_specs=[p...  16.4 us
    unnamed x77, local copies, waits for them, and re-layouts  14.2 us
    pallas_call x5, Pallas kernels, relay(): pl.pallas_call(kernel, grid=(2,), in_specs=[tile] * 4 + [pl.BlockSpec(mem...  11.9 us
    pallas_call x3, Pallas kernels, choose(): pl.pallas_call(kernel, grid=(columns // 128,), in_specs=[tile] * 2 + [pl....  10.3 us
  transfers between devices with their start and end apart: 40, of which 25 were waited for; matrix products, arithmetic and copies ran while one was open for 2% of the time, Pallas kernels for 31%

profile of v5, /device:TPU:0, one launch (start us, length us, event | category | flops | bytes accessed | tf_op | source)
XLA Modules:
  0.0 269.4 jit_solution(1380476757401479895)
XLA Ops:
  2.4 2.7 shard_map.158._
  5.8 4.1 %shard_map.159 = (f32[2,512,256]{2,1,0:T(8,128)}, f32[2,512,256]{2,1,0:T(8,128)}, f32[2,512,256]{2,1,0:T(8,128)}, f32[2,512,256]{2,1,0:T(8,128)}, f32[2,2,8,1024...) custom-call(s32[8]{0:T(128)} %bitcast.21, s32[8]{0:T(128)} %slot.1, f32[4,512,256]{2,1,0:T(8,128)} %pool.1, ...), custom_call_target="tpu_custom_call" | custom-call | bytes 7340032 | tf_op jit(solution)/shard_map/pallas_call | solution.py:305
  10.4 2.8 %collective-permute-start.9 = (f32[512,1024]{1,0:T(8,128)S(1)}, f32[512,1024]{1,0:T(8,128)}, u32[]{:S(2)}, u32[]{:S(2)}) collective-permute-start(f32[512,1024]{1,0:T(8,128)S(1)} %copy-done.3), channel_id=1, source_target_pairs={{0,65},{1,64},{2,67},{3,66},{4,69},{5,68},{6,71},{7,70},{8,73},{9,... | collective-permute-start | bytes 6291464 | tf_op jit(solution)/shard_map/ppermute | solution.py:24
  14.3 1.3 collective-permute-done
  16.8 4.0 %collective-permute-done.1.refs_1_ = f32[2,8,1024]{2,1,0:T(8,128)S(1)} collective-permute-done((f32[2,8,1024]{2,1,0:T(8,128)S(1)}, f32[2,8,1024]{2,1,0:T(8,128)S(1)}, u32[]{:S(2)}, u32[]{:S(2)}) %collective-permute-start.1) | collective-permute-done | bytes 65568 | tf_op jit(solution)/shard_map/ppermute | solution.py:24
  21.5 2.9 %fusion = (f32[512,256]{1,0:T(8,128)}, f32[512,256]{1,0:T(8,128)}) fusion(f32[2,512,256]{2,1,0:T(8,128)} %collective-permute-done.3.near_1, f32[2,512,256]{2,1,0:T(8,128)} %shard_map.161, f32[2,512,256]{2,1,0:T(8,128)S(1)} %collective-permute-done.2.near_0), kind=kLoop, calls=%fused_computation.1 | loop fusion | flops 262144 | bytes 3145728 | tf_op jit(solution)/shard_map/add | solution.py:722
  24.6 1.8 collective-permute-start.4
  27.7 16.4 %shard_map.160 = (f32[2,512,512]{2,1,0:T(8,128)}, bf16[2,512,256]{2,1,0:T(8,128)(2,1)}, f32[2,512,8]{2,1,0:T(8,128)}, f32[2,512,256]{2,1,0:T(8,128)}) custom-call(s32[2]{0:T(128)} %lengths.3, bf16[2,512,512]{2,1,0:T(8,128)(2,1)} %x_ref.1, bf16[2,512,4096]{2,1,0:T(8,128)(2,1)} %c_ref.1, bf16[2,512,4096]{2,1,0:T(8,128)(2,1)} %c_ref.1, ...), custom_call_target="tpu_custom_call" | custom-call | flops 872415232 | bytes 12582912 | tf_op jit(solution)/shard_map/pallas_call | solution.py:182
  44.1 5.0 %collective-permute-done.4.far_0 = f32[512,256]{1,0:T(8,128)} collective-permute-done((f32[512,256]{1,0:T(8,128)}, f32[512,256]{1,0:T(8,128)}, u32[]{:S(2)}, u32[]{:S(2)}) %collective-permute-start.4) | collective-permute-done | bytes 524320 | tf_op jit(solution)/shard_map/ppermute | solution.py:24
  49.1 6.9 %shard_map.162 = (f32[256,512]{1,0:T(8,128)}, f32[512,512]{1,0:T(8,128)}, f32[256,512]{1,0:T(8,128)}, f32[2,512,256]{2,1,0:T(8,128)}) custom-call(s32[2]{0:T(128)} %lengths.3, f32[2,512,512]{2,1,0:T(8,128)} %get-tuple-element.65.y_ref, bf16[2,512,256]{2,1,0:T(8,128)(2,1)} %get-tuple-element.66.c_ref, f32[2,512,8]{2,1,0:T(8,128)} %get-tuple-element.67.decay_ref, ...), custom_call_target="tpu_custom_call" | custom-call | flops 268435456 | bytes 12582912 | tf_op jit(solution)/shard_map/pallas_call | solution.py:360
  56.0 1.5 collective-permute-start.7
  57.7 12.7 %collective-permute-done.7.far_ref.refs_3_ = f32[256,512]{1,0:T(8,128)S(1)} collective-permute-done((f32[256,512]{1,0:T(8,128)}, f32[256,512]{1,0:T(8,128)S(1)}, u32[]{:S(2)}, u32[]{:S(2)}) %collective-permute-start.7) | collective-permute-done | bytes 524320 | tf_op jit(solution)/shard_map/ppermute | solution.py:24
  72.1 3.3 %shard_map.163.refs_1_ = f32[256,512]{1,0:T(8,128)} custom-call(f32[256,512]{1,0:T(8,128)} %copy-done.6, f32[256,512]{1,0:T(8,128)} %copy-done.5), custom_call_target="tpu_custom_call" | custom-call | bytes 3145728 | tf_op jit(solution)/shard_map/pallas_call | solution.py:398
  76.8 8.8 %collective-permute-done.8.refs_2_.refs_1_ = f32[256,512]{1,0:T(8,128)S(1)} collective-permute-done((f32[256,512]{1,0:T(8,128)S(1)}, f32[256,512]{1,0:T(8,128)S(1)}, u32[]{:S(2)}, u32[]{:S(2)}) %collective-permute-start.8) | collective-permute-done | bytes 524320 | tf_op jit(solution)/shard_map/ppermute | solution.py:31
  86.4 2.8 %collective-permute-start.14 = (f32[512,512]{1,0:T(8,128)}, f32[512,512]{1,0:T(8,128)S(1)}, u32[]{:S(2)}, u32[]{:S(2)}) collective-permute-start(f32[512,512]{1,0:T(8,128)} %shard_map.167.refs_0_), channel_id=1, source_target_pairs={{0,65},{1,64},{2,67},{3,66},{4,69},{5,68},{6,71},{7,70},{8,73},{9,... | collective-permute-start | bytes 3145736 | tf_op jit(solution)/shard_map/ppermute | solution.py:24
  89.3 7.2 %shard_map.165 = (f32[128,2048]{1,0:T(8,128)}, f32[128,2048]{1,0:T(8,128)}, bf16[512,2048]{1,0:T(8,128)(2,1)}) custom-call(f32[256,512]{1,0:T(8,128)} %get-tuple-element.73.refs_0_, f32[256,512]{1,0:T(8,128)} %copy-done.6, f32[256,512]{1,0:T(8,128)} %copy-done.7, f32[256,512]{1,0:T(8,128)} %copy-done.5, bf16[512,8192]{1,0:T(8,128)(2,1)} %refs_4_.11, ...), custom_call_target="tpu_custom_call" | custom-call | flops 1073741824 | bytes 6815744 | tf_op jit(solution)/shard_map/pallas_call | solution.py:487
  96.4 3.0 %collective-permute-start.12 = (f32[128,2048]{1,0:T(8,128)}, f32[128,2048]{1,0:T(8,128)S(1)}, u32[]{:S(2)}, u32[]{:S(2)}) collective-permute-start(f32[128,2048]{1,0:T(8,128)} %get-tuple-element.79), channel_id=1, source_target_pairs={{0,6},{1,7},{2,4},{3,5},{4,2},{5,3},{6,0},{7,1},{8,14},{9,15},{10,... | collective-permute-start | bytes 3145736 | tf_op jit(solution)/shard_map/ppermute | solution.py:24
  99.6 5.7 %shard_map.166 = (f32[64,2048]{1,0:T(8,128)}, f32[64,2048]{1,0:T(8,128)}, f32[64,2048]{1,0:T(8,128)}, f32[64,2048]{1,0:T(8,128)}) custom-call(f32[256,512]{1,0:T(8,128)} %get-tuple-element.73.refs_0_, f32[256,512]{1,0:T(8,128)} %copy-done.6, f32[256,512]{1,0:T(8,128)} %copy-done.7, f32[256,512]{1,0:T(8,128)} %copy-done.5, bf16[512,8192]{1,0:T(8,128)(2,1)} %refs_4_.11, ...), custom_call_target="tpu_custom_call" | custom-call | flops 1073741824 | bytes 6815744 | tf_op jit(solution)/shard_map/pallas_call | solution.py:487
  105.3 7.2 %collective-permute-done.14.far_ref.refs_3_ = f32[512,512]{1,0:T(8,128)S(1)} collective-permute-done((f32[512,512]{1,0:T(8,128)}, f32[512,512]{1,0:T(8,128)S(1)}, u32[]{:S(2)}, u32[]{:S(2)}) %collective-permute-start.14) | collective-permute-done | bytes 1048608 | tf_op jit(solution)/shard_map/ppermute | solution.py:24
  112.5 1.3 collective-permute-done.13.near_ref.refs_1_
  113.9 1.0 copy-done.1
  114.8 3.6 %shard_map.168.refs_4_ = f32[512,512]{1,0:T(8,128)} custom-call(f32[512,512]{1,0:T(8,128)} %copy-done.1, f32[512,512]{1,0:T(8,128)} %copy-done, f32[64,2048]{1,0:T(8,128)} %get-tuple-element.76.refs_0_), custom_call_target="tpu_custom_call" | custom-call | bytes 3145728 | tf_op jit(solution)/shard_map/pallas_call | solution.py:398
  118.8 1.0 copy-done.10
  119.8 2.4 shard_map.169
  122.1 3.0 %collective-permute-start.15 = (f32[64,2048]{1,0:T(8,128)}, f32[64,2048]{1,0:T(8,128)S(1)}, u32[]{:S(2)}, u32[]{:S(2)}) collective-permute-start(f32[64,2048]{1,0:T(8,128)} %get-tuple-element.81), channel_id=1, source_target_pairs={{0,6},{1,7},{2,4},{3,5},{4,2},{5,3},{6,0},{7,1},{8,14},{9,15},{10,... | collective-permute-start | bytes 1572872 | tf_op jit(solution)/shard_map/ppermute | solution.py:24
  125.3 8.2 %collective-permute-done.17.refs_2_.refs_1_ = f32[512,512]{1,0:T(8,128)S(1)} collective-permute-done((f32[512,512]{1,0:T(8,128)}, f32[512,512]{1,0:T(8,128)S(1)}, u32[]{:S(2)}, u32[]{:S(2)}) %collective-permute-start.17) | collective-permute-done | bytes 1048608 | tf_op jit(solution)/shard_map/ppermute | solution.py:31
  133.5 1.0 collective-permute-done.16.refs_6_.refs_5_
  135.4 7.4 %shard_map.170 = (f32[256,2048]{1,0:T(8,128)}, f32[256,2048]{1,0:T(8,128)}) custom-call(f32[512,512]{1,0:T(8,128)} %shard_map.167.refs_0_, f32[512,512]{1,0:T(8,128)} %copy-done.1, f32[512,512]{1,0:T(8,128)} %copy-done.2, f32[512,512]{1,0:T(8,128)} %copy-done, bf16[512,8192]{1,0:T(8,128)(2,1)} %refs_4_.11, bf16[512,2048]{1,0:T(8,128)(2,1)} %get-tuple-element.74.refs_5_, ...), custom_call_target="tpu_custom_call" | custom-call | flops 2147483648 | bytes 9437184 | tf_op jit(solution)/shard_map/pallas_call | solution.py:487
  142.8 3.0 %collective-permute-start.19 = (f32[256,2048]{1,0:T(8,128)}, f32[256,2048]{1,0:T(8,128)S(1)}, u32[]{:S(2)}, u32[]{:S(2)}) collective-permute-start(f32[256,2048]{1,0:T(8,128)} %get-tuple-element.88), channel_id=1, source_target_pairs={{0,6},{1,7},{2,4},{3,5},{4,2},{5,3},{6,0},{7,1},{8,14},{9,15},{10,... | collective-permute-start | bytes 6291464 | tf_op jit(solution)/shard_map/ppermute | solution.py:24
  146.0 1.8 collective-permute-start.21
  147.8 7.3 %shard_map.171 = (f32[128,2048]{1,0:T(8,128)}, f32[128,2048]{1,0:T(8,128)}, f32[128,2048]{1,0:T(8,128)}, f32[128,2048]{1,0:T(8,128)}) custom-call(f32[512,512]{1,0:T(8,128)} %shard_map.167.refs_0_, f32[512,512]{1,0:T(8,128)} %copy-done.1, f32[512,512]{1,0:T(8,128)} %copy-done.2, f32[512,512]{1,0:T(8,128)} %copy-done, bf16[512,8192]{1,0:T(8,128)(2,1)} %refs_4_.11, ...), custom_call_target="tpu_custom_call" | custom-call | flops 2147483648 | bytes 9437184 | tf_op jit(solution)/shard_map/pallas_call | solution.py:487
  155.1 5.6 %collective-permute-done.21.far_ref.refs_3_ = f32[256,512]{1,0:T(8,128)S(1)} collective-permute-done((f32[256,512]{1,0:T(8,128)}, f32[256,512]{1,0:T(8,128)S(1)}, u32[]{:S(2)}, u32[]{:S(2)}) %collective-permute-start.21) | collective-permute-done | bytes 524320 | tf_op jit(solution)/shard_map/ppermute | solution.py:24
  162.0 3.4 %shard_map.173.refs_4_ = f32[256,512]{1,0:T(8,128)} custom-call(f32[256,512]{1,0:T(8,128)} %copy-done.9, f32[256,512]{1,0:T(8,128)} %copy-done.8, f32[128,2048]{1,0:T(8,128)} %get-tuple-element.85.refs_0_.refs_6_), custom_call_target="tpu_custom_call" | custom-call | bytes 3145728 | tf_op jit(solution)/shard_map/pallas_call | solution.py:398
  165.7 4.6 %collective-permute-done.19.refs_3_.refs_10_ = f32[256,2048]{1,0:T(8,128)S(1)} collective-permute-done((f32[256,2048]{1,0:T(8,128)}, f32[256,2048]{1,0:T(8,128)S(1)}, u32[]{:S(2)}, u32[]{:S(2)}) %collective-permute-start.19) | collective-permute-done | bytes 2097184 | tf_op jit(solution)/shard_map/ppermute | solution.py:24
  170.3 1.9 collective-permute-done.18.refs_2_.refs_7_
  172.2 3.2 %shard_map.174 = (f32[128,2048]{1,0:T(8,128)}, f32[128,2048]{1,0:T(8,128)}) custom-call(f32[128,2048]{1,0:T(8,128)} %get-tuple-element.86.refs_0_, f32[128,2048]{1,0:T(8,128)} %get-tuple-element.87.refs_1_, f32[256,2048]{1,0:T(8,128)} %collective-permute-done.18.refs_2_.refs_7_, f32[256,2048]{1,0:T(8,128)} %copy-done.4, f32[256,512]{1,0:T(8,128)} %shard_map.173.refs_4_), custom_call_target="tpu_custom_call" | custom-call | bytes 6291456 | tf_op jit(solution)/shard_map/pallas_call | solution.py:515
  175.4 2.4 collective-permute-start.22
  178.7 5.6 %shard_map.175 = (f32[128,2048]{1,0:T(8,128)}, f32[128,2048]{1,0:T(8,128)}) custom-call(f32[256,512]{1,0:T(8,128)} %shard_map.172.refs_0_, f32[256,512]{1,0:T(8,128)} %copy-done.9, f32[256,512]{1,0:T(8,128)} %copy-done.19, f32[256,512]{1,0:T(8,128)} %copy-done.8, bf16[512,8192]{1,0:T(8,128)(2,1)} %refs_4_.11, bf16[512,2048]{1,0:T(8,128)(2,1)} %get-tuple-element.74.refs_5_, ...), custom_call_target="tpu_custom_call" | custom-call | flops 1073741824 | bytes 6815744 | tf_op jit(solution)/shard_map/pallas_call | solution.py:487
  185.1 1.4 collective-permute-start.27
  186.5 5.6 %shard_map.176 = (f32[64,2048]{1,0:T(8,128)}, f32[64,2048]{1,0:T(8,128)}, f32[64,2048]{1,0:T(8,128)}, f32[64,2048]{1,0:T(8,128)}) custom-call(f32[256,512]{1,0:T(8,128)} %shard_map.172.refs_0_, f32[256,512]{1,0:T(8,128)} %copy-done.9, f32[256,512]{1,0:T(8,128)} %copy-done.19, f32[256,512]{1,0:T(8,128)} %copy-done.8, bf16[512,8192]{1,0:T(8,128)(2,1)} %refs_4_.11, ...), custom_call_target="tpu_custom_call" | custom-call | flops 1073741824 | bytes 6815744 | tf_op jit(solution)/shard_map/pallas_call | solution.py:487
  193.1 5.9 %shard_map.177 = (f32[96,2048]{1,0:T(8,128)}, f32[96,2048]{1,0:T(8,128)}, f32[48,2048]{1,0:T(8,128)}, f32[48,2048]{1,0:T(8,128)}, f32[48,2048]{1,0:T(8,128)}, /*index=5*/f32[48,2048]{1,0:T(8,128)}) custom-call(f32[64,2048]{1,0:T(8,128)} %get-tuple-element.76.refs_0_, f32[128,2048]{1,0:T(8,128)} %collective-permute-done.11.refs_2_.refs_1_, ...), custom_call_target="tpu_custom_call" | custom-call | bytes 12582912 | tf_op jit(solution)/shard_map/pallas_call | solution.py:559
  199.0 2.0 collective-permute-start.25
  201.0 2.5 collective-permute-start.26
  203.9 4.3 %collective-permute-done.27.refs_2_.refs_1_ = f32[128,2048]{1,0:T(8,128)S(1)} collective-permute-done((f32[128,2048]{1,0:T(8,128)}, f32[128,2048]{1,0:T(8,128)S(1)}, u32[]{:S(2)}, u32[]{:S(2)}) %collective-permute-start.27) | collective-permute-done | bytes 1048608 | tf_op jit(solution)/shard_map/ppermute | solution.py:24
  208.2 1.0 copy-done.12
  209.2 2.4 shard_map.178
  211.6 2.3 collective-permute-done.25.refs_2_.refs_1_
  213.9 5.4 %collective-permute-done.26.refs_3_.refs_4_ = f32[96,2048]{1,0:T(8,128)S(1)} collective-permute-done((f32[96,2048]{1,0:T(8,128)}, f32[96,2048]{1,0:T(8,128)S(1)}, u32[]{:S(2)}, u32[]{:S(2)}) %collective-permute-start.26) | collective-permute-done | bytes 786464 | tf_op jit(solution)/shard_map/ppermute | solution.py:24
  220.2 2.2 shard_map.179
  223.4 4.0 %shard_map.180 = (f32[32,2048]{1,0:T(8,128)}, f32[32,2048]{1,0:T(8,128)}, f32[16,2048]{1,0:T(8,128)}, f32[16,2048]{1,0:T(8,128)}, f32[16,2048]{1,0:T(8,128)}, /*index=5*/f32[16,2048]{1,0:T(8,128)}) custom-call(f32[64,2048]{1,0:T(8,128)} %get-tuple-element.94.refs_12_.refs_0_, f32[128,2048]{1,0:T(8,128)} %copy-done.12, f32[64,2048]{1,0:T(8,128)} %copy-done.23, ...), custom_call_target="tpu_custom_call" | custom-call | bytes 4194304 | tf_op jit(solution)/shard_map/pallas_call | solution.py:559
  227.4 3.1 %collective-permute-start.33 = (f32[32,2048]{1,0:T(8,128)}, f32[32,2048]{1,0:T(8,128)S(1)}, u32[]{:S(2)}, u32[]{:S(2)}) collective-permute-start(f32[32,2048]{1,0:T(8,128)} %get-tuple-element.110), channel_id=1, source_target_pairs={{0,8},{1,9},{2,10},{3,11},{4,12},{5,13},{6,14},{7,15},{8,0},{9,1},... | collective-permute-start | bytes 786440 | tf_op jit(solution)/shard_map/ppermute | solution.py:24
  230.5 2.5 collective-permute-start.34
  235.1 3.2 %collective-permute-done.34.refs_3_.refs_10_ = f32[32,2048]{1,0:T(8,128)S(1)} collective-permute-done((f32[32,2048]{1,0:T(8,128)}, f32[32,2048]{1,0:T(8,128)S(1)}, u32[]{:S(2)}, u32[]{:S(2)}) %collective-permute-start.34) | collective-permute-done | bytes 262176 | tf_op jit(solution)/shard_map/ppermute | solution.py:24
  239.0 1.7 shard_map.181
  240.7 2.5 collective-permute-start.35
  243.4 3.7 %collective-permute-done.35.refs_8_ = f32[16,2048]{1,0:T(8,128)S(1)} collective-permute-done((f32[16,2048]{1,0:T(8,128)}, f32[16,2048]{1,0:T(8,128)S(1)}, u32[]{:S(2)}, u32[]{:S(2)}) %collective-permute-start.35) | collective-permute-done | bytes 131104 | tf_op jit(solution)/shard_map/ppermute | solution.py:24
  247.1 1.3 collective-permute-done.36.refs_11_
  249.1 3.2 %shard_map.182 = (f32[32,2048]{1,0:T(8,128)}, f32[32,2048]{1,0:T(8,128)}, f32[32,2048]{1,0:T(8,128)}, f32[32,2048]{1,0:T(8,128)}) custom-call(f32[48,2048]{1,0:T(8,128)} %get-tuple-element.95.refs_4_.refs_0_, f32[96,2048]{1,0:T(8,128)} %copy-done.13, f32[48,2048]{1,0:T(8,128)} %copy-done.26, f32[48,2048]{1,0:T(8,128)} %get-tuple-element.105.refs_3_, ...), custom_call_target="tpu_custom_call" | custom-call | bytes 4194304 | tf_op jit(solution)/shard_map/pallas_call | solution.py:593
  252.4 1.8 collective-permute-start.37
  254.2 2.2 collective-permute-start.38
  257.1 1.9 collective-permute-done.37.near
  259.0 4.8 %collective-permute-done.38.across = f32[32,2048]{1,0:T(8,128)S(1)} collective-permute-done((f32[32,2048]{1,0:T(8,128)}, f32[32,2048]{1,0:T(8,128)S(1)}, u32[]{:S(2)}, u32[]{:S(2)}) %collective-permute-start.38) | collective-permute-done | bytes 262176 | tf_op jit(solution)/shard_map/ppermute | solution.py:24
  263.7 2.7 %collective-permute-done.39.far = f32[32,2048]{1,0:T(8,128)S(1)} collective-permute-done((f32[32,2048]{1,0:T(8,128)}, f32[32,2048]{1,0:T(8,128)S(1)}, u32[]{:S(2)}, u32[]{:S(2)}) %collective-permute-start.39) | collective-permute-done | bytes 262176 | tf_op jit(solution)/shard_map/ppermute | solution.py:24
  267.2 2.2 shard_map.183
  (129 shorter events, 24.4 us)
Async XLA Ops:
  5.8 4.6 %copy-start.3 = (f32[512,1024]{1,0:T(8,128)S(1)}, f32[512,1024]{1,0:T(8,128)}, u32[]{:S(2)}) copy-start(f32[512,1024]{1,0:T(8,128)} %shard_map.158._) | copy-start | bytes 6291460
  9.9 11.5 %collective-permute-start.2 = (f32[2,512,256]{2,1,0:T(8,128)}, f32[2,512,256]{2,1,0:T(8,128)S(1)}, u32[]{:S(2)}, u32[]{:S(2)}) collective-permute-start(f32[2,512,256]{2,1,0:T(8,128)} %get-tuple-element.70), channel_id=1, source_target_pairs={{0,32},{1,33},{2,34},{3,35},{4,36},{5,37},{6,38},{7,39},{8,40},{9,... | collective-permute-start | bytes 3145736 | tf_op jit(solution)/shard_map/ppermute | solution.py:24
  9.9 11.5 %collective-permute-start.3 = (f32[2,512,256]{2,1,0:T(8,128)}, f32[2,512,256]{2,1,0:T(8,128)}, u32[]{:S(2)}, u32[]{:S(2)}) collective-permute-start(f32[2,512,256]{2,1,0:T(8,128)} %get-tuple-element.71), channel_id=1, source_target_pairs={{0,32},{1,33},{2,34},{3,35},{4,36},{5,37},{6,38},{7,39},{8,40},{9,... | collective-permute-start | bytes 3145736 | tf_op jit(solution)/shard_map/ppermute | solution.py:24
  10.4 65.0 %collective-permute-start.9 = (f32[512,1024]{1,0:T(8,128)S(1)}, f32[512,1024]{1,0:T(8,128)}, u32[]{:S(2)}, u32[]{:S(2)}) collective-permute-start(f32[512,1024]{1,0:T(8,128)S(1)} %copy-done.3), channel_id=1, source_target_pairs={{0,65},{1,64},{2,67},{3,66},{4,69},{5,68},{6,71},{7,70},{8,73},{9,... | collective-permute-start | bytes 6291464 | tf_op jit(solution)/shard_map/ppermute | solution.py:24
  14.2 1.4 collective-permute-start
  16.5 4.3 %collective-permute-start.1 = (f32[2,8,1024]{2,1,0:T(8,128)S(1)}, f32[2,8,1024]{2,1,0:T(8,128)S(1)}, u32[]{:S(2)}, u32[]{:S(2)}) collective-permute-start(f32[2,8,1024]{2,1,0:T(8,128)S(1)} %fusion.6), channel_id=1, source_target_pairs={{0,64},{1,65},{2,66},{3,67},{4,68},{5,69},{6,70},{7,71},{8,72},{9,... | collective-permute-start | bytes 196616 | tf_op jit(solution)/shard_map/ppermute | solution.py:24
  21.4 4.9 %copy-start.36 = (f32[8]{0:T(128)S(1)}, f32[8]{0:T(128)}, u32[]{:S(2)}) copy-start(f32[8]{0:T(128)} %param.19) | copy-start | bytes 100
  21.4 5.6 %copy-start.29 = (f32[2,8,1024]{2,1,0:T(8,128)S(1)}, f32[2,8,1024]{2,1,0:T(8,128)}, u32[]{:S(2)}) copy-start(f32[2,8,1024]{2,1,0:T(8,128)} %copy-done.28) | copy-start | bytes 196612
  21.4 5.6 %copy-start.35 = (f32[2,8,1024]{2,1,0:T(8,128)S(1)}, f32[2,8,1024]{2,1,0:T(8,128)}, u32[]{:S(2)}) copy-start(f32[2,8,1024]{2,1,0:T(8,128)} %get-tuple-element.62) | copy-start | bytes 196612
  21.4 22.6 %copy-start.15 = (f32[2,512,256]{2,1,0:T(8,128)}, f32[2,512,256]{2,1,0:T(8,128)S(1)}, u32[]{:S(2)}) copy-start(f32[2,512,256]{2,1,0:T(8,128)S(1)} %collective-permute-done.2.near_0) | copy-start | bytes 3145732
  24.3 19.7 %collective-permute-start.5 = (f32[512,256]{1,0:T(8,128)}, f32[512,256]{1,0:T(8,128)}, u32[]{:S(2)}, u32[]{:S(2)}) collective-permute-start(f32[512,256]{1,0:T(8,128)} %get-tuple-element.122), channel_id=1, source_target_pairs={{0,64},{1,65},{2,66},{3,67},{4,68},{5,69},{6,70},{7,71},{8,72},{9,... | collective-permute-start | bytes 1572872 | tf_op jit(solution)/shard_map/ppermute | solution.py:24
  24.6 24.6 %collective-permute-start.4 = (f32[512,256]{1,0:T(8,128)}, f32[512,256]{1,0:T(8,128)}, u32[]{:S(2)}, u32[]{:S(2)}) collective-permute-start(f32[512,256]{1,0:T(8,128)} %get-tuple-element.123), channel_id=1, source_target_pairs={{0,64},{1,65},{2,66},{3,67},{4,68},{5,69},{6,70},{7,71},{8,72},{9,... | collective-permute-start | bytes 1572872 | tf_op jit(solution)/shard_map/ppermute | solution.py:24
  56.0 14.4 %collective-permute-start.7 = (f32[256,512]{1,0:T(8,128)}, f32[256,512]{1,0:T(8,128)S(1)}, u32[]{:S(2)}, u32[]{:S(2)}) collective-permute-start(f32[256,512]{1,0:T(8,128)} %get-tuple-element.73.refs_0_), channel_id=1, source_target_pairs={{0,65},{1,64},{2,67},{3,66},{4,69},{5,68},{6,71},{7,70},{8,73},{9,... | collective-permute-start | bytes 1572872 | tf_op jit(solution)/shard_map/ppermute | solution.py:24
  57.5 13.0 %collective-permute-start.6 = (f32[256,512]{1,0:T(8,128)}, f32[256,512]{1,0:T(8,128)S(1)}, u32[]{:S(2)}, u32[]{:S(2)}) collective-permute-start(f32[256,512]{1,0:T(8,128)} %get-tuple-element.73.refs_0_), channel_id=1, source_target_pairs={{0,64},{1,65},{2,66},{3,67},{4,68},{5,69},{6,70},{7,71},{8,72},{9,... | collective-permute-start | bytes 1572872 | tf_op jit(solution)/shard_map/ppermute | solution.py:24
  75.4 1.0 copy-start.18
  75.4 13.9 %collective-permute-start.10 = (f32[512,1024]{1,0:T(8,128)}, f32[512,1024]{1,0:T(8,128)}, u32[]{:S(2)}, u32[]{:S(2)}) collective-permute-start(f32[512,1024]{1,0:T(8,128)} %shard_map.164.refs_5_), channel_id=1, source_target_pairs={{0,32},{1,33},{2,34},{3,35},{4,36},{5,37},{6,38},{7,39},{8,40},{9,... | collective-permute-start | bytes 6291464 | tf_op jit(solution)/shard_map/ppermute | solution.py:24
  76.4 9.2 %collective-permute-start.8 = (f32[256,512]{1,0:T(8,128)S(1)}, f32[256,512]{1,0:T(8,128)S(1)}, u32[]{:S(2)}, u32[]{:S(2)}) collective-permute-start(f32[256,512]{1,0:T(8,128)S(1)} %copy-done.18), channel_id=1, source_target_pairs={{0,64},{1,65},{2,66},{3,67},{4,68},{5,69},{6,70},{7,71},{8,72},{9,... | collective-permute-start | bytes 1572872 | tf_op jit(solution)/shard_map/ppermute | solution.py:31
  86.4 26.1 %collective-permute-start.14 = (f32[512,512]{1,0:T(8,128)}, f32[512,512]{1,0:T(8,128)S(1)}, u32[]{:S(2)}, u32[]{:S(2)}) collective-permute-start(f32[512,512]{1,0:T(8,128)} %shard_map.167.refs_0_), channel_id=1, source_target_pairs={{0,65},{1,64},{2,67},{3,66},{4,69},{5,68},{6,71},{7,70},{8,73},{9,... | collective-permute-start | bytes 3145736 | tf_op jit(solution)/shard_map/ppermute | solution.py:24
  89.2 24.6 %collective-permute-start.13 = (f32[512,512]{1,0:T(8,128)}, f32[512,512]{1,0:T(8,128)S(1)}, u32[]{:S(2)}, u32[]{:S(2)}) collective-permute-start(f32[512,512]{1,0:T(8,128)} %shard_map.167.refs_0_), channel_id=1, source_target_pairs={{0,64},{1,65},{2,66},{3,67},{4,68},{5,69},{6,70},{7,71},{8,72},{9,... | collective-permute-start | bytes 3145736 | tf_op jit(solution)/shard_map/ppermute | solution.py:24
  96.4 22.4 %collective-permute-start.12 = (f32[128,2048]{1,0:T(8,128)}, f32[128,2048]{1,0:T(8,128)S(1)}, u32[]{:S(2)}, u32[]{:S(2)}) collective-permute-start(f32[128,2048]{1,0:T(8,128)} %get-tuple-element.79), channel_id=1, source_target_pairs={{0,6},{1,7},{2,4},{3,5},{4,2},{5,3},{6,0},{7,1},{8,14},{9,15},{10,... | collective-permute-start | bytes 3145736 | tf_op jit(solution)/shard_map/ppermute | solution.py:24
  99.4 19.4 %collective-permute-start.11 = (f32[128,2048]{1,0:T(8,128)}, f32[128,2048]{1,0:T(8,128)}, u32[]{:S(2)}, u32[]{:S(2)}) collective-permute-start(f32[128,2048]{1,0:T(8,128)} %get-tuple-element.75.refs_6_), channel_id=1, source_target_pairs={{0,2},{1,3},{2,0},{3,1},{4,6},{5,7},{6,4},{7,5},{8,10},{9,11},{10,... | collective-permute-start | bytes 3145736 | tf_op jit(solution)/shard_map/ppermute | solution.py:24
  112.5 1.4 copy-start
  113.9 1.0 copy-start.1
  118.5 15.0 %collective-permute-start.17 = (f32[512,512]{1,0:T(8,128)}, f32[512,512]{1,0:T(8,128)S(1)}, u32[]{:S(2)}, u32[]{:S(2)}) collective-permute-start(f32[512,512]{1,0:T(8,128)} %shard_map.168.refs_4_), channel_id=1, source_target_pairs={{0,64},{1,65},{2,66},{3,67},{4,68},{5,69},{6,70},{7,71},{8,72},{9,... | collective-permute-start | bytes 3145736 | tf_op jit(solution)/shard_map/ppermute | solution.py:31
  118.8 1.0 copy-start.10
  122.1 11.4 %collective-permute-start.15 = (f32[64,2048]{1,0:T(8,128)}, f32[64,2048]{1,0:T(8,128)S(1)}, u32[]{:S(2)}, u32[]{:S(2)}) collective-permute-start(f32[64,2048]{1,0:T(8,128)} %get-tuple-element.81), channel_id=1, source_target_pairs={{0,6},{1,7},{2,4},{3,5},{4,2},{5,3},{6,0},{7,1},{8,14},{9,15},{10,... | collective-permute-start | bytes 1572872 | tf_op jit(solution)/shard_map/ppermute | solution.py:24
  125.1 9.4 %collective-permute-start.16 = (f32[64,2048]{1,0:T(8,128)}, f32[64,2048]{1,0:T(8,128)S(1)}, u32[]{:S(2)}, u32[]{:S(2)}) collective-permute-start(f32[64,2048]{1,0:T(8,128)} %get-tuple-element.83.refs_2_), channel_id=1, source_target_pairs={{0,2},{1,3},{2,0},{3,1},{4,6},{5,7},{6,4},{7,5},{8,10},{9,11},{10,... | collective-permute-start | bytes 1572872 | tf_op jit(solution)/shard_map/ppermute | solution.py:24
  133.5 1.0 copy-start.2
  133.5 1.1 copy-start.16
  142.8 27.5 %collective-permute-start.19 = (f32[256,2048]{1,0:T(8,128)}, f32[256,2048]{1,0:T(8,128)S(1)}, u32[]{:S(2)}, u32[]{:S(2)}) collective-permute-start(f32[256,2048]{1,0:T(8,128)} %get-tuple-element.88), channel_id=1, source_target_pairs={{0,6},{1,7},{2,4},{3,5},{4,2},{5,3},{6,0},{7,1},{8,14},{9,15},{10,... | collective-permute-start | bytes 6291464 | tf_op jit(solution)/shard_map/ppermute | solution.py:24
  145.8 26.4 %collective-permute-start.18 = (f32[256,2048]{1,0:T(8,128)}, f32[256,2048]{1,0:T(8,128)}, u32[]{:S(2)}, u32[]{:S(2)}) collective-permute-start(f32[256,2048]{1,0:T(8,128)} %get-tuple-element.84.refs_6_), channel_id=1, source_target_pairs={{0,2},{1,3},{2,0},{3,1},{4,6},{5,7},{6,4},{7,5},{8,10},{9,11},{10,... | collective-permute-start | bytes 6291464 | tf_op jit(solution)/shard_map/ppermute | solution.py:24
  146.0 14.7 %collective-permute-start.21 = (f32[256,512]{1,0:T(8,128)}, f32[256,512]{1,0:T(8,128)S(1)}, u32[]{:S(2)}, u32[]{:S(2)}) collective-permute-start(f32[256,512]{1,0:T(8,128)} %shard_map.172.refs_0_), channel_id=1, source_target_pairs={{0,65},{1,64},{2,67},{3,66},{4,69},{5,68},{6,71},{7,70},{8,73},{9,... | collective-permute-start | bytes 1572872 | tf_op jit(solution)/shard_map/ppermute | solution.py:24
  147.8 13.4 %collective-permute-start.20 = (f32[256,512]{1,0:T(8,128)}, f32[256,512]{1,0:T(8,128)S(1)}, u32[]{:S(2)}, u32[]{:S(2)}) collective-permute-start(f32[256,512]{1,0:T(8,128)} %shard_map.172.refs_0_), channel_id=1, source_target_pairs={{0,64},{1,65},{2,66},{3,67},{4,68},{5,69},{6,70},{7,71},{8,72},{9,... | collective-permute-start | bytes 1572872 | tf_op jit(solution)/shard_map/ppermute | solution.py:24
  165.4 12.5 %collective-permute-start.24 = (f32[256,512]{1,0:T(8,128)}, f32[256,512]{1,0:T(8,128)S(1)}, u32[]{:S(2)}, u32[]{:S(2)}) collective-permute-start(f32[256,512]{1,0:T(8,128)} %shard_map.173.refs_4_), channel_id=1, source_target_pairs={{0,64},{1,65},{2,66},{3,67},{4,68},{5,69},{6,70},{7,71},{8,72},{9,... | collective-permute-start | bytes 1572872 | tf_op jit(solution)/shard_map/ppermute | solution.py:31
  170.3 1.9 copy-start.4
  175.4 16.7 %collective-permute-start.22 = (f32[128,2048]{1,0:T(8,128)}, f32[128,2048]{1,0:T(8,128)S(1)}, u32[]{:S(2)}, u32[]{:S(2)}) collective-permute-start(f32[128,2048]{1,0:T(8,128)} %get-tuple-element.90), channel_id=1, source_target_pairs={{0,6},{1,7},{2,4},{3,5},{4,2},{5,3},{6,0},{7,1},{8,14},{9,15},{10,... | collective-permute-start | bytes 3145736 | tf_op jit(solution)/shard_map/ppermute | solution.py:24
  177.8 15.1 %collective-permute-start.23 = (f32[128,2048]{1,0:T(8,128)}, f32[128,2048]{1,0:T(8,128)}, u32[]{:S(2)}, u32[]{:S(2)}) collective-permute-start(f32[128,2048]{1,0:T(8,128)} %get-tuple-element.92.refs_6_), channel_id=1, source_target_pairs={{0,2},{1,3},{2,0},{3,1},{4,6},{5,7},{6,4},{7,5},{8,10},{9,11},{10,... | collective-permute-start | bytes 3145736 | tf_op jit(solution)/shard_map/ppermute | solution.py:24
  184.3 19.6 %collective-permute-start.28 = (f32[128,2048]{1,0:T(8,128)}, f32[128,2048]{1,0:T(8,128)S(1)}, u32[]{:S(2)}, u32[]{:S(2)}) collective-permute-start(f32[128,2048]{1,0:T(8,128)} %get-tuple-element.102), channel_id=1, source_target_pairs={{0,6},{1,7},{2,4},{3,5},{4,2},{5,3},{6,0},{7,1},{8,14},{9,15},{10,... | collective-permute-start | bytes 3145736 | tf_op jit(solution)/shard_map/ppermute | solution.py:24
  185.1 23.1 %collective-permute-start.27 = (f32[128,2048]{1,0:T(8,128)}, f32[128,2048]{1,0:T(8,128)S(1)}, u32[]{:S(2)}, u32[]{:S(2)}) collective-permute-start(f32[128,2048]{1,0:T(8,128)} %get-tuple-element.93.refs_6_), channel_id=1, source_target_pairs={{0,2},{1,3},{2,0},{3,1},{4,6},{5,7},{6,4},{7,5},{8,10},{9,11},{10,... | collective-permute-start | bytes 3145736 | tf_op jit(solution)/shard_map/ppermute | solution.py:24
  192.1 1.0 copy-start.20
  199.0 14.9 %collective-permute-start.25 = (f32[96,2048]{1,0:T(8,128)}, f32[96,2048]{1,0:T(8,128)S(1)}, u32[]{:S(2)}, u32[]{:S(2)}) collective-permute-start(f32[96,2048]{1,0:T(8,128)} %get-tuple-element.96), channel_id=1, source_target_pairs={{0,8},{1,9},{2,10},{3,11},{4,12},{5,13},{6,14},{7,15},{8,0},{9,1},... | collective-permute-start | bytes 2359304 | tf_op jit(solution)/shard_map/ppermute | solution.py:24
  201.0 18.4 %collective-permute-start.26 = (f32[96,2048]{1,0:T(8,128)}, f32[96,2048]{1,0:T(8,128)S(1)}, u32[]{:S(2)}, u32[]{:S(2)}) collective-permute-start(f32[96,2048]{1,0:T(8,128)} %get-tuple-element.99), channel_id=1, source_target_pairs={{0,24},{1,25},{2,26},{3,27},{4,28},{5,29},{6,30},{7,31},{8,16},{9,... | collective-permute-start | bytes 2359304 | tf_op jit(solution)/shard_map/ppermute | solution.py:24
  203.9 4.3 %copy-start.11 = (f32[128,2048]{1,0:T(8,128)}, f32[128,2048]{1,0:T(8,128)S(1)}, u32[]{:S(2)}) copy-start(f32[128,2048]{1,0:T(8,128)S(1)} %collective-permute-done.28.refs_3_.refs_4_) | copy-start | bytes 3145732
  208.2 1.0 copy-start.12
  211.5 10.9 %collective-permute-start.31 = (f32[64,2048]{1,0:T(8,128)}, f32[64,2048]{1,0:T(8,128)S(1)}, u32[]{:S(2)}, u32[]{:S(2)}) collective-permute-start(f32[64,2048]{1,0:T(8,128)} %get-tuple-element.107), channel_id=1, source_target_pairs={{0,6},{1,7},{2,4},{3,5},{4,2},{5,3},{6,0},{7,1},{8,14},{9,15},{10,... | collective-permute-start | bytes 1572872 | tf_op jit(solution)/shard_map/ppermute | solution.py:24
  211.5 11.0 %collective-permute-start.32 = (f32[64,2048]{1,0:T(8,128)}, f32[64,2048]{1,0:T(8,128)S(1)}, u32[]{:S(2)}, u32[]{:S(2)}) collective-permute-start(f32[64,2048]{1,0:T(8,128)} %get-tuple-element.103.refs_4_), channel_id=1, source_target_pairs={{0,2},{1,3},{2,0},{3,1},{4,6},{5,7},{6,4},{7,5},{8,10},{9,11},{10,... | collective-permute-start | bytes 1572872 | tf_op jit(solution)/shard_map/ppermute | solution.py:24
  213.9 5.4 %copy-start.13 = (f32[96,2048]{1,0:T(8,128)}, f32[96,2048]{1,0:T(8,128)S(1)}, u32[]{:S(2)}) copy-start(f32[96,2048]{1,0:T(8,128)S(1)} %collective-permute-done.25.refs_2_.refs_1_) | copy-start | bytes 2359300
  223.4 9.6 %copy-start.37 = (f32[48,2048]{1,0:T(8,128)S(1)}, f32[48,2048]{1,0:T(8,128)}, u32[]{:S(2)}) copy-start(f32[48,2048]{1,0:T(8,128)} %get-tuple-element.104) | copy-start | bytes 1179652
  223.4 10.3 %copy-start.25 = (f32[48,2048]{1,0:T(8,128)S(1)}, f32[48,2048]{1,0:T(8,128)}, u32[]{:S(2)}) copy-start(f32[48,2048]{1,0:T(8,128)} %get-tuple-element.106.refs_6_) | copy-start | bytes 1179652
  227.4 7.7 %collective-permute-start.33 = (f32[32,2048]{1,0:T(8,128)}, f32[32,2048]{1,0:T(8,128)S(1)}, u32[]{:S(2)}, u32[]{:S(2)}) collective-permute-start(f32[32,2048]{1,0:T(8,128)} %get-tuple-element.110), channel_id=1, source_target_pairs={{0,8},{1,9},{2,10},{3,11},{4,12},{5,13},{6,14},{7,15},{8,0},{9,1},... | collective-permute-start | bytes 786440 | tf_op jit(solution)/shard_map/ppermute | solution.py:24
  230.5 7.8 %collective-permute-start.34 = (f32[32,2048]{1,0:T(8,128)}, f32[32,2048]{1,0:T(8,128)S(1)}, u32[]{:S(2)}, u32[]{:S(2)}) collective-permute-start(f32[32,2048]{1,0:T(8,128)} %get-tuple-element.113), channel_id=1, source_target_pairs={{0,24},{1,25},{2,26},{3,27},{4,28},{5,29},{6,30},{7,31},{8,16},{9,... | collective-permute-start | bytes 786440 | tf_op jit(solution)/shard_map/ppermute | solution.py:24
  233.1 10.3 %collective-permute-start.29 = (f32[48,2048]{1,0:T(8,128)S(1)}, f32[48,2048]{1,0:T(8,128)S(1)}, u32[]{:S(2)}, u32[]{:S(2)}) collective-permute-start(f32[48,2048]{1,0:T(8,128)S(1)} %copy-done.37), channel_id=1, source_target_pairs={{0,24},{1,25},{2,26},{3,27},{4,28},{5,29},{6,30},{7,31},{8,16},{9,... | collective-permute-start | bytes 1179656 | tf_op jit(solution)/shard_map/ppermute | solution.py:24
  233.8 9.6 %collective-permute-start.30 = (f32[48,2048]{1,0:T(8,128)S(1)}, f32[48,2048]{1,0:T(8,128)S(1)}, u32[]{:S(2)}, u32[]{:S(2)}) collective-permute-start(f32[48,2048]{1,0:T(8,128)S(1)} %copy-done.25), channel_id=1, source_target_pairs={{0,8},{1,9},{2,10},{3,11},{4,12},{5,13},{6,14},{7,15},{8,0},{9,1},... | collective-permute-start | bytes 1179656 | tf_op jit(solution)/shard_map/ppermute | solution.py:24
  235.1 3.2 %copy-start.21 = (f32[32,2048]{1,0:T(8,128)}, f32[32,2048]{1,0:T(8,128)S(1)}, u32[]{:S(2)}) copy-start(f32[32,2048]{1,0:T(8,128)S(1)} %collective-permute-done.33.refs_2_.refs_7_) | copy-start | bytes 786436
  240.7 6.4 %collective-permute-start.35 = (f32[16,2048]{1,0:T(8,128)}, f32[16,2048]{1,0:T(8,128)S(1)}, u32[]{:S(2)}, u32[]{:S(2)}) collective-permute-start(f32[16,2048]{1,0:T(8,128)} %get-tuple-element.114), channel_id=1, source_target_pairs={{0,24},{1,25},{2,26},{3,27},{4,28},{5,29},{6,30},{7,31},{8,16},{9,... | collective-permute-start | bytes 393224 | tf_op jit(solution)/shard_map/ppermute | solution.py:24
  243.3 5.2 %collective-permute-start.36 = (f32[16,2048]{1,0:T(8,128)}, f32[16,2048]{1,0:T(8,128)S(1)}, u32[]{:S(2)}, u32[]{:S(2)}) collective-permute-start(f32[16,2048]{1,0:T(8,128)} %get-tuple-element.116), channel_id=1, source_target_pairs={{0,8},{1,9},{2,10},{3,11},{4,12},{5,13},{6,14},{7,15},{8,0},{9,1},... | collective-permute-start | bytes 393224 | tf_op jit(solution)/shard_map/ppermute | solution.py:24
  243.4 5.1 %copy-start.26 = (f32[48,2048]{1,0:T(8,128)}, f32[48,2048]{1,0:T(8,128)S(1)}, u32[]{:S(2)}) copy-start(f32[48,2048]{1,0:T(8,128)S(1)} %collective-permute-done.29.refs_2_) | copy-start | bytes 1179652
  243.4 5.1 %copy-start.27 = (f32[48,2048]{1,0:T(8,128)}, f32[48,2048]{1,0:T(8,128)S(1)}, u32[]{:S(2)}) copy-start(f32[48,2048]{1,0:T(8,128)S(1)} %collective-permute-done.30.refs_5_) | copy-start | bytes 1179652
  247.1 1.3 copy-start.33
  252.4 6.6 %collective-permute-start.37 = (f32[32,2048]{1,0:T(8,128)}, f32[32,2048]{1,0:T(8,128)S(1)}, u32[]{:S(2)}, u32[]{:S(2)}) collective-permute-start(f32[32,2048]{1,0:T(8,128)} %get-tuple-element.118), channel_id=1, source_target_pairs={{0,64},{1,65},{2,66},{3,67},{4,68},{5,69},{6,70},{7,71},{8,72},{9,... | collective-permute-start | bytes 786440 | tf_op jit(solution)/shard_map/ppermute | solution.py:24
  254.2 9.6 %collective-permute-start.38 = (f32[32,2048]{1,0:T(8,128)}, f32[32,2048]{1,0:T(8,128)S(1)}, u32[]{:S(2)}, u32[]{:S(2)}) collective-permute-start(f32[32,2048]{1,0:T(8,128)} %get-tuple-element.119), channel_id=1, source_target_pairs={{0,1},{1,0},{2,3},{3,2},{4,5},{5,4},{6,7},{7,6},{8,9},{9,8},{10,11... | collective-permute-start | bytes 786440 | tf_op jit(solution)/shard_map/ppermute | solution.py:24
  256.4 10.1 %collective-permute-start.39 = (f32[32,2048]{1,0:T(8,128)}, f32[32,2048]{1,0:T(8,128)S(1)}, u32[]{:S(2)}, u32[]{:S(2)}) collective-permute-start(f32[32,2048]{1,0:T(8,128)} %get-tuple-element.120), channel_id=1, source_target_pairs={{0,65},{1,64},{2,67},{3,66},{4,69},{5,68},{6,71},{7,70},{8,73},{9,... | collective-permute-start | bytes 786440 | tf_op jit(solution)/shard_map/ppermute | solution.py:24
  258.9 7.5 %copy-start.30 = (f32[32,2048]{1,0:T(8,128)}, f32[32,2048]{1,0:T(8,128)S(1)}, u32[]{:S(2)}) copy-start(f32[32,2048]{1,0:T(8,128)S(1)} %collective-permute-done.37.near) | copy-start | bytes 786436
  263.7 2.7 %copy-start.31 = (f32[32,2048]{1,0:T(8,128)}, f32[32,2048]{1,0:T(8,128)S(1)}, u32[]{:S(2)}) copy-start(f32[32,2048]{1,0:T(8,128)S(1)} %collective-permute-done.38.across) | copy-start | bytes 786436
  (14 other events, 11.0 us)

commit v6 on v5

--- a/solution.py
+++ b/solution.py
@@ -242,36 +242,28 @@
     )
 
 
-def outgoing_kernel(weight, outgoing, columns, semaphore):
+def prepare_kernel(
+    owner,
+    slot,
+    pool,
+    tails,
+    weight,
+    away_0,
+    away_1,
+    mine,
+    chip,
+    tail_away,
+    tail_mine,
+    tail_chip,
+    outgoing,
+    columns,
+    semaphore,
+):
     _, _, hi, lo, core = place_in_mesh()
     half = columns.shape[1]
     start = pl.multiple_of(((3 - 2 * hi - lo) * 2 + core) * half, half)
     copy = pltpu.make_async_copy(weight.at[:, pl.ds(start, half)], columns, semaphore)
     copy.start()
-    copy.wait()
-    outgoing[...] = columns[...].astype(jnp.float32)
-
-
-def outgoing_weights(weight):
-    half = weight.shape[1] // 8
-    return pl.pallas_call(
-        outgoing_kernel,
-        in_specs=[pl.BlockSpec(memory_space=pl.ANY)],
-        out_specs=pl.BlockSpec(memory_space=pltpu.VMEM),
-        out_shape=jax.ShapeDtypeStruct((weight.shape[0], half), jnp.float32),
-        scratch_shapes=[
-            pltpu.VMEM((weight.shape[0], half), weight.dtype),
-            pltpu.SemaphoreType.DMA,
-        ],
-        compiler_params=pltpu.CompilerParams(vmem_limit_bytes=VMEM),
-        cost_estimate=pl.CostEstimate(flops=0, bytes_accessed=3 * MIB, transcendentals=0),
-    )(weight)
-
-
-def prepare_kernel(
-    owner, slot, pool, tails, _, away_0, away_1, mine, chip, tail_away, tail_mine, tail_chip
-):
-    _, _, _, lo, core = place_in_mesh()
     me = 2 * lo + core
     for j in range(2):
         away = (away_0, away_1)[j]
@@ -286,10 +278,13 @@
             at = slot[request]
             state[...] = jnp.where(here, pool[at], 0.0)
             tail[...] = jnp.where(here, tails[at], 0.0)
-
-
-def prepare(owner, slot, pool, tails, outgoing):
+    copy.wait()
+    outgoing[...] = columns[...].astype(jnp.float32)
+
+
+def prepare(owner, slot, pool, tails, weight):
     _, width, state = pool.shape
+    half = weight.shape[1] // 8
     columns = tails.shape[2]
     vmem = pl.BlockSpec(memory_space=pltpu.VMEM)
     smem = pl.BlockSpec(memory_space=pltpu.SMEM)
@@ -301,15 +296,20 @@
         (2, 2, 8, columns),
         (2, 8, columns),
         (2, 8, columns),
+        (weight.shape[0], half),
     )
     return pl.pallas_call(
         prepare_kernel,
         in_specs=[smem, smem, vmem, vmem, pl.BlockSpec(memory_space=pl.ANY)],
         out_specs=[vmem] * len(shapes),
         out_shape=[jax.ShapeDtypeStruct(s, jnp.float32) for s in shapes],
+        scratch_shapes=[
+            pltpu.VMEM((weight.shape[0], half), weight.dtype),
+            pltpu.SemaphoreType.DMA,
+        ],
         compiler_params=pltpu.CompilerParams(vmem_limit_bytes=VMEM),
         cost_estimate=pl.CostEstimate(flops=0, bytes_accessed=7 * MIB, transcendentals=0),
-    )(owner, slot, pool, tails, outgoing)
+    )(owner, slot, pool, tails, weight)
 
 
 def gate_kernel(
@@ -389,7 +389,7 @@
 
 def choose(near, far, *others):
     rows, columns = near.shape
-    tile = pl.BlockSpec((rows, 128), lambda i: (0, i))
+    tile = pl.BlockSpec((rows // 2, columns), lambda i: (i, 0))
 
     def kernel(near_ref, far_ref, *refs):
         core = lax.axis_index("req") & 1
@@ -397,7 +397,7 @@
 
     return pl.pallas_call(
         kernel,
-        grid=(columns // 128,),
+        grid=(2,),
         in_specs=[tile] * 2 + [pl.BlockSpec(memory_space=pl.ANY)] * len(others),
         out_specs=tile,
         out_shape=jax.ShapeDtypeStruct(near.shape, near.dtype),
@@ -702,16 +702,15 @@
     pool_slot,
     lengths,
 ):
-    outgoing = outgoing_weights(out_weight)
-    w_near = swap(outgoing, hi=1, lo=1)
     group = lax.axis_index("head").astype(jnp.uint32) * a_log.shape[0] >> 5
     bc_tail = pool_bctail.reshape(pool_bctail.shape[:2] + (2, GROUPS, STATE))
     bc_tail = lax.dynamic_index_in_dim(bc_tail, group, 3, keepdims=False)
     tails = jnp.concatenate([pool_xtail, bc_tail.reshape(bc_tail.shape[:2] + (2 * STATE,))], axis=-1)
     tails = jnp.pad(tails.astype(jnp.float32), ((0, 0), (5, 0), (0, 0)))
-    away_0, away_1, mine, chip, tail_away, tail_mine, tail_chip = prepare(
-        pool_dev.reshape(-1), pool_slot, pool_state, tails, outgoing
-    )
+    away_0, away_1, mine, chip, tail_away, tail_mine, tail_chip, outgoing = prepare(
+        pool_dev.reshape(-1), pool_slot, pool_state, tails, out_weight
+    )
+    w_near = swap(outgoing, hi=1, lo=1)
     tail_near = swap(tail_away, core=1)
     near_0 = swap(away_0, core=1)
     near_1 = swap(away_1, core=1)

time: 271 us -> 267 us (0.985)
  Pallas kernels: 106 us -> 101 us
    pallas_call x4 -> x3, Pallas kernels: 13 us -> 6.21 us  [choose(): pl.pallas_call(kernel, grid=(2,), in_specs=[tile] * 2 + [pl.BlockSpec(mem...]
  transfers between devices with their start and end apart: 40 -> 40, of which waited for: 25 -> 24; matrix products, arithmetic and copies ran while one was open for 2% -> 2% of each run, Pallas kernels for 31% -> 30%
where the time goes in v6:
time: 267 us; the launch traced here: 266 us
  Pallas kernels  101 us (38%)
  waiting for transfers between devices  95.5 us (36%)
  starting transfers between devices  46.3 us (17%)
  local copies, waits for them, and re-layouts  17.2 us (6%)
  other arithmetic  5.1 us (2%)
    ppermute x37, waiting for transfers between devices, swap(): return lax.ppermute(array, AXES, pairs)  78.5 us
    ppermute x37, starting transfers between devices, swap(): return lax.ppermute(array, AXES, pairs)  45.3 us
    pallas_call x6, Pallas kernels, product(): pl.pallas_call(kernel, grid=(2 * tiles,), in_specs=[pl.BlockSpec(b.shape,...  38.7 us
    ppermute x3, waiting for transfers between devices, cross(): return lax.ppermute(array, AXES, pairs)  17 us
    pallas_call x1, Pallas kernels, scan(): pl.pallas_call(scan_kernel, grid=(requests, length // BLOCK), in_specs=[p...  16.4 us
    unnamed x77, local copies, waits for them, and re-layouts  14.6 us
    pallas_call x5, Pallas kernels, relay(): pl.pallas_call(kernel, grid=(2,), in_specs=[tile] * 4 + [pl.BlockSpec(mem...  11.9 us
    pallas_call x2, Pallas kernels, combine(): pl.pallas_call(kernel, grid=(columns // TILE,), in_specs=specs + [pl.Bloc...  9.82 us
  transfers between devices with their start and end apart: 40, of which 24 were waited for; matrix products, arithmetic and copies ran while one was open for 2% of the time, Pallas kernels for 30%

profile of v6, /device:TPU:0, one launch (start us, length us, event | category | flops | bytes accessed | tf_op | source)
XLA Modules:
  0.0 266.1 jit_solution(3185706774748083930)
XLA Ops:
  3.1 5.6 %shard_map.158 = (f32[2,512,256]{2,1,0:T(8,128)}, f32[2,512,256]{2,1,0:T(8,128)}, f32[2,512,256]{2,1,0:T(8,128)}, f32[2,512,256]{2,1,0:T(8,128)}, f32[2,2,8,1024...) custom-call(s32[8]{0:T(128)} %bitcast.21, s32[8]{0:T(128)} %slot.1, ...), custom_call_target="tpu_custom_call" | custom-call | bytes 7340032 | tf_op jit(solution)/shard_map/pallas_call | solution.py:301
  9.3 2.8 %collective-permute-start.9 = (f32[512,1024]{1,0:T(8,128)}, f32[512,1024]{1,0:T(8,128)S(1)}, u32[]{:S(2)}, u32[]{:S(2)}) collective-permute-start(f32[512,1024]{1,0:T(8,128)} %get-tuple-element.75), channel_id=1, source_target_pairs={{0,65},{1,64},{2,67},{3,66},{4,69},{5,68},{6,71},{7,70},{8,73},{9,... | collective-permute-start | bytes 6291464 | tf_op jit(solution)/shard_map/ppermute | solution.py:24
  13.2 1.3 collective-permute-done
  15.6 4.0 %collective-permute-done.1.refs_1_ = f32[2,8,1024]{2,1,0:T(8,128)S(1)} collective-permute-done((f32[2,8,1024]{2,1,0:T(8,128)S(1)}, f32[2,8,1024]{2,1,0:T(8,128)S(1)}, u32[]{:S(2)}, u32[]{:S(2)}) %collective-permute-start.1) | collective-permute-done | bytes 65568 | tf_op jit(solution)/shard_map/ppermute | solution.py:24
  20.3 3.0 %fusion = (f32[512,256]{1,0:T(8,128)}, f32[512,256]{1,0:T(8,128)}) fusion(f32[2,512,256]{2,1,0:T(8,128)} %collective-permute-done.3.near_1, f32[2,512,256]{2,1,0:T(8,128)} %shard_map.160, f32[2,512,256]{2,1,0:T(8,128)S(1)} %collective-permute-done.2.near_0), kind=kLoop, calls=%fused_computation.1 | loop fusion | flops 262144 | bytes 3145728 | tf_op jit(solution)/shard_map/add | solution.py:721
  23.5 1.8 collective-permute-start.4
  26.6 16.4 %shard_map.159 = (f32[2,512,512]{2,1,0:T(8,128)}, bf16[2,512,256]{2,1,0:T(8,128)(2,1)}, f32[2,512,8]{2,1,0:T(8,128)}, f32[2,512,256]{2,1,0:T(8,128)}) custom-call(s32[2]{0:T(128)} %lengths.3, bf16[2,512,512]{2,1,0:T(8,128)(2,1)} %x_ref.1, bf16[2,512,4096]{2,1,0:T(8,128)(2,1)} %c_ref.1, bf16[2,512,4096]{2,1,0:T(8,128)(2,1)} %c_ref.1, ...), custom_call_target="tpu_custom_call" | custom-call | flops 872415232 | bytes 12582912 | tf_op jit(solution)/shard_map/pallas_call | solution.py:182
  43.0 4.9 %collective-permute-done.4.far_0 = f32[512,256]{1,0:T(8,128)} collective-permute-done((f32[512,256]{1,0:T(8,128)}, f32[512,256]{1,0:T(8,128)}, u32[]{:S(2)}, u32[]{:S(2)}) %collective-permute-start.4) | collective-permute-done | bytes 524320 | tf_op jit(solution)/shard_map/ppermute | solution.py:24
  48.0 6.9 %shard_map.161 = (f32[256,512]{1,0:T(8,128)}, f32[512,512]{1,0:T(8,128)}, f32[256,512]{1,0:T(8,128)}, f32[2,512,256]{2,1,0:T(8,128)}) custom-call(s32[2]{0:T(128)} %lengths.3, f32[2,512,512]{2,1,0:T(8,128)} %get-tuple-element.66.y_ref, bf16[2,512,256]{2,1,0:T(8,128)(2,1)} %get-tuple-element.67.c_ref, f32[2,512,8]{2,1,0:T(8,128)} %get-tuple-element.68.decay_ref, ...), custom_call_target="tpu_custom_call" | custom-call | flops 268435456 | bytes 12582912 | tf_op jit(solution)/shard_map/pallas_call | solution.py:360
  54.9 1.5 collective-permute-start.7
  56.6 13.0 %collective-permute-done.7.far_ref.refs_3_ = f32[256,512]{1,0:T(8,128)S(1)} collective-permute-done((f32[256,512]{1,0:T(8,128)}, f32[256,512]{1,0:T(8,128)S(1)}, u32[]{:S(2)}, u32[]{:S(2)}) %collective-permute-start.7) | collective-permute-done | bytes 524320 | tf_op jit(solution)/shard_map/ppermute | solution.py:24
  71.2 1.9 shard_map.162.refs_1_
  73.1 1.3 copy-done.4
  74.8 8.8 %collective-permute-done.8.refs_2_.refs_1_ = f32[256,512]{1,0:T(8,128)S(1)} collective-permute-done((f32[256,512]{1,0:T(8,128)S(1)}, f32[256,512]{1,0:T(8,128)S(1)}, u32[]{:S(2)}, u32[]{:S(2)}) %collective-permute-start.8) | collective-permute-done | bytes 524320 | tf_op jit(solution)/shard_map/ppermute | solution.py:31
  84.5 2.8 %collective-permute-start.14 = (f32[512,512]{1,0:T(8,128)}, f32[512,512]{1,0:T(8,128)S(1)}, u32[]{:S(2)}, u32[]{:S(2)}) collective-permute-start(f32[512,512]{1,0:T(8,128)} %shard_map.166.refs_0_), channel_id=1, source_target_pairs={{0,65},{1,64},{2,67},{3,66},{4,69},{5,68},{6,71},{7,70},{8,73},{9,... | collective-permute-start | bytes 3145736 | tf_op jit(solution)/shard_map/ppermute | solution.py:24
  87.3 7.1 %shard_map.164 = (f32[128,2048]{1,0:T(8,128)}, f32[128,2048]{1,0:T(8,128)}, bf16[512,2048]{1,0:T(8,128)(2,1)}) custom-call(f32[256,512]{1,0:T(8,128)} %get-tuple-element.74.refs_0_, f32[256,512]{1,0:T(8,128)} %copy-done.6, f32[256,512]{1,0:T(8,128)} %copy-done.7, f32[256,512]{1,0:T(8,128)} %copy-done.5, bf16[512,8192]{1,0:T(8,128)(2,1)} %refs_4_.11, ...), custom_call_target="tpu_custom_call" | custom-call | flops 1073741824 | bytes 6815744 | tf_op jit(solution)/shard_map/pallas_call | solution.py:487
  94.4 3.0 %collective-permute-start.12 = (f32[128,2048]{1,0:T(8,128)}, f32[128,2048]{1,0:T(8,128)S(1)}, u32[]{:S(2)}, u32[]{:S(2)}) collective-permute-start(f32[128,2048]{1,0:T(8,128)} %get-tuple-element.81), channel_id=1, source_target_pairs={{0,6},{1,7},{2,4},{3,5},{4,2},{5,3},{6,0},{7,1},{8,14},{9,15},{10,... | collective-permute-start | bytes 3145736 | tf_op jit(solution)/shard_map/ppermute | solution.py:24
  97.5 5.7 %shard_map.165 = (f32[64,2048]{1,0:T(8,128)}, f32[64,2048]{1,0:T(8,128)}, f32[64,2048]{1,0:T(8,128)}, f32[64,2048]{1,0:T(8,128)}) custom-call(f32[256,512]{1,0:T(8,128)} %get-tuple-element.74.refs_0_, f32[256,512]{1,0:T(8,128)} %copy-done.6, f32[256,512]{1,0:T(8,128)} %copy-done.7, f32[256,512]{1,0:T(8,128)} %copy-done.5, bf16[512,8192]{1,0:T(8,128)(2,1)} %refs_4_.11, ...), custom_call_target="tpu_custom_call" | custom-call | flops 1073741824 | bytes 6815744 | tf_op jit(solution)/shard_map/pallas_call | solution.py:487
  103.2 8.2 %collective-permute-done.14.far_ref.refs_3_ = f32[512,512]{1,0:T(8,128)S(1)} collective-permute-done((f32[512,512]{1,0:T(8,128)}, f32[512,512]{1,0:T(8,128)S(1)}, u32[]{:S(2)}, u32[]{:S(2)}) %collective-permute-start.14) | collective-permute-done | bytes 1048608 | tf_op jit(solution)/shard_map/ppermute | solution.py:24
  111.5 1.3 collective-permute-done.13.near_ref.refs_1_
  112.8 1.0 copy-done.1
  113.8 2.4 shard_map.167.refs_4_
  117.5 2.4 shard_map.168
  119.8 3.0 %collective-permute-start.15 = (f32[64,2048]{1,0:T(8,128)}, f32[64,2048]{1,0:T(8,128)S(1)}, u32[]{:S(2)}, u32[]{:S(2)}) collective-permute-start(f32[64,2048]{1,0:T(8,128)} %get-tuple-element.83), channel_id=1, source_target_pairs={{0,6},{1,7},{2,4},{3,5},{4,2},{5,3},{6,0},{7,1},{8,14},{9,15},{10,... | collective-permute-start | bytes 1572872 | tf_op jit(solution)/shard_map/ppermute | solution.py:24
  123.0 8.2 %collective-permute-done.17.refs_2_.refs_1_ = f32[512,512]{1,0:T(8,128)S(1)} collective-permute-done((f32[512,512]{1,0:T(8,128)}, f32[512,512]{1,0:T(8,128)S(1)}, u32[]{:S(2)}, u32[]{:S(2)}) %collective-permute-start.17) | collective-permute-done | bytes 1048608 | tf_op jit(solution)/shard_map/ppermute | solution.py:31
  131.2 1.0 collective-permute-done.16.refs_6_.refs_5_
  133.1 7.4 %shard_map.169 = (f32[256,2048]{1,0:T(8,128)}, f32[256,2048]{1,0:T(8,128)}) custom-call(f32[512,512]{1,0:T(8,128)} %shard_map.166.refs_0_, f32[512,512]{1,0:T(8,128)} %copy-done.1, f32[512,512]{1,0:T(8,128)} %copy-done.2, f32[512,512]{1,0:T(8,128)} %copy-done, bf16[512,8192]{1,0:T(8,128)(2,1)} %refs_4_.11, bf16[512,2048]{1,0:T(8,128)(2,1)} %get-tuple-element.76.refs_5_, ...), custom_call_target="tpu_custom_call" | custom-call | flops 2147483648 | bytes 9437184 | tf_op jit(solution)/shard_map/pallas_call | solution.py:487
  140.5 3.0 %collective-permute-start.19 = (f32[256,2048]{1,0:T(8,128)}, f32[256,2048]{1,0:T(8,128)S(1)}, u32[]{:S(2)}, u32[]{:S(2)}) collective-permute-start(f32[256,2048]{1,0:T(8,128)} %get-tuple-element.90), channel_id=1, source_target_pairs={{0,6},{1,7},{2,4},{3,5},{4,2},{5,3},{6,0},{7,1},{8,14},{9,15},{10,... | collective-permute-start | bytes 6291464 | tf_op jit(solution)/shard_map/ppermute | solution.py:24
  143.7 1.8 collective-permute-start.21
  145.5 7.3 %shard_map.170 = (f32[128,2048]{1,0:T(8,128)}, f32[128,2048]{1,0:T(8,128)}, f32[128,2048]{1,0:T(8,128)}, f32[128,2048]{1,0:T(8,128)}) custom-call(f32[512,512]{1,0:T(8,128)} %shard_map.166.refs_0_, f32[512,512]{1,0:T(8,128)} %copy-done.1, f32[512,512]{1,0:T(8,128)} %copy-done.2, f32[512,512]{1,0:T(8,128)} %copy-done, bf16[512,8192]{1,0:T(8,128)(2,1)} %refs_4_.11, ...), custom_call_target="tpu_custom_call" | custom-call | flops 2147483648 | bytes 9437184 | tf_op jit(solution)/shard_map/pallas_call | solution.py:487
  152.8 6.4 %collective-permute-done.21.far_ref.refs_3_ = f32[256,512]{1,0:T(8,128)S(1)} collective-permute-done((f32[256,512]{1,0:T(8,128)}, f32[256,512]{1,0:T(8,128)S(1)}, u32[]{:S(2)}, u32[]{:S(2)}) %collective-permute-start.21) | collective-permute-done | bytes 524320 | tf_op jit(solution)/shard_map/ppermute | solution.py:24
  160.5 1.9 shard_map.172.refs_4_
  162.7 5.2 %collective-permute-done.19.refs_3_.refs_10_ = f32[256,2048]{1,0:T(8,128)S(1)} collective-permute-done((f32[256,2048]{1,0:T(8,128)}, f32[256,2048]{1,0:T(8,128)S(1)}, u32[]{:S(2)}, u32[]{:S(2)}) %collective-permute-start.19) | collective-permute-done | bytes 2097184 | tf_op jit(solution)/shard_map/ppermute | solution.py:24
  168.0 1.9 collective-permute-done.18.refs_2_.refs_7_
  169.9 3.2 %shard_map.173 = (f32[128,2048]{1,0:T(8,128)}, f32[128,2048]{1,0:T(8,128)}) custom-call(f32[128,2048]{1,0:T(8,128)} %get-tuple-element.88.refs_0_, f32[128,2048]{1,0:T(8,128)} %get-tuple-element.89.refs_1_, f32[256,2048]{1,0:T(8,128)} %collective-permute-done.18.refs_2_.refs_7_, f32[256,2048]{1,0:T(8,128)} %copy-done.3, f32[256,512]{1,0:T(8,128)} %shard_map.172.refs_4_), custom_call_target="tpu_custom_call" | custom-call | bytes 6291456 | tf_op jit(solution)/shard_map/pallas_call | solution.py:515
  173.1 2.4 collective-permute-start.22
  176.4 5.6 %shard_map.174 = (f32[128,2048]{1,0:T(8,128)}, f32[128,2048]{1,0:T(8,128)}) custom-call(f32[256,512]{1,0:T(8,128)} %shard_map.171.refs_0_, f32[256,512]{1,0:T(8,128)} %copy-done.9, f32[256,512]{1,0:T(8,128)} %copy-done.19, f32[256,512]{1,0:T(8,128)} %copy-done.8, bf16[512,8192]{1,0:T(8,128)(2,1)} %refs_4_.11, bf16[512,2048]{1,0:T(8,128)(2,1)} %get-tuple-element.76.refs_5_, ...), custom_call_target="tpu_custom_call" | custom-call | flops 1073741824 | bytes 6815744 | tf_op jit(solution)/shard_map/pallas_call | solution.py:487
  182.8 1.4 collective-permute-start.27
  184.2 5.6 %shard_map.175 = (f32[64,2048]{1,0:T(8,128)}, f32[64,2048]{1,0:T(8,128)}, f32[64,2048]{1,0:T(8,128)}, f32[64,2048]{1,0:T(8,128)}) custom-call(f32[256,512]{1,0:T(8,128)} %shard_map.171.refs_0_, f32[256,512]{1,0:T(8,128)} %copy-done.9, f32[256,512]{1,0:T(8,128)} %copy-done.19, f32[256,512]{1,0:T(8,128)} %copy-done.8, bf16[512,8192]{1,0:T(8,128)(2,1)} %refs_4_.11, ...), custom_call_target="tpu_custom_call" | custom-call | flops 1073741824 | bytes 6815744 | tf_op jit(solution)/shard_map/pallas_call | solution.py:487
  190.8 5.9 %shard_map.176 = (f32[96,2048]{1,0:T(8,128)}, f32[96,2048]{1,0:T(8,128)}, f32[48,2048]{1,0:T(8,128)}, f32[48,2048]{1,0:T(8,128)}, f32[48,2048]{1,0:T(8,128)}, /*index=5*/f32[48,2048]{1,0:T(8,128)}) custom-call(f32[64,2048]{1,0:T(8,128)} %get-tuple-element.78.refs_0_, f32[128,2048]{1,0:T(8,128)} %collective-permute-done.11.refs_2_.refs_1_, ...), custom_call_target="tpu_custom_call" | custom-call | bytes 12582912 | tf_op jit(solution)/shard_map/pallas_call | solution.py:559
  196.6 2.0 collective-permute-start.25
  198.6 2.5 collective-permute-start.26
  201.2 4.0 %collective-permute-done.27.refs_2_.refs_1_ = f32[128,2048]{1,0:T(8,128)S(1)} collective-permute-done((f32[128,2048]{1,0:T(8,128)}, f32[128,2048]{1,0:T(8,128)S(1)}, u32[]{:S(2)}, u32[]{:S(2)}) %collective-permute-start.27) | collective-permute-done | bytes 1048608 | tf_op jit(solution)/shard_map/ppermute | solution.py:24
  205.2 1.0 copy-done.12
  206.1 2.4 shard_map.177
  208.6 2.3 collective-permute-done.25.refs_2_.refs_1_
  210.9 5.4 %collective-permute-done.26.refs_3_.refs_4_ = f32[96,2048]{1,0:T(8,128)S(1)} collective-permute-done((f32[96,2048]{1,0:T(8,128)}, f32[96,2048]{1,0:T(8,128)S(1)}, u32[]{:S(2)}, u32[]{:S(2)}) %collective-permute-start.26) | collective-permute-done | bytes 786464 | tf_op jit(solution)/shard_map/ppermute | solution.py:24
  217.2 2.2 shard_map.178
  220.4 4.0 %shard_map.179 = (f32[32,2048]{1,0:T(8,128)}, f32[32,2048]{1,0:T(8,128)}, f32[16,2048]{1,0:T(8,128)}, f32[16,2048]{1,0:T(8,128)}, f32[16,2048]{1,0:T(8,128)}, /*index=5*/f32[16,2048]{1,0:T(8,128)}) custom-call(f32[64,2048]{1,0:T(8,128)} %get-tuple-element.96.refs_12_.refs_0_, f32[128,2048]{1,0:T(8,128)} %copy-done.12, f32[64,2048]{1,0:T(8,128)} %copy-done.23, ...), custom_call_target="tpu_custom_call" | custom-call | bytes 4194304 | tf_op jit(solution)/shard_map/pallas_call | solution.py:559
  224.4 3.1 %collective-permute-start.33 = (f32[32,2048]{1,0:T(8,128)}, f32[32,2048]{1,0:T(8,128)S(1)}, u32[]{:S(2)}, u32[]{:S(2)}) collective-permute-start(f32[32,2048]{1,0:T(8,128)} %get-tuple-element.112), channel_id=1, source_target_pairs={{0,8},{1,9},{2,10},{3,11},{4,12},{5,13},{6,14},{7,15},{8,0},{9,1},... | collective-permute-start | bytes 786440 | tf_op jit(solution)/shard_map/ppermute | solution.py:24
  227.5 2.5 collective-permute-start.34
  232.0 3.2 %collective-permute-done.34.refs_3_.refs_10_ = f32[32,2048]{1,0:T(8,128)S(1)} collective-permute-done((f32[32,2048]{1,0:T(8,128)}, f32[32,2048]{1,0:T(8,128)S(1)}, u32[]{:S(2)}, u32[]{:S(2)}) %collective-permute-start.34) | collective-permute-done | bytes 262176 | tf_op jit(solution)/shard_map/ppermute | solution.py:24
  236.0 1.7 shard_map.180
  237.7 2.5 collective-permute-start.35
  240.4 3.7 %collective-permute-done.35.refs_8_ = f32[16,2048]{1,0:T(8,128)S(1)} collective-permute-done((f32[16,2048]{1,0:T(8,128)}, f32[16,2048]{1,0:T(8,128)S(1)}, u32[]{:S(2)}, u32[]{:S(2)}) %collective-permute-start.35) | collective-permute-done | bytes 131104 | tf_op jit(solution)/shard_map/ppermute | solution.py:24
  244.1 1.3 collective-permute-done.36.refs_11_
  246.1 3.2 %shard_map.181 = (f32[32,2048]{1,0:T(8,128)}, f32[32,2048]{1,0:T(8,128)}, f32[32,2048]{1,0:T(8,128)}, f32[32,2048]{1,0:T(8,128)}) custom-call(f32[48,2048]{1,0:T(8,128)} %get-tuple-element.97.refs_4_.refs_0_, f32[96,2048]{1,0:T(8,128)} %copy-done.13, f32[48,2048]{1,0:T(8,128)} %copy-done.26, f32[48,2048]{1,0:T(8,128)} %get-tuple-element.107.refs_3_, ...), custom_call_target="tpu_custom_call" | custom-call | bytes 4194304 | tf_op jit(solution)/shard_map/pallas_call | solution.py:593
  249.3 1.5 collective-permute-start.37
  250.8 2.2 collective-permute-start.38
  253.0 1.0 collective-permute-start.39
  254.0 1.9 collective-permute-done.37.near
  255.9 4.5 %collective-permute-done.38.across = f32[32,2048]{1,0:T(8,128)S(1)} collective-permute-done((f32[32,2048]{1,0:T(8,128)}, f32[32,2048]{1,0:T(8,128)S(1)}, u32[]{:S(2)}, u32[]{:S(2)}) %collective-permute-start.38) | collective-permute-done | bytes 262176 | tf_op jit(solution)/shard_map/ppermute | solution.py:24
  260.4 2.7 %collective-permute-done.39.far = f32[32,2048]{1,0:T(8,128)S(1)} collective-permute-done((f32[32,2048]{1,0:T(8,128)}, f32[32,2048]{1,0:T(8,128)S(1)}, u32[]{:S(2)}, u32[]{:S(2)}) %collective-permute-start.39) | collective-permute-done | bytes 262176 | tf_op jit(solution)/shard_map/ppermute | solution.py:24
  263.8 2.2 shard_map.182
  (128 shorter events, 23.4 us)
Async XLA Ops:
  8.7 11.6 %collective-permute-start.2 = (f32[2,512,256]{2,1,0:T(8,128)}, f32[2,512,256]{2,1,0:T(8,128)S(1)}, u32[]{:S(2)}, u32[]{:S(2)}) collective-permute-start(f32[2,512,256]{2,1,0:T(8,128)} %get-tuple-element.71), channel_id=1, source_target_pairs={{0,32},{1,33},{2,34},{3,35},{4,36},{5,37},{6,38},{7,39},{8,40},{9,... | collective-permute-start | bytes 3145736 | tf_op jit(solution)/shard_map/ppermute | solution.py:24
  8.8 11.5 %collective-permute-start.3 = (f32[2,512,256]{2,1,0:T(8,128)}, f32[2,512,256]{2,1,0:T(8,128)}, u32[]{:S(2)}, u32[]{:S(2)}) collective-permute-start(f32[2,512,256]{2,1,0:T(8,128)} %get-tuple-element.72), channel_id=1, source_target_pairs={{0,32},{1,33},{2,34},{3,35},{4,36},{5,37},{6,38},{7,39},{8,40},{9,... | collective-permute-start | bytes 3145736 | tf_op jit(solution)/shard_map/ppermute | solution.py:24
  9.3 63.8 %collective-permute-start.9 = (f32[512,1024]{1,0:T(8,128)}, f32[512,1024]{1,0:T(8,128)S(1)}, u32[]{:S(2)}, u32[]{:S(2)}) collective-permute-start(f32[512,1024]{1,0:T(8,128)} %get-tuple-element.75), channel_id=1, source_target_pairs={{0,65},{1,64},{2,67},{3,66},{4,69},{5,68},{6,71},{7,70},{8,73},{9,... | collective-permute-start | bytes 6291464 | tf_op jit(solution)/shard_map/ppermute | solution.py:24
  13.1 1.4 collective-permute-start
  15.3 4.3 %collective-permute-start.1 = (f32[2,8,1024]{2,1,0:T(8,128)S(1)}, f32[2,8,1024]{2,1,0:T(8,128)S(1)}, u32[]{:S(2)}, u32[]{:S(2)}) collective-permute-start(f32[2,8,1024]{2,1,0:T(8,128)S(1)} %fusion.6), channel_id=1, source_target_pairs={{0,64},{1,65},{2,66},{3,67},{4,68},{5,69},{6,70},{7,71},{8,72},{9,... | collective-permute-start | bytes 196616 | tf_op jit(solution)/shard_map/ppermute | solution.py:24
  20.3 5.0 %copy-start.36 = (f32[8]{0:T(128)S(1)}, f32[8]{0:T(128)}, u32[]{:S(2)}) copy-start(f32[8]{0:T(128)} %param.19) | copy-start | bytes 100
  20.3 5.7 %copy-start.29 = (f32[2,8,1024]{2,1,0:T(8,128)S(1)}, f32[2,8,1024]{2,1,0:T(8,128)}, u32[]{:S(2)}) copy-start(f32[2,8,1024]{2,1,0:T(8,128)} %copy-done.28) | copy-start | bytes 196612
  20.3 5.7 %copy-start.35 = (f32[2,8,1024]{2,1,0:T(8,128)S(1)}, f32[2,8,1024]{2,1,0:T(8,128)}, u32[]{:S(2)}) copy-start(f32[2,8,1024]{2,1,0:T(8,128)} %get-tuple-element.63) | copy-start | bytes 196612
  20.3 22.7 %copy-start.15 = (f32[2,512,256]{2,1,0:T(8,128)}, f32[2,512,256]{2,1,0:T(8,128)S(1)}, u32[]{:S(2)}) copy-start(f32[2,512,256]{2,1,0:T(8,128)S(1)} %collective-permute-done.2.near_0) | copy-start | bytes 3145732
  23.3 19.7 %collective-permute-start.5 = (f32[512,256]{1,0:T(8,128)}, f32[512,256]{1,0:T(8,128)}, u32[]{:S(2)}, u32[]{:S(2)}) collective-permute-start(f32[512,256]{1,0:T(8,128)} %get-tuple-element.124), channel_id=1, source_target_pairs={{0,64},{1,65},{2,66},{3,67},{4,68},{5,69},{6,70},{7,71},{8,72},{9,... | collective-permute-start | bytes 1572872 | tf_op jit(solution)/shard_map/ppermute | solution.py:24
  23.5 24.4 %collective-permute-start.4 = (f32[512,256]{1,0:T(8,128)}, f32[512,256]{1,0:T(8,128)}, u32[]{:S(2)}, u32[]{:S(2)}) collective-permute-start(f32[512,256]{1,0:T(8,128)} %get-tuple-element.125), channel_id=1, source_target_pairs={{0,64},{1,65},{2,66},{3,67},{4,68},{5,69},{6,70},{7,71},{8,72},{9,... | collective-permute-start | bytes 1572872 | tf_op jit(solution)/shard_map/ppermute | solution.py:24
  54.9 14.7 %collective-permute-start.7 = (f32[256,512]{1,0:T(8,128)}, f32[256,512]{1,0:T(8,128)S(1)}, u32[]{:S(2)}, u32[]{:S(2)}) collective-permute-start(f32[256,512]{1,0:T(8,128)} %get-tuple-element.74.refs_0_), channel_id=1, source_target_pairs={{0,65},{1,64},{2,67},{3,66},{4,69},{5,68},{6,71},{7,70},{8,73},{9,... | collective-permute-start | bytes 1572872 | tf_op jit(solution)/shard_map/ppermute | solution.py:24
  56.4 13.2 %collective-permute-start.6 = (f32[256,512]{1,0:T(8,128)}, f32[256,512]{1,0:T(8,128)S(1)}, u32[]{:S(2)}, u32[]{:S(2)}) collective-permute-start(f32[256,512]{1,0:T(8,128)} %get-tuple-element.74.refs_0_), channel_id=1, source_target_pairs={{0,64},{1,65},{2,66},{3,67},{4,68},{5,69},{6,70},{7,71},{8,72},{9,... | collective-permute-start | bytes 1572872 | tf_op jit(solution)/shard_map/ppermute | solution.py:24
  73.1 1.4 copy-start.18
  73.1 1.3 copy-start.4
  74.4 12.9 %collective-permute-start.10 = (f32[512,1024]{1,0:T(8,128)}, f32[512,1024]{1,0:T(8,128)}, u32[]{:S(2)}, u32[]{:S(2)}) collective-permute-start(f32[512,1024]{1,0:T(8,128)} %shard_map.163.refs_5_), channel_id=1, source_target_pairs={{0,32},{1,33},{2,34},{3,35},{4,36},{5,37},{6,38},{7,39},{8,40},{9,... | collective-permute-start | bytes 6291464 | tf_op jit(solution)/shard_map/ppermute | solution.py:24
  74.5 9.2 %collective-permute-start.8 = (f32[256,512]{1,0:T(8,128)S(1)}, f32[256,512]{1,0:T(8,128)S(1)}, u32[]{:S(2)}, u32[]{:S(2)}) collective-permute-start(f32[256,512]{1,0:T(8,128)S(1)} %copy-done.18), channel_id=1, source_target_pairs={{0,64},{1,65},{2,66},{3,67},{4,68},{5,69},{6,70},{7,71},{8,72},{9,... | collective-permute-start | bytes 1572872 | tf_op jit(solution)/shard_map/ppermute | solution.py:31
  84.5 27.0 %collective-permute-start.14 = (f32[512,512]{1,0:T(8,128)}, f32[512,512]{1,0:T(8,128)S(1)}, u32[]{:S(2)}, u32[]{:S(2)}) collective-permute-start(f32[512,512]{1,0:T(8,128)} %shard_map.166.refs_0_), channel_id=1, source_target_pairs={{0,65},{1,64},{2,67},{3,66},{4,69},{5,68},{6,71},{7,70},{8,73},{9,... | collective-permute-start | bytes 3145736 | tf_op jit(solution)/shard_map/ppermute | solution.py:24
  87.3 25.5 %collective-permute-start.13 = (f32[512,512]{1,0:T(8,128)}, f32[512,512]{1,0:T(8,128)S(1)}, u32[]{:S(2)}, u32[]{:S(2)}) collective-permute-start(f32[512,512]{1,0:T(8,128)} %shard_map.166.refs_0_), channel_id=1, source_target_pairs={{0,64},{1,65},{2,66},{3,67},{4,68},{5,69},{6,70},{7,71},{8,72},{9,... | collective-permute-start | bytes 3145736 | tf_op jit(solution)/shard_map/ppermute | solution.py:24
  94.4 22.1 %collective-permute-start.12 = (f32[128,2048]{1,0:T(8,128)}, f32[128,2048]{1,0:T(8,128)S(1)}, u32[]{:S(2)}, u32[]{:S(2)}) collective-permute-start(f32[128,2048]{1,0:T(8,128)} %get-tuple-element.81), channel_id=1, source_target_pairs={{0,6},{1,7},{2,4},{3,5},{4,2},{5,3},{6,0},{7,1},{8,14},{9,15},{10,... | collective-permute-start | bytes 3145736 | tf_op jit(solution)/shard_map/ppermute | solution.py:24
  97.4 19.1 %collective-permute-start.11 = (f32[128,2048]{1,0:T(8,128)}, f32[128,2048]{1,0:T(8,128)}, u32[]{:S(2)}, u32[]{:S(2)}) collective-permute-start(f32[128,2048]{1,0:T(8,128)} %get-tuple-element.77.refs_6_), channel_id=1, source_target_pairs={{0,2},{1,3},{2,0},{3,1},{4,6},{5,7},{6,4},{7,5},{8,10},{9,11},{10,... | collective-permute-start | bytes 3145736 | tf_op jit(solution)/shard_map/ppermute | solution.py:24
  111.5 1.4 copy-start
  112.8 1.0 copy-start.1
  116.2 15.0 %collective-permute-start.17 = (f32[512,512]{1,0:T(8,128)}, f32[512,512]{1,0:T(8,128)S(1)}, u32[]{:S(2)}, u32[]{:S(2)}) collective-permute-start(f32[512,512]{1,0:T(8,128)} %shard_map.167.refs_4_), channel_id=1, source_target_pairs={{0,64},{1,65},{2,66},{3,67},{4,68},{5,69},{6,70},{7,71},{8,72},{9,... | collective-permute-start | bytes 3145736 | tf_op jit(solution)/shard_map/ppermute | solution.py:31
  116.5 1.0 copy-start.10
  119.8 11.4 %collective-permute-start.15 = (f32[64,2048]{1,0:T(8,128)}, f32[64,2048]{1,0:T(8,128)S(1)}, u32[]{:S(2)}, u32[]{:S(2)}) collective-permute-start(f32[64,2048]{1,0:T(8,128)} %get-tuple-element.83), channel_id=1, source_target_pairs={{0,6},{1,7},{2,4},{3,5},{4,2},{5,3},{6,0},{7,1},{8,14},{9,15},{10,... | collective-permute-start | bytes 1572872 | tf_op jit(solution)/shard_map/ppermute | solution.py:24
  122.8 9.4 %collective-permute-start.16 = (f32[64,2048]{1,0:T(8,128)}, f32[64,2048]{1,0:T(8,128)S(1)}, u32[]{:S(2)}, u32[]{:S(2)}) collective-permute-start(f32[64,2048]{1,0:T(8,128)} %get-tuple-element.85.refs_2_), channel_id=1, source_target_pairs={{0,2},{1,3},{2,0},{3,1},{4,6},{5,7},{6,4},{7,5},{8,10},{9,11},{10,... | collective-permute-start | bytes 1572872 | tf_op jit(solution)/shard_map/ppermute | solution.py:24
  131.2 1.0 copy-start.2
  131.2 1.1 copy-start.16
  140.5 27.5 %collective-permute-start.19 = (f32[256,2048]{1,0:T(8,128)}, f32[256,2048]{1,0:T(8,128)S(1)}, u32[]{:S(2)}, u32[]{:S(2)}) collective-permute-start(f32[256,2048]{1,0:T(8,128)} %get-tuple-element.90), channel_id=1, source_target_pairs={{0,6},{1,7},{2,4},{3,5},{4,2},{5,3},{6,0},{7,1},{8,14},{9,15},{10,... | collective-permute-start | bytes 6291464 | tf_op jit(solution)/shard_map/ppermute | solution.py:24
  143.5 26.4 %collective-permute-start.18 = (f32[256,2048]{1,0:T(8,128)}, f32[256,2048]{1,0:T(8,128)}, u32[]{:S(2)}, u32[]{:S(2)}) collective-permute-start(f32[256,2048]{1,0:T(8,128)} %get-tuple-element.86.refs_6_), channel_id=1, source_target_pairs={{0,2},{1,3},{2,0},{3,1},{4,6},{5,7},{6,4},{7,5},{8,10},{9,11},{10,... | collective-permute-start | bytes 6291464 | tf_op jit(solution)/shard_map/ppermute | solution.py:24
  143.7 15.5 %collective-permute-start.21 = (f32[256,512]{1,0:T(8,128)}, f32[256,512]{1,0:T(8,128)S(1)}, u32[]{:S(2)}, u32[]{:S(2)}) collective-permute-start(f32[256,512]{1,0:T(8,128)} %shard_map.171.refs_0_), channel_id=1, source_target_pairs={{0,65},{1,64},{2,67},{3,66},{4,69},{5,68},{6,71},{7,70},{8,73},{9,... | collective-permute-start | bytes 1572872 | tf_op jit(solution)/shard_map/ppermute | solution.py:24
  145.5 14.2 %collective-permute-start.20 = (f32[256,512]{1,0:T(8,128)}, f32[256,512]{1,0:T(8,128)S(1)}, u32[]{:S(2)}, u32[]{:S(2)}) collective-permute-start(f32[256,512]{1,0:T(8,128)} %shard_map.171.refs_0_), channel_id=1, source_target_pairs={{0,64},{1,65},{2,66},{3,67},{4,68},{5,69},{6,70},{7,71},{8,72},{9,... | collective-permute-start | bytes 1572872 | tf_op jit(solution)/shard_map/ppermute | solution.py:24
  162.4 13.1 %collective-permute-start.24 = (f32[256,512]{1,0:T(8,128)}, f32[256,512]{1,0:T(8,128)S(1)}, u32[]{:S(2)}, u32[]{:S(2)}) collective-permute-start(f32[256,512]{1,0:T(8,128)} %shard_map.172.refs_4_), channel_id=1, source_target_pairs={{0,64},{1,65},{2,66},{3,67},{4,68},{5,69},{6,70},{7,71},{8,72},{9,... | collective-permute-start | bytes 1572872 | tf_op jit(solution)/shard_map/ppermute | solution.py:31
  168.0 1.9 copy-start.3
  173.1 16.7 %collective-permute-start.22 = (f32[128,2048]{1,0:T(8,128)}, f32[128,2048]{1,0:T(8,128)S(1)}, u32[]{:S(2)}, u32[]{:S(2)}) collective-permute-start(f32[128,2048]{1,0:T(8,128)} %get-tuple-element.92), channel_id=1, source_target_pairs={{0,6},{1,7},{2,4},{3,5},{4,2},{5,3},{6,0},{7,1},{8,14},{9,15},{10,... | collective-permute-start | bytes 3145736 | tf_op jit(solution)/shard_map/ppermute | solution.py:24
  175.5 15.1 %collective-permute-start.23 = (f32[128,2048]{1,0:T(8,128)}, f32[128,2048]{1,0:T(8,128)}, u32[]{:S(2)}, u32[]{:S(2)}) collective-permute-start(f32[128,2048]{1,0:T(8,128)} %get-tuple-element.94.refs_6_), channel_id=1, source_target_pairs={{0,2},{1,3},{2,0},{3,1},{4,6},{5,7},{6,4},{7,5},{8,10},{9,11},{10,... | collective-permute-start | bytes 3145736 | tf_op jit(solution)/shard_map/ppermute | solution.py:24
  182.0 19.2 %collective-permute-start.28 = (f32[128,2048]{1,0:T(8,128)}, f32[128,2048]{1,0:T(8,128)S(1)}, u32[]{:S(2)}, u32[]{:S(2)}) collective-permute-start(f32[128,2048]{1,0:T(8,128)} %get-tuple-element.104), channel_id=1, source_target_pairs={{0,6},{1,7},{2,4},{3,5},{4,2},{5,3},{6,0},{7,1},{8,14},{9,15},{10,... | collective-permute-start | bytes 3145736 | tf_op jit(solution)/shard_map/ppermute | solution.py:24
  182.8 22.3 %collective-permute-start.27 = (f32[128,2048]{1,0:T(8,128)}, f32[128,2048]{1,0:T(8,128)S(1)}, u32[]{:S(2)}, u32[]{:S(2)}) collective-permute-start(f32[128,2048]{1,0:T(8,128)} %get-tuple-element.95.refs_6_), channel_id=1, source_target_pairs={{0,2},{1,3},{2,0},{3,1},{4,6},{5,7},{6,4},{7,5},{8,10},{9,11},{10,... | collective-permute-start | bytes 3145736 | tf_op jit(solution)/shard_map/ppermute | solution.py:24
  189.8 1.0 copy-start.20
  196.6 14.2 %collective-permute-start.25 = (f32[96,2048]{1,0:T(8,128)}, f32[96,2048]{1,0:T(8,128)S(1)}, u32[]{:S(2)}, u32[]{:S(2)}) collective-permute-start(f32[96,2048]{1,0:T(8,128)} %get-tuple-element.98), channel_id=1, source_target_pairs={{0,8},{1,9},{2,10},{3,11},{4,12},{5,13},{6,14},{7,15},{8,0},{9,1},... | collective-permute-start | bytes 2359304 | tf_op jit(solution)/shard_map/ppermute | solution.py:24
  198.6 17.6 %collective-permute-start.26 = (f32[96,2048]{1,0:T(8,128)}, f32[96,2048]{1,0:T(8,128)S(1)}, u32[]{:S(2)}, u32[]{:S(2)}) collective-permute-start(f32[96,2048]{1,0:T(8,128)} %get-tuple-element.101), channel_id=1, source_target_pairs={{0,24},{1,25},{2,26},{3,27},{4,28},{5,29},{6,30},{7,31},{8,16},{9,... | collective-permute-start | bytes 2359304 | tf_op jit(solution)/shard_map/ppermute | solution.py:24
  201.2 4.0 %copy-start.11 = (f32[128,2048]{1,0:T(8,128)}, f32[128,2048]{1,0:T(8,128)S(1)}, u32[]{:S(2)}) copy-start(f32[128,2048]{1,0:T(8,128)S(1)} %collective-permute-done.28.refs_3_.refs_4_) | copy-start | bytes 3145732
  205.1 1.0 copy-start.12
  208.5 11.0 %collective-permute-start.31 = (f32[64,2048]{1,0:T(8,128)}, f32[64,2048]{1,0:T(8,128)S(1)}, u32[]{:S(2)}, u32[]{:S(2)}) collective-permute-start(f32[64,2048]{1,0:T(8,128)} %get-tuple-element.109), channel_id=1, source_target_pairs={{0,6},{1,7},{2,4},{3,5},{4,2},{5,3},{6,0},{7,1},{8,14},{9,15},{10,... | collective-permute-start | bytes 1572872 | tf_op jit(solution)/shard_map/ppermute | solution.py:24
  208.5 11.0 %collective-permute-start.32 = (f32[64,2048]{1,0:T(8,128)}, f32[64,2048]{1,0:T(8,128)S(1)}, u32[]{:S(2)}, u32[]{:S(2)}) collective-permute-start(f32[64,2048]{1,0:T(8,128)} %get-tuple-element.105.refs_4_), channel_id=1, source_target_pairs={{0,2},{1,3},{2,0},{3,1},{4,6},{5,7},{6,4},{7,5},{8,10},{9,11},{10,... | collective-permute-start | bytes 1572872 | tf_op jit(solution)/shard_map/ppermute | solution.py:24
  210.8 5.4 %copy-start.13 = (f32[96,2048]{1,0:T(8,128)}, f32[96,2048]{1,0:T(8,128)S(1)}, u32[]{:S(2)}) copy-start(f32[96,2048]{1,0:T(8,128)S(1)} %collective-permute-done.25.refs_2_.refs_1_) | copy-start | bytes 2359300
  220.4 9.6 %copy-start.37 = (f32[48,2048]{1,0:T(8,128)S(1)}, f32[48,2048]{1,0:T(8,128)}, u32[]{:S(2)}) copy-start(f32[48,2048]{1,0:T(8,128)} %get-tuple-element.106) | copy-start | bytes 1179652
  220.4 10.3 %copy-start.25 = (f32[48,2048]{1,0:T(8,128)S(1)}, f32[48,2048]{1,0:T(8,128)}, u32[]{:S(2)}) copy-start(f32[48,2048]{1,0:T(8,128)} %get-tuple-element.108.refs_6_) | copy-start | bytes 1179652
  224.4 7.7 %collective-permute-start.33 = (f32[32,2048]{1,0:T(8,128)}, f32[32,2048]{1,0:T(8,128)S(1)}, u32[]{:S(2)}, u32[]{:S(2)}) collective-permute-start(f32[32,2048]{1,0:T(8,128)} %get-tuple-element.112), channel_id=1, source_target_pairs={{0,8},{1,9},{2,10},{3,11},{4,12},{5,13},{6,14},{7,15},{8,0},{9,1},... | collective-permute-start | bytes 786440 | tf_op jit(solution)/shard_map/ppermute | solution.py:24
  227.5 7.8 %collective-permute-start.34 = (f32[32,2048]{1,0:T(8,128)}, f32[32,2048]{1,0:T(8,128)S(1)}, u32[]{:S(2)}, u32[]{:S(2)}) collective-permute-start(f32[32,2048]{1,0:T(8,128)} %get-tuple-element.115), channel_id=1, source_target_pairs={{0,24},{1,25},{2,26},{3,27},{4,28},{5,29},{6,30},{7,31},{8,16},{9,... | collective-permute-start | bytes 786440 | tf_op jit(solution)/shard_map/ppermute | solution.py:24
  230.0 10.3 %collective-permute-start.29 = (f32[48,2048]{1,0:T(8,128)S(1)}, f32[48,2048]{1,0:T(8,128)S(1)}, u32[]{:S(2)}, u32[]{:S(2)}) collective-permute-start(f32[48,2048]{1,0:T(8,128)S(1)} %copy-done.37), channel_id=1, source_target_pairs={{0,24},{1,25},{2,26},{3,27},{4,28},{5,29},{6,30},{7,31},{8,16},{9,... | collective-permute-start | bytes 1179656 | tf_op jit(solution)/shard_map/ppermute | solution.py:24
  230.7 9.6 %collective-permute-start.30 = (f32[48,2048]{1,0:T(8,128)S(1)}, f32[48,2048]{1,0:T(8,128)S(1)}, u32[]{:S(2)}, u32[]{:S(2)}) collective-permute-start(f32[48,2048]{1,0:T(8,128)S(1)} %copy-done.25), channel_id=1, source_target_pairs={{0,8},{1,9},{2,10},{3,11},{4,12},{5,13},{6,14},{7,15},{8,0},{9,1},... | collective-permute-start | bytes 1179656 | tf_op jit(solution)/shard_map/ppermute | solution.py:24
  232.0 3.2 %copy-start.21 = (f32[32,2048]{1,0:T(8,128)}, f32[32,2048]{1,0:T(8,128)S(1)}, u32[]{:S(2)}) copy-start(f32[32,2048]{1,0:T(8,128)S(1)} %collective-permute-done.33.refs_2_.refs_7_) | copy-start | bytes 786436
  237.7 6.4 %collective-permute-start.35 = (f32[16,2048]{1,0:T(8,128)}, f32[16,2048]{1,0:T(8,128)S(1)}, u32[]{:S(2)}, u32[]{:S(2)}) collective-permute-start(f32[16,2048]{1,0:T(8,128)} %get-tuple-element.116), channel_id=1, source_target_pairs={{0,24},{1,25},{2,26},{3,27},{4,28},{5,29},{6,30},{7,31},{8,16},{9,... | collective-permute-start | bytes 393224 | tf_op jit(solution)/shard_map/ppermute | solution.py:24
  240.2 5.2 %collective-permute-start.36 = (f32[16,2048]{1,0:T(8,128)}, f32[16,2048]{1,0:T(8,128)S(1)}, u32[]{:S(2)}, u32[]{:S(2)}) collective-permute-start(f32[16,2048]{1,0:T(8,128)} %get-tuple-element.118), channel_id=1, source_target_pairs={{0,8},{1,9},{2,10},{3,11},{4,12},{5,13},{6,14},{7,15},{8,0},{9,1},... | collective-permute-start | bytes 393224 | tf_op jit(solution)/shard_map/ppermute | solution.py:24
  240.4 5.1 %copy-start.26 = (f32[48,2048]{1,0:T(8,128)}, f32[48,2048]{1,0:T(8,128)S(1)}, u32[]{:S(2)}) copy-start(f32[48,2048]{1,0:T(8,128)S(1)} %collective-permute-done.29.refs_2_) | copy-start | bytes 1179652
  240.4 5.1 %copy-start.27 = (f32[48,2048]{1,0:T(8,128)}, f32[48,2048]{1,0:T(8,128)S(1)}, u32[]{:S(2)}) copy-start(f32[48,2048]{1,0:T(8,128)S(1)} %collective-permute-done.30.refs_5_) | copy-start | bytes 1179652
  244.1 1.3 copy-start.33
  249.3 6.6 %collective-permute-start.37 = (f32[32,2048]{1,0:T(8,128)}, f32[32,2048]{1,0:T(8,128)S(1)}, u32[]{:S(2)}, u32[]{:S(2)}) collective-permute-start(f32[32,2048]{1,0:T(8,128)} %get-tuple-element.120), channel_id=1, source_target_pairs={{0,64},{1,65},{2,66},{3,67},{4,68},{5,69},{6,70},{7,71},{8,72},{9,... | collective-permute-start | bytes 786440 | tf_op jit(solution)/shard_map/ppermute | solution.py:24
  250.8 9.6 %collective-permute-start.38 = (f32[32,2048]{1,0:T(8,128)}, f32[32,2048]{1,0:T(8,128)S(1)}, u32[]{:S(2)}, u32[]{:S(2)}) collective-permute-start(f32[32,2048]{1,0:T(8,128)} %get-tuple-element.121), channel_id=1, source_target_pairs={{0,1},{1,0},{2,3},{3,2},{4,5},{5,4},{6,7},{7,6},{8,9},{9,8},{10,11... | collective-permute-start | bytes 786440 | tf_op jit(solution)/shard_map/ppermute | solution.py:24
  253.0 10.1 %collective-permute-start.39 = (f32[32,2048]{1,0:T(8,128)}, f32[32,2048]{1,0:T(8,128)S(1)}, u32[]{:S(2)}, u32[]{:S(2)}) collective-permute-start(f32[32,2048]{1,0:T(8,128)} %get-tuple-element.122), channel_id=1, source_target_pairs={{0,65},{1,64},{2,67},{3,66},{4,69},{5,68},{6,71},{7,70},{8,73},{9,... | collective-permute-start | bytes 786440 | tf_op jit(solution)/shard_map/ppermute | solution.py:24
  255.9 7.2 %copy-start.30 = (f32[32,2048]{1,0:T(8,128)}, f32[32,2048]{1,0:T(8,128)S(1)}, u32[]{:S(2)}) copy-start(f32[32,2048]{1,0:T(8,128)S(1)} %collective-permute-done.37.near) | copy-start | bytes 786436
  260.4 2.7 %copy-start.31 = (f32[32,2048]{1,0:T(8,128)}, f32[32,2048]{1,0:T(8,128)S(1)}, u32[]{:S(2)}) copy-start(f32[32,2048]{1,0:T(8,128)S(1)} %collective-permute-done.38.across) | copy-start | bytes 786436
  (14 other events, 11.0 us)
